TPU v7x, 32 devices: a whole 2x2x4 slice. The times are simulated.
32 devices in a mesh: section: 1, expert: 32 (over z, y, x, core).
Axes of the slice: x: 2, y: 2, z: 4, core: 2. Of those that a mesh axis runs over, the one named last changes fastest.
Arguments:
- states_orig: bfloat16 [1, 256, 2048], P(None, 'expert'), may hold values from -400 to 400
- states_pruned: bfloat16 [1, 256, 2048], P(None, 'expert'), may hold values from -400 to 400
- ids_orig: int32 [1, 1, 256, 8], P('section', None, 'expert'), may hold values from 0 to 15, all different within a row; in each aligned block of 8 rows (0 to 7, 8 to 15, ..., all dimensions but the last counted through in order) at most 8 rows name the same one
- ids_pruned: int32 [1, 1, 256, 8], P('section', None, 'expert'), may hold values from 0 to 15, all different within a row; in each aligned block of 8 rows (0 to 7, 8 to 15, ..., all dimensions but the last counted through in order) at most 8 rows name the same one
- gates_orig: float32 [1, 1, 256, 8], P('section', None, 'expert'), may hold values from 0.02 to 2.7
- gates_pruned: float32 [1, 1, 256, 8], P('section', None, 'expert'), may hold values from 0.02 to 2.7
- keep_mask: int32 [1, 16], P('section'), may hold values 0 or 1
- w_in: bfloat16 [1, 32, 2048, 768], P('section', 'expert'), may hold values from -0.125 to 0.125
- w_out: bfloat16 [1, 32, 384, 2048], P('section', 'expert'), may hold values from -0.21875 to 0.21875
Outputs:
- moe_orig: bfloat16 [1, 1, 256, 2048], P('section', None, 'expert')
- moe_pruned: bfloat16 [1, 1, 256, 2048], P('section', None, 'expert')
- expert_loss: float32 [1, 16], P('section')
Inputs may be any that keep to these rules, and one draw needn't show every extreme that they name: `ids_orig`: for each layer, micro-batch and device along expert, no expert is picked by more than 8 of that device's 8 tokens, and some expert is picked by exactly 8. The 8 picks of a token are different experts. `ids_pruned`: for each layer, micro-batch and device along expert, no expert is picked by more than 8 of that device's 8 tokens, and some expert is picked by exactly 8. The 8 picks of a token are different experts. `keep_mask`: 1 keeps an expert in the pruned model, 0 removes it.
All inputs are finite; a program needn't handle non-finite values. No bound on the sum of `keep_mask` on one device may be relied on, other than what follows from the above.
Results may differ from a plain program's by a relative error of at most 0.012.
Values may be sent and summed in bfloat16 or wider, within the bound.
No kernel may reach another device: no remote copies, remote signals or barrier semaphores. Data moves between devices by JAX's collectives and lax.ppermute only.
A program may use at most 64 MiB of HBM per device.

v0:
```python
import jax
import jax.numpy as jnp
from jax import lax
from jax.sharding import PartitionSpec as P


def partner(value, axis, apart):
    mask = 2**apart
    pairs = [(source, source ^ mask) for source in range(lax.axis_size(axis))]
    return lax.ppermute(value, axis, pairs)


def from_behind(value, axis, by):
    peers = lax.axis_size(axis)
    pairs = [(i, i + by) for i in range(peers) if 0 <= i + by < peers]
    return lax.ppermute(value, axis, pairs)


def normalize_rows(state_rows):
    values = state_rows.astype(jnp.float32)
    factor = lax.rsqrt(jnp.mean(values * values, axis=-1, keepdims=True) + 1e-06)
    return (values * factor).astype(jnp.bfloat16)


def route_tables(picked, experts, expert_cap, slot_count, holder_turn):
    tok_rows, top_count = picked.shape
    flat_picks = picked.reshape(-1)
    choose = (flat_picks[:, None] == jnp.arange(experts, dtype=jnp.int32)[None, :]).astype(
        jnp.int32
    )
    before = jnp.cumsum(choose, axis=0) - choose
    pick_ranks = jnp.sum(before * choose, axis=1)
    turned_ranks = (pick_ranks + holder_turn * slot_count) % expert_cap
    positions = flat_picks * expert_cap + turned_ranks
    buffer_rows = experts * expert_cap
    placed = positions[None, :] == jnp.arange(buffer_rows, dtype=jnp.int32)[:, None]
    return (choose, placed.reshape(buffer_rows, tok_rows, top_count))


def dispatch_rows(normed, placed, devices, slot_count):
    send_table = jnp.sum(placed.astype(jnp.float32), axis=2).astype(jnp.bfloat16)
    gathered = jnp.dot(send_table, normed, preferred_element_type=jnp.float32).astype(jnp.bfloat16)
    return gathered.reshape(devices, slot_count, normed.shape[1])


def combine_rows(returned, placed, weights):
    weight_table = jnp.sum(jnp.where(placed, weights[None, :, :], 0.0), axis=2)
    flat_rows = returned.reshape(-1, returned.shape[-1]).astype(jnp.float32)
    return jnp.einsum("bt,bd->td", weight_table, flat_rows, precision=lax.Precision.HIGHEST)


def slice_apply(rows_in, pair_weight, down_weight):
    hidden_width = down_weight.shape[0]
    both_parts = jnp.dot(rows_in, pair_weight, preferred_element_type=jnp.float32)
    hidden = (jax.nn.silu(both_parts[:, :hidden_width]) * both_parts[:, hidden_width:]).astype(
        jnp.bfloat16
    )
    return jnp.dot(hidden, down_weight, preferred_element_type=jnp.float32)


def store_micro(buffer, values, position, active):
    previous = lax.dynamic_index_in_dim(buffer, position, 0, keepdims=False)
    return lax.dynamic_update_index_in_dim(buffer, jnp.where(active, values, previous), position, 0)


def on_device(
    states_orig,
    states_pruned,
    ids_orig,
    ids_pruned,
    gates_orig,
    gates_pruned,
    keep_mask,
    w_in,
    w_out,
):
    devices = lax.axis_size("expert")
    section_count = lax.axis_size("section")
    section_index = lax.axis_index("section")
    micro_count, tok_rows, model_width = states_orig.shape
    experts = keep_mask.shape[1]
    top_count = ids_orig.shape[-1]
    split_count = devices // experts
    expert_cap = min(
        tok_rows, split_count * max(1, 2 * tok_rows * top_count // (experts * split_count))
    )
    slot_count = expert_cap // split_count
    holder_turn = lax.axis_index("expert") % split_count
    factor = experts / (top_count * micro_count * tok_rows * devices)
    own_in = w_in[0, 0]
    own_out = w_out[0, 0]
    other_in, other_out = partner((own_in, own_out), "expert", 0)
    slice_width = own_out.shape[0]
    full_in = jnp.concatenate(
        [
            own_in[:, :slice_width],
            other_in[:, :slice_width],
            own_in[:, slice_width:],
            other_in[:, slice_width:],
        ],
        axis=1,
    )
    full_out = jnp.concatenate([own_out, other_out], axis=0)
    kept_scale = keep_mask[0].astype(jnp.float32)
    item_count = 2 * micro_count
    step_count = item_count + section_count - 1
    carry_state = jnp.zeros((tok_rows, model_width), jnp.bfloat16)
    held_orig = jnp.zeros((tok_rows, model_width), jnp.float32)
    moe_orig = jnp.zeros((micro_count, tok_rows, model_width), jnp.bfloat16)
    moe_pruned = moe_orig
    loss_running = jnp.zeros((experts,), jnp.float32)
    for tick_index in range(step_count):
        item_index = tick_index - section_index
        active = jnp.logical_and(item_index >= 0, item_index < item_count)
        clipped = jnp.clip(item_index, 0, item_count - 1)
        position = clipped // 2
        pruned_kind = clipped % 2 == 1
        if tick_index < item_count:
            if tick_index % 2 == 0:
                first_input = states_orig[tick_index // 2]
            else:
                first_input = states_pruned[tick_index // 2]
            state_in = jnp.where(section_index == 0, first_input, carry_state)
        else:
            state_in = carry_state
        picked_orig = lax.dynamic_index_in_dim(ids_orig[0], position, 0, keepdims=False)
        picked_pruned = lax.dynamic_index_in_dim(ids_pruned[0], position, 0, keepdims=False)
        weight_orig = lax.dynamic_index_in_dim(gates_orig[0], position, 0, keepdims=False)
        choose_orig, placed_orig = route_tables(
            picked_orig, experts, expert_cap, slot_count, holder_turn
        )
        choose_pruned, placed_pruned = route_tables(
            picked_pruned, experts, expert_cap, slot_count, holder_turn
        )
        kept_picks = jnp.sum(choose_pruned.astype(jnp.float32) * kept_scale[None, :], axis=1)
        weight_pruned = lax.dynamic_index_in_dim(
            gates_pruned[0], position, 0, keepdims=False
        ) * kept_picks.reshape(tok_rows, top_count)
        placed = jnp.where(pruned_kind, placed_pruned, placed_orig)
        weights = jnp.where(pruned_kind, weight_pruned, weight_orig)
        outgoing = dispatch_rows(normalize_rows(state_in), placed, devices, slot_count)
        received = lax.all_to_all(outgoing, "expert", split_axis=0, concat_axis=0, tiled=True)
        flat_rows = received.reshape(-1, received.shape[-1])
        finished = slice_apply(flat_rows, full_in, full_out).astype(jnp.bfloat16)
        returned = lax.all_to_all(
            finished.reshape(received.shape), "expert", split_axis=0, concat_axis=0, tiled=True
        )
        moe_value = combine_rows(returned, placed, weights)
        differ = held_orig - moe_value
        errors = jnp.mean(differ * differ, axis=1)
        weighted = (weight_orig * errors[:, None]).reshape(-1)
        expert_terms = factor * jnp.sum(choose_orig.astype(jnp.float32) * weighted[:, None], axis=0)
        expert_terms = jnp.where(jnp.logical_and(active, pruned_kind), expert_terms, 0.0)
        loss_running = loss_running + lax.psum(expert_terms, "expert")
        rounded = moe_value.astype(jnp.bfloat16)
        moe_orig = store_micro(
            moe_orig, rounded, position, jnp.logical_and(active, jnp.logical_not(pruned_kind))
        )
        moe_pruned = store_micro(
            moe_pruned, rounded, position, jnp.logical_and(active, pruned_kind)
        )
        held_orig = moe_value
        if tick_index + 1 < step_count:
            state_next = (state_in.astype(jnp.float32) + moe_value).astype(jnp.bfloat16)
            carry_state = from_behind(state_next, "section", 1)
    return (moe_orig[None], moe_pruned[None], loss_running[None])


def solution(mesh):
    return jax.shard_map(
        on_device,
        mesh=mesh,
        in_specs=(
            P(None, "expert", None),
            P(None, "expert", None),
            P("section", None, "expert", None),
            P("section", None, "expert", None),
            P("section", None, "expert", None),
            P("section", None, "expert", None),
            P("section", None),
            P("section", "expert", None, None),
            P("section", "expert", None, None),
        ),
        out_specs=(
            P("section", None, "expert", None),
            P("section", None, "expert", None),
            P("section", None),
        ),
        check_vma=False,
    )
```

profile of v0, /device:TPU:0, one launch (start us, length us, event | category | flops | bytes accessed | tf_op | source)
XLA Modules:
  0.0 138.3 jit_solution(11877391718913465543)
XLA Ops:
  0.6 0.5 collective-permute-start
  1.2 1.0 eq.48
  2.3 0.1 reduce_window_sum.20
  2.4 0.2 select_reduce_fusion.1
  2.5 0.8 eq.41
  3.4 0.1 reduce_window_sum.19
  3.5 0.2 select_reduce_fusion.3
  3.8 0.7 fusion.21
  4.5 0.9 fusion.8
  5.4 0.8 convert_reduce_fusion.1
  6.2 1.9 %convolution_convert_fusion.3 = bf16[128,2048]{1,0:T(8,128)(2,1)} fusion(bf16[1,8,2048]{2,1,0:T(8,128)(2,1)} %param.9, f32[8]{0:T(128)S(1)} %add_rsqrt_fusion.1, bf16[128,8]{0,1:T(8,128)(2,1)S(1)} %get-tuple-element.5), kind=kOutput, calls=%fused_computation.5 | convolution fusion | flops 4505600 | bytes 559136 | tf_op jit(solution)/shard_map/dot_general | solution.py:42
  8.1 2.0 %reshape.207 = bf16[32,4,2048]{2,1,0:T(4,128)(2,1)} reshape(bf16[128,2048]{1,0:T(8,128)(2,1)} %convolution_convert_fusion.3) | data formatting | bytes 1048576 | tf_op jit(solution)/shard_map/reshape | solution.py:43
  10.1 7.0 %all-to-all-start = ((bf16[32,4,2048]{2,1,0:T(4,128)(2,1)}), bf16[32,4,2048]{2,1,0:T(4,128)(2,1)}, u32[]{:S(2)}, u32[]{:S(2)}) async-start(bf16[32,4,2048]{2,1,0:T(4,128)(2,1)} %reshape.207), calls=%async_computation | async-start | bytes 1048576 | tf_op jit(solution)/shard_map/all_to_all | solution.py:142
  17.2 0.7 convert_bitcast_fusion.2
  17.9 0.2 multiply_reduce_fusion.2
  18.1 0.9 fusion.10
  19.0 0.7 fusion.23
  19.7 0.7 bitcast_multiply_fusion
  20.4 0.1 convert_reduce_fusion
  20.5 1.9 %convolution_convert_fusion.1 = bf16[128,2048]{1,0:T(8,128)(2,1)} fusion(bf16[1,8,2048]{2,1,0:T(8,128)(2,1)} %param.10, f32[8]{0:T(128)S(1)} %add_rsqrt_fusion, bf16[128,8]{0,1:T(8,128)(2,1)S(1)} %get-tuple-element.3), kind=kOutput, calls=%fused_computation.3 | convolution fusion | flops 4505600 | bytes 559136 | tf_op jit(solution)/shard_map/dot_general | solution.py:42
  22.5 2.1 %reshape.212 = bf16[32,4,2048]{2,1,0:T(4,128)(2,1)} reshape(bf16[128,2048]{1,0:T(8,128)(2,1)} %convolution_convert_fusion.1) | data formatting | bytes 1048576 | tf_op jit(solution)/shard_map/reshape | solution.py:43
  24.5 8.1 %all-to-all-done = bf16[32,4,2048]{2,1,0:T(4,128)(2,1)} async-done(((bf16[32,4,2048]{2,1,0:T(4,128)(2,1)}), bf16[32,4,2048]{2,1,0:T(4,128)(2,1)}, u32[]{:S(2)}, u32[]{:S(2)}) %all-to-all-start) | async-done | bytes 524320 | tf_op jit(solution)/shard_map/all_to_all | solution.py:142
  32.7 3.3 %all-to-all-start.2 = ((bf16[32,4,2048]{2,1,0:T(4,128)(2,1)}), bf16[32,4,2048]{2,1,0:T(4,128)(2,1)}, u32[]{:S(2)}, u32[]{:S(2)}) async-start(bf16[32,4,2048]{2,1,0:T(4,128)(2,1)} %reshape.212), calls=%async_computation.2 | async-start | bytes 1048576 | tf_op jit(solution)/shard_map/all_to_all | solution.py:142
  36.0 0.1 collective-permute-start.1
  36.1 2.0 %fusion.32 = (bf16[2048,384]{1,0:T(8,128)(2,1)}, bf16[2048,384]{1,0:T(8,128)(2,1)}) fusion(bf16[2048,768]{1,0:T(8,128)(2,1)S(1)} %bitcast.46), kind=kLoop, calls=%fused_computation.69 | loop fusion | bytes 6291456 | tf_op jit(solution)/shard_map/slice | solution.py:96
  38.1 1.2 reshape.208
  39.2 12.3 %all-to-all-done.2 = bf16[32,4,2048]{2,1,0:T(4,128)(2,1)} async-done(((bf16[32,4,2048]{2,1,0:T(4,128)(2,1)}), bf16[32,4,2048]{2,1,0:T(4,128)(2,1)}, u32[]{:S(2)}, u32[]{:S(2)}) %all-to-all-start.2) | async-done | bytes 524320 | tf_op jit(solution)/shard_map/all_to_all | solution.py:142
  51.5 1.2 reshape.213
  52.7 2.3 %fusion.33 = (bf16[2048,384]{1,0:T(8,128)(2,1)S(1)}, bf16[2048,384]{1,0:T(8,128)(2,1)S(1)}) fusion(bf16[2048,768]{1,0:T(8,128)(2,1)} %collective-permute-done), kind=kLoop, calls=%fused_computation.70 | loop fusion | bytes 6291456 | tf_op jit(solution)/shard_map/slice | solution.py:97
  55.1 0.4 copy-done.2
  55.5 1.0 fusion.1
  56.6 0.2 copy-done.4
  56.7 0.9 copy-done.6
  57.6 2.0 %convolution_convert_fusion.2 = bf16[128,2048]{1,0:T(8,128)(2,1)S(1)} fusion(bf16[384,2048]{1,0:T(8,128)(2,1)} %collective-permute-done.1, bf16[384,2048]{1,0:T(8,128)(2,1)S(1)} %bitcast.49, f32[128,1536]{1,0:T(8,128)S(1)} %fusion.1), kind=kOutput, calls=%fused_computation.4 | convolution fusion | flops 409796608 | bytes 4456448 | tf_op jit(solution)/shard_map/dot_general | solution.py:58
  59.6 1.0 reshape.209
  60.6 3.0 %all-to-all-start.1 = ((bf16[32,4,2048]{2,1,0:T(4,128)(2,1)}), bf16[32,4,2048]{2,1,0:T(4,128)(2,1)S(1)}, u32[]{:S(2)}, u32[]{:S(2)}) async-start(bf16[32,4,2048]{2,1,0:T(4,128)(2,1)} %reshape.209), calls=%async_computation.1 | async-start | bytes 1048576 | tf_op jit(solution)/shard_map/all_to_all | solution.py:145
  63.7 5.7 %fusion = f32[128,1536]{1,0:T(8,128)S(1)} fusion(bf16[128,2048]{1,0:T(8,128)(2,1)S(1)} %reshape.213, bf16[2048,384]{1,0:T(8,128)(2,1)} %copy-done.4, bf16[2048,384]{1,0:T(8,128)(2,1)} %get-tuple-element.8, bf16[2048,384]{1,0:T(8,128)(2,1)} %copy-done.3, bf16[2048,384]{1,0:T(8,128)(2,1)S(1)} %copy-done.1), kind=kOutput, calls=%fused_computation.6 | convolution fusion | flops 830472192 | bytes 7602176 | tf_op jit(solution)/shard_map/dot_general | solution.py:54
  69.4 2.0 %convolution_convert_fusion = bf16[128,2048]{1,0:T(8,128)(2,1)S(1)} fusion(bf16[384,2048]{1,0:T(8,128)(2,1)} %collective-permute-done.1, bf16[384,2048]{1,0:T(8,128)(2,1)S(1)} %bitcast.50, f32[128,1536]{1,0:T(8,128)S(1)} %fusion), kind=kOutput, calls=%fused_computation.2 | convolution fusion | flops 409796608 | bytes 4456448 | tf_op jit(solution)/shard_map/dot_general | solution.py:58
  71.4 1.0 reshape.214
  72.4 6.8 %all-to-all-done.1 = bf16[32,4,2048]{2,1,0:T(4,128)(2,1)S(1)} async-done(((bf16[32,4,2048]{2,1,0:T(4,128)(2,1)}), bf16[32,4,2048]{2,1,0:T(4,128)(2,1)S(1)}, u32[]{:S(2)}, u32[]{:S(2)}) %all-to-all-start.1) | async-done | bytes 524320 | tf_op jit(solution)/shard_map/all_to_all | solution.py:145
  79.2 3.1 %all-to-all-start.3 = ((bf16[32,4,2048]{2,1,0:T(4,128)(2,1)}), bf16[32,4,2048]{2,1,0:T(4,128)(2,1)S(1)}, u32[]{:S(2)}, u32[]{:S(2)}) async-start(bf16[32,4,2048]{2,1,0:T(4,128)(2,1)} %reshape.214), calls=%async_computation.3 | async-start | bytes 1048576 | tf_op jit(solution)/shard_map/all_to_all | solution.py:145
  82.4 0.1 reshape.210
  82.5 0.3 fusion.34
  82.8 15.0 %all-to-all-done.3 = bf16[32,4,2048]{2,1,0:T(4,128)(2,1)S(1)} async-done(((bf16[32,4,2048]{2,1,0:T(4,128)(2,1)}), bf16[32,4,2048]{2,1,0:T(4,128)(2,1)S(1)}, u32[]{:S(2)}, u32[]{:S(2)}) %all-to-all-start.3) | async-done | bytes 524320 | tf_op jit(solution)/shard_map/all_to_all | solution.py:145
  97.8 0.1 reshape.215
  97.9 1.0 multiply_reduce_fusion
  99.2 0.1 multiply_reduce_fusion.1
  99.3 39.0 %psum.6 = f32[1,16]{1,0:T(1,128)} all-reduce(f32[1,16]{1,0:T(1,128)S(1)} %multiply_bitcast_fusion), channel_id=1, replica_groups=mesh['section'=1,'expert'=32] {'expert'}, use_global_device_ids=true, to_apply=%region_13.14 | all-reduce | flops 16 | bytes 128 | tf_op jit(solution)/shard_map/psum | solution.py:154
  (29 shorter events, 0.7 us)
Async XLA Ops:
  0.6 35.5 %copy-start = (bf16[1,1,2048,768]{3,2,1,0:T(8,128)(2,1)S(1)}, bf16[1,1,2048,768]{3,2,1,0:T(8,128)(2,1)}, u32[]{:S(2)}) copy-start(bf16[1,1,2048,768]{3,2,1,0:T(8,128)(2,1)} %param.16) | copy-start | bytes 9437188
  0.6 52.1 %collective-permute-start = (bf16[2048,768]{1,0:T(8,128)(2,1)}, bf16[2048,768]{1,0:T(8,128)(2,1)}, u32[]{:S(2)}, u32[]{:S(2)}) collective-permute-start(bf16[2048,768]{1,0:T(8,128)(2,1)} %bitcast.45), channel_id=1, source_target_pairs={{0,1},{1,0},{2,3},{3,2},{4,5},{5,4},{6,7},{7,6},{8,9},{9,8},{10,11... | collective-permute-start | bytes 9437192 | tf_op jit(solution)/shard_map/ppermute | solution.py:10
  10.1 22.5 %all-to-all-start = ((bf16[32,4,2048]{2,1,0:T(4,128)(2,1)}), bf16[32,4,2048]{2,1,0:T(4,128)(2,1)}, u32[]{:S(2)}, u32[]{:S(2)}) async-start(bf16[32,4,2048]{2,1,0:T(4,128)(2,1)} %reshape.207), calls=%async_computation | async-start | bytes 1048576 | tf_op jit(solution)/shard_map/all_to_all | solution.py:142
  32.7 18.9 %all-to-all-start.2 = ((bf16[32,4,2048]{2,1,0:T(4,128)(2,1)}), bf16[32,4,2048]{2,1,0:T(4,128)(2,1)}, u32[]{:S(2)}, u32[]{:S(2)}) async-start(bf16[32,4,2048]{2,1,0:T(4,128)(2,1)} %reshape.212), calls=%async_computation.2 | async-start | bytes 1048576 | tf_op jit(solution)/shard_map/all_to_all | solution.py:142
  36.0 20.7 %collective-permute-start.1 = (bf16[384,2048]{1,0:T(8,128)(2,1)}, bf16[384,2048]{1,0:T(8,128)(2,1)}, u32[]{:S(2)}, u32[]{:S(2)}) collective-permute-start(bf16[384,2048]{1,0:T(8,128)(2,1)} %bitcast.48), channel_id=1, source_target_pairs={{0,1},{1,0},{2,3},{3,2},{4,5},{5,4},{6,7},{7,6},{8,9},{9,8},{10,11... | collective-permute-start | bytes 4718600 | tf_op jit(solution)/shard_map/ppermute | solution.py:10
  52.7 2.4 %copy-start.1 = (bf16[2048,384]{1,0:T(8,128)(2,1)S(1)}, bf16[2048,384]{1,0:T(8,128)(2,1)}, u32[]{:S(2)}) copy-start(bf16[2048,384]{1,0:T(8,128)(2,1)} %get-tuple-element.7) | copy-start | bytes 4718596
  52.7 2.8 %copy-start.2 = (bf16[2048,384]{1,0:T(8,128)(2,1)S(1)}, bf16[2048,384]{1,0:T(8,128)(2,1)}, u32[]{:S(2)}) copy-start(bf16[2048,384]{1,0:T(8,128)(2,1)} %get-tuple-element.8) | copy-start | bytes 4718596
  55.1 1.5 %copy-start.3 = (bf16[2048,384]{1,0:T(8,128)(2,1)}, bf16[2048,384]{1,0:T(8,128)(2,1)S(1)}, u32[]{:S(2)}) copy-start(bf16[2048,384]{1,0:T(8,128)(2,1)S(1)} %get-tuple-element.9) | copy-start | bytes 4718596
  55.1 1.6 %copy-start.4 = (bf16[2048,384]{1,0:T(8,128)(2,1)}, bf16[2048,384]{1,0:T(8,128)(2,1)S(1)}, u32[]{:S(2)}) copy-start(bf16[2048,384]{1,0:T(8,128)(2,1)S(1)} %get-tuple-element.10) | copy-start | bytes 4718596
  55.5 2.1 %copy-start.6 = (bf16[1,1,384,2048]{3,2,1,0:T(8,128)(2,1)S(1)}, bf16[1,1,384,2048]{3,2,1,0:T(8,128)(2,1)}, u32[]{:S(2)}) copy-start(bf16[1,1,384,2048]{3,2,1,0:T(8,128)(2,1)} %param.17) | copy-start | bytes 4718596
  60.6 18.6 %all-to-all-start.1 = ((bf16[32,4,2048]{2,1,0:T(4,128)(2,1)}), bf16[32,4,2048]{2,1,0:T(4,128)(2,1)S(1)}, u32[]{:S(2)}, u32[]{:S(2)}) async-start(bf16[32,4,2048]{2,1,0:T(4,128)(2,1)} %reshape.209), calls=%async_computation.1 | async-start | bytes 1048576 | tf_op jit(solution)/shard_map/all_to_all | solution.py:145
  63.6 5.7 %copy-start.7 = (bf16[1,1,384,2048]{3,2,1,0:T(8,128)(2,1)S(1)}, bf16[1,1,384,2048]{3,2,1,0:T(8,128)(2,1)}, u32[]{:S(2)}) copy-start(bf16[1,1,384,2048]{3,2,1,0:T(8,128)(2,1)} %param.17) | copy-start | bytes 4718596
  69.3 12.9 %copy-start.5 = (f32[1,1,8,8]{3,2,1,0:T(8,128)S(1)}, f32[1,1,8,8]{3,2,1,0:T(8,128)}, u32[]{:S(2)}) copy-start(f32[1,1,8,8]{3,2,1,0:T(8,128)} %param.13) | copy-start | bytes 772
  79.2 18.6 %all-to-all-start.3 = ((bf16[32,4,2048]{2,1,0:T(4,128)(2,1)}), bf16[32,4,2048]{2,1,0:T(4,128)(2,1)S(1)}, u32[]{:S(2)}, u32[]{:S(2)}) async-start(bf16[32,4,2048]{2,1,0:T(4,128)(2,1)} %reshape.214), calls=%async_computation.3 | async-start | bytes 1048576 | tf_op jit(solution)/shard_map/all_to_all | solution.py:145
where the time goes:
time: 139 us; the launch traced here: 138 us
  waiting for transfers between devices  42.2 us (30%)
  blocking collectives  39 us (28%)
  starting transfers between devices  17.1 us (12%)
  local copies, waits for them, and re-layouts  16.7 us (12%)
  matrix products  16 us (12%)
  other arithmetic  6.43 us (5%)
    psum x1, blocking collectives, on_device(): loss_running = loss_running + lax.psum(expert_terms, 'expert')  39 us
    all_to_all x2, waiting for transfers between devices, on_device(): lax.all_to_all(finished.reshape(received.shape), 'expert', split_axis=0,...  21.8 us
    all_to_all x2, waiting for transfers between devices, on_device(): lax.all_to_all(outgoing, 'expert', split_axis=0, concat_axis=0, tiled=True)  20.4 us
    all_to_all x2, starting transfers between devices, on_device(): lax.all_to_all(outgoing, 'expert', split_axis=0, concat_axis=0, tiled=True)  10.3 us
    dot_general x2, matrix products, slice_apply(): jnp.dot(rows_in, pair_weight, preferred_element_type=jnp.float32)  6.7 us
    all_to_all x2, starting transfers between devices, on_device(): lax.all_to_all(finished.reshape(received.shape), 'expert', split_axis=0,...  6.08 us
    reshape x2, local copies, waits for them, and re-layouts, dispatch_rows(): return gathered.reshape(devices, slot_count, normed.shape[1])  4.1 us
    dot_general x2, matrix products, slice_apply(): return jnp.dot(hidden, down_weight, preferred_element_type=jnp.float32)  4.05 us
  transfers between devices with their start and end apart: 6, of which 4 were waited for; matrix products, arithmetic and copies ran while one was open for 24% of the time, Pallas kernels for 0%

commit v1 on v0

v1 whole, which is shorter than its diff:
```python
import functools

import jax
import jax.numpy as jnp
from jax import lax
from jax.experimental import pallas as pl
from jax.experimental.pallas import tpu as pltpu
from jax.sharding import PartitionSpec as P

SPLIT = 2
LANES = 128


def whole(memory_space=pltpu.VMEM):
    return pl.BlockSpec(memory_space=memory_space)


def normalize_rows(values):
    factor = lax.rsqrt(jnp.mean(values * values, axis=-1, keepdims=True) + 1e-06)
    return values * factor


def dense_weights(picked, gates, experts, width):
    rows = picked.shape[0]
    label = lax.broadcasted_iota(jnp.int32, (rows, width), 1) % experts
    total = jnp.zeros((rows, width), jnp.float32)
    for k in range(picked.shape[1]):
        total = total + jnp.where(picked[:, k : k + 1] == label, gates[:, k : k + 1], 0.0)
    return total


def pack_kernel(experts, so_ref, sp_ref, io_ref, ip_ref, go_ref, gp_ref, keep_ref, out_ref):
    model_width = so_ref.shape[1]
    extra = out_ref.shape[1] - model_width
    states = jnp.concatenate(
        [so_ref[...].astype(jnp.float32), sp_ref[...].astype(jnp.float32)], axis=0
    )
    out_ref[:, :model_width] = normalize_rows(states).astype(jnp.bfloat16)
    dense_orig = dense_weights(io_ref[...], go_ref[...], experts, extra)
    dense_pruned = dense_weights(ip_ref[...], gp_ref[...], experts, extra)
    dense_pruned = dense_pruned * keep_ref[...]
    dense = jnp.concatenate([dense_orig, dense_pruned], axis=0)
    high = dense.astype(jnp.bfloat16).astype(jnp.float32)
    lane = lax.broadcasted_iota(jnp.int32, dense.shape, 1)
    out_ref[:, model_width:] = jnp.where(lane < experts, high, dense - high).astype(jnp.bfloat16)


def expert_kernel(experts, rows_ref, in_a_ref, in_b_ref, out_a_ref, out_b_ref, result_ref, hidden):
    half = out_a_ref.shape[0]
    model_width = out_a_ref.shape[1]
    expert = lax.axis_index("expert") // SPLIT
    extra = rows_ref[:, model_width:].astype(jnp.float32)
    lane = lax.broadcasted_iota(jnp.int32, extra.shape, 1)
    mine = jnp.logical_or(lane == expert, lane == expert + experts)
    weight = jnp.sum(jnp.where(mine, extra, 0.0), axis=1, keepdims=True)
    for place, in_ref in enumerate((in_a_ref, in_b_ref)):
        both = jnp.dot(
            rows_ref[:, :model_width], in_ref[...], preferred_element_type=jnp.float32
        )
        gate, up = both[:, :half], both[:, half:]
        hidden[:, place * half : (place + 1) * half] = (
            gate / (1.0 + jnp.exp(-gate)) * up
        ).astype(jnp.bfloat16)
    step = 512
    for start in range(0, model_width, step):
        value = jnp.dot(
            hidden[:, :half], out_a_ref[:, start : start + step], preferred_element_type=jnp.float32
        ) + jnp.dot(
            hidden[:, half:], out_b_ref[:, start : start + step], preferred_element_type=jnp.float32
        )
        result_ref[:, start : start + step] = (value * weight).astype(jnp.bfloat16)


def on_device(
    states_orig,
    states_pruned,
    ids_orig,
    ids_pruned,
    gates_orig,
    gates_pruned,
    keep_mask,
    w_in,
    w_out,
):
    devices = lax.axis_size("expert")
    section_count = lax.axis_size("section")
    section_index = lax.axis_index("section")
    micro_count, tok_rows, model_width = states_orig.shape
    experts = keep_mask.shape[1]
    top_count = ids_orig.shape[-1]
    loss_factor = experts / (top_count * micro_count * tok_rows * devices)
    extra = -(-2 * experts // LANES) * LANES
    rows = 2 * tok_rows
    own_in, own_out = w_in[0, 0], w_out[0, 0]
    pairs = [(source, source ^ 1) for source in range(devices)]
    other_in = lax.ppermute(own_in, "expert", pairs)
    other_out = lax.ppermute(own_out, "expert", pairs)
    groups = [list(range(core, devices, SPLIT)) for core in range(SPLIT)]
    kept = jnp.tile(keep_mask.astype(jnp.float32), (1, -(-extra // experts)))[:, :extra]

    step_count = micro_count + section_count - 1
    carry = jnp.zeros((2, tok_rows, model_width), jnp.bfloat16)
    moe_orig = jnp.zeros((micro_count, tok_rows, model_width), jnp.bfloat16)
    moe_pruned = moe_orig
    terms = jnp.zeros((experts,), jnp.float32)
    for tick in range(step_count):
        if section_count == 1:
            position, active = tick, True
            item = lambda buffer: buffer[position]
        else:
            position = jnp.clip(tick - section_index, 0, micro_count - 1)
            active = jnp.logical_and(
                tick - section_index >= 0, tick - section_index < micro_count
            )
            item = lambda buffer: lax.dynamic_index_in_dim(buffer, position, 0, keepdims=False)
        fresh = min(tick, micro_count - 1)
        state_orig, state_pruned = states_orig[fresh], states_pruned[fresh]
        if section_count > 1:
            state_orig = jnp.where(section_index == 0, state_orig, carry[0])
            state_pruned = jnp.where(section_index == 0, state_pruned, carry[1])
        picked_orig, weight_orig = item(ids_orig[0]), item(gates_orig[0])
        packed = pl.pallas_call(
            functools.partial(pack_kernel, experts),
            out_shape=jax.ShapeDtypeStruct((rows, model_width + extra), jnp.bfloat16),
            in_specs=[whole()] * 7,
            out_specs=whole(),
        )(
            state_orig,
            state_pruned,
            picked_orig,
            item(ids_pruned[0]),
            weight_orig,
            item(gates_pruned[0]),
            kept,
        )
        gathered = lax.all_gather(
            packed, "expert", axis_index_groups=groups, axis=0, tiled=True
        )
        partial = pl.pallas_call(
            functools.partial(expert_kernel, experts),
            out_shape=jax.ShapeDtypeStruct((gathered.shape[0], model_width), jnp.bfloat16),
            in_specs=[whole()] * 5,
            out_specs=whole(),
            scratch_shapes=[
                pltpu.VMEM((gathered.shape[0], SPLIT * own_out.shape[0]), jnp.bfloat16)
            ],
            compiler_params=pltpu.CompilerParams(vmem_limit_bytes=40 * 2**20),
        )(gathered, own_in, other_in, own_out, other_out)
        moe = lax.psum_scatter(
            partial, "expert", axis_index_groups=groups, scatter_dimension=0, tiled=True
        ).astype(jnp.float32)
        value_orig, value_pruned = moe[:tok_rows], moe[tok_rows:]
        differ = value_orig - value_pruned
        errors = jnp.mean(differ * differ, axis=1)
        chosen = picked_orig[:, :, None] == jnp.arange(experts, dtype=jnp.int32)
        tick_terms = loss_factor * jnp.sum(
            jnp.where(chosen, (weight_orig * errors[:, None])[:, :, None], 0.0), axis=(0, 1)
        )
        round_orig, round_pruned = moe[:tok_rows], moe[tok_rows:]
        round_orig = value_orig.astype(jnp.bfloat16)
        round_pruned = value_pruned.astype(jnp.bfloat16)
        if section_count > 1:
            tick_terms = jnp.where(active, tick_terms, 0.0)
            round_orig = jnp.where(active, round_orig, item(moe_orig))
            round_pruned = jnp.where(active, round_pruned, item(moe_pruned))
        terms = terms + tick_terms
        moe_orig = lax.dynamic_update_index_in_dim(moe_orig, round_orig, position, 0)
        moe_pruned = lax.dynamic_update_index_in_dim(moe_pruned, round_pruned, position, 0)
        if tick + 1 < step_count and section_count > 1:
            following = jnp.stack(
                [
                    (state_orig.astype(jnp.float32) + value_orig).astype(jnp.bfloat16),
                    (state_pruned.astype(jnp.float32) + value_pruned).astype(jnp.bfloat16),
                ]
            )
            onward = [(i, i + 1) for i in range(section_count - 1)]
            carry = lax.ppermute(following, "section", onward)
    spread = jnp.broadcast_to(terms[None], (devices, experts))
    shared = lax.all_to_all(spread, "expert", split_axis=0, concat_axis=0, tiled=True)
    loss = jnp.sum(shared, axis=0)
    return (moe_orig[None], moe_pruned[None], loss[None])


def solution(mesh):
    return jax.shard_map(
        on_device,
        mesh=mesh,
        in_specs=(
            P(None, "expert", None),
            P(None, "expert", None),
            P("section", None, "expert", None),
            P("section", None, "expert", None),
            P("section", None, "expert", None),
            P("section", None, "expert", None),
            P("section", None),
            P("section", "expert", None, None),
            P("section", "expert", None, None),
        ),
        out_specs=(
            P("section", None, "expert", None),
            P("section", None, "expert", None),
            P("section", None),
        ),
        check_vma=False,
    )
```

time: 139 us -> 175 us (1.26)
  waiting for transfers between devices: 42.2 us -> 141 us
  blocking collectives: 39 us -> 0 us
  matrix products: 16 us -> 0 us
  starting transfers between devices: 17.1 us -> 3.29 us
  between operations: 0.88 us -> 14.1 us
  local copies, waits for them, and re-layouts: 16.7 us -> 8.96 us
  Pallas kernels: 0 us -> 5.51 us
  other arithmetic: 6.43 us -> 2.38 us
    reduce_scatter x0 -> x1, waiting for transfers between devices: none -> 76.7 us  [on_device(): lax.psum_scatter(partial, 'expert', axis_index_groups=groups, scatter_dim...]
    all_gather x0 -> x1, waiting for transfers between devices: none -> 52.6 us  [on_device(): lax.all_gather(packed, 'expert', axis_index_groups=groups, axis=0, tiled=...]
    psum x1 -> x0, blocking collectives: 39 us -> none  [on_device(): loss_running = loss_running + lax.psum(expert_terms, 'expert')]
    all_to_all x4 -> x1, waiting for transfers between devices: 42.2 us -> 6.51 us  [on_device(): lax.all_to_all(spread, 'expert', split_axis=0, concat_axis=0, tiled=True)]
    dot_general x8 -> x0, matrix products: 16 us -> none  [the longest x2 6.7 us: slice_apply(): jnp.dot(rows_in, pair_weight, preferred_element_type=jnp.float32)]
    all_to_all x4 -> x1, starting transfers between devices: 16.4 us -> 2.57 us  [on_device(): lax.all_to_all(spread, 'expert', split_axis=0, concat_axis=0, tiled=True)]
    reshape x9 -> x0, local copies, waits for them, and re-layouts: 8.73 us -> none  [the longest x2 4.1 us: dispatch_rows(): return gathered.reshape(devices, slot_count, normed.shape[1])]
    unnamed x16 -> x14, local copies, waits for them, and re-layouts: 1.47 us -> 7.11 us
  transfers between devices with their start and end apart: 6 -> 5, of which waited for: 4 -> 4; matrix products, arithmetic and copies ran while one was open for 24% -> 1% of each run, Pallas kernels for 0% -> 1%
where the time goes in v1:
time: 175 us
  waiting for transfers between devices  141 us (81%)
  between operations  14.1 us (8%)
  local copies, waits for them, and re-layouts  8.96 us (5%)
  Pallas kernels  5.51 us (3%)
  starting transfers between devices  3.29 us (2%)
  other arithmetic  2.38 us (1%)
    reduce_scatter x1, waiting for transfers between devices, on_device(): lax.psum_scatter(partial, 'expert', axis_index_groups=groups, scatter_dim...  76.7 us
    all_gather x1, waiting for transfers between devices, on_device(): lax.all_gather(packed, 'expert', axis_index_groups=groups, axis=0, tiled=...  52.6 us
    unnamed x14, local copies, waits for them, and re-layouts  7.11 us
    all_to_all x1, waiting for transfers between devices, on_device(): lax.all_to_all(spread, 'expert', split_axis=0, concat_axis=0, tiled=True)  6.51 us
    ppermute x1, waiting for transfers between devices, on_device(): other_out = lax.ppermute(own_out, 'expert', pairs)  4.71 us
    pallas_call x1, Pallas kernels, on_device(): pl.pallas_call(functools.partial(expert_kernel, experts), out_shape=jax.S...  3.93 us
  transfers between devices with their start and end apart: 5, of which 4 were waited for; matrix products, arithmetic and copies ran while one was open for 1% of the time, Pallas kernels for 1%

profile of v1, /device:TPU:0, one launch (start us, length us, event | category | flops | bytes accessed | tf_op | source)
XLA Modules:
  0.0 174.8 jit_solution(12739326003611827380)
XLA Ops:
  7.2 0.0 all-gather.2.cloned.1.call-start
  7.2 0.5 collective-permute-start
  7.7 0.7 convert_bitcast_fusion
  8.4 0.6 tile.13.keep_ref
  9.0 1.6 shard_map.112
  10.6 0.0 copy-start.5
  10.6 0.0 copy-start.6
  10.6 0.0 all-gather.2.cloned.1.call-update
  10.6 0.0 reduce-scatter.2.cloned.1.call-start
  10.6 0.1 collective-permute-start.1
  10.8 4.7 %collective-permute-done.1.out_b_ref = bf16[384,2048]{1,0:T(8,128)(2,1)S(1)} collective-permute-done((bf16[384,2048]{1,0:T(8,128)(2,1)}, bf16[384,2048]{1,0:T(8,128)(2,1)S(1)}, u32[]{:S(2)}, u32[]{:S(2)}) %collective-permute-start.1) | collective-permute-done | bytes 1572896 | tf_op jit(solution)/shard_map/ppermute | solution.py:97
  15.5 0.0 copy-start.2
  15.5 1.2 copy-done.2
  16.6 52.6 %all-gather.2.cloned.1.call-done.rows_ref = bf16[256,2176]{1,0:T(8,128)(2,1)} async-done(((bf16[16,2176]{1,0:T(8,128)(2,1)}), bf16[256,2176]{1,0:T(8,128)(2,1)}) %all-gather.2.cloned.1.call-update) | async-done | bytes 1114128 | tf_op jit(solution)/shard_map/all_gather | solution.py:136
  69.3 0.0 collective-permute-done.in_b_ref
  69.3 0.0 copy-start
  69.3 1.9 %copy-done = bf16[1,1,2048,768]{3,2,1,0:T(8,128)(2,1)S(1)} copy-done((bf16[1,1,2048,768]{3,2,1,0:T(8,128)(2,1)S(1)}, bf16[1,1,2048,768]{3,2,1,0:T(8,128)(2,1)}, u32[]{:S(2)}) %copy-start) | copy-done | bytes 3145752
  71.2 0.0 copy-start.1
  71.2 1.4 copy-done.1
  72.6 0.0 copy-start.3
  72.6 1.4 copy-done.3
  74.0 0.0 copy-start.4
  74.0 1.2 copy-done.4
  75.2 3.9 %shard_map.113 = bf16[256,2048]{1,0:T(8,128)(2,1)} custom-call(bf16[256,2176]{1,0:T(8,128)(2,1)S(1)} %copy-done.4, bf16[2048,768]{1,0:T(8,128)(2,1)S(1)} %bitcast.17, bf16[2048,768]{1,0:T(8,128)(2,1)S(1)} %collective-permute-done.in_b_ref, bf16[384,2048]{1,0:T(8,128)(2,1)S(1)} %bitcast.19, bf16[384,2048]{1,0:T(8,128)(2,1)S(1)} %copy-done.3), custom_call_target="tpu_custom_call" | custom-call | tf_op jit(solution)/shard_map/pallas_call | solution.py:139
  79.1 0.0 reduce-scatter.2.cloned.1.call-update
  79.2 76.7 %reduce-scatter.2.cloned.1.call-done = bf16[16,2048]{1,0:T(8,128)(2,1)} async-done(((bf16[256,2048]{1,0:T(8,128)(2,1)}), bf16[16,2048]{1,0:T(8,128)(2,1)}) %reduce-scatter.2.cloned.1.call-update) | async-done | bytes 65552 | tf_op jit(solution)/shard_map/reduce_scatter | solution.py:149
  155.9 0.8 convert_element_type.13
  156.7 0.1 multiply_reduce_fusion
  156.8 0.0 copy-done.5
  156.8 0.1 broadcast_multiply_fusion
  156.9 0.0 copy-done.6
  156.9 0.1 select_reduce_fusion
  157.0 0.6 broadcast_in_dim.38
  157.6 2.6 %all-to-all-start = ((f32[32,1,16]{2,1,0:T(1,128)}), f32[32,1,16]{2,1,0:T(1,128)S(1)}, u32[]{:S(2)}, u32[]{:S(2)}) async-start(f32[32,1,16]{2,1,0:T(1,128)} %broadcast_in_dim.38), calls=%async_computation.1 | async-start | bytes 32768 | tf_op jit(solution)/shard_map/all_to_all | solution.py:179
  160.2 0.6 fusion.1
  160.9 6.5 %all-to-all-done = f32[32,1,16]{2,1,0:T(1,128)S(1)} async-done(((f32[32,1,16]{2,1,0:T(1,128)}), f32[32,1,16]{2,1,0:T(1,128)S(1)}, u32[]{:S(2)}, u32[]{:S(2)}) %all-to-all-start) | async-done | bytes 2080 | tf_op jit(solution)/shard_map/all_to_all | solution.py:179
  167.4 0.6 reduce_sum.29
  (3 shorter events, 0.0 us)
Async XLA Ops:
  7.2 62.1 %all-gather.2.cloned.1.call-start = ((), (), s32[]{:S(2)}) async-start(), calls=%async_computation.2 | async-start | bytes 1183744 | tf_op jit(solution)/shard_map/all_gather | solution.py:136
  7.2 62.1 %collective-permute-start = (bf16[2048,768]{1,0:T(8,128)(2,1)}, bf16[2048,768]{1,0:T(8,128)(2,1)S(1)}, u32[]{:S(2)}, u32[]{:S(2)}) collective-permute-start(bf16[2048,768]{1,0:T(8,128)(2,1)} %bitcast.16), channel_id=1, source_target_pairs={{0,1},{1,0},{2,3},{3,2},{4,5},{5,4},{6,7},{7,6},{8,9},{9,8},{10,11... | collective-permute-start | bytes 9437192 | tf_op jit(solution)/shard_map/ppermute | solution.py:96
  10.6 146.3 %copy-start.5 = (f32[1,1,8,8]{3,2,1,0:T(8,128)S(1)}, f32[1,1,8,8]{3,2,1,0:T(8,128)}, u32[]{:S(2)}) copy-start(f32[1,1,8,8]{3,2,1,0:T(8,128)} %param.13) | copy-start | bytes 772
  10.6 146.4 %copy-start.6 = (s32[1,1,8,8]{3,2,1,0:T(8,128)S(1)}, s32[1,1,8,8]{3,2,1,0:T(8,128)}, u32[]{:S(2)}) copy-start(s32[1,1,8,8]{3,2,1,0:T(8,128)} %param.11) | copy-start | bytes 772
  10.6 145.3 %reduce-scatter.2.cloned.1.call-start = ((), (), s32[]{:S(2)}) async-start(), calls=%async_computation.3 | async-start | bytes 1114112 | tf_op jit(solution)/shard_map/reduce_scatter | solution.py:149
  10.6 4.8 %collective-permute-start.1 = (bf16[384,2048]{1,0:T(8,128)(2,1)}, bf16[384,2048]{1,0:T(8,128)(2,1)S(1)}, u32[]{:S(2)}, u32[]{:S(2)}) collective-permute-start(bf16[384,2048]{1,0:T(8,128)(2,1)} %bitcast.18), channel_id=1, source_target_pairs={{0,1},{1,0},{2,3},{3,2},{4,5},{5,4},{6,7},{7,6},{8,9},{9,8},{10,11... | collective-permute-start | bytes 4718600 | tf_op jit(solution)/shard_map/ppermute | solution.py:97
  15.5 1.2 copy-start.2
  69.3 1.9 %copy-start = (bf16[1,1,2048,768]{3,2,1,0:T(8,128)(2,1)S(1)}, bf16[1,1,2048,768]{3,2,1,0:T(8,128)(2,1)}, u32[]{:S(2)}) copy-start(bf16[1,1,2048,768]{3,2,1,0:T(8,128)(2,1)} %param.16) | copy-start | bytes 9437188
  71.2 1.4 copy-start.1
  72.6 1.4 copy-start.3
  74.0 1.2 copy-start.4
  157.6 9.7 %all-to-all-start = ((f32[32,1,16]{2,1,0:T(1,128)}), f32[32,1,16]{2,1,0:T(1,128)S(1)}, u32[]{:S(2)}, u32[]{:S(2)}) async-start(f32[32,1,16]{2,1,0:T(1,128)} %broadcast_in_dim.38), calls=%async_computation.1 | async-start | bytes 32768 | tf_op jit(solution)/shard_map/all_to_all | solution.py:179
Sparse Core Ops, SparseCore 0:
  10.7 58.4 all-gather.1
  79.3 76.5 reduce-scatter.1

commit v2 on v1

v2 whole, which is shorter than its diff:
```python
import functools

import jax
import jax.numpy as jnp
from jax import lax
from jax.experimental import pallas as pl
from jax.experimental.pallas import tpu as pltpu
from jax.sharding import PartitionSpec as P

SPLIT = 2
LANES = 128
MIB = 2**20


def run_kernel(body, outs, operands, scratch=(), limit=16):
    return pl.pallas_call(
        body,
        out_shape=outs,
        in_specs=[pl.BlockSpec(memory_space=pltpu.VMEM)] * len(operands),
        out_specs=jax.tree.map(lambda _: pl.BlockSpec(memory_space=pltpu.VMEM), outs),
        scratch_shapes=list(scratch),
        compiler_params=pltpu.CompilerParams(vmem_limit_bytes=limit * MIB),
    )(*operands)


def like(rows, columns, dtype=jnp.bfloat16):
    return jax.ShapeDtypeStruct((rows, columns), dtype)


def exclusive(value, mask):
    pairs = [(source, source ^ mask) for source in range(lax.axis_size("expert"))]
    return lax.ppermute(value, "expert", pairs)


def normalize_rows(values):
    factor = lax.rsqrt(jnp.mean(values * values, axis=-1, keepdims=True) + 1e-06)
    return values * factor


def dense_weights(picked, gates, experts):
    rows = picked.shape[0]
    label = lax.broadcasted_iota(jnp.int32, (rows, experts), 1)
    total = jnp.zeros((rows, experts), jnp.float32)
    for k in range(picked.shape[1]):
        total = total + jnp.where(picked[:, k : k + 1] == label, gates[:, k : k + 1], 0.0)
    return total


def pack_kernel(so_ref, sp_ref, io_ref, ip_ref, go_ref, gp_ref, keep_ref, out_ref):
    model_width = so_ref.shape[1]
    extra = out_ref.shape[1] - model_width
    experts = keep_ref.shape[1]
    states = jnp.concatenate(
        [so_ref[...].astype(jnp.float32), sp_ref[...].astype(jnp.float32)], axis=0
    )
    out_ref[:, :model_width] = normalize_rows(states).astype(jnp.bfloat16)
    dense_orig = dense_weights(io_ref[...], go_ref[...], experts)
    dense_pruned = dense_weights(ip_ref[...], gp_ref[...], experts)
    dense_pruned = dense_pruned * keep_ref[...].astype(jnp.float32)
    dense = jnp.concatenate([dense_orig, dense_pruned], axis=0)
    high = dense.astype(jnp.bfloat16)
    low = (dense - high.astype(jnp.float32)).astype(jnp.bfloat16)
    source = lax.broadcasted_iota(jnp.int32, (experts, extra), 0)
    lane = lax.broadcasted_iota(jnp.int32, (experts, extra), 1)
    out_ref[:, model_width:] = (
        jnp.dot(
            high,
            (lane == source).astype(jnp.float32).astype(jnp.bfloat16),
            preferred_element_type=jnp.float32,
        )
        + jnp.dot(
            low,
            (lane == source + experts).astype(jnp.float32).astype(jnp.bfloat16),
            preferred_element_type=jnp.float32,
        )
    ).astype(jnp.bfloat16)


def join_kernel(*refs):
    part_refs, out_ref = refs[:-1], refs[-1]
    size = part_refs[0].shape[0]
    for place, ref in enumerate(part_refs):
        out_ref[place * size : (place + 1) * size, :] = ref[...]


def expert_kernel(experts, row_count, sizes, *refs):
    row_refs, refs = refs[:row_count], refs[row_count:]
    in_refs, out_refs, refs = refs[:SPLIT], refs[SPLIT : 2 * SPLIT], refs[2 * SPLIT :]
    result_refs, (rows, hidden) = refs[: len(sizes)], refs[len(sizes) :]
    half, model_width = out_refs[0].shape
    expert = lax.axis_index("expert") // SPLIT
    weights = []
    filled = 0
    for row_ref in row_refs:
        size = row_ref.shape[0]
        rows[filled : filled + size, :] = row_ref[:, :model_width]
        filled += size
        extra = row_ref[:, model_width:].astype(jnp.float32)
        lane = lax.broadcasted_iota(jnp.int32, extra.shape, 1)
        mine = jnp.logical_or(lane == expert, lane == expert + experts)
        weights.append(jnp.sum(jnp.where(mine, extra, 0.0), axis=1, keepdims=True))
    weight = jnp.concatenate(weights, axis=0)
    for place, in_ref in enumerate(in_refs):
        both = jnp.dot(rows[...], in_ref[...], preferred_element_type=jnp.float32)
        gate, up = both[:, :half], both[:, half:]
        hidden[:, place * half : (place + 1) * half] = (
            gate / (1.0 + jnp.exp(-gate)) * up
        ).astype(jnp.bfloat16)
    step = min(512, model_width)
    for start in range(0, model_width, step):
        value = sum(
            jnp.dot(
                hidden[:, place * half : (place + 1) * half],
                out_ref[:, start : start + step],
                preferred_element_type=jnp.float32,
            )
            for place, out_ref in enumerate(out_refs)
        )
        value = (value * weight).astype(jnp.bfloat16)
        filled = 0
        for size, result_ref in zip(sizes, result_refs):
            result_ref[:, start : start + step] = value[filled : filled + size]
            filled += size


def run_expert(experts, row_arrays, weights, sizes):
    total = sum(array.shape[0] for array in row_arrays)
    half, model_width = weights[-1].shape
    return run_kernel(
        functools.partial(expert_kernel, experts, len(row_arrays), sizes),
        [like(size, model_width) for size in sizes],
        list(row_arrays) + list(weights),
        [
            pltpu.VMEM((total, model_width), jnp.bfloat16),
            pltpu.VMEM((total, SPLIT * half), jnp.bfloat16),
        ],
        limit=24,
    )


def plane_kernel(inner, outer, *refs):
    mine_ref, near_refs, far_refs = refs[0], refs[1:inner], refs[inner : 2 * inner - 1]
    kept_ref, *send_refs = refs[2 * inner - 1 :]
    size = kept_ref.shape[0]
    kept_ref[...] = mine_ref[:size, :].astype(jnp.float32) + sum(
        ref[...].astype(jnp.float32) for ref in near_refs
    )
    for j in range(1, outer):
        total = mine_ref[j * size : (j + 1) * size, :].astype(jnp.float32)
        for ref in far_refs:
            total = total + ref[(j - 1) * size : j * size, :].astype(jnp.float32)
        send_refs[j - 1][...] = total.astype(jnp.bfloat16)


def final_kernel(parts, factor, *refs):
    part_refs, refs = refs[:parts], refs[parts:]
    ids_ref, gates_ref, orig_ref, pruned_ref, terms_ref, *value_refs = refs
    total = sum(ref[...].astype(jnp.float32) for ref in part_refs)
    tok_rows = orig_ref.shape[0]
    for value_ref in value_refs:
        value_ref[...] = total
    value_orig, value_pruned = total[:tok_rows], total[tok_rows:]
    orig_ref[...] = value_orig.astype(jnp.bfloat16)
    pruned_ref[...] = value_pruned.astype(jnp.bfloat16)
    differ = value_orig - value_pruned
    errors = jnp.mean(differ * differ, axis=1, keepdims=True)
    dense = dense_weights(ids_ref[...], gates_ref[...], terms_ref.shape[1])
    terms_ref[...] = factor * jnp.sum(dense * errors, axis=0, keepdims=True)


def add_kernel(*refs):
    refs[-1][...] = sum(ref[...] for ref in refs[:-1])


def sum_over(value, masks):
    parts = [value] + [exclusive(value, mask) for mask in masks]
    return run_kernel(add_kernel, like(*value.shape, jnp.float32), parts)


def on_device(
    states_orig,
    states_pruned,
    ids_orig,
    ids_pruned,
    gates_orig,
    gates_pruned,
    keep_mask,
    w_in,
    w_out,
):
    devices = lax.axis_size("expert")
    section_count = lax.axis_size("section")
    section_index = lax.axis_index("section")
    micro_count, tok_rows, model_width = states_orig.shape
    experts = keep_mask.shape[1]
    top_count = ids_orig.shape[-1]
    loss_factor = experts / (top_count * micro_count * tok_rows * devices)
    extra = -(-2 * experts // LANES) * LANES
    rows = 2 * tok_rows
    chips = devices // SPLIT
    inner = min(4, chips)
    outer = chips // inner
    inner_masks = [SPLIT * i for i in range(1, inner)]
    outer_masks = [SPLIT * inner * j for j in range(1, outer)]
    own_in, own_out = w_in[0, 0], w_out[0, 0]
    other_in, other_out = exclusive(own_in, 1), exclusive(own_out, 1)
    weights = [own_in, other_in, own_out, other_out]

    step_count = micro_count + section_count - 1
    carry = jnp.zeros((2, tok_rows, model_width), jnp.bfloat16)
    moe_orig = jnp.zeros((micro_count, tok_rows, model_width), jnp.bfloat16)
    moe_pruned = moe_orig
    terms = jnp.zeros((1, experts), jnp.float32)
    for tick in range(step_count):
        if section_count == 1:
            position = tick
            item = lambda buffer: buffer[position]
        else:
            position = jnp.clip(tick - section_index, 0, micro_count - 1)
            active = jnp.logical_and(
                tick - section_index >= 0, tick - section_index < micro_count
            )
            item = lambda buffer: lax.dynamic_index_in_dim(buffer, position, 0, keepdims=False)
        fresh = min(tick, micro_count - 1)
        state_orig, state_pruned = states_orig[fresh], states_pruned[fresh]
        if section_count > 1:
            state_orig = jnp.where(section_index == 0, state_orig, carry[0])
            state_pruned = jnp.where(section_index == 0, state_pruned, carry[1])
        picked_orig, weight_orig = item(ids_orig[0]), item(gates_orig[0])
        packed = run_kernel(
            pack_kernel,
            like(rows, model_width + extra),
            [
                state_orig,
                state_pruned,
                picked_orig,
                item(ids_pruned[0]),
                weight_orig,
                item(gates_pruned[0]),
                keep_mask,
            ],
        )
        column = [exclusive(packed, mask) for mask in outer_masks]
        near = [exclusive(packed, mask) for mask in inner_masks]
        joined = run_kernel(join_kernel, like((outer - 1) * rows, model_width + extra), column)
        far = [exclusive(joined, mask) for mask in inner_masks]
        mine, *near_out = run_expert(
            experts,
            [packed, joined] + near,
            weights,
            [outer * rows] + [rows] * (inner - 1),
        )
        far_out = run_expert(experts, far, weights, [(outer - 1) * rows] * (inner - 1))
        near_back = [exclusive(part, mask) for part, mask in zip(near_out, inner_masks)]
        far_back = [exclusive(part, mask) for part, mask in zip(far_out, inner_masks)]
        kept_rows, *outgoing = run_kernel(
            functools.partial(plane_kernel, inner, outer),
            [like(rows, model_width, jnp.float32)] + [like(rows, model_width)] * (outer - 1),
            [mine] + near_back + far_back,
        )
        incoming = [exclusive(part, mask) for part, mask in zip(outgoing, outer_masks)]
        round_orig, round_pruned, tick_terms, *moe = run_kernel(
            functools.partial(final_kernel, outer, loss_factor),
            [like(tok_rows, model_width)] * 2
            + [like(1, experts, jnp.float32)]
            + [like(rows, model_width, jnp.float32)] * (section_count > 1),
            [kept_rows] + incoming + [picked_orig, weight_orig],
        )
        if section_count > 1:
            tick_terms = jnp.where(active, tick_terms, 0.0)
            round_orig = jnp.where(active, round_orig, item(moe_orig))
            round_pruned = jnp.where(active, round_pruned, item(moe_pruned))
        terms = tick_terms if tick == 0 else terms + tick_terms
        moe_orig = lax.dynamic_update_index_in_dim(moe_orig, round_orig, position, 0)
        moe_pruned = lax.dynamic_update_index_in_dim(moe_pruned, round_pruned, position, 0)
        if tick + 1 < step_count and section_count > 1:
            state = jnp.stack([state_orig, state_pruned]).astype(jnp.float32)
            following = (state + moe[0].reshape(state.shape)).astype(jnp.bfloat16)
            onward = [(i, i + 1) for i in range(section_count - 1)]
            carry = lax.ppermute(following, "section", onward)
    for masks in ([1], inner_masks, outer_masks):
        terms = sum_over(terms, masks)
    return (moe_orig[None], moe_pruned[None], terms)


def solution(mesh):
    return jax.shard_map(
        on_device,
        mesh=mesh,
        in_specs=(
            P(None, "expert", None),
            P(None, "expert", None),
            P("section", None, "expert", None),
            P("section", None, "expert", None),
            P("section", None, "expert", None),
            P("section", None, "expert", None),
            P("section", None),
            P("section", "expert", None, None),
            P("section", "expert", None, None),
        ),
        out_specs=(
            P("section", None, "expert", None),
            P("section", None, "expert", None),
            P("section", None),
        ),
        check_vma=False,
    )
```

time: 175 us -> 79.2 us (0.45)
  waiting for transfers between devices: 141 us -> 28.8 us
  starting transfers between devices: 3.29 us -> 35.8 us
  between operations: 14.1 us -> 0.71 us
  other arithmetic: 2.38 us -> 0 us
    reduce_scatter x1 -> x0, waiting for transfers between devices: 76.7 us -> none  [on_device(): lax.psum_scatter(partial, 'expert', axis_index_groups=groups, scatter_dim...]
    all_gather x1 -> x0, waiting for transfers between devices: 52.6 us -> none  [on_device(): lax.all_gather(packed, 'expert', axis_index_groups=groups, axis=0, tiled=...]
    ppermute x2 -> x27, starting transfers between devices: 0.64 us -> 35.8 us  [exclusive(): return lax.ppermute(value, 'expert', pairs)]
    ppermute x2 -> x27, waiting for transfers between devices: 4.71 us -> 28.8 us  [exclusive(): return lax.ppermute(value, 'expert', pairs)]
    all_to_all x1 -> x0, waiting for transfers between devices: 6.51 us -> none  [on_device(): lax.all_to_all(spread, 'expert', split_axis=0, concat_axis=0, tiled=True)]
    all_to_all x1 -> x0, starting transfers between devices: 2.57 us -> none  [on_device(): lax.all_to_all(spread, 'expert', split_axis=0, concat_axis=0, tiled=True)]
    unnamed x14 -> x24, local copies, waits for them, and re-layouts: 7.11 us -> 8.22 us
    pallas_call x2 -> x9, Pallas kernels: 5.51 us -> 5.17 us  [run_kernel(): pl.pallas_call(body, out_shape=outs, in_specs=[pl.BlockSpec(memory_space=...]
  transfers between devices with their start and end apart: 5 -> 27, of which waited for: 4 -> 14; matrix products, arithmetic and copies ran while one was open for 1% -> 0% of each run, Pallas kernels for 1% -> 5%
where the time goes in v2:
time: 79.2 us; the launch traced here: 78.7 us
  starting transfers between devices  35.8 us (45%)
  waiting for transfers between devices  28.8 us (36%)
  local copies, waits for them, and re-layouts  8.22 us (10%)
  Pallas kernels  5.17 us (7%)
    ppermute x27, starting transfers between devices, exclusive(): return lax.ppermute(value, 'expert', pairs)  35.8 us
    ppermute x27, waiting for transfers between devices, exclusive(): return lax.ppermute(value, 'expert', pairs)  28.8 us
    unnamed x24, local copies, waits for them, and re-layouts  8.22 us
    pallas_call x9, Pallas kernels, run_kernel(): pl.pallas_call(body, out_shape=outs, in_specs=[pl.BlockSpec(memory_space=...  5.17 us
  transfers between devices with their start and end apart: 27, of which 14 were waited for; matrix products, arithmetic and copies ran while one was open for 0% of the time, Pallas kernels for 5%

profile of v2, /device:TPU:0, one launch (start us, length us, event | category | flops | bytes accessed | tf_op | source)
XLA Modules:
  0.0 78.7 jit_solution(721482993354493896)
XLA Ops:
  0.6 0.5 collective-permute-start.6
  1.2 0.8 copy-done.3
  2.0 0.8 copy-done.4
  2.7 0.7 copy-done.5
  3.4 0.7 copy-done.7
  4.1 0.7 copy-done.9
  4.8 0.7 copy-done.10
  5.5 0.7 copy-done.11
  6.4 3.0 %collective-permute-start = (bf16[16,2176]{1,0:T(8,128)(2,1)S(1)}, bf16[16,2176]{1,0:T(8,128)(2,1)S(1)}, u32[]{:S(2)}, u32[]{:S(2)}) collective-permute-start(bf16[16,2176]{1,0:T(8,128)(2,1)S(1)} %shard_map.112.refs_0_), channel_id=1, source_target_pairs={{0,8},{1,9},{2,10},{3,11},{4,12},{5,13},{6,14},{7,15},{8,0},{9,1},... | collective-permute-start | bytes 208904 | tf_op jit(solution)/shard_map/ppermute | solution.py:32
  9.4 2.6 %collective-permute-start.1 = (bf16[16,2176]{1,0:T(8,128)(2,1)S(1)}, bf16[16,2176]{1,0:T(8,128)(2,1)S(1)}, u32[]{:S(2)}, u32[]{:S(2)}) collective-permute-start(bf16[16,2176]{1,0:T(8,128)(2,1)S(1)} %shard_map.112.refs_0_), channel_id=1, source_target_pairs={{0,16},{1,17},{2,18},{3,19},{4,20},{5,21},{6,22},{7,23},{8,24},{9,... | collective-permute-start | bytes 208904 | tf_op jit(solution)/shard_map/ppermute | solution.py:32
  12.0 5.2 %collective-permute-done.1.refs_1_ = bf16[16,2176]{1,0:T(8,128)(2,1)S(1)} collective-permute-done((bf16[16,2176]{1,0:T(8,128)(2,1)S(1)}, bf16[16,2176]{1,0:T(8,128)(2,1)S(1)}, u32[]{:S(2)}, u32[]{:S(2)}) %collective-permute-start.1) | collective-permute-done | bytes 69664 | tf_op jit(solution)/shard_map/ppermute | solution.py:32
  17.2 1.0 %collective-permute-done.2.refs_2_ = bf16[16,2176]{1,0:T(8,128)(2,1)S(1)} collective-permute-done((bf16[16,2176]{1,0:T(8,128)(2,1)S(1)}, bf16[16,2176]{1,0:T(8,128)(2,1)S(1)}, u32[]{:S(2)}, u32[]{:S(2)}) %collective-permute-start.2) | collective-permute-done | bytes 69664 | tf_op jit(solution)/shard_map/ppermute | solution.py:32
  18.2 1.6 %collective-permute-start.11 = (bf16[48,2176]{1,0:T(8,128)(2,1)S(1)}, bf16[48,2176]{1,0:T(8,128)(2,1)S(1)}, u32[]{:S(2)}, u32[]{:S(2)}) collective-permute-start(bf16[48,2176]{1,0:T(8,128)(2,1)S(1)} %shard_map.113.refs_1_), channel_id=1, source_target_pairs={{0,2},{1,3},{2,0},{3,1},{4,6},{5,7},{6,4},{7,5},{8,10},{9,11},{10,... | collective-permute-start | bytes 626696 | tf_op jit(solution)/shard_map/ppermute | solution.py:32
  19.8 1.5 %collective-permute-start.12 = (bf16[48,2176]{1,0:T(8,128)(2,1)S(1)}, bf16[48,2176]{1,0:T(8,128)(2,1)S(1)}, u32[]{:S(2)}, u32[]{:S(2)}) collective-permute-start(bf16[48,2176]{1,0:T(8,128)(2,1)S(1)} %shard_map.113.refs_1_), channel_id=1, source_target_pairs={{0,4},{1,5},{2,6},{3,7},{4,0},{5,1},{6,2},{7,3},{8,12},{9,13},{10,... | collective-permute-start | bytes 626696 | tf_op jit(solution)/shard_map/ppermute | solution.py:32
  21.8 4.5 %collective-permute-done.11.refs_0_ = bf16[48,2176]{1,0:T(8,128)(2,1)S(1)} collective-permute-done((bf16[48,2176]{1,0:T(8,128)(2,1)S(1)}, bf16[48,2176]{1,0:T(8,128)(2,1)S(1)}, u32[]{:S(2)}, u32[]{:S(2)}) %collective-permute-start.11) | collective-permute-done | bytes 208928 | tf_op jit(solution)/shard_map/ppermute | solution.py:32
  26.3 1.6 %collective-permute-start.3 = (bf16[16,2176]{1,0:T(8,128)(2,1)S(1)}, bf16[16,2176]{1,0:T(8,128)(2,1)S(1)}, u32[]{:S(2)}, u32[]{:S(2)}) collective-permute-start(bf16[16,2176]{1,0:T(8,128)(2,1)S(1)} %shard_map.112.refs_0_), channel_id=1, source_target_pairs={{0,2},{1,3},{2,0},{3,1},{4,6},{5,7},{6,4},{7,5},{8,10},{9,11},{10,... | collective-permute-start | bytes 208904 | tf_op jit(solution)/shard_map/ppermute | solution.py:32
  27.9 1.3 %collective-permute-done.12.refs_1_ = bf16[48,2176]{1,0:T(8,128)(2,1)S(1)} collective-permute-done((bf16[48,2176]{1,0:T(8,128)(2,1)S(1)}, bf16[48,2176]{1,0:T(8,128)(2,1)S(1)}, u32[]{:S(2)}, u32[]{:S(2)}) %collective-permute-start.12) | collective-permute-done | bytes 208928 | tf_op jit(solution)/shard_map/ppermute | solution.py:32
  29.2 2.6 %collective-permute-start.4 = (bf16[16,2176]{1,0:T(8,128)(2,1)S(1)}, bf16[16,2176]{1,0:T(8,128)(2,1)S(1)}, u32[]{:S(2)}, u32[]{:S(2)}) collective-permute-start(bf16[16,2176]{1,0:T(8,128)(2,1)S(1)} %shard_map.112.refs_0_), channel_id=1, source_target_pairs={{0,4},{1,5},{2,6},{3,7},{4,0},{5,1},{6,2},{7,3},{8,12},{9,13},{10,... | collective-permute-start | bytes 208904 | tf_op jit(solution)/shard_map/ppermute | solution.py:32
  31.8 0.5 collective-permute-start.5
  32.3 1.9 %copy-done = bf16[1,1,2048,768]{3,2,1,0:T(8,128)(2,1)S(1)} copy-done((bf16[1,1,2048,768]{3,2,1,0:T(8,128)(2,1)S(1)}, bf16[1,1,2048,768]{3,2,1,0:T(8,128)(2,1)}, u32[]{:S(2)}) %copy-start) | copy-done | bytes 3145752
  34.2 1.4 %copy-done.2 = bf16[1,1,384,2048]{3,2,1,0:T(8,128)(2,1)S(1)} copy-done((bf16[1,1,384,2048]{3,2,1,0:T(8,128)(2,1)S(1)}, bf16[1,1,384,2048]{3,2,1,0:T(8,128)(2,1)}, u32[]{:S(2)}) %copy-start.2) | copy-done | bytes 1572888
  35.6 1.9 %shard_map.115 = (bf16[48,2048]{1,0:T(8,128)(2,1)S(1)}, bf16[48,2048]{1,0:T(8,128)(2,1)S(1)}, bf16[48,2048]{1,0:T(8,128)(2,1)S(1)}) custom-call(bf16[48,2176]{1,0:T(8,128)(2,1)S(1)} %collective-permute-done.11.refs_0_, bf16[48,2176]{1,0:T(8,128)(2,1)S(1)} %collective-permute-done.12.refs_1_, bf16[48,2176]{1,0:T(8,128)(2,1)S(1)} %collective-permute-done.13.refs_2_, ...), custom_call_target="tpu_custom_call" | custom-call | tf_op jit(solution)/shard_map/pallas_call | solution.py:16
  37.5 1.0 %collective-permute-start.14 = (bf16[48,2048]{1,0:T(8,128)(2,1)S(1)}, bf16[48,2048]{1,0:T(8,128)(2,1)S(1)}, u32[]{:S(2)}, u32[]{:S(2)}) collective-permute-start(bf16[48,2048]{1,0:T(8,128)(2,1)S(1)} %get-tuple-element.21), channel_id=1, source_target_pairs={{0,2},{1,3},{2,0},{3,1},{4,6},{5,7},{6,4},{7,5},{8,10},{9,11},{10,... | collective-permute-start | bytes 589832 | tf_op jit(solution)/shard_map/ppermute | solution.py:32
  38.5 2.0 %collective-permute-start.15 = (bf16[48,2048]{1,0:T(8,128)(2,1)S(1)}, bf16[48,2048]{1,0:T(8,128)(2,1)S(1)}, u32[]{:S(2)}, u32[]{:S(2)}) collective-permute-start(bf16[48,2048]{1,0:T(8,128)(2,1)S(1)} %get-tuple-element.22), channel_id=1, source_target_pairs={{0,4},{1,5},{2,6},{3,7},{4,0},{5,1},{6,2},{7,3},{8,12},{9,13},{10,... | collective-permute-start | bytes 589832 | tf_op jit(solution)/shard_map/ppermute | solution.py:32
  40.5 0.6 collective-permute-start.16
  41.1 1.7 %shard_map.114 = (bf16[64,2048]{1,0:T(8,128)(2,1)S(1)}, bf16[16,2048]{1,0:T(8,128)(2,1)S(1)}, bf16[16,2048]{1,0:T(8,128)(2,1)S(1)}, bf16[16,2048]{1,0:T(8,128)(2,1)S(1)}) custom-call(bf16[16,2176]{1,0:T(8,128)(2,1)S(1)} %shard_map.112.refs_0_, bf16[48,2176]{1,0:T(8,128)(2,1)S(1)} %shard_map.113.refs_1_, bf16[16,2176]{1,0:T(8,128)(2,1)S(1)} %collective-permute-done.3.refs_2_, ...), custom_call_target="tpu_custom_call" | custom-call | tf_op jit(solution)/shard_map/pallas_call | solution.py:16
  42.9 2.4 %collective-permute-start.10 = (bf16[16,2048]{1,0:T(8,128)(2,1)S(1)}, bf16[16,2048]{1,0:T(8,128)(2,1)S(1)}, u32[]{:S(2)}, u32[]{:S(2)}) collective-permute-start(bf16[16,2048]{1,0:T(8,128)(2,1)S(1)} %get-tuple-element.20), channel_id=1, source_target_pairs={{0,6},{1,7},{2,4},{3,5},{4,2},{5,3},{6,0},{7,1},{8,14},{9,15},{10,... | collective-permute-start | bytes 196616 | tf_op jit(solution)/shard_map/ppermute | solution.py:32
  45.3 1.1 %collective-permute-start.8 = (bf16[16,2048]{1,0:T(8,128)(2,1)S(1)}, bf16[16,2048]{1,0:T(8,128)(2,1)S(1)}, u32[]{:S(2)}, u32[]{:S(2)}) collective-permute-start(bf16[16,2048]{1,0:T(8,128)(2,1)S(1)} %get-tuple-element.18), channel_id=1, source_target_pairs={{0,2},{1,3},{2,0},{3,1},{4,6},{5,7},{6,4},{7,5},{8,10},{9,11},{10,... | collective-permute-start | bytes 196616 | tf_op jit(solution)/shard_map/ppermute | solution.py:32
  46.3 1.8 %collective-permute-done.10.refs_3_ = bf16[16,2048]{1,0:T(8,128)(2,1)S(1)} collective-permute-done((bf16[16,2048]{1,0:T(8,128)(2,1)S(1)}, bf16[16,2048]{1,0:T(8,128)(2,1)S(1)}, u32[]{:S(2)}, u32[]{:S(2)}) %collective-permute-start.10) | collective-permute-done | bytes 65568 | tf_op jit(solution)/shard_map/ppermute | solution.py:32
  48.1 1.9 %collective-permute-start.9 = (bf16[16,2048]{1,0:T(8,128)(2,1)S(1)}, bf16[16,2048]{1,0:T(8,128)(2,1)S(1)}, u32[]{:S(2)}, u32[]{:S(2)}) collective-permute-start(bf16[16,2048]{1,0:T(8,128)(2,1)S(1)} %get-tuple-element.19), channel_id=1, source_target_pairs={{0,4},{1,5},{2,6},{3,7},{4,0},{5,1},{6,2},{7,3},{8,12},{9,13},{10,... | collective-permute-start | bytes 196616 | tf_op jit(solution)/shard_map/ppermute | solution.py:32
  50.1 2.3 %collective-permute-done.9.refs_2_ = bf16[16,2048]{1,0:T(8,128)(2,1)S(1)} collective-permute-done((bf16[16,2048]{1,0:T(8,128)(2,1)S(1)}, bf16[16,2048]{1,0:T(8,128)(2,1)S(1)}, u32[]{:S(2)}, u32[]{:S(2)}) %collective-permute-start.9) | collective-permute-done | bytes 65568 | tf_op jit(solution)/shard_map/ppermute | solution.py:32
  52.5 1.4 %collective-permute-start.17 = (bf16[16,2048]{1,0:T(8,128)(2,1)S(1)}, bf16[16,2048]{1,0:T(8,128)(2,1)S(1)}, u32[]{:S(2)}, u32[]{:S(2)}) collective-permute-start(bf16[16,2048]{1,0:T(8,128)(2,1)S(1)} %get-tuple-element.25), channel_id=1, source_target_pairs={{0,8},{1,9},{2,10},{3,11},{4,12},{5,13},{6,14},{7,15},{8,0},{9,1},... | collective-permute-start | bytes 196616 | tf_op jit(solution)/shard_map/ppermute | solution.py:32
  53.9 1.0 %collective-permute-start.18 = (bf16[16,2048]{1,0:T(8,128)(2,1)S(1)}, bf16[16,2048]{1,0:T(8,128)(2,1)S(1)}, u32[]{:S(2)}, u32[]{:S(2)}) collective-permute-start(bf16[16,2048]{1,0:T(8,128)(2,1)S(1)} %get-tuple-element.26), channel_id=1, source_target_pairs={{0,16},{1,17},{2,18},{3,19},{4,20},{5,21},{6,22},{7,23},{8,24},{9,... | collective-permute-start | bytes 196616 | tf_op jit(solution)/shard_map/ppermute | solution.py:32
  54.9 2.0 %collective-permute-start.19 = (bf16[16,2048]{1,0:T(8,128)(2,1)S(1)}, bf16[16,2048]{1,0:T(8,128)(2,1)S(1)}, u32[]{:S(2)}, u32[]{:S(2)}) collective-permute-start(bf16[16,2048]{1,0:T(8,128)(2,1)S(1)} %get-tuple-element.27), channel_id=1, source_target_pairs={{0,24},{1,25},{2,26},{3,27},{4,28},{5,29},{6,30},{7,31},{8,16},{9,... | collective-permute-start | bytes 196616 | tf_op jit(solution)/shard_map/ppermute | solution.py:32
  57.0 2.8 %collective-permute-done.18.refs_2_ = bf16[16,2048]{1,0:T(8,128)(2,1)S(1)} collective-permute-done((bf16[16,2048]{1,0:T(8,128)(2,1)S(1)}, bf16[16,2048]{1,0:T(8,128)(2,1)S(1)}, u32[]{:S(2)}, u32[]{:S(2)}) %collective-permute-start.18) | collective-permute-done | bytes 65568 | tf_op jit(solution)/shard_map/ppermute | solution.py:32
  59.8 1.3 %collective-permute-done.19.refs_3_ = bf16[16,2048]{1,0:T(8,128)(2,1)S(1)} collective-permute-done((bf16[16,2048]{1,0:T(8,128)(2,1)S(1)}, bf16[16,2048]{1,0:T(8,128)(2,1)S(1)}, u32[]{:S(2)}, u32[]{:S(2)}) %collective-permute-start.19) | collective-permute-done | bytes 65568 | tf_op jit(solution)/shard_map/ppermute | solution.py:32
  61.1 0.7 shard_map.117
  61.8 1.1 %collective-permute-done.20.refs_1_ = f32[1,16]{1,0:T(1,128)S(1)} collective-permute-done((f32[1,16]{1,0:T(1,128)S(1)}, f32[1,16]{1,0:T(1,128)S(1)}, u32[]{:S(2)}, u32[]{:S(2)}) %collective-permute-start.20) | collective-permute-done | bytes 96 | tf_op jit(solution)/shard_map/ppermute | solution.py:32
  62.9 1.1 %collective-permute-start.21 = (f32[1,16]{1,0:T(1,128)S(1)}, f32[1,16]{1,0:T(1,128)S(1)}, u32[]{:S(2)}, u32[]{:S(2)}) collective-permute-start(f32[1,16]{1,0:T(1,128)S(1)} %shard_map.118.refs_0_), channel_id=1, source_target_pairs={{0,2},{1,3},{2,0},{3,1},{4,6},{5,7},{6,4},{7,5},{8,10},{9,11},{10,... | collective-permute-start | bytes 200 | tf_op jit(solution)/shard_map/ppermute | solution.py:32
  64.1 1.9 %collective-permute-start.22 = (f32[1,16]{1,0:T(1,128)S(1)}, f32[1,16]{1,0:T(1,128)S(1)}, u32[]{:S(2)}, u32[]{:S(2)}) collective-permute-start(f32[1,16]{1,0:T(1,128)S(1)} %shard_map.118.refs_0_), channel_id=1, source_target_pairs={{0,4},{1,5},{2,6},{3,7},{4,0},{5,1},{6,2},{7,3},{8,12},{9,13},{10,... | collective-permute-start | bytes 200 | tf_op jit(solution)/shard_map/ppermute | solution.py:32
  66.5 1.1 %collective-permute-done.22.refs_2_ = f32[1,16]{1,0:T(1,128)S(1)} collective-permute-done((f32[1,16]{1,0:T(1,128)S(1)}, f32[1,16]{1,0:T(1,128)S(1)}, u32[]{:S(2)}, u32[]{:S(2)}) %collective-permute-start.22) | collective-permute-done | bytes 96 | tf_op jit(solution)/shard_map/ppermute | solution.py:32
  67.6 2.8 %collective-permute-done.23.refs_3_ = f32[1,16]{1,0:T(1,128)S(1)} collective-permute-done((f32[1,16]{1,0:T(1,128)S(1)}, f32[1,16]{1,0:T(1,128)S(1)}, u32[]{:S(2)}, u32[]{:S(2)}) %collective-permute-start.23) | collective-permute-done | bytes 96 | tf_op jit(solution)/shard_map/ppermute | solution.py:32
  70.4 0.7 collective-permute-start.24
  71.2 1.7 %collective-permute-start.25 = (f32[1,16]{1,0:T(1,128)S(1)}, f32[1,16]{1,0:T(1,128)S(1)}, u32[]{:S(2)}, u32[]{:S(2)}) collective-permute-start(f32[1,16]{1,0:T(1,128)S(1)} %shard_map.119.refs_0_), channel_id=1, source_target_pairs={{0,16},{1,17},{2,18},{3,19},{4,20},{5,21},{6,22},{7,23},{8,24},{9,... | collective-permute-start | bytes 200 | tf_op jit(solution)/shard_map/ppermute | solution.py:32
  72.9 2.0 %collective-permute-start.26 = (f32[1,16]{1,0:T(1,128)S(1)}, f32[1,16]{1,0:T(1,128)S(1)}, u32[]{:S(2)}, u32[]{:S(2)}) collective-permute-start(f32[1,16]{1,0:T(1,128)S(1)} %shard_map.119.refs_0_), channel_id=1, source_target_pairs={{0,24},{1,25},{2,26},{3,27},{4,28},{5,29},{6,30},{7,31},{8,16},{9,... | collective-permute-start | bytes 200 | tf_op jit(solution)/shard_map/ppermute | solution.py:32
  74.8 0.8 %collective-permute-done.25.refs_2_ = f32[1,16]{1,0:T(1,128)S(1)} collective-permute-done((f32[1,16]{1,0:T(1,128)S(1)}, f32[1,16]{1,0:T(1,128)S(1)}, u32[]{:S(2)}, u32[]{:S(2)}) %collective-permute-start.25) | collective-permute-done | bytes 96 | tf_op jit(solution)/shard_map/ppermute | solution.py:32
  75.6 2.6 %collective-permute-done.26.refs_3_ = f32[1,16]{1,0:T(1,128)S(1)} collective-permute-done((f32[1,16]{1,0:T(1,128)S(1)}, f32[1,16]{1,0:T(1,128)S(1)}, u32[]{:S(2)}, u32[]{:S(2)}) %collective-permute-start.26) | collective-permute-done | bytes 96 | tf_op jit(solution)/shard_map/ppermute | solution.py:32
  78.2 0.5 shard_map.120
  (39 shorter events, 1.5 us)
Async XLA Ops:
  0.6 31.7 %collective-permute-start.6 = (bf16[2048,768]{1,0:T(8,128)(2,1)}, bf16[2048,768]{1,0:T(8,128)(2,1)S(1)}, u32[]{:S(2)}, u32[]{:S(2)}) collective-permute-start(bf16[2048,768]{1,0:T(8,128)(2,1)} %bitcast.10), channel_id=1, source_target_pairs={{0,1},{1,0},{2,3},{3,2},{4,5},{5,4},{6,7},{7,6},{8,9},{9,8},{10,11... | collective-permute-start | bytes 9437192 | tf_op jit(solution)/shard_map/ppermute | solution.py:32
  1.1 31.2 %collective-permute-start.7 = (bf16[384,2048]{1,0:T(8,128)(2,1)}, bf16[384,2048]{1,0:T(8,128)(2,1)S(1)}, u32[]{:S(2)}, u32[]{:S(2)}) collective-permute-start(bf16[384,2048]{1,0:T(8,128)(2,1)} %bitcast.13), channel_id=1, source_target_pairs={{0,1},{1,0},{2,3},{3,2},{4,5},{5,4},{6,7},{7,6},{8,9},{9,8},{10,11... | collective-permute-start | bytes 4718600 | tf_op jit(solution)/shard_map/ppermute | solution.py:32
  1.2 0.8 copy-start.3
  2.0 0.8 copy-start.4
  2.7 0.7 copy-start.5
  3.4 0.7 copy-start.7
  4.1 0.7 copy-start.9
  4.8 0.7 copy-start.10
  5.5 0.7 copy-start.11
  6.4 5.6 %collective-permute-start = (bf16[16,2176]{1,0:T(8,128)(2,1)S(1)}, bf16[16,2176]{1,0:T(8,128)(2,1)S(1)}, u32[]{:S(2)}, u32[]{:S(2)}) collective-permute-start(bf16[16,2176]{1,0:T(8,128)(2,1)S(1)} %shard_map.112.refs_0_), channel_id=1, source_target_pairs={{0,8},{1,9},{2,10},{3,11},{4,12},{5,13},{6,14},{7,15},{8,0},{9,1},... | collective-permute-start | bytes 208904 | tf_op jit(solution)/shard_map/ppermute | solution.py:32
  9.4 7.8 %collective-permute-start.1 = (bf16[16,2176]{1,0:T(8,128)(2,1)S(1)}, bf16[16,2176]{1,0:T(8,128)(2,1)S(1)}, u32[]{:S(2)}, u32[]{:S(2)}) collective-permute-start(bf16[16,2176]{1,0:T(8,128)(2,1)S(1)} %shard_map.112.refs_0_), channel_id=1, source_target_pairs={{0,16},{1,17},{2,18},{3,19},{4,20},{5,21},{6,22},{7,23},{8,24},{9,... | collective-permute-start | bytes 208904 | tf_op jit(solution)/shard_map/ppermute | solution.py:32
  12.0 6.2 %collective-permute-start.2 = (bf16[16,2176]{1,0:T(8,128)(2,1)S(1)}, bf16[16,2176]{1,0:T(8,128)(2,1)S(1)}, u32[]{:S(2)}, u32[]{:S(2)}) collective-permute-start(bf16[16,2176]{1,0:T(8,128)(2,1)S(1)} %shard_map.112.refs_0_), channel_id=1, source_target_pairs={{0,24},{1,25},{2,26},{3,27},{4,28},{5,29},{6,30},{7,31},{8,16},{9,... | collective-permute-start | bytes 208904 | tf_op jit(solution)/shard_map/ppermute | solution.py:32
  18.2 8.1 %collective-permute-start.11 = (bf16[48,2176]{1,0:T(8,128)(2,1)S(1)}, bf16[48,2176]{1,0:T(8,128)(2,1)S(1)}, u32[]{:S(2)}, u32[]{:S(2)}) collective-permute-start(bf16[48,2176]{1,0:T(8,128)(2,1)S(1)} %shard_map.113.refs_1_), channel_id=1, source_target_pairs={{0,2},{1,3},{2,0},{3,1},{4,6},{5,7},{6,4},{7,5},{8,10},{9,11},{10,... | collective-permute-start | bytes 626696 | tf_op jit(solution)/shard_map/ppermute | solution.py:32
  19.8 9.4 %collective-permute-start.12 = (bf16[48,2176]{1,0:T(8,128)(2,1)S(1)}, bf16[48,2176]{1,0:T(8,128)(2,1)S(1)}, u32[]{:S(2)}, u32[]{:S(2)}) collective-permute-start(bf16[48,2176]{1,0:T(8,128)(2,1)S(1)} %shard_map.113.refs_1_), channel_id=1, source_target_pairs={{0,4},{1,5},{2,6},{3,7},{4,0},{5,1},{6,2},{7,3},{8,12},{9,13},{10,... | collective-permute-start | bytes 626696 | tf_op jit(solution)/shard_map/ppermute | solution.py:32
  21.3 10.5 %collective-permute-start.13 = (bf16[48,2176]{1,0:T(8,128)(2,1)S(1)}, bf16[48,2176]{1,0:T(8,128)(2,1)S(1)}, u32[]{:S(2)}, u32[]{:S(2)}) collective-permute-start(bf16[48,2176]{1,0:T(8,128)(2,1)S(1)} %shard_map.113.refs_1_), channel_id=1, source_target_pairs={{0,6},{1,7},{2,4},{3,5},{4,2},{5,3},{6,0},{7,1},{8,14},{9,15},{10,... | collective-permute-start | bytes 626696 | tf_op jit(solution)/shard_map/ppermute | solution.py:32
  26.3 14.2 %collective-permute-start.3 = (bf16[16,2176]{1,0:T(8,128)(2,1)S(1)}, bf16[16,2176]{1,0:T(8,128)(2,1)S(1)}, u32[]{:S(2)}, u32[]{:S(2)}) collective-permute-start(bf16[16,2176]{1,0:T(8,128)(2,1)S(1)} %shard_map.112.refs_0_), channel_id=1, source_target_pairs={{0,2},{1,3},{2,0},{3,1},{4,6},{5,7},{6,4},{7,5},{8,10},{9,11},{10,... | collective-permute-start | bytes 208904 | tf_op jit(solution)/shard_map/ppermute | solution.py:32
  29.2 12.0 %collective-permute-start.4 = (bf16[16,2176]{1,0:T(8,128)(2,1)S(1)}, bf16[16,2176]{1,0:T(8,128)(2,1)S(1)}, u32[]{:S(2)}, u32[]{:S(2)}) collective-permute-start(bf16[16,2176]{1,0:T(8,128)(2,1)S(1)} %shard_map.112.refs_0_), channel_id=1, source_target_pairs={{0,4},{1,5},{2,6},{3,7},{4,0},{5,1},{6,2},{7,3},{8,12},{9,13},{10,... | collective-permute-start | bytes 208904 | tf_op jit(solution)/shard_map/ppermute | solution.py:32
  31.8 9.4 %collective-permute-start.5 = (bf16[16,2176]{1,0:T(8,128)(2,1)S(1)}, bf16[16,2176]{1,0:T(8,128)(2,1)S(1)}, u32[]{:S(2)}, u32[]{:S(2)}) collective-permute-start(bf16[16,2176]{1,0:T(8,128)(2,1)S(1)} %shard_map.112.refs_0_), channel_id=1, source_target_pairs={{0,6},{1,7},{2,4},{3,5},{4,2},{5,3},{6,0},{7,1},{8,14},{9,15},{10,... | collective-permute-start | bytes 208904 | tf_op jit(solution)/shard_map/ppermute | solution.py:32
  32.3 1.9 %copy-start = (bf16[1,1,2048,768]{3,2,1,0:T(8,128)(2,1)S(1)}, bf16[1,1,2048,768]{3,2,1,0:T(8,128)(2,1)}, u32[]{:S(2)}) copy-start(bf16[1,1,2048,768]{3,2,1,0:T(8,128)(2,1)} %param.16) | copy-start | bytes 9437188
  34.2 1.4 %copy-start.2 = (bf16[1,1,384,2048]{3,2,1,0:T(8,128)(2,1)S(1)}, bf16[1,1,384,2048]{3,2,1,0:T(8,128)(2,1)}, u32[]{:S(2)}) copy-start(bf16[1,1,384,2048]{3,2,1,0:T(8,128)(2,1)} %param.17) | copy-start | bytes 4718596
  35.6 5.5 %copy-start.1 = (bf16[1,1,2048,768]{3,2,1,0:T(8,128)(2,1)S(1)}, bf16[1,1,2048,768]{3,2,1,0:T(8,128)(2,1)}, u32[]{:S(2)}) copy-start(bf16[1,1,2048,768]{3,2,1,0:T(8,128)(2,1)} %param.16) | copy-start | bytes 9437188
  37.5 14.9 %collective-permute-start.14 = (bf16[48,2048]{1,0:T(8,128)(2,1)S(1)}, bf16[48,2048]{1,0:T(8,128)(2,1)S(1)}, u32[]{:S(2)}, u32[]{:S(2)}) collective-permute-start(bf16[48,2048]{1,0:T(8,128)(2,1)S(1)} %get-tuple-element.21), channel_id=1, source_target_pairs={{0,2},{1,3},{2,0},{3,1},{4,6},{5,7},{6,4},{7,5},{8,10},{9,11},{10,... | collective-permute-start | bytes 589832 | tf_op jit(solution)/shard_map/ppermute | solution.py:32
  38.5 13.9 %collective-permute-start.15 = (bf16[48,2048]{1,0:T(8,128)(2,1)S(1)}, bf16[48,2048]{1,0:T(8,128)(2,1)S(1)}, u32[]{:S(2)}, u32[]{:S(2)}) collective-permute-start(bf16[48,2048]{1,0:T(8,128)(2,1)S(1)} %get-tuple-element.22), channel_id=1, source_target_pairs={{0,4},{1,5},{2,6},{3,7},{4,0},{5,1},{6,2},{7,3},{8,12},{9,13},{10,... | collective-permute-start | bytes 589832 | tf_op jit(solution)/shard_map/ppermute | solution.py:32
  40.5 20.6 %copy-start.6 = (s32[1,1,8,8]{3,2,1,0:T(8,128)S(1)}, s32[1,1,8,8]{3,2,1,0:T(8,128)}, u32[]{:S(2)}) copy-start(s32[1,1,8,8]{3,2,1,0:T(8,128)} %param.11) | copy-start | bytes 772
  40.5 20.6 %copy-start.8 = (f32[1,1,8,8]{3,2,1,0:T(8,128)S(1)}, f32[1,1,8,8]{3,2,1,0:T(8,128)}, u32[]{:S(2)}) copy-start(f32[1,1,8,8]{3,2,1,0:T(8,128)} %param.13) | copy-start | bytes 772
  40.5 11.8 %collective-permute-start.16 = (bf16[48,2048]{1,0:T(8,128)(2,1)S(1)}, bf16[48,2048]{1,0:T(8,128)(2,1)S(1)}, u32[]{:S(2)}, u32[]{:S(2)}) collective-permute-start(bf16[48,2048]{1,0:T(8,128)(2,1)S(1)} %get-tuple-element.23), channel_id=1, source_target_pairs={{0,6},{1,7},{2,4},{3,5},{4,2},{5,3},{6,0},{7,1},{8,14},{9,15},{10,... | collective-permute-start | bytes 589832 | tf_op jit(solution)/shard_map/ppermute | solution.py:32
  42.9 5.2 %collective-permute-start.10 = (bf16[16,2048]{1,0:T(8,128)(2,1)S(1)}, bf16[16,2048]{1,0:T(8,128)(2,1)S(1)}, u32[]{:S(2)}, u32[]{:S(2)}) collective-permute-start(bf16[16,2048]{1,0:T(8,128)(2,1)S(1)} %get-tuple-element.20), channel_id=1, source_target_pairs={{0,6},{1,7},{2,4},{3,5},{4,2},{5,3},{6,0},{7,1},{8,14},{9,15},{10,... | collective-permute-start | bytes 196616 | tf_op jit(solution)/shard_map/ppermute | solution.py:32
  45.3 4.8 %collective-permute-start.8 = (bf16[16,2048]{1,0:T(8,128)(2,1)S(1)}, bf16[16,2048]{1,0:T(8,128)(2,1)S(1)}, u32[]{:S(2)}, u32[]{:S(2)}) collective-permute-start(bf16[16,2048]{1,0:T(8,128)(2,1)S(1)} %get-tuple-element.18), channel_id=1, source_target_pairs={{0,2},{1,3},{2,0},{3,1},{4,6},{5,7},{6,4},{7,5},{8,10},{9,11},{10,... | collective-permute-start | bytes 196616 | tf_op jit(solution)/shard_map/ppermute | solution.py:32
  48.1 4.3 %collective-permute-start.9 = (bf16[16,2048]{1,0:T(8,128)(2,1)S(1)}, bf16[16,2048]{1,0:T(8,128)(2,1)S(1)}, u32[]{:S(2)}, u32[]{:S(2)}) collective-permute-start(bf16[16,2048]{1,0:T(8,128)(2,1)S(1)} %get-tuple-element.19), channel_id=1, source_target_pairs={{0,4},{1,5},{2,6},{3,7},{4,0},{5,1},{6,2},{7,3},{8,12},{9,13},{10,... | collective-permute-start | bytes 196616 | tf_op jit(solution)/shard_map/ppermute | solution.py:32
  52.5 4.5 %collective-permute-start.17 = (bf16[16,2048]{1,0:T(8,128)(2,1)S(1)}, bf16[16,2048]{1,0:T(8,128)(2,1)S(1)}, u32[]{:S(2)}, u32[]{:S(2)}) collective-permute-start(bf16[16,2048]{1,0:T(8,128)(2,1)S(1)} %get-tuple-element.25), channel_id=1, source_target_pairs={{0,8},{1,9},{2,10},{3,11},{4,12},{5,13},{6,14},{7,15},{8,0},{9,1},... | collective-permute-start | bytes 196616 | tf_op jit(solution)/shard_map/ppermute | solution.py:32
  53.9 5.9 %collective-permute-start.18 = (bf16[16,2048]{1,0:T(8,128)(2,1)S(1)}, bf16[16,2048]{1,0:T(8,128)(2,1)S(1)}, u32[]{:S(2)}, u32[]{:S(2)}) collective-permute-start(bf16[16,2048]{1,0:T(8,128)(2,1)S(1)} %get-tuple-element.26), channel_id=1, source_target_pairs={{0,16},{1,17},{2,18},{3,19},{4,20},{5,21},{6,22},{7,23},{8,24},{9,... | collective-permute-start | bytes 196616 | tf_op jit(solution)/shard_map/ppermute | solution.py:32
  54.9 6.2 %collective-permute-start.19 = (bf16[16,2048]{1,0:T(8,128)(2,1)S(1)}, bf16[16,2048]{1,0:T(8,128)(2,1)S(1)}, u32[]{:S(2)}, u32[]{:S(2)}) collective-permute-start(bf16[16,2048]{1,0:T(8,128)(2,1)S(1)} %get-tuple-element.27), channel_id=1, source_target_pairs={{0,24},{1,25},{2,26},{3,27},{4,28},{5,29},{6,30},{7,31},{8,16},{9,... | collective-permute-start | bytes 196616 | tf_op jit(solution)/shard_map/ppermute | solution.py:32
  61.8 1.1 %collective-permute-start.20 = (f32[1,16]{1,0:T(1,128)S(1)}, f32[1,16]{1,0:T(1,128)S(1)}, u32[]{:S(2)}, u32[]{:S(2)}) collective-permute-start(f32[1,16]{1,0:T(1,128)S(1)} %get-tuple-element.30.refs_0_), channel_id=1, source_target_pairs={{0,1},{1,0},{2,3},{3,2},{4,5},{5,4},{6,7},{7,6},{8,9},{9,8},{10,11... | collective-permute-start | bytes 200 | tf_op jit(solution)/shard_map/ppermute | solution.py:32
  62.9 3.5 %collective-permute-start.21 = (f32[1,16]{1,0:T(1,128)S(1)}, f32[1,16]{1,0:T(1,128)S(1)}, u32[]{:S(2)}, u32[]{:S(2)}) collective-permute-start(f32[1,16]{1,0:T(1,128)S(1)} %shard_map.118.refs_0_), channel_id=1, source_target_pairs={{0,2},{1,3},{2,0},{3,1},{4,6},{5,7},{6,4},{7,5},{8,10},{9,11},{10,... | collective-permute-start | bytes 200 | tf_op jit(solution)/shard_map/ppermute | solution.py:32
  64.1 3.5 %collective-permute-start.22 = (f32[1,16]{1,0:T(1,128)S(1)}, f32[1,16]{1,0:T(1,128)S(1)}, u32[]{:S(2)}, u32[]{:S(2)}) collective-permute-start(f32[1,16]{1,0:T(1,128)S(1)} %shard_map.118.refs_0_), channel_id=1, source_target_pairs={{0,4},{1,5},{2,6},{3,7},{4,0},{5,1},{6,2},{7,3},{8,12},{9,13},{10,... | collective-permute-start | bytes 200 | tf_op jit(solution)/shard_map/ppermute | solution.py:32
  66.0 4.4 %collective-permute-start.23 = (f32[1,16]{1,0:T(1,128)S(1)}, f32[1,16]{1,0:T(1,128)S(1)}, u32[]{:S(2)}, u32[]{:S(2)}) collective-permute-start(f32[1,16]{1,0:T(1,128)S(1)} %shard_map.118.refs_0_), channel_id=1, source_target_pairs={{0,6},{1,7},{2,4},{3,5},{4,2},{5,3},{6,0},{7,1},{8,14},{9,15},{10,... | collective-permute-start | bytes 200 | tf_op jit(solution)/shard_map/ppermute | solution.py:32
  70.4 4.4 %collective-permute-start.24 = (f32[1,16]{1,0:T(1,128)S(1)}, f32[1,16]{1,0:T(1,128)S(1)}, u32[]{:S(2)}, u32[]{:S(2)}) collective-permute-start(f32[1,16]{1,0:T(1,128)S(1)} %shard_map.119.refs_0_), channel_id=1, source_target_pairs={{0,8},{1,9},{2,10},{3,11},{4,12},{5,13},{6,14},{7,15},{8,0},{9,1},... | collective-permute-start | bytes 200 | tf_op jit(solution)/shard_map/ppermute | solution.py:32
  71.2 4.4 %collective-permute-start.25 = (f32[1,16]{1,0:T(1,128)S(1)}, f32[1,16]{1,0:T(1,128)S(1)}, u32[]{:S(2)}, u32[]{:S(2)}) collective-permute-start(f32[1,16]{1,0:T(1,128)S(1)} %shard_map.119.refs_0_), channel_id=1, source_target_pairs={{0,16},{1,17},{2,18},{3,19},{4,20},{5,21},{6,22},{7,23},{8,24},{9,... | collective-permute-start | bytes 200 | tf_op jit(solution)/shard_map/ppermute | solution.py:32
  72.9 5.3 %collective-permute-start.26 = (f32[1,16]{1,0:T(1,128)S(1)}, f32[1,16]{1,0:T(1,128)S(1)}, u32[]{:S(2)}, u32[]{:S(2)}) collective-permute-start(f32[1,16]{1,0:T(1,128)S(1)} %shard_map.119.refs_0_), channel_id=1, source_target_pairs={{0,24},{1,25},{2,26},{3,27},{4,28},{5,29},{6,30},{7,31},{8,16},{9,... | collective-permute-start | bytes 200 | tf_op jit(solution)/shard_map/ppermute | solution.py:32

commit v3 on v2

--- a/solution.py
+++ b/solution.py
@@ -12,15 +12,19 @@
 MIB = 2**20
 
 
-def run_kernel(body, outs, operands, scratch=(), limit=16):
+def run_kernel(body, outs, operands, scratch=(), limit=16, space=pltpu.VMEM):
     return pl.pallas_call(
         body,
         out_shape=outs,
-        in_specs=[pl.BlockSpec(memory_space=pltpu.VMEM)] * len(operands),
+        in_specs=[pl.BlockSpec(memory_space=space)] * len(operands),
         out_specs=jax.tree.map(lambda _: pl.BlockSpec(memory_space=pltpu.VMEM), outs),
         scratch_shapes=list(scratch),
         compiler_params=pltpu.CompilerParams(vmem_limit_bytes=limit * MIB),
     )(*operands)
+
+
+def in_hbm(value):
+    return pltpu.with_memory_space_constraint(value, pltpu.HBM)
 
 
 def like(rows, columns, dtype=jnp.bfloat16):
@@ -46,7 +50,18 @@
     return total
 
 
-def pack_kernel(so_ref, sp_ref, io_ref, ip_ref, go_ref, gp_ref, keep_ref, out_ref):
+def pack_kernel(count, *refs):
+    sources, (out_ref, spread_ref), scratch = refs[:count], refs[count : count + 2], refs[count + 2 :]
+    held, sems = scratch[:count], scratch[count]
+    copies = [
+        pltpu.make_async_copy(source, target, sems.at[place])
+        for place, (source, target) in enumerate(zip(sources, held))
+    ]
+    for copy in copies:
+        copy.start()
+    for copy in copies:
+        copy.wait()
+    so_ref, sp_ref, io_ref, ip_ref, go_ref, gp_ref, keep_ref = held
     model_width = so_ref.shape[1]
     extra = out_ref.shape[1] - model_width
     experts = keep_ref.shape[1]
@@ -76,11 +91,39 @@
     ).astype(jnp.bfloat16)
 
 
-def join_kernel(*refs):
-    part_refs, out_ref = refs[:-1], refs[-1]
-    size = part_refs[0].shape[0]
-    for place, ref in enumerate(part_refs):
-        out_ref[place * size : (place + 1) * size, :] = ref[...]
+    rows = out_ref.shape[0]
+    for place in range(spread_ref.shape[0] // rows):
+        spread_ref[place * rows : (place + 1) * rows, :] = out_ref[...]
+
+
+def at_distance(j, inner, rows):
+    layer = lax.axis_index("expert") // (SPLIT * inner)
+    return pl.ds(pl.multiple_of((layer ^ j) * rows, rows), rows)
+
+
+def stage_kernel(count, *refs):
+    sources, targets, sems = refs[:count], refs[count : 2 * count], refs[2 * count]
+    copies = [
+        pltpu.make_async_copy(source, target, sems.at[place])
+        for place, (source, target) in enumerate(zip(sources, targets))
+    ]
+    for copy in copies:
+        copy.start()
+    for copy in copies:
+        copy.wait()
+
+
+def join_kernel(inner, column_ref, packed_ref, *refs):
+    near_refs, (far_ref, early_ref) = refs[:-2], refs[-2:]
+    rows = packed_ref.shape[0]
+    early_ref[:rows, :] = packed_ref[...]
+    for j in range(1, column_ref.shape[0] // rows):
+        block = column_ref[at_distance(j, inner, rows), :]
+        far_ref[(j - 1) * rows : j * rows, :] = block
+        early_ref[j * rows : (j + 1) * rows, :] = block
+    for place, near_ref in enumerate(near_refs):
+        start = column_ref.shape[0] + place * rows
+        early_ref[start : start + rows, :] = near_ref[...]
 
 
 def expert_kernel(experts, row_count, sizes, *refs):
@@ -138,25 +181,29 @@
     )
 
 
-def plane_kernel(inner, outer, *refs):
-    mine_ref, near_refs, far_refs = refs[0], refs[1:inner], refs[inner : 2 * inner - 1]
-    kept_ref, *send_refs = refs[2 * inner - 1 :]
-    size = kept_ref.shape[0]
-    kept_ref[...] = mine_ref[:size, :].astype(jnp.float32) + sum(
-        ref[...].astype(jnp.float32) for ref in near_refs
-    )
-    for j in range(1, outer):
-        total = mine_ref[j * size : (j + 1) * size, :].astype(jnp.float32)
-        for ref in far_refs:
-            total = total + ref[(j - 1) * size : j * size, :].astype(jnp.float32)
-        send_refs[j - 1][...] = total.astype(jnp.bfloat16)
+def plane_kernel(inner, mine_ref, *refs):
+    part_refs, out_ref = refs[:-1], refs[-1]
+    rows = mine_ref.shape[0] - part_refs[0].shape[0]
+    for j in range(out_ref.shape[0] // rows):
+        if j == 0:
+            total = jnp.zeros((rows, out_ref.shape[1]), jnp.float32)
+        else:
+            total = mine_ref[j * rows : (j + 1) * rows, :].astype(jnp.float32)
+            for ref in part_refs:
+                total = total + ref[(j - 1) * rows : j * rows, :].astype(jnp.float32)
+        out_ref[at_distance(j, inner, rows), :] = total.astype(jnp.bfloat16)
 
 
 def final_kernel(parts, factor, *refs):
-    part_refs, refs = refs[:parts], refs[parts:]
+    column_ref, mine_ref, near_refs, refs = refs[0], refs[1], refs[2:parts], refs[parts:]
     ids_ref, gates_ref, orig_ref, pruned_ref, terms_ref, *value_refs = refs
-    total = sum(ref[...].astype(jnp.float32) for ref in part_refs)
     tok_rows = orig_ref.shape[0]
+    rows = 2 * tok_rows
+    total = mine_ref[:rows, :].astype(jnp.float32)
+    for ref in near_refs:
+        total = total + ref[...].astype(jnp.float32)
+    for place in range(column_ref.shape[0] // rows):
+        total = total + column_ref[place * rows : (place + 1) * rows, :].astype(jnp.float32)
     for value_ref in value_refs:
         value_ref[...] = total
     value_orig, value_pruned = total[:tok_rows], total[tok_rows:]
@@ -164,17 +211,14 @@
     pruned_ref[...] = value_pruned.astype(jnp.bfloat16)
     differ = value_orig - value_pruned
     errors = jnp.mean(differ * differ, axis=1, keepdims=True)
-    dense = dense_weights(ids_ref[...], gates_ref[...], terms_ref.shape[1])
-    terms_ref[...] = factor * jnp.sum(dense * errors, axis=0, keepdims=True)
-
-
-def add_kernel(*refs):
-    refs[-1][...] = sum(ref[...] for ref in refs[:-1])
-
-
-def sum_over(value, masks):
-    parts = [value] + [exclusive(value, mask) for mask in masks]
-    return run_kernel(add_kernel, like(*value.shape, jnp.float32), parts)
+    experts = terms_ref.shape[1]
+    dense = dense_weights(ids_ref[...], gates_ref[...], experts)
+    terms = factor * jnp.sum(dense * errors, axis=0, keepdims=True)
+    terms_ref[...] = jnp.broadcast_to(terms, terms_ref.shape)
+
+
+def add_kernel(parts_ref, out_ref):
+    out_ref[...] = jnp.sum(parts_ref[...], axis=0, keepdims=True)
 
 
 def on_device(
@@ -201,16 +245,33 @@
     inner = min(4, chips)
     outer = chips // inner
     inner_masks = [SPLIT * i for i in range(1, inner)]
-    outer_masks = [SPLIT * inner * j for j in range(1, outer)]
+    columns = [
+        [place + SPLIT * inner * j for j in range(outer)] for place in range(SPLIT * inner)
+    ]
+    along_column = functools.partial(
+        lax.all_to_all,
+        axis_name="expert",
+        split_axis=0,
+        concat_axis=0,
+        axis_index_groups=columns,
+        tiled=True,
+    )
     own_in, own_out = w_in[0, 0], w_out[0, 0]
     other_in, other_out = exclusive(own_in, 1), exclusive(own_out, 1)
     weights = [own_in, other_in, own_out, other_out]
+    weights = run_kernel(
+        functools.partial(stage_kernel, len(weights)),
+        [pltpu.VMEM(value.shape, value.dtype) for value in weights],
+        [in_hbm(own_in), other_in, in_hbm(own_out), other_out],
+        [pltpu.SemaphoreType.DMA((len(weights),))],
+        space=pl.ANY,
+    )
 
     step_count = micro_count + section_count - 1
     carry = jnp.zeros((2, tok_rows, model_width), jnp.bfloat16)
     moe_orig = jnp.zeros((micro_count, tok_rows, model_width), jnp.bfloat16)
     moe_pruned = moe_orig
-    terms = jnp.zeros((1, experts), jnp.float32)
+    terms = jnp.zeros((devices, experts), jnp.float32)
     for tick in range(step_count):
         if section_count == 1:
             position = tick
@@ -227,44 +288,55 @@
             state_orig = jnp.where(section_index == 0, state_orig, carry[0])
             state_pruned = jnp.where(section_index == 0, state_pruned, carry[1])
         picked_orig, weight_orig = item(ids_orig[0]), item(gates_orig[0])
-        packed = run_kernel(
-            pack_kernel,
-            like(rows, model_width + extra),
+        operands = [
+            state_orig,
+            state_pruned,
+            picked_orig,
+            item(ids_pruned[0]),
+            weight_orig,
+            item(gates_pruned[0]),
+            keep_mask,
+        ]
+        packed, spread = run_kernel(
+            functools.partial(pack_kernel, len(operands)),
+            [like(rows, model_width + extra), like(outer * rows, model_width + extra)],
+            [in_hbm(value) for value in operands],
+            [pltpu.VMEM(value.shape, value.dtype) for value in operands]
+            + [pltpu.SemaphoreType.DMA((len(operands),))],
+            space=pl.ANY,
+        )
+        column = along_column(spread)
+        near = [exclusive(packed, mask) for mask in inner_masks]
+        joined, early = run_kernel(
+            functools.partial(join_kernel, inner),
             [
-                state_orig,
-                state_pruned,
-                picked_orig,
-                item(ids_pruned[0]),
-                weight_orig,
-                item(gates_pruned[0]),
-                keep_mask,
+                like((outer - 1) * rows, model_width + extra),
+                like((outer + inner - 1) * rows, model_width + extra),
             ],
-        )
-        column = [exclusive(packed, mask) for mask in outer_masks]
-        near = [exclusive(packed, mask) for mask in inner_masks]
-        joined = run_kernel(join_kernel, like((outer - 1) * rows, model_width + extra), column)
+            [column, packed] + near,
+        )
         far = [exclusive(joined, mask) for mask in inner_masks]
+        far_out = run_expert(experts, far, weights, [(outer - 1) * rows] * (inner - 1))
+        far_back = [exclusive(part, mask) for part, mask in zip(far_out, inner_masks)]
         mine, *near_out = run_expert(
             experts,
-            [packed, joined] + near,
+            [early],
             weights,
             [outer * rows] + [rows] * (inner - 1),
         )
-        far_out = run_expert(experts, far, weights, [(outer - 1) * rows] * (inner - 1))
         near_back = [exclusive(part, mask) for part, mask in zip(near_out, inner_masks)]
-        far_back = [exclusive(part, mask) for part, mask in zip(far_out, inner_masks)]
-        kept_rows, *outgoing = run_kernel(
-            functools.partial(plane_kernel, inner, outer),
-            [like(rows, model_width, jnp.float32)] + [like(rows, model_width)] * (outer - 1),
-            [mine] + near_back + far_back,
-        )
-        incoming = [exclusive(part, mask) for part, mask in zip(outgoing, outer_masks)]
+        outgoing = run_kernel(
+            functools.partial(plane_kernel, inner),
+            like(outer * rows, model_width),
+            [mine] + far_back,
+        )
+        incoming = along_column(outgoing)
         round_orig, round_pruned, tick_terms, *moe = run_kernel(
-            functools.partial(final_kernel, outer, loss_factor),
+            functools.partial(final_kernel, inner + 1, loss_factor),
             [like(tok_rows, model_width)] * 2
-            + [like(1, experts, jnp.float32)]
+            + [like(devices, experts, jnp.float32)]
             + [like(rows, model_width, jnp.float32)] * (section_count > 1),
-            [kept_rows] + incoming + [picked_orig, weight_orig],
+            [incoming, mine] + near_back + [picked_orig, weight_orig],
         )
         if section_count > 1:
             tick_terms = jnp.where(active, tick_terms, 0.0)
@@ -278,9 +350,9 @@
             following = (state + moe[0].reshape(state.shape)).astype(jnp.bfloat16)
             onward = [(i, i + 1) for i in range(section_count - 1)]
             carry = lax.ppermute(following, "section", onward)
-    for masks in ([1], inner_masks, outer_masks):
-        terms = sum_over(terms, masks)
-    return (moe_orig[None], moe_pruned[None], terms)
+    shared = lax.all_to_all(terms, "expert", split_axis=0, concat_axis=0, tiled=True)
+    loss = run_kernel(add_kernel, like(1, experts, jnp.float32), [shared])
+    return (moe_orig[None], moe_pruned[None], loss)
 
 
 def solution(mesh):

time: 79.2 us -> 70.3 us (0.89)
  waiting for transfers between devices: 28.8 us -> 15.9 us
  blocking collectives: 0 us -> 12.2 us
  starting transfers between devices: 35.8 us -> 26.2 us
  Pallas kernels: 5.17 us -> 9.61 us
  local copies, waits for them, and re-layouts: 8.22 us -> 5.25 us
    ppermute x27 -> x14, starting transfers between devices: 35.8 us -> 14.7 us  [exclusive(): return lax.ppermute(value, 'expert', pairs)]
    ppermute x27 -> x14, waiting for transfers between devices: 28.8 us -> 15.2 us  [exclusive(): return lax.ppermute(value, 'expert', pairs)]
    all_to_all x0 -> x1, blocking collectives: none -> 12.2 us  [on_device(): lax.all_to_all(terms, 'expert', split_axis=0, concat_axis=0, tiled=True)]
    all_to_all x0 -> x2, starting transfers between devices: none -> 11.5 us  [the longest x1 6.29 us: on_device(): column = along_column(spread)]
    pallas_call x9 -> x8, Pallas kernels: 5.17 us -> 9.61 us  [run_kernel(): pl.pallas_call(body, out_shape=outs, in_specs=[pl.BlockSpec(memory_space=...]
    unnamed x24 -> x18, local copies, waits for them, and re-layouts: 8.22 us -> 5.25 us
  transfers between devices with their start and end apart: 27 -> 16, of which waited for: 14 -> 11; matrix products, arithmetic and copies ran while one was open for 0% -> 0% of each run, Pallas kernels for 5% -> 8%
where the time goes in v3:
time: 70.3 us; the launch traced here: 69.8 us
  starting transfers between devices  26.2 us (37%)
  waiting for transfers between devices  15.9 us (23%)
  blocking collectives  12.2 us (17%)
  Pallas kernels  9.61 us (14%)
  local copies, waits for them, and re-layouts  5.25 us (7%)
    ppermute x14, waiting for transfers between devices, exclusive(): return lax.ppermute(value, 'expert', pairs)  15.2 us
    ppermute x14, starting transfers between devices, exclusive(): return lax.ppermute(value, 'expert', pairs)  14.7 us
    all_to_all x1, blocking collectives, on_device(): lax.all_to_all(terms, 'expert', split_axis=0, concat_axis=0, tiled=True)  12.2 us
    pallas_call x8, Pallas kernels, run_kernel(): pl.pallas_call(body, out_shape=outs, in_specs=[pl.BlockSpec(memory_space=...  9.61 us
    all_to_all x1, starting transfers between devices, on_device(): column = along_column(spread)  6.29 us
    unnamed x18, local copies, waits for them, and re-layouts  5.25 us
    all_to_all x1, starting transfers between devices, on_device(): incoming = along_column(outgoing)  5.19 us
  transfers between devices with their start and end apart: 16, of which 11 were waited for; matrix products, arithmetic and copies ran while one was open for 0% of the time, Pallas kernels for 8%

profile of v3, /device:TPU:0, one launch (start us, length us, event | category | flops | bytes accessed | tf_op | source)
XLA Modules:
  0.0 69.8 jit_solution(3647319456023819496)
XLA Ops:
  0.6 0.5 collective-permute-start.3
  1.1 0.1 collective-permute-start.4
  1.2 1.1 %shard_map.112 = (bf16[16,2176]{1,0:T(8,128)(2,1)S(1)}, bf16[64,2176]{1,0:T(8,128)(2,1)S(1)}) custom-call(bf16[8,2048]{1,0:T(8,128)(2,1)} %bitcast.31, bf16[8,2048]{1,0:T(8,128)(2,1)} %bitcast.32, s32[8,8]{1,0:T(8,128)} %bitcast.22, s32[8,8]{1,0:T(8,128)} %bitcast.33, f32[8,8]{1,0:T(8,128)} %bitcast.24, f32[8,8]{1,0:T(8,128)} %bitcast.34, s32[1,16]{1,0:T(1,128)} %refs_6_.1), custom_call_target="tpu_custom_call" | custom-call | tf_op jit(solution)/shard_map/pallas_call | solution.py:16
  2.3 0.7 %copy-done = bf16[64,2176]{1,0:T(8,128)(2,1)} copy-done((bf16[64,2176]{1,0:T(8,128)(2,1)}, bf16[64,2176]{1,0:T(8,128)(2,1)S(1)}, u32[]{:S(2)}) %copy-start) | copy-done | bytes 278552
  3.1 6.3 %all-to-all-start = ((bf16[4,16,2176]{2,1,0:T(8,128)(2,1)}), bf16[4,16,2176]{2,1,0:T(8,128)(2,1)S(1)}, u32[]{:S(2)}, u32[]{:S(2)}) async-start(bf16[4,16,2176]{2,1,0:T(8,128)(2,1)} %bitcast.20), calls=%async_computation | async-start | bytes 557056 | tf_op jit(solution)/shard_map/all_to_all | solution.py:308
  9.4 1.5 %collective-permute-start = (bf16[16,2176]{1,0:T(8,128)(2,1)S(1)}, bf16[16,2176]{1,0:T(8,128)(2,1)S(1)}, u32[]{:S(2)}, u32[]{:S(2)}) collective-permute-start(bf16[16,2176]{1,0:T(8,128)(2,1)S(1)} %get-tuple-element.22.packed_ref), channel_id=1, source_target_pairs={{0,2},{1,3},{2,0},{3,1},{4,6},{5,7},{6,4},{7,5},{8,10},{9,11},{10,... | collective-permute-start | bytes 208904 | tf_op jit(solution)/shard_map/ppermute | solution.py:36
  10.9 1.5 %collective-permute-start.1 = (bf16[16,2176]{1,0:T(8,128)(2,1)S(1)}, bf16[16,2176]{1,0:T(8,128)(2,1)S(1)}, u32[]{:S(2)}, u32[]{:S(2)}) collective-permute-start(bf16[16,2176]{1,0:T(8,128)(2,1)S(1)} %get-tuple-element.22.packed_ref), channel_id=1, source_target_pairs={{0,4},{1,5},{2,6},{3,7},{4,0},{5,1},{6,2},{7,3},{8,12},{9,13},{10,... | collective-permute-start | bytes 208904 | tf_op jit(solution)/shard_map/ppermute | solution.py:36
  12.4 0.5 collective-permute-start.2
  12.9 0.8 %collective-permute-done.refs_0_ = bf16[16,2176]{1,0:T(8,128)(2,1)S(1)} collective-permute-done((bf16[16,2176]{1,0:T(8,128)(2,1)S(1)}, bf16[16,2176]{1,0:T(8,128)(2,1)S(1)}, u32[]{:S(2)}, u32[]{:S(2)}) %collective-permute-start) | collective-permute-done | bytes 69664 | tf_op jit(solution)/shard_map/ppermute | solution.py:36
  13.7 0.6 copy-done.1
  14.3 0.9 %collective-permute-done.1.refs_1_ = bf16[16,2176]{1,0:T(8,128)(2,1)S(1)} collective-permute-done((bf16[16,2176]{1,0:T(8,128)(2,1)S(1)}, bf16[16,2176]{1,0:T(8,128)(2,1)S(1)}, u32[]{:S(2)}, u32[]{:S(2)}) %collective-permute-start.1) | collective-permute-done | bytes 69664 | tf_op jit(solution)/shard_map/ppermute | solution.py:36
  15.2 0.6 copy-done.3
  15.8 1.8 %collective-permute-done.2.refs_2_ = bf16[16,2176]{1,0:T(8,128)(2,1)S(1)} collective-permute-done((bf16[16,2176]{1,0:T(8,128)(2,1)S(1)}, bf16[16,2176]{1,0:T(8,128)(2,1)S(1)}, u32[]{:S(2)}, u32[]{:S(2)}) %collective-permute-start.2) | collective-permute-done | bytes 69664 | tf_op jit(solution)/shard_map/ppermute | solution.py:36
  17.6 0.6 copy-done.5
  18.2 0.7 all-to-all-done
  18.9 0.9 %copy-done.2 = bf16[16,2176]{1,0:T(8,128)(2,1)S(1)} copy-done((bf16[16,2176]{1,0:T(8,128)(2,1)S(1)}, bf16[16,2176]{1,0:T(8,128)(2,1)}, u32[]{:S(2)}) %copy-start.2) | copy-done | bytes 69656
  19.8 0.9 %copy-done.4 = bf16[16,2176]{1,0:T(8,128)(2,1)S(1)} copy-done((bf16[16,2176]{1,0:T(8,128)(2,1)S(1)}, bf16[16,2176]{1,0:T(8,128)(2,1)}, u32[]{:S(2)}) %copy-start.4) | copy-done | bytes 69656
  20.6 0.9 %copy-done.6 = bf16[16,2176]{1,0:T(8,128)(2,1)S(1)} copy-done((bf16[16,2176]{1,0:T(8,128)(2,1)S(1)}, bf16[16,2176]{1,0:T(8,128)(2,1)}, u32[]{:S(2)}) %copy-start.6) | copy-done | bytes 69656
  21.6 1.6 %collective-permute-start.5 = (bf16[48,2176]{1,0:T(8,128)(2,1)S(1)}, bf16[48,2176]{1,0:T(8,128)(2,1)S(1)}, u32[]{:S(2)}, u32[]{:S(2)}) collective-permute-start(bf16[48,2176]{1,0:T(8,128)(2,1)S(1)} %get-tuple-element.29), channel_id=1, source_target_pairs={{0,2},{1,3},{2,0},{3,1},{4,6},{5,7},{6,4},{7,5},{8,10},{9,11},{10,... | collective-permute-start | bytes 626696 | tf_op jit(solution)/shard_map/ppermute | solution.py:36
  23.1 1.5 %collective-permute-start.6 = (bf16[48,2176]{1,0:T(8,128)(2,1)S(1)}, bf16[48,2176]{1,0:T(8,128)(2,1)S(1)}, u32[]{:S(2)}, u32[]{:S(2)}) collective-permute-start(bf16[48,2176]{1,0:T(8,128)(2,1)S(1)} %get-tuple-element.29), channel_id=1, source_target_pairs={{0,4},{1,5},{2,6},{3,7},{4,0},{5,1},{6,2},{7,3},{8,12},{9,13},{10,... | collective-permute-start | bytes 626696 | tf_op jit(solution)/shard_map/ppermute | solution.py:36
  24.7 0.5 collective-permute-start.7
  25.1 0.0 collective-permute-done.4.refs_3_
  25.1 0.0 collective-permute-done.3.refs_1_
  25.1 2.9 %shard_map.114 = (bf16[2048,768]{1,0:T(8,128)(2,1)S(1)}, bf16[2048,768]{1,0:T(8,128)(2,1)S(1)}, bf16[384,2048]{1,0:T(8,128)(2,1)S(1)}, bf16[384,2048]{1,0:T(8,128)(2,1)S(1)}) custom-call(bf16[2048,768]{1,0:T(8,128)(2,1)} %bitcast.28, bf16[2048,768]{1,0:T(8,128)(2,1)S(1)} %collective-permute-done.3.refs_1_, bf16[384,2048]{1,0:T(8,128)(2,1)} %bitcast.30, ...), custom_call_target="tpu_custom_call" | custom-call | tf_op jit(solution)/shard_map/pallas_call | solution.py:16
  28.1 1.2 %collective-permute-done.5.refs_0_ = bf16[48,2176]{1,0:T(8,128)(2,1)S(1)} collective-permute-done((bf16[48,2176]{1,0:T(8,128)(2,1)S(1)}, bf16[48,2176]{1,0:T(8,128)(2,1)S(1)}, u32[]{:S(2)}, u32[]{:S(2)}) %collective-permute-start.5) | collective-permute-done | bytes 208928 | tf_op jit(solution)/shard_map/ppermute | solution.py:36
  29.3 3.4 %collective-permute-done.6.refs_1_ = bf16[48,2176]{1,0:T(8,128)(2,1)S(1)} collective-permute-done((bf16[48,2176]{1,0:T(8,128)(2,1)S(1)}, bf16[48,2176]{1,0:T(8,128)(2,1)S(1)}, u32[]{:S(2)}, u32[]{:S(2)}) %collective-permute-start.6) | collective-permute-done | bytes 208928 | tf_op jit(solution)/shard_map/ppermute | solution.py:36
  32.7 0.0 collective-permute-done.7.refs_2_
  32.7 1.8 %shard_map.116 = (bf16[48,2048]{1,0:T(8,128)(2,1)S(1)}, bf16[48,2048]{1,0:T(8,128)(2,1)S(1)}, bf16[48,2048]{1,0:T(8,128)(2,1)S(1)}) custom-call(bf16[48,2176]{1,0:T(8,128)(2,1)S(1)} %collective-permute-done.5.refs_0_, bf16[48,2176]{1,0:T(8,128)(2,1)S(1)} %collective-permute-done.6.refs_1_, bf16[48,2176]{1,0:T(8,128)(2,1)S(1)} %collective-permute-done.7.refs_2_, ...), custom_call_target="tpu_custom_call" | custom-call | tf_op jit(solution)/shard_map/pallas_call | solution.py:16
  34.5 1.1 %collective-permute-start.8 = (bf16[48,2048]{1,0:T(8,128)(2,1)S(1)}, bf16[48,2048]{1,0:T(8,128)(2,1)S(1)}, u32[]{:S(2)}, u32[]{:S(2)}) collective-permute-start(bf16[48,2048]{1,0:T(8,128)(2,1)S(1)} %get-tuple-element.30), channel_id=1, source_target_pairs={{0,2},{1,3},{2,0},{3,1},{4,6},{5,7},{6,4},{7,5},{8,10},{9,11},{10,... | collective-permute-start | bytes 589832 | tf_op jit(solution)/shard_map/ppermute | solution.py:36
  35.6 0.8 %collective-permute-start.9 = (bf16[48,2048]{1,0:T(8,128)(2,1)S(1)}, bf16[48,2048]{1,0:T(8,128)(2,1)S(1)}, u32[]{:S(2)}, u32[]{:S(2)}) collective-permute-start(bf16[48,2048]{1,0:T(8,128)(2,1)S(1)} %get-tuple-element.31), channel_id=1, source_target_pairs={{0,4},{1,5},{2,6},{3,7},{4,0},{5,1},{6,2},{7,3},{8,12},{9,13},{10,... | collective-permute-start | bytes 589832 | tf_op jit(solution)/shard_map/ppermute | solution.py:36
  36.4 1.6 %collective-permute-start.10 = (bf16[48,2048]{1,0:T(8,128)(2,1)S(1)}, bf16[48,2048]{1,0:T(8,128)(2,1)S(1)}, u32[]{:S(2)}, u32[]{:S(2)}) collective-permute-start(bf16[48,2048]{1,0:T(8,128)(2,1)S(1)} %get-tuple-element.32), channel_id=1, source_target_pairs={{0,6},{1,7},{2,4},{3,5},{4,2},{5,3},{6,0},{7,1},{8,14},{9,15},{10,... | collective-permute-start | bytes 589832 | tf_op jit(solution)/shard_map/ppermute | solution.py:36
  38.1 1.7 %shard_map.115 = (bf16[64,2048]{1,0:T(8,128)(2,1)S(1)}, bf16[16,2048]{1,0:T(8,128)(2,1)S(1)}, bf16[16,2048]{1,0:T(8,128)(2,1)S(1)}, bf16[16,2048]{1,0:T(8,128)(2,1)S(1)}) custom-call(bf16[112,2176]{1,0:T(8,128)(2,1)S(1)} %get-tuple-element.23.refs_0_, bf16[2048,768]{1,0:T(8,128)(2,1)S(1)} %get-tuple-element.24.refs_1_.refs_3_, ...), custom_call_target="tpu_custom_call" | custom-call | tf_op jit(solution)/shard_map/pallas_call | solution.py:16
  39.8 0.5 collective-permute-done.8.refs_0_
  40.3 3.1 %collective-permute-done.9.refs_1_ = bf16[48,2048]{1,0:T(8,128)(2,1)S(1)} collective-permute-done((bf16[48,2048]{1,0:T(8,128)(2,1)S(1)}, bf16[48,2048]{1,0:T(8,128)(2,1)S(1)}, u32[]{:S(2)}, u32[]{:S(2)}) %collective-permute-start.9) | collective-permute-done | bytes 196640 | tf_op jit(solution)/shard_map/ppermute | solution.py:36
  43.4 0.0 collective-permute-done.10.refs_2_
  43.4 0.8 %shard_map.117 = bf16[64,2048]{1,0:T(8,128)(2,1)} custom-call(bf16[64,2048]{1,0:T(8,128)(2,1)S(1)} %get-tuple-element.28.mine_ref.refs_1_, bf16[48,2048]{1,0:T(8,128)(2,1)S(1)} %collective-permute-done.8.refs_0_, bf16[48,2048]{1,0:T(8,128)(2,1)S(1)} %collective-permute-done.9.refs_1_, bf16[48,2048]{1,0:T(8,128)(2,1)S(1)} %collective-permute-done.10.refs_2_), custom_call_target="tpu_custom_call" | custom-call | tf_op jit(solution)/shard_map/pallas_call | solution.py:16
  44.2 5.2 %all-to-all-start.1 = ((bf16[4,16,2048]{2,1,0:T(8,128)(2,1)}), bf16[4,16,2048]{2,1,0:T(8,128)(2,1)S(1)}, u32[]{:S(2)}, u32[]{:S(2)}) async-start(bf16[4,16,2048]{2,1,0:T(8,128)(2,1)} %bitcast.10), calls=%async_computation.1 | async-start | bytes 524288 | tf_op jit(solution)/shard_map/all_to_all | solution.py:333
  49.4 0.4 collective-permute-start.11
  49.7 1.5 %collective-permute-start.12 = (bf16[16,2048]{1,0:T(8,128)(2,1)S(1)}, bf16[16,2048]{1,0:T(8,128)(2,1)S(1)}, u32[]{:S(2)}, u32[]{:S(2)}) collective-permute-start(bf16[16,2048]{1,0:T(8,128)(2,1)S(1)} %get-tuple-element.34), channel_id=1, source_target_pairs={{0,4},{1,5},{2,6},{3,7},{4,0},{5,1},{6,2},{7,3},{8,12},{9,13},{10,... | collective-permute-start | bytes 196616 | tf_op jit(solution)/shard_map/ppermute | solution.py:36
  51.2 1.7 %collective-permute-start.13 = (bf16[16,2048]{1,0:T(8,128)(2,1)S(1)}, bf16[16,2048]{1,0:T(8,128)(2,1)S(1)}, u32[]{:S(2)}, u32[]{:S(2)}) collective-permute-start(bf16[16,2048]{1,0:T(8,128)(2,1)S(1)} %get-tuple-element.35), channel_id=1, source_target_pairs={{0,6},{1,7},{2,4},{3,5},{4,2},{5,3},{6,0},{7,1},{8,14},{9,15},{10,... | collective-permute-start | bytes 196616 | tf_op jit(solution)/shard_map/ppermute | solution.py:36
  52.9 0.8 %collective-permute-done.11.refs_2_ = bf16[16,2048]{1,0:T(8,128)(2,1)S(1)} collective-permute-done((bf16[16,2048]{1,0:T(8,128)(2,1)S(1)}, bf16[16,2048]{1,0:T(8,128)(2,1)S(1)}, u32[]{:S(2)}, u32[]{:S(2)}) %collective-permute-start.11) | collective-permute-done | bytes 65568 | tf_op jit(solution)/shard_map/ppermute | solution.py:36
  53.6 0.4 collective-permute-done.12.refs_3_
  54.0 2.4 %collective-permute-done.13.refs_4_ = bf16[16,2048]{1,0:T(8,128)(2,1)S(1)} collective-permute-done((bf16[16,2048]{1,0:T(8,128)(2,1)S(1)}, bf16[16,2048]{1,0:T(8,128)(2,1)S(1)}, u32[]{:S(2)}, u32[]{:S(2)}) %collective-permute-start.13) | collective-permute-done | bytes 65568 | tf_op jit(solution)/shard_map/ppermute | solution.py:36
  56.3 0.0 all-to-all-done.1
  56.3 0.0 copy-done.8
  56.4 0.7 %shard_map.118 = (bf16[8,2048]{1,0:T(8,128)(2,1)}, bf16[8,2048]{1,0:T(8,128)(2,1)}, f32[32,16]{1,0:T(8,128)S(1)}) custom-call(bf16[64,2048]{1,0:T(8,128)(2,1)S(1)} %bitcast.19, bf16[64,2048]{1,0:T(8,128)(2,1)S(1)} %get-tuple-element.28.mine_ref.refs_1_, bf16[16,2048]{1,0:T(8,128)(2,1)S(1)} %collective-permute-done.11.refs_2_, ...), custom_call_target="tpu_custom_call" | custom-call | tf_op jit(solution)/shard_map/pallas_call | solution.py:16
  57.1 12.2 %all_to_all.33 = f32[32,1,16]{2,1,0:T(1,128)S(1)} all-to-all(f32[32,1,16]{2,1,0:T(1,128)S(1)} %bitcast.26), channel_id=1, replica_groups=mesh['section'=1,'expert'=32] {'expert'}, dimensions={0} | all-to-all | bytes 4096 | tf_op jit(solution)/shard_map/all_to_all | solution.py:353
  69.3 0.5 shard_map.119
  (11 shorter events, 0.1 us)
Async XLA Ops:
  0.6 24.5 %collective-permute-start.3 = (bf16[2048,768]{1,0:T(8,128)(2,1)}, bf16[2048,768]{1,0:T(8,128)(2,1)S(1)}, u32[]{:S(2)}, u32[]{:S(2)}) collective-permute-start(bf16[2048,768]{1,0:T(8,128)(2,1)} %bitcast.27), channel_id=1, source_target_pairs={{0,1},{1,0},{2,3},{3,2},{4,5},{5,4},{6,7},{7,6},{8,9},{9,8},{10,11... | collective-permute-start | bytes 9437192 | tf_op jit(solution)/shard_map/ppermute | solution.py:36
  1.1 24.0 %collective-permute-start.4 = (bf16[384,2048]{1,0:T(8,128)(2,1)}, bf16[384,2048]{1,0:T(8,128)(2,1)}, u32[]{:S(2)}, u32[]{:S(2)}) collective-permute-start(bf16[384,2048]{1,0:T(8,128)(2,1)} %bitcast.29), channel_id=1, source_target_pairs={{0,1},{1,0},{2,3},{3,2},{4,5},{5,4},{6,7},{7,6},{8,9},{9,8},{10,11... | collective-permute-start | bytes 4718600 | tf_op jit(solution)/shard_map/ppermute | solution.py:36
  2.3 0.7 %copy-start = (bf16[64,2176]{1,0:T(8,128)(2,1)}, bf16[64,2176]{1,0:T(8,128)(2,1)S(1)}, u32[]{:S(2)}) copy-start(bf16[64,2176]{1,0:T(8,128)(2,1)S(1)} %get-tuple-element.21) | copy-start | bytes 835588
  3.1 15.8 %all-to-all-start = ((bf16[4,16,2176]{2,1,0:T(8,128)(2,1)}), bf16[4,16,2176]{2,1,0:T(8,128)(2,1)S(1)}, u32[]{:S(2)}, u32[]{:S(2)}) async-start(bf16[4,16,2176]{2,1,0:T(8,128)(2,1)} %bitcast.20), calls=%async_computation | async-start | bytes 557056 | tf_op jit(solution)/shard_map/all_to_all | solution.py:308
  9.4 4.3 %collective-permute-start = (bf16[16,2176]{1,0:T(8,128)(2,1)S(1)}, bf16[16,2176]{1,0:T(8,128)(2,1)S(1)}, u32[]{:S(2)}, u32[]{:S(2)}) collective-permute-start(bf16[16,2176]{1,0:T(8,128)(2,1)S(1)} %get-tuple-element.22.packed_ref), channel_id=1, source_target_pairs={{0,2},{1,3},{2,0},{3,1},{4,6},{5,7},{6,4},{7,5},{8,10},{9,11},{10,... | collective-permute-start | bytes 208904 | tf_op jit(solution)/shard_map/ppermute | solution.py:36
  10.9 4.3 %collective-permute-start.1 = (bf16[16,2176]{1,0:T(8,128)(2,1)S(1)}, bf16[16,2176]{1,0:T(8,128)(2,1)S(1)}, u32[]{:S(2)}, u32[]{:S(2)}) collective-permute-start(bf16[16,2176]{1,0:T(8,128)(2,1)S(1)} %get-tuple-element.22.packed_ref), channel_id=1, source_target_pairs={{0,4},{1,5},{2,6},{3,7},{4,0},{5,1},{6,2},{7,3},{8,12},{9,13},{10,... | collective-permute-start | bytes 208904 | tf_op jit(solution)/shard_map/ppermute | solution.py:36
  12.4 5.2 %collective-permute-start.2 = (bf16[16,2176]{1,0:T(8,128)(2,1)S(1)}, bf16[16,2176]{1,0:T(8,128)(2,1)S(1)}, u32[]{:S(2)}, u32[]{:S(2)}) collective-permute-start(bf16[16,2176]{1,0:T(8,128)(2,1)S(1)} %get-tuple-element.22.packed_ref), channel_id=1, source_target_pairs={{0,6},{1,7},{2,4},{3,5},{4,2},{5,3},{6,0},{7,1},{8,14},{9,15},{10,... | collective-permute-start | bytes 208904 | tf_op jit(solution)/shard_map/ppermute | solution.py:36
  13.7 0.6 copy-start.1
  15.2 0.6 copy-start.3
  17.6 0.6 copy-start.5
  18.9 0.9 %copy-start.2 = (bf16[16,2176]{1,0:T(8,128)(2,1)S(1)}, bf16[16,2176]{1,0:T(8,128)(2,1)}, u32[]{:S(2)}) copy-start(bf16[16,2176]{1,0:T(8,128)(2,1)} %copy-done.1) | copy-start | bytes 208900
  19.8 0.9 %copy-start.4 = (bf16[16,2176]{1,0:T(8,128)(2,1)S(1)}, bf16[16,2176]{1,0:T(8,128)(2,1)}, u32[]{:S(2)}) copy-start(bf16[16,2176]{1,0:T(8,128)(2,1)} %copy-done.3) | copy-start | bytes 208900
  20.6 0.9 %copy-start.6 = (bf16[16,2176]{1,0:T(8,128)(2,1)S(1)}, bf16[16,2176]{1,0:T(8,128)(2,1)}, u32[]{:S(2)}) copy-start(bf16[16,2176]{1,0:T(8,128)(2,1)} %copy-done.5) | copy-start | bytes 208900
  21.6 7.7 %collective-permute-start.5 = (bf16[48,2176]{1,0:T(8,128)(2,1)S(1)}, bf16[48,2176]{1,0:T(8,128)(2,1)S(1)}, u32[]{:S(2)}, u32[]{:S(2)}) collective-permute-start(bf16[48,2176]{1,0:T(8,128)(2,1)S(1)} %get-tuple-element.29), channel_id=1, source_target_pairs={{0,2},{1,3},{2,0},{3,1},{4,6},{5,7},{6,4},{7,5},{8,10},{9,11},{10,... | collective-permute-start | bytes 626696 | tf_op jit(solution)/shard_map/ppermute | solution.py:36
  23.1 9.5 %collective-permute-start.6 = (bf16[48,2176]{1,0:T(8,128)(2,1)S(1)}, bf16[48,2176]{1,0:T(8,128)(2,1)S(1)}, u32[]{:S(2)}, u32[]{:S(2)}) collective-permute-start(bf16[48,2176]{1,0:T(8,128)(2,1)S(1)} %get-tuple-element.29), channel_id=1, source_target_pairs={{0,4},{1,5},{2,6},{3,7},{4,0},{5,1},{6,2},{7,3},{8,12},{9,13},{10,... | collective-permute-start | bytes 626696 | tf_op jit(solution)/shard_map/ppermute | solution.py:36
  24.7 8.0 %collective-permute-start.7 = (bf16[48,2176]{1,0:T(8,128)(2,1)S(1)}, bf16[48,2176]{1,0:T(8,128)(2,1)S(1)}, u32[]{:S(2)}, u32[]{:S(2)}) collective-permute-start(bf16[48,2176]{1,0:T(8,128)(2,1)S(1)} %get-tuple-element.29), channel_id=1, source_target_pairs={{0,6},{1,7},{2,4},{3,5},{4,2},{5,3},{6,0},{7,1},{8,14},{9,15},{10,... | collective-permute-start | bytes 626696 | tf_op jit(solution)/shard_map/ppermute | solution.py:36
  34.5 5.8 %collective-permute-start.8 = (bf16[48,2048]{1,0:T(8,128)(2,1)S(1)}, bf16[48,2048]{1,0:T(8,128)(2,1)S(1)}, u32[]{:S(2)}, u32[]{:S(2)}) collective-permute-start(bf16[48,2048]{1,0:T(8,128)(2,1)S(1)} %get-tuple-element.30), channel_id=1, source_target_pairs={{0,2},{1,3},{2,0},{3,1},{4,6},{5,7},{6,4},{7,5},{8,10},{9,11},{10,... | collective-permute-start | bytes 589832 | tf_op jit(solution)/shard_map/ppermute | solution.py:36
  35.6 7.8 %collective-permute-start.9 = (bf16[48,2048]{1,0:T(8,128)(2,1)S(1)}, bf16[48,2048]{1,0:T(8,128)(2,1)S(1)}, u32[]{:S(2)}, u32[]{:S(2)}) collective-permute-start(bf16[48,2048]{1,0:T(8,128)(2,1)S(1)} %get-tuple-element.31), channel_id=1, source_target_pairs={{0,4},{1,5},{2,6},{3,7},{4,0},{5,1},{6,2},{7,3},{8,12},{9,13},{10,... | collective-permute-start | bytes 589832 | tf_op jit(solution)/shard_map/ppermute | solution.py:36
  36.4 7.0 %collective-permute-start.10 = (bf16[48,2048]{1,0:T(8,128)(2,1)S(1)}, bf16[48,2048]{1,0:T(8,128)(2,1)S(1)}, u32[]{:S(2)}, u32[]{:S(2)}) collective-permute-start(bf16[48,2048]{1,0:T(8,128)(2,1)S(1)} %get-tuple-element.32), channel_id=1, source_target_pairs={{0,6},{1,7},{2,4},{3,5},{4,2},{5,3},{6,0},{7,1},{8,14},{9,15},{10,... | collective-permute-start | bytes 589832 | tf_op jit(solution)/shard_map/ppermute | solution.py:36
  38.1 18.3 %copy-start.7 = (s32[1,1,8,8]{3,2,1,0:T(8,128)S(1)}, s32[1,1,8,8]{3,2,1,0:T(8,128)}, u32[]{:S(2)}) copy-start(s32[1,1,8,8]{3,2,1,0:T(8,128)} %param.11) | copy-start | bytes 772
  38.1 18.3 %copy-start.8 = (f32[1,1,8,8]{3,2,1,0:T(8,128)S(1)}, f32[1,1,8,8]{3,2,1,0:T(8,128)}, u32[]{:S(2)}) copy-start(f32[1,1,8,8]{3,2,1,0:T(8,128)} %param.13) | copy-start | bytes 772
  44.2 12.2 %all-to-all-start.1 = ((bf16[4,16,2048]{2,1,0:T(8,128)(2,1)}), bf16[4,16,2048]{2,1,0:T(8,128)(2,1)S(1)}, u32[]{:S(2)}, u32[]{:S(2)}) async-start(bf16[4,16,2048]{2,1,0:T(8,128)(2,1)} %bitcast.10), calls=%async_computation.1 | async-start | bytes 524288 | tf_op jit(solution)/shard_map/all_to_all | solution.py:333
  49.4 4.3 %collective-permute-start.11 = (bf16[16,2048]{1,0:T(8,128)(2,1)S(1)}, bf16[16,2048]{1,0:T(8,128)(2,1)S(1)}, u32[]{:S(2)}, u32[]{:S(2)}) collective-permute-start(bf16[16,2048]{1,0:T(8,128)(2,1)S(1)} %get-tuple-element.33), channel_id=1, source_target_pairs={{0,2},{1,3},{2,0},{3,1},{4,6},{5,7},{6,4},{7,5},{8,10},{9,11},{10,... | collective-permute-start | bytes 196616 | tf_op jit(solution)/shard_map/ppermute | solution.py:36
  49.7 4.3 %collective-permute-start.12 = (bf16[16,2048]{1,0:T(8,128)(2,1)S(1)}, bf16[16,2048]{1,0:T(8,128)(2,1)S(1)}, u32[]{:S(2)}, u32[]{:S(2)}) collective-permute-start(bf16[16,2048]{1,0:T(8,128)(2,1)S(1)} %get-tuple-element.34), channel_id=1, source_target_pairs={{0,4},{1,5},{2,6},{3,7},{4,0},{5,1},{6,2},{7,3},{8,12},{9,13},{10,... | collective-permute-start | bytes 196616 | tf_op jit(solution)/shard_map/ppermute | solution.py:36
  51.2 5.2 %collective-permute-start.13 = (bf16[16,2048]{1,0:T(8,128)(2,1)S(1)}, bf16[16,2048]{1,0:T(8,128)(2,1)S(1)}, u32[]{:S(2)}, u32[]{:S(2)}) collective-permute-start(bf16[16,2048]{1,0:T(8,128)(2,1)S(1)} %get-tuple-element.35), channel_id=1, source_target_pairs={{0,6},{1,7},{2,4},{3,5},{4,2},{5,3},{6,0},{7,1},{8,14},{9,15},{10,... | collective-permute-start | bytes 196616 | tf_op jit(solution)/shard_map/ppermute | solution.py:36

commit v4 on v3

--- a/solution.py
+++ b/solution.py
@@ -51,7 +51,7 @@
 
 
 def pack_kernel(count, *refs):
-    sources, (out_ref, spread_ref), scratch = refs[:count], refs[count : count + 2], refs[count + 2 :]
+    sources, out_ref, scratch = refs[:count], refs[count], refs[count + 1 :]
     held, sems = scratch[:count], scratch[count]
     copies = [
         pltpu.make_async_copy(source, target, sems.at[place])
@@ -91,16 +91,6 @@
     ).astype(jnp.bfloat16)
 
 
-    rows = out_ref.shape[0]
-    for place in range(spread_ref.shape[0] // rows):
-        spread_ref[place * rows : (place + 1) * rows, :] = out_ref[...]
-
-
-def at_distance(j, inner, rows):
-    layer = lax.axis_index("expert") // (SPLIT * inner)
-    return pl.ds(pl.multiple_of((layer ^ j) * rows, rows), rows)
-
-
 def stage_kernel(count, *refs):
     sources, targets, sems = refs[:count], refs[count : 2 * count], refs[2 * count]
     copies = [
@@ -113,17 +103,27 @@
         copy.wait()
 
 
-def join_kernel(inner, column_ref, packed_ref, *refs):
-    near_refs, (far_ref, early_ref) = refs[:-2], refs[-2:]
+def stage_weights(own_in, own_out, awaited):
+    sent_out, _ = lax.optimization_barrier((own_out, awaited))
+    other_in, other_out = exclusive(own_in, 1), exclusive(sent_out, 1)
+    weights = [in_hbm(own_in), other_in, in_hbm(own_out), other_out]
+    return run_kernel(
+        functools.partial(stage_kernel, len(weights)),
+        [pltpu.VMEM(value.shape, value.dtype) for value in weights],
+        weights,
+        [pltpu.SemaphoreType.DMA((len(weights),))],
+        space=pl.ANY,
+    )
+
+
+def join_kernel(outer, packed_ref, *refs):
+    part_refs, (far_ref, early_ref) = refs[:-2], refs[-2:]
     rows = packed_ref.shape[0]
     early_ref[:rows, :] = packed_ref[...]
-    for j in range(1, column_ref.shape[0] // rows):
-        block = column_ref[at_distance(j, inner, rows), :]
-        far_ref[(j - 1) * rows : j * rows, :] = block
-        early_ref[j * rows : (j + 1) * rows, :] = block
-    for place, near_ref in enumerate(near_refs):
-        start = column_ref.shape[0] + place * rows
-        early_ref[start : start + rows, :] = near_ref[...]
+    for place, part_ref in enumerate(part_refs):
+        early_ref[(place + 1) * rows : (place + 2) * rows, :] = part_ref[...]
+        if place < outer - 1:
+            far_ref[place * rows : (place + 1) * rows, :] = part_ref[...]
 
 
 def expert_kernel(experts, row_count, sizes, *refs):
@@ -181,29 +181,27 @@
     )
 
 
-def plane_kernel(inner, mine_ref, *refs):
-    part_refs, out_ref = refs[:-1], refs[-1]
-    rows = mine_ref.shape[0] - part_refs[0].shape[0]
-    for j in range(out_ref.shape[0] // rows):
-        if j == 0:
-            total = jnp.zeros((rows, out_ref.shape[1]), jnp.float32)
-        else:
-            total = mine_ref[j * rows : (j + 1) * rows, :].astype(jnp.float32)
-            for ref in part_refs:
-                total = total + ref[(j - 1) * rows : j * rows, :].astype(jnp.float32)
-        out_ref[at_distance(j, inner, rows), :] = total.astype(jnp.bfloat16)
+def plane_kernel(inner, outer, mine_ref, *refs):
+    far_refs, near_refs, refs = refs[: inner - 1], refs[inner - 1 : 2 * inner - 2], refs[2 * inner - 2 :]
+    sum_refs, sent_refs = refs[: outer - 1], refs[outer - 1 :]
+    rows = near_refs[0].shape[0]
+    for place, sum_ref in enumerate(sum_refs):
+        total = mine_ref[(place + 1) * rows : (place + 2) * rows, :].astype(jnp.float32)
+        for ref in far_refs:
+            total = total + ref[place * rows : (place + 1) * rows, :].astype(jnp.float32)
+        sum_ref[...] = total.astype(jnp.bfloat16)
+    for near_ref, sent_ref in zip(near_refs, sent_refs):
+        sent_ref[...] = near_ref[...]
 
 
 def final_kernel(parts, factor, *refs):
-    column_ref, mine_ref, near_refs, refs = refs[0], refs[1], refs[2:parts], refs[parts:]
+    mine_ref, part_refs, refs = refs[0], refs[1:parts], refs[parts:]
     ids_ref, gates_ref, orig_ref, pruned_ref, terms_ref, *value_refs = refs
     tok_rows = orig_ref.shape[0]
     rows = 2 * tok_rows
     total = mine_ref[:rows, :].astype(jnp.float32)
-    for ref in near_refs:
+    for ref in part_refs:
         total = total + ref[...].astype(jnp.float32)
-    for place in range(column_ref.shape[0] // rows):
-        total = total + column_ref[place * rows : (place + 1) * rows, :].astype(jnp.float32)
     for value_ref in value_refs:
         value_ref[...] = total
     value_orig, value_pruned = total[:tok_rows], total[tok_rows:]
@@ -245,28 +243,8 @@
     inner = min(4, chips)
     outer = chips // inner
     inner_masks = [SPLIT * i for i in range(1, inner)]
-    columns = [
-        [place + SPLIT * inner * j for j in range(outer)] for place in range(SPLIT * inner)
-    ]
-    along_column = functools.partial(
-        lax.all_to_all,
-        axis_name="expert",
-        split_axis=0,
-        concat_axis=0,
-        axis_index_groups=columns,
-        tiled=True,
-    )
+    outer_masks = [SPLIT * inner * j for j in reversed(range(1, outer))]
     own_in, own_out = w_in[0, 0], w_out[0, 0]
-    other_in, other_out = exclusive(own_in, 1), exclusive(own_out, 1)
-    weights = [own_in, other_in, own_out, other_out]
-    weights = run_kernel(
-        functools.partial(stage_kernel, len(weights)),
-        [pltpu.VMEM(value.shape, value.dtype) for value in weights],
-        [in_hbm(own_in), other_in, in_hbm(own_out), other_out],
-        [pltpu.SemaphoreType.DMA((len(weights),))],
-        space=pl.ANY,
-    )
-
     step_count = micro_count + section_count - 1
     carry = jnp.zeros((2, tok_rows, model_width), jnp.bfloat16)
     moe_orig = jnp.zeros((micro_count, tok_rows, model_width), jnp.bfloat16)
@@ -297,24 +275,26 @@
             item(gates_pruned[0]),
             keep_mask,
         ]
-        packed, spread = run_kernel(
+        packed = run_kernel(
             functools.partial(pack_kernel, len(operands)),
-            [like(rows, model_width + extra), like(outer * rows, model_width + extra)],
+            like(rows, model_width + extra),
             [in_hbm(value) for value in operands],
             [pltpu.VMEM(value.shape, value.dtype) for value in operands]
             + [pltpu.SemaphoreType.DMA((len(operands),))],
             space=pl.ANY,
         )
-        column = along_column(spread)
+        column = [exclusive(packed, mask) for mask in outer_masks]
         near = [exclusive(packed, mask) for mask in inner_masks]
         joined, early = run_kernel(
-            functools.partial(join_kernel, inner),
+            functools.partial(join_kernel, outer),
             [
                 like((outer - 1) * rows, model_width + extra),
                 like((outer + inner - 1) * rows, model_width + extra),
             ],
-            [column, packed] + near,
-        )
+            [packed] + column + near,
+        )
+        if tick == 0:
+            weights = stage_weights(own_in, own_out, joined)
         far = [exclusive(joined, mask) for mask in inner_masks]
         far_out = run_expert(experts, far, weights, [(outer - 1) * rows] * (inner - 1))
         far_back = [exclusive(part, mask) for part, mask in zip(far_out, inner_masks)]
@@ -324,19 +304,20 @@
             weights,
             [outer * rows] + [rows] * (inner - 1),
         )
-        near_back = [exclusive(part, mask) for part, mask in zip(near_out, inner_masks)]
         outgoing = run_kernel(
-            functools.partial(plane_kernel, inner),
-            like(outer * rows, model_width),
-            [mine] + far_back,
-        )
-        incoming = along_column(outgoing)
+            functools.partial(plane_kernel, inner, outer),
+            [like(rows, model_width)] * (outer + inner - 2),
+            [mine] + far_back + near_out,
+        )
+        incoming = [
+            exclusive(part, mask) for part, mask in zip(outgoing, outer_masks + inner_masks)
+        ]
         round_orig, round_pruned, tick_terms, *moe = run_kernel(
-            functools.partial(final_kernel, inner + 1, loss_factor),
+            functools.partial(final_kernel, outer + inner - 1, loss_factor),
             [like(tok_rows, model_width)] * 2
             + [like(devices, experts, jnp.float32)]
             + [like(rows, model_width, jnp.float32)] * (section_count > 1),
-            [incoming, mine] + near_back + [picked_orig, weight_orig],
+            [mine] + incoming + [picked_orig, weight_orig],
         )
         if section_count > 1:
             tick_terms = jnp.where(active, tick_terms, 0.0)

time: 70.3 us -> 69.4 us (0.987)
  waiting for transfers between devices: 15.9 us -> 22.5 us
  local copies, waits for them, and re-layouts: 5.25 us -> 0.01 us
  blocking collectives: 12.2 us -> 10.7 us
  Pallas kernels: 9.61 us -> 8.47 us
    ppermute x14 -> x20, starting transfers between devices: 14.7 us -> 26.8 us  [exclusive(): return lax.ppermute(value, 'expert', pairs)]
    all_to_all x2 -> x0, starting transfers between devices: 11.5 us -> none  [the longest x1 6.29 us: on_device(): column = along_column(spread)]
    ppermute x14 -> x20, waiting for transfers between devices: 15.2 us -> 22.5 us  [exclusive(): return lax.ppermute(value, 'expert', pairs)]
    unnamed x18 -> x4, local copies, waits for them, and re-layouts: 5.25 us -> 0.01 us
    all_to_all x1, blocking collectives: 12.2 us -> 10.7 us  [on_device(): lax.all_to_all(terms, 'expert', split_axis=0, concat_axis=0, tiled=True)]
    pallas_call x8, Pallas kernels: 9.61 us -> 8.47 us  [run_kernel(): pl.pallas_call(body, out_shape=outs, in_specs=[pl.BlockSpec(memory_space=...]
  transfers between devices with their start and end apart: 16 -> 20, of which waited for: 11 -> 11; matrix products, arithmetic and copies ran while one was open for 0% -> 0% of each run, Pallas kernels for 8% -> 8%
where the time goes in v4:
time: 69.4 us; the launch traced here: 69.2 us
  starting transfers between devices  26.8 us (39%)
  waiting for transfers between devices  22.5 us (32%)
  blocking collectives  10.7 us (15%)
  Pallas kernels  8.47 us (12%)
  between operations  0.7 us (1%)
    ppermute x20, starting transfers between devices, exclusive(): return lax.ppermute(value, 'expert', pairs)  26.8 us
    ppermute x20, waiting for transfers between devices, exclusive(): return lax.ppermute(value, 'expert', pairs)  22.5 us
    all_to_all x1, blocking collectives, on_device(): lax.all_to_all(terms, 'expert', split_axis=0, concat_axis=0, tiled=True)  10.7 us
    pallas_call x8, Pallas kernels, run_kernel(): pl.pallas_call(body, out_shape=outs, in_specs=[pl.BlockSpec(memory_space=...  8.47 us
  transfers between devices with their start and end apart: 20, of which 11 were waited for; matrix products, arithmetic and copies ran while one was open for 0% of the time, Pallas kernels for 8%

profile of v4, /device:TPU:0, one launch (start us, length us, event | category | flops | bytes accessed | tf_op | source)
XLA Modules:
  0.0 69.2 jit_solution(5942968148914628152)
XLA Ops:
  0.6 0.5 collective-permute-start.6
  1.1 1.1 %shard_map.112.packed_ref = bf16[16,2176]{1,0:T(8,128)(2,1)S(1)} custom-call(bf16[8,2048]{1,0:T(8,128)(2,1)} %bitcast.24, bf16[8,2048]{1,0:T(8,128)(2,1)} %bitcast.25, s32[8,8]{1,0:T(8,128)} %bitcast.16, s32[8,8]{1,0:T(8,128)} %bitcast.26, f32[8,8]{1,0:T(8,128)} %bitcast.18, f32[8,8]{1,0:T(8,128)} %bitcast.27, s32[1,16]{1,0:T(1,128)} %refs_6_.1), custom_call_target="tpu_custom_call" | custom-call | tf_op jit(solution)/shard_map/pallas_call | solution.py:16
  2.2 4.7 %collective-permute-start = (bf16[16,2176]{1,0:T(8,128)(2,1)S(1)}, bf16[16,2176]{1,0:T(8,128)(2,1)S(1)}, u32[]{:S(2)}, u32[]{:S(2)}) collective-permute-start(bf16[16,2176]{1,0:T(8,128)(2,1)S(1)} %shard_map.112.packed_ref), channel_id=1, source_target_pairs={{0,24},{1,25},{2,26},{3,27},{4,28},{5,29},{6,30},{7,31},{8,16},{9,... | collective-permute-start | bytes 208904 | tf_op jit(solution)/shard_map/ppermute | solution.py:36
  6.9 0.0 collective-permute-start.1
  6.9 0.6 collective-permute-start.2
  7.6 1.6 %collective-permute-start.3 = (bf16[16,2176]{1,0:T(8,128)(2,1)S(1)}, bf16[16,2176]{1,0:T(8,128)(2,1)S(1)}, u32[]{:S(2)}, u32[]{:S(2)}) collective-permute-start(bf16[16,2176]{1,0:T(8,128)(2,1)S(1)} %shard_map.112.packed_ref), channel_id=1, source_target_pairs={{0,2},{1,3},{2,0},{3,1},{4,6},{5,7},{6,4},{7,5},{8,10},{9,11},{10,... | collective-permute-start | bytes 208904 | tf_op jit(solution)/shard_map/ppermute | solution.py:36
  9.2 0.8 %collective-permute-done.refs_0_ = bf16[16,2176]{1,0:T(8,128)(2,1)S(1)} collective-permute-done((bf16[16,2176]{1,0:T(8,128)(2,1)S(1)}, bf16[16,2176]{1,0:T(8,128)(2,1)S(1)}, u32[]{:S(2)}, u32[]{:S(2)}) %collective-permute-start) | collective-permute-done | bytes 69664 | tf_op jit(solution)/shard_map/ppermute | solution.py:36
  10.0 1.6 %collective-permute-start.4 = (bf16[16,2176]{1,0:T(8,128)(2,1)S(1)}, bf16[16,2176]{1,0:T(8,128)(2,1)S(1)}, u32[]{:S(2)}, u32[]{:S(2)}) collective-permute-start(bf16[16,2176]{1,0:T(8,128)(2,1)S(1)} %shard_map.112.packed_ref), channel_id=1, source_target_pairs={{0,4},{1,5},{2,6},{3,7},{4,0},{5,1},{6,2},{7,3},{8,12},{9,13},{10,... | collective-permute-start | bytes 208904 | tf_op jit(solution)/shard_map/ppermute | solution.py:36
  11.6 1.8 %collective-permute-done.1.refs_1_ = bf16[16,2176]{1,0:T(8,128)(2,1)S(1)} collective-permute-done((bf16[16,2176]{1,0:T(8,128)(2,1)S(1)}, bf16[16,2176]{1,0:T(8,128)(2,1)S(1)}, u32[]{:S(2)}, u32[]{:S(2)}) %collective-permute-start.1) | collective-permute-done | bytes 69664 | tf_op jit(solution)/shard_map/ppermute | solution.py:36
  13.4 2.4 %collective-permute-start.5 = (bf16[16,2176]{1,0:T(8,128)(2,1)S(1)}, bf16[16,2176]{1,0:T(8,128)(2,1)S(1)}, u32[]{:S(2)}, u32[]{:S(2)}) collective-permute-start(bf16[16,2176]{1,0:T(8,128)(2,1)S(1)} %shard_map.112.packed_ref), channel_id=1, source_target_pairs={{0,6},{1,7},{2,4},{3,5},{4,2},{5,3},{6,0},{7,1},{8,14},{9,15},{10,... | collective-permute-start | bytes 208904 | tf_op jit(solution)/shard_map/ppermute | solution.py:36
  15.8 0.0 collective-permute-done.2.refs_2_
  15.8 0.0 collective-permute-done.3.refs_3_
  15.8 0.0 collective-permute-done.4.refs_4_
  15.8 2.7 %collective-permute-done.5.refs_5_ = bf16[16,2176]{1,0:T(8,128)(2,1)S(1)} collective-permute-done((bf16[16,2176]{1,0:T(8,128)(2,1)S(1)}, bf16[16,2176]{1,0:T(8,128)(2,1)S(1)}, u32[]{:S(2)}, u32[]{:S(2)}) %collective-permute-start.5) | collective-permute-done | bytes 69664 | tf_op jit(solution)/shard_map/ppermute | solution.py:36
  18.6 0.1 collective-permute-start.7
  18.7 1.6 %collective-permute-start.8 = (bf16[48,2176]{1,0:T(8,128)(2,1)S(1)}, bf16[48,2176]{1,0:T(8,128)(2,1)S(1)}, u32[]{:S(2)}, u32[]{:S(2)}) collective-permute-start(bf16[48,2176]{1,0:T(8,128)(2,1)S(1)} %get-tuple-element.27), channel_id=1, source_target_pairs={{0,2},{1,3},{2,0},{3,1},{4,6},{5,7},{6,4},{7,5},{8,10},{9,11},{10,... | collective-permute-start | bytes 626696 | tf_op jit(solution)/shard_map/ppermute | solution.py:36
  20.3 1.5 %collective-permute-start.9 = (bf16[48,2176]{1,0:T(8,128)(2,1)S(1)}, bf16[48,2176]{1,0:T(8,128)(2,1)S(1)}, u32[]{:S(2)}, u32[]{:S(2)}) collective-permute-start(bf16[48,2176]{1,0:T(8,128)(2,1)S(1)} %get-tuple-element.27), channel_id=1, source_target_pairs={{0,4},{1,5},{2,6},{3,7},{4,0},{5,1},{6,2},{7,3},{8,12},{9,13},{10,... | collective-permute-start | bytes 626696 | tf_op jit(solution)/shard_map/ppermute | solution.py:36
  21.8 0.5 collective-permute-start.10
  22.3 0.1 collective-permute-done.7.refs_3_
  22.3 0.0 collective-permute-done.6.refs_1_
  22.3 2.4 %shard_map.114 = (bf16[2048,768]{1,0:T(8,128)(2,1)S(1)}, bf16[2048,768]{1,0:T(8,128)(2,1)S(1)}, bf16[384,2048]{1,0:T(8,128)(2,1)S(1)}, bf16[384,2048]{1,0:T(8,128)(2,1)S(1)}) custom-call(bf16[2048,768]{1,0:T(8,128)(2,1)} %bitcast.21, bf16[2048,768]{1,0:T(8,128)(2,1)S(1)} %collective-permute-done.6.refs_1_, bf16[384,2048]{1,0:T(8,128)(2,1)} %bitcast.23, ...), custom_call_target="tpu_custom_call" | custom-call | tf_op jit(solution)/shard_map/pallas_call | solution.py:16
  24.8 2.0 %collective-permute-done.8.refs_0_ = bf16[48,2176]{1,0:T(8,128)(2,1)S(1)} collective-permute-done((bf16[48,2176]{1,0:T(8,128)(2,1)S(1)}, bf16[48,2176]{1,0:T(8,128)(2,1)S(1)}, u32[]{:S(2)}, u32[]{:S(2)}) %collective-permute-start.8) | collective-permute-done | bytes 208928 | tf_op jit(solution)/shard_map/ppermute | solution.py:36
  26.8 5.2 %collective-permute-done.9.refs_1_ = bf16[48,2176]{1,0:T(8,128)(2,1)S(1)} collective-permute-done((bf16[48,2176]{1,0:T(8,128)(2,1)S(1)}, bf16[48,2176]{1,0:T(8,128)(2,1)S(1)}, u32[]{:S(2)}, u32[]{:S(2)}) %collective-permute-start.9) | collective-permute-done | bytes 208928 | tf_op jit(solution)/shard_map/ppermute | solution.py:36
  32.0 0.0 collective-permute-done.10.refs_2_
  32.0 1.9 %shard_map.116 = (bf16[48,2048]{1,0:T(8,128)(2,1)S(1)}, bf16[48,2048]{1,0:T(8,128)(2,1)S(1)}, bf16[48,2048]{1,0:T(8,128)(2,1)S(1)}) custom-call(bf16[48,2176]{1,0:T(8,128)(2,1)S(1)} %collective-permute-done.8.refs_0_, bf16[48,2176]{1,0:T(8,128)(2,1)S(1)} %collective-permute-done.9.refs_1_, bf16[48,2176]{1,0:T(8,128)(2,1)S(1)} %collective-permute-done.10.refs_2_, ...), custom_call_target="tpu_custom_call" | custom-call | tf_op jit(solution)/shard_map/pallas_call | solution.py:16
  33.9 1.3 %collective-permute-start.11 = (bf16[48,2048]{1,0:T(8,128)(2,1)S(1)}, bf16[48,2048]{1,0:T(8,128)(2,1)S(1)}, u32[]{:S(2)}, u32[]{:S(2)}) collective-permute-start(bf16[48,2048]{1,0:T(8,128)(2,1)S(1)} %get-tuple-element.34), channel_id=1, source_target_pairs={{0,2},{1,3},{2,0},{3,1},{4,6},{5,7},{6,4},{7,5},{8,10},{9,11},{10,... | collective-permute-start | bytes 589832 | tf_op jit(solution)/shard_map/ppermute | solution.py:36
  35.2 0.8 %collective-permute-start.12 = (bf16[48,2048]{1,0:T(8,128)(2,1)S(1)}, bf16[48,2048]{1,0:T(8,128)(2,1)S(1)}, u32[]{:S(2)}, u32[]{:S(2)}) collective-permute-start(bf16[48,2048]{1,0:T(8,128)(2,1)S(1)} %get-tuple-element.35), channel_id=1, source_target_pairs={{0,4},{1,5},{2,6},{3,7},{4,0},{5,1},{6,2},{7,3},{8,12},{9,13},{10,... | collective-permute-start | bytes 589832 | tf_op jit(solution)/shard_map/ppermute | solution.py:36
  36.0 1.4 %collective-permute-start.13 = (bf16[48,2048]{1,0:T(8,128)(2,1)S(1)}, bf16[48,2048]{1,0:T(8,128)(2,1)S(1)}, u32[]{:S(2)}, u32[]{:S(2)}) collective-permute-start(bf16[48,2048]{1,0:T(8,128)(2,1)S(1)} %get-tuple-element.36), channel_id=1, source_target_pairs={{0,6},{1,7},{2,4},{3,5},{4,2},{5,3},{6,0},{7,1},{8,14},{9,15},{10,... | collective-permute-start | bytes 589832 | tf_op jit(solution)/shard_map/ppermute | solution.py:36
  37.4 1.7 %shard_map.115 = (bf16[64,2048]{1,0:T(8,128)(2,1)S(1)}, bf16[16,2048]{1,0:T(8,128)(2,1)S(1)}, bf16[16,2048]{1,0:T(8,128)(2,1)S(1)}, bf16[16,2048]{1,0:T(8,128)(2,1)S(1)}) custom-call(bf16[112,2176]{1,0:T(8,128)(2,1)S(1)} %get-tuple-element.26.refs_0_, bf16[2048,768]{1,0:T(8,128)(2,1)S(1)} %get-tuple-element.29.refs_1_.refs_3_, ...), custom_call_target="tpu_custom_call" | custom-call | tf_op jit(solution)/shard_map/pallas_call | solution.py:16
  39.1 2.6 %collective-permute-done.11.refs_0_ = bf16[48,2048]{1,0:T(8,128)(2,1)S(1)} collective-permute-done((bf16[48,2048]{1,0:T(8,128)(2,1)S(1)}, bf16[48,2048]{1,0:T(8,128)(2,1)S(1)}, u32[]{:S(2)}, u32[]{:S(2)}) %collective-permute-start.11) | collective-permute-done | bytes 196640 | tf_op jit(solution)/shard_map/ppermute | solution.py:36
  41.8 3.8 %collective-permute-done.12.refs_1_ = bf16[48,2048]{1,0:T(8,128)(2,1)S(1)} collective-permute-done((bf16[48,2048]{1,0:T(8,128)(2,1)S(1)}, bf16[48,2048]{1,0:T(8,128)(2,1)S(1)}, u32[]{:S(2)}, u32[]{:S(2)}) %collective-permute-start.12) | collective-permute-done | bytes 196640 | tf_op jit(solution)/shard_map/ppermute | solution.py:36
  45.6 0.0 collective-permute-done.13.refs_2_
  45.6 0.1 shard_map.117
  45.7 2.5 %collective-permute-start.14 = (bf16[16,2048]{1,0:T(8,128)(2,1)S(1)}, bf16[16,2048]{1,0:T(8,128)(2,1)S(1)}, u32[]{:S(2)}, u32[]{:S(2)}) collective-permute-start(bf16[16,2048]{1,0:T(8,128)(2,1)S(1)} %get-tuple-element.40), channel_id=1, source_target_pairs={{0,24},{1,25},{2,26},{3,27},{4,28},{5,29},{6,30},{7,31},{8,16},{9,... | collective-permute-start | bytes 196616 | tf_op jit(solution)/shard_map/ppermute | solution.py:36
  48.2 0.0 collective-permute-start.15
  48.2 1.9 %collective-permute-start.16 = (bf16[16,2048]{1,0:T(8,128)(2,1)S(1)}, bf16[16,2048]{1,0:T(8,128)(2,1)S(1)}, u32[]{:S(2)}, u32[]{:S(2)}) collective-permute-start(bf16[16,2048]{1,0:T(8,128)(2,1)S(1)} %get-tuple-element.42), channel_id=1, source_target_pairs={{0,8},{1,9},{2,10},{3,11},{4,12},{5,13},{6,14},{7,15},{8,0},{9,1},... | collective-permute-start | bytes 196616 | tf_op jit(solution)/shard_map/ppermute | solution.py:36
  50.1 0.6 collective-permute-start.17
  50.7 1.4 %collective-permute-start.18 = (bf16[16,2048]{1,0:T(8,128)(2,1)S(1)}, bf16[16,2048]{1,0:T(8,128)(2,1)S(1)}, u32[]{:S(2)}, u32[]{:S(2)}) collective-permute-start(bf16[16,2048]{1,0:T(8,128)(2,1)S(1)} %get-tuple-element.44), channel_id=1, source_target_pairs={{0,4},{1,5},{2,6},{3,7},{4,0},{5,1},{6,2},{7,3},{8,12},{9,13},{10,... | collective-permute-start | bytes 196616 | tf_op jit(solution)/shard_map/ppermute | solution.py:36
  52.1 0.0 collective-permute-done.14.refs_1_
  52.1 1.7 %collective-permute-start.19 = (bf16[16,2048]{1,0:T(8,128)(2,1)S(1)}, bf16[16,2048]{1,0:T(8,128)(2,1)S(1)}, u32[]{:S(2)}, u32[]{:S(2)}) collective-permute-start(bf16[16,2048]{1,0:T(8,128)(2,1)S(1)} %get-tuple-element.45), channel_id=1, source_target_pairs={{0,6},{1,7},{2,4},{3,5},{4,2},{5,3},{6,0},{7,1},{8,14},{9,15},{10,... | collective-permute-start | bytes 196616 | tf_op jit(solution)/shard_map/ppermute | solution.py:36
  53.9 0.0 collective-permute-done.15.refs_2_
  53.9 0.0 collective-permute-done.16.refs_3_
  53.9 0.5 collective-permute-done.17.refs_4_
  54.4 0.6 collective-permute-done.18.refs_5_
  55.0 2.3 %collective-permute-done.19.refs_6_ = bf16[16,2048]{1,0:T(8,128)(2,1)S(1)} collective-permute-done((bf16[16,2048]{1,0:T(8,128)(2,1)S(1)}, bf16[16,2048]{1,0:T(8,128)(2,1)S(1)}, u32[]{:S(2)}, u32[]{:S(2)}) %collective-permute-start.19) | collective-permute-done | bytes 65568 | tf_op jit(solution)/shard_map/ppermute | solution.py:36
  57.3 0.7 %shard_map.118 = (bf16[8,2048]{1,0:T(8,128)(2,1)}, bf16[8,2048]{1,0:T(8,128)(2,1)}, f32[32,16]{1,0:T(8,128)S(1)}) custom-call(bf16[64,2048]{1,0:T(8,128)(2,1)S(1)} %get-tuple-element.33.mine_ref.refs_0_, bf16[16,2048]{1,0:T(8,128)(2,1)S(1)} %collective-permute-done.14.refs_1_, bf16[16,2048]{1,0:T(8,128)(2,1)S(1)} %collective-permute-done.15.refs_2_, ...), custom_call_target="tpu_custom_call" | custom-call | tf_op jit(solution)/shard_map/pallas_call | solution.py:16
  58.0 10.7 %all_to_all.11 = f32[32,1,16]{2,1,0:T(1,128)S(1)} all-to-all(f32[32,1,16]{2,1,0:T(1,128)S(1)} %bitcast.15), channel_id=1, replica_groups=mesh['section'=1,'expert'=32] {'expert'}, dimensions={0} | all-to-all | bytes 4096 | tf_op jit(solution)/shard_map/all_to_all | solution.py:334
  68.7 0.5 shard_map.119
  (5 shorter events, 0.1 us)
Async XLA Ops:
  0.6 21.7 %collective-permute-start.6 = (bf16[2048,768]{1,0:T(8,128)(2,1)}, bf16[2048,768]{1,0:T(8,128)(2,1)S(1)}, u32[]{:S(2)}, u32[]{:S(2)}) collective-permute-start(bf16[2048,768]{1,0:T(8,128)(2,1)} %bitcast.20), channel_id=1, source_target_pairs={{0,1},{1,0},{2,3},{3,2},{4,5},{5,4},{6,7},{7,6},{8,9},{9,8},{10,11... | collective-permute-start | bytes 9437192 | tf_op jit(solution)/shard_map/ppermute | solution.py:36
  2.2 7.8 %collective-permute-start = (bf16[16,2176]{1,0:T(8,128)(2,1)S(1)}, bf16[16,2176]{1,0:T(8,128)(2,1)S(1)}, u32[]{:S(2)}, u32[]{:S(2)}) collective-permute-start(bf16[16,2176]{1,0:T(8,128)(2,1)S(1)} %shard_map.112.packed_ref), channel_id=1, source_target_pairs={{0,24},{1,25},{2,26},{3,27},{4,28},{5,29},{6,30},{7,31},{8,16},{9,... | collective-permute-start | bytes 208904 | tf_op jit(solution)/shard_map/ppermute | solution.py:36
  6.9 6.5 %collective-permute-start.1 = (bf16[16,2176]{1,0:T(8,128)(2,1)S(1)}, bf16[16,2176]{1,0:T(8,128)(2,1)S(1)}, u32[]{:S(2)}, u32[]{:S(2)}) collective-permute-start(bf16[16,2176]{1,0:T(8,128)(2,1)S(1)} %shard_map.112.packed_ref), channel_id=1, source_target_pairs={{0,16},{1,17},{2,18},{3,19},{4,20},{5,21},{6,22},{7,23},{8,24},{9,... | collective-permute-start | bytes 208904 | tf_op jit(solution)/shard_map/ppermute | solution.py:36
  6.9 8.9 %collective-permute-start.2 = (bf16[16,2176]{1,0:T(8,128)(2,1)S(1)}, bf16[16,2176]{1,0:T(8,128)(2,1)S(1)}, u32[]{:S(2)}, u32[]{:S(2)}) collective-permute-start(bf16[16,2176]{1,0:T(8,128)(2,1)S(1)} %shard_map.112.packed_ref), channel_id=1, source_target_pairs={{0,8},{1,9},{2,10},{3,11},{4,12},{5,13},{6,14},{7,15},{8,0},{9,1},... | collective-permute-start | bytes 208904 | tf_op jit(solution)/shard_map/ppermute | solution.py:36
  7.6 8.3 %collective-permute-start.3 = (bf16[16,2176]{1,0:T(8,128)(2,1)S(1)}, bf16[16,2176]{1,0:T(8,128)(2,1)S(1)}, u32[]{:S(2)}, u32[]{:S(2)}) collective-permute-start(bf16[16,2176]{1,0:T(8,128)(2,1)S(1)} %shard_map.112.packed_ref), channel_id=1, source_target_pairs={{0,2},{1,3},{2,0},{3,1},{4,6},{5,7},{6,4},{7,5},{8,10},{9,11},{10,... | collective-permute-start | bytes 208904 | tf_op jit(solution)/shard_map/ppermute | solution.py:36
  10.0 5.8 %collective-permute-start.4 = (bf16[16,2176]{1,0:T(8,128)(2,1)S(1)}, bf16[16,2176]{1,0:T(8,128)(2,1)S(1)}, u32[]{:S(2)}, u32[]{:S(2)}) collective-permute-start(bf16[16,2176]{1,0:T(8,128)(2,1)S(1)} %shard_map.112.packed_ref), channel_id=1, source_target_pairs={{0,4},{1,5},{2,6},{3,7},{4,0},{5,1},{6,2},{7,3},{8,12},{9,13},{10,... | collective-permute-start | bytes 208904 | tf_op jit(solution)/shard_map/ppermute | solution.py:36
  13.4 5.2 %collective-permute-start.5 = (bf16[16,2176]{1,0:T(8,128)(2,1)S(1)}, bf16[16,2176]{1,0:T(8,128)(2,1)S(1)}, u32[]{:S(2)}, u32[]{:S(2)}) collective-permute-start(bf16[16,2176]{1,0:T(8,128)(2,1)S(1)} %shard_map.112.packed_ref), channel_id=1, source_target_pairs={{0,6},{1,7},{2,4},{3,5},{4,2},{5,3},{6,0},{7,1},{8,14},{9,15},{10,... | collective-permute-start | bytes 208904 | tf_op jit(solution)/shard_map/ppermute | solution.py:36
  18.6 3.7 %collective-permute-start.7 = (bf16[384,2048]{1,0:T(8,128)(2,1)}, bf16[384,2048]{1,0:T(8,128)(2,1)S(1)}, u32[]{:S(2)}, u32[]{:S(2)}) collective-permute-start(bf16[384,2048]{1,0:T(8,128)(2,1)} %bitcast.22), channel_id=1, source_target_pairs={{0,1},{1,0},{2,3},{3,2},{4,5},{5,4},{6,7},{7,6},{8,9},{9,8},{10,11... | collective-permute-start | bytes 4718600 | tf_op jit(solution)/shard_map/ppermute | solution.py:36
  18.7 8.0 %collective-permute-start.8 = (bf16[48,2176]{1,0:T(8,128)(2,1)S(1)}, bf16[48,2176]{1,0:T(8,128)(2,1)S(1)}, u32[]{:S(2)}, u32[]{:S(2)}) collective-permute-start(bf16[48,2176]{1,0:T(8,128)(2,1)S(1)} %get-tuple-element.27), channel_id=1, source_target_pairs={{0,2},{1,3},{2,0},{3,1},{4,6},{5,7},{6,4},{7,5},{8,10},{9,11},{10,... | collective-permute-start | bytes 626696 | tf_op jit(solution)/shard_map/ppermute | solution.py:36
  20.3 11.7 %collective-permute-start.9 = (bf16[48,2176]{1,0:T(8,128)(2,1)S(1)}, bf16[48,2176]{1,0:T(8,128)(2,1)S(1)}, u32[]{:S(2)}, u32[]{:S(2)}) collective-permute-start(bf16[48,2176]{1,0:T(8,128)(2,1)S(1)} %get-tuple-element.27), channel_id=1, source_target_pairs={{0,4},{1,5},{2,6},{3,7},{4,0},{5,1},{6,2},{7,3},{8,12},{9,13},{10,... | collective-permute-start | bytes 626696 | tf_op jit(solution)/shard_map/ppermute | solution.py:36
  21.8 10.2 %collective-permute-start.10 = (bf16[48,2176]{1,0:T(8,128)(2,1)S(1)}, bf16[48,2176]{1,0:T(8,128)(2,1)S(1)}, u32[]{:S(2)}, u32[]{:S(2)}) collective-permute-start(bf16[48,2176]{1,0:T(8,128)(2,1)S(1)} %get-tuple-element.27), channel_id=1, source_target_pairs={{0,6},{1,7},{2,4},{3,5},{4,2},{5,3},{6,0},{7,1},{8,14},{9,15},{10,... | collective-permute-start | bytes 626696 | tf_op jit(solution)/shard_map/ppermute | solution.py:36
  33.9 7.9 %collective-permute-start.11 = (bf16[48,2048]{1,0:T(8,128)(2,1)S(1)}, bf16[48,2048]{1,0:T(8,128)(2,1)S(1)}, u32[]{:S(2)}, u32[]{:S(2)}) collective-permute-start(bf16[48,2048]{1,0:T(8,128)(2,1)S(1)} %get-tuple-element.34), channel_id=1, source_target_pairs={{0,2},{1,3},{2,0},{3,1},{4,6},{5,7},{6,4},{7,5},{8,10},{9,11},{10,... | collective-permute-start | bytes 589832 | tf_op jit(solution)/shard_map/ppermute | solution.py:36
  35.2 10.4 %collective-permute-start.12 = (bf16[48,2048]{1,0:T(8,128)(2,1)S(1)}, bf16[48,2048]{1,0:T(8,128)(2,1)S(1)}, u32[]{:S(2)}, u32[]{:S(2)}) collective-permute-start(bf16[48,2048]{1,0:T(8,128)(2,1)S(1)} %get-tuple-element.35), channel_id=1, source_target_pairs={{0,4},{1,5},{2,6},{3,7},{4,0},{5,1},{6,2},{7,3},{8,12},{9,13},{10,... | collective-permute-start | bytes 589832 | tf_op jit(solution)/shard_map/ppermute | solution.py:36
  36.0 9.6 %collective-permute-start.13 = (bf16[48,2048]{1,0:T(8,128)(2,1)S(1)}, bf16[48,2048]{1,0:T(8,128)(2,1)S(1)}, u32[]{:S(2)}, u32[]{:S(2)}) collective-permute-start(bf16[48,2048]{1,0:T(8,128)(2,1)S(1)} %get-tuple-element.36), channel_id=1, source_target_pairs={{0,6},{1,7},{2,4},{3,5},{4,2},{5,3},{6,0},{7,1},{8,14},{9,15},{10,... | collective-permute-start | bytes 589832 | tf_op jit(solution)/shard_map/ppermute | solution.py:36
  37.4 19.9 %copy-start = (s32[1,1,8,8]{3,2,1,0:T(8,128)S(1)}, s32[1,1,8,8]{3,2,1,0:T(8,128)}, u32[]{:S(2)}) copy-start(s32[1,1,8,8]{3,2,1,0:T(8,128)} %param.11) | copy-start | bytes 772
  37.4 19.9 %copy-start.1 = (f32[1,1,8,8]{3,2,1,0:T(8,128)S(1)}, f32[1,1,8,8]{3,2,1,0:T(8,128)}, u32[]{:S(2)}) copy-start(f32[1,1,8,8]{3,2,1,0:T(8,128)} %param.13) | copy-start | bytes 772
  45.7 6.5 %collective-permute-start.14 = (bf16[16,2048]{1,0:T(8,128)(2,1)S(1)}, bf16[16,2048]{1,0:T(8,128)(2,1)S(1)}, u32[]{:S(2)}, u32[]{:S(2)}) collective-permute-start(bf16[16,2048]{1,0:T(8,128)(2,1)S(1)} %get-tuple-element.40), channel_id=1, source_target_pairs={{0,24},{1,25},{2,26},{3,27},{4,28},{5,29},{6,30},{7,31},{8,16},{9,... | collective-permute-start | bytes 196616 | tf_op jit(solution)/shard_map/ppermute | solution.py:36
  48.2 5.7 %collective-permute-start.15 = (bf16[16,2048]{1,0:T(8,128)(2,1)S(1)}, bf16[16,2048]{1,0:T(8,128)(2,1)S(1)}, u32[]{:S(2)}, u32[]{:S(2)}) collective-permute-start(bf16[16,2048]{1,0:T(8,128)(2,1)S(1)} %get-tuple-element.41), channel_id=1, source_target_pairs={{0,16},{1,17},{2,18},{3,19},{4,20},{5,21},{6,22},{7,23},{8,24},{9,... | collective-permute-start | bytes 196616 | tf_op jit(solution)/shard_map/ppermute | solution.py:36
  48.2 5.7 %collective-permute-start.16 = (bf16[16,2048]{1,0:T(8,128)(2,1)S(1)}, bf16[16,2048]{1,0:T(8,128)(2,1)S(1)}, u32[]{:S(2)}, u32[]{:S(2)}) collective-permute-start(bf16[16,2048]{1,0:T(8,128)(2,1)S(1)} %get-tuple-element.42), channel_id=1, source_target_pairs={{0,8},{1,9},{2,10},{3,11},{4,12},{5,13},{6,14},{7,15},{8,0},{9,1},... | collective-permute-start | bytes 196616 | tf_op jit(solution)/shard_map/ppermute | solution.py:36
  50.1 4.3 %collective-permute-start.17 = (bf16[16,2048]{1,0:T(8,128)(2,1)S(1)}, bf16[16,2048]{1,0:T(8,128)(2,1)S(1)}, u32[]{:S(2)}, u32[]{:S(2)}) collective-permute-start(bf16[16,2048]{1,0:T(8,128)(2,1)S(1)} %get-tuple-element.43), channel_id=1, source_target_pairs={{0,2},{1,3},{2,0},{3,1},{4,6},{5,7},{6,4},{7,5},{8,10},{9,11},{10,... | collective-permute-start | bytes 196616 | tf_op jit(solution)/shard_map/ppermute | solution.py:36
  50.7 4.3 %collective-permute-start.18 = (bf16[16,2048]{1,0:T(8,128)(2,1)S(1)}, bf16[16,2048]{1,0:T(8,128)(2,1)S(1)}, u32[]{:S(2)}, u32[]{:S(2)}) collective-permute-start(bf16[16,2048]{1,0:T(8,128)(2,1)S(1)} %get-tuple-element.44), channel_id=1, source_target_pairs={{0,4},{1,5},{2,6},{3,7},{4,0},{5,1},{6,2},{7,3},{8,12},{9,13},{10,... | collective-permute-start | bytes 196616 | tf_op jit(solution)/shard_map/ppermute | solution.py:36
  52.1 5.2 %collective-permute-start.19 = (bf16[16,2048]{1,0:T(8,128)(2,1)S(1)}, bf16[16,2048]{1,0:T(8,128)(2,1)S(1)}, u32[]{:S(2)}, u32[]{:S(2)}) collective-permute-start(bf16[16,2048]{1,0:T(8,128)(2,1)S(1)} %get-tuple-element.45), channel_id=1, source_target_pairs={{0,6},{1,7},{2,4},{3,5},{4,2},{5,3},{6,0},{7,1},{8,14},{9,15},{10,... | collective-permute-start | bytes 196616 | tf_op jit(solution)/shard_map/ppermute | solution.py:36

commit v5 on v4

--- a/solution.py
+++ b/solution.py
@@ -103,9 +103,7 @@
         copy.wait()
 
 
-def stage_weights(own_in, own_out, awaited):
-    sent_out, _ = lax.optimization_barrier((own_out, awaited))
-    other_in, other_out = exclusive(own_in, 1), exclusive(sent_out, 1)
+def stage_weights(own_in, own_out, other_in, other_out):
     weights = [in_hbm(own_in), other_in, in_hbm(own_out), other_out]
     return run_kernel(
         functools.partial(stage_kernel, len(weights)),
@@ -116,14 +114,20 @@
     )
 
 
-def join_kernel(outer, packed_ref, *refs):
-    part_refs, (far_ref, early_ref) = refs[:-2], refs[-2:]
-    rows = packed_ref.shape[0]
-    early_ref[:rows, :] = packed_ref[...]
+def after(value, *awaited):
+    return lax.optimization_barrier((value, awaited))[0]
+
+
+def join_kernel(*refs):
+    part_refs, out_ref = refs[:-1], refs[-1]
+    rows = part_refs[0].shape[0]
     for place, part_ref in enumerate(part_refs):
-        early_ref[(place + 1) * rows : (place + 2) * rows, :] = part_ref[...]
-        if place < outer - 1:
-            far_ref[place * rows : (place + 1) * rows, :] = part_ref[...]
+        out_ref[place * rows : (place + 1) * rows, :] = part_ref[...]
+
+
+def join_rows(parts):
+    rows, columns = parts[0].shape
+    return run_kernel(join_kernel, like(len(parts) * rows, columns), parts)
 
 
 def expert_kernel(experts, row_count, sizes, *refs):
@@ -181,27 +185,20 @@
     )
 
 
-def plane_kernel(inner, outer, mine_ref, *refs):
-    far_refs, near_refs, refs = refs[: inner - 1], refs[inner - 1 : 2 * inner - 2], refs[2 * inner - 2 :]
-    sum_refs, sent_refs = refs[: outer - 1], refs[outer - 1 :]
-    rows = near_refs[0].shape[0]
-    for place, sum_ref in enumerate(sum_refs):
-        total = mine_ref[(place + 1) * rows : (place + 2) * rows, :].astype(jnp.float32)
-        for ref in far_refs:
-            total = total + ref[place * rows : (place + 1) * rows, :].astype(jnp.float32)
-        sum_ref[...] = total.astype(jnp.bfloat16)
-    for near_ref, sent_ref in zip(near_refs, sent_refs):
-        sent_ref[...] = near_ref[...]
+def plane_kernel(count, *refs):
+    part_refs, out_refs = refs[:count], refs[count:]
+    rows = out_refs[0].shape[0]
+    for place, out_ref in enumerate(out_refs):
+        out_ref[...] = sum(
+            ref[place * rows : (place + 1) * rows, :].astype(jnp.float32) for ref in part_refs
+        ).astype(out_ref.dtype)
 
 
 def final_kernel(parts, factor, *refs):
-    mine_ref, part_refs, refs = refs[0], refs[1:parts], refs[parts:]
+    part_refs, refs = refs[:parts], refs[parts:]
     ids_ref, gates_ref, orig_ref, pruned_ref, terms_ref, *value_refs = refs
     tok_rows = orig_ref.shape[0]
-    rows = 2 * tok_rows
-    total = mine_ref[:rows, :].astype(jnp.float32)
-    for ref in part_refs:
-        total = total + ref[...].astype(jnp.float32)
+    total = sum(ref[...].astype(jnp.float32) for ref in part_refs)
     for value_ref in value_refs:
         value_ref[...] = total
     value_orig, value_pruned = total[:tok_rows], total[tok_rows:]
@@ -243,8 +240,13 @@
     inner = min(4, chips)
     outer = chips // inner
     inner_masks = [SPLIT * i for i in range(1, inner)]
-    outer_masks = [SPLIT * inner * j for j in reversed(range(1, outer))]
+    layer_mask = lambda j: SPLIT * inner * j
+    nearer = list(range(1, outer // 2 + 1))
+    streams = [[j for j in range(outer) if j not in nearer], nearer]
     own_in, own_out = w_in[0, 0], w_out[0, 0]
+    other_out, other_in = exclusive(own_out, 1), exclusive(own_in, 1)
+    weights = None
+
     step_count = micro_count + section_count - 1
     carry = jnp.zeros((2, tok_rows, model_width), jnp.bfloat16)
     moe_orig = jnp.zeros((micro_count, tok_rows, model_width), jnp.bfloat16)
@@ -283,41 +285,40 @@
             + [pltpu.SemaphoreType.DMA((len(operands),))],
             space=pl.ANY,
         )
-        column = [exclusive(packed, mask) for mask in outer_masks]
-        near = [exclusive(packed, mask) for mask in inner_masks]
-        joined, early = run_kernel(
-            functools.partial(join_kernel, outer),
-            [
-                like((outer - 1) * rows, model_width + extra),
-                like((outer + inner - 1) * rows, model_width + extra),
-            ],
-            [packed] + column + near,
-        )
-        if tick == 0:
-            weights = stage_weights(own_in, own_out, joined)
-        far = [exclusive(joined, mask) for mask in inner_masks]
-        far_out = run_expert(experts, far, weights, [(outer - 1) * rows] * (inner - 1))
-        far_back = [exclusive(part, mask) for part, mask in zip(far_out, inner_masks)]
-        mine, *near_out = run_expert(
-            experts,
-            [early],
-            weights,
-            [outer * rows] + [rows] * (inner - 1),
-        )
-        outgoing = run_kernel(
-            functools.partial(plane_kernel, inner, outer),
-            [like(rows, model_width)] * (outer + inner - 2),
-            [mine] + far_back + near_out,
-        )
-        incoming = [
-            exclusive(part, mask) for part, mask in zip(outgoing, outer_masks + inner_masks)
-        ]
+        column = {0: packed}
+        for j in streams[1][::-1] + streams[0][1:]:
+            column[j] = exclusive(packed, layer_mask(j))
+        blocks = []
+        for stream, layers in enumerate(streams):
+            joined = join_rows([column[j] for j in layers])
+            block = [joined]
+            for mask in inner_masks:
+                block.append(exclusive(joined, mask))
+                if stream == 0 and tick == 0:
+                    joined = after(joined, other_out if len(block) == 2 else other_in)
+            blocks.append(block)
+        if weights is None:
+            weights = stage_weights(own_in, own_out, other_in, other_out)
+        summed = []
+        for stream, layers in enumerate(streams):
+            partial = run_expert(
+                experts, blocks[stream], weights, [len(layers) * rows] * inner
+            )
+            returned = [partial[0]] + [
+                exclusive(part, mask) for part, mask in zip(partial[1:], inner_masks)
+            ]
+            outs = [like(rows, model_width)] * len(layers)
+            if stream == 0:
+                outs[0] = like(rows, model_width, jnp.float32)
+            sums = run_kernel(functools.partial(plane_kernel, inner), outs, returned)
+            for j, value in list(zip(layers, sums))[::-1]:
+                summed.append(exclusive(value, layer_mask(j)) if j else value)
         round_orig, round_pruned, tick_terms, *moe = run_kernel(
-            functools.partial(final_kernel, outer + inner - 1, loss_factor),
+            functools.partial(final_kernel, outer, loss_factor),
             [like(tok_rows, model_width)] * 2
             + [like(devices, experts, jnp.float32)]
             + [like(rows, model_width, jnp.float32)] * (section_count > 1),
-            [mine] + incoming + [picked_orig, weight_orig],
+            summed + [picked_orig, weight_orig],
         )
         if section_count > 1:
             tick_terms = jnp.where(active, tick_terms, 0.0)

time: 69.4 us -> 58.1 us (0.84)
  waiting for transfers between devices: 22.5 us -> 9.42 us
  starting transfers between devices: 26.8 us -> 28.3 us
    ppermute x20, waiting for transfers between devices: 22.5 us -> 9.42 us  [exclusive(): return lax.ppermute(value, 'expert', pairs)]
    ppermute x20, starting transfers between devices: 26.8 us -> 28.3 us  [exclusive(): return lax.ppermute(value, 'expert', pairs)]
    pallas_call x8 -> x10, Pallas kernels: 8.47 us -> 8.25 us  [run_kernel(): pl.pallas_call(body, out_shape=outs, in_specs=[pl.BlockSpec(memory_space=...]
  transfers between devices with their start and end apart: 20 -> 20, of which waited for: 11 -> 4; matrix products, arithmetic and copies ran while one was open for 0% -> 0% of each run, Pallas kernels for 8% -> 12%
where the time goes in v5:
time: 58.1 us; the launch traced here: 57.9 us
  starting transfers between devices  28.3 us (49%)
  blocking collectives  11.2 us (19%)
  waiting for transfers between devices  9.42 us (16%)
  Pallas kernels  8.25 us (14%)
  between operations  0.72 us (1%)
    ppermute x20, starting transfers between devices, exclusive(): return lax.ppermute(value, 'expert', pairs)  28.3 us
    all_to_all x1, blocking collectives, on_device(): lax.all_to_all(terms, 'expert', split_axis=0, concat_axis=0, tiled=True)  11.2 us
    ppermute x20, waiting for transfers between devices, exclusive(): return lax.ppermute(value, 'expert', pairs)  9.42 us
    pallas_call x10, Pallas kernels, run_kernel(): pl.pallas_call(body, out_shape=outs, in_specs=[pl.BlockSpec(memory_space=...  8.25 us
  transfers between devices with their start and end apart: 20, of which 4 were waited for; matrix products, arithmetic and copies ran while one was open for 0% of the time, Pallas kernels for 12%

profile of v5, /device:TPU:0, one launch (start us, length us, event | category | flops | bytes accessed | tf_op | source)
XLA Modules:
  0.0 57.9 jit_solution(16790922057939901545)
XLA Ops:
  0.6 0.5 collective-permute-start.4
  1.1 0.1 collective-permute-start.2
  1.2 1.1 %shard_map.112.refs_0_ = bf16[16,2176]{1,0:T(8,128)(2,1)S(1)} custom-call(bf16[8,2048]{1,0:T(8,128)(2,1)} %bitcast.24, bf16[8,2048]{1,0:T(8,128)(2,1)} %bitcast.25, s32[8,8]{1,0:T(8,128)} %bitcast.15, s32[8,8]{1,0:T(8,128)} %bitcast.26, f32[8,8]{1,0:T(8,128)} %bitcast.17, f32[8,8]{1,0:T(8,128)} %bitcast.27, s32[1,16]{1,0:T(1,128)} %refs_6_.1), custom_call_target="tpu_custom_call" | custom-call | tf_op jit(solution)/shard_map/pallas_call | solution.py:16
  2.3 3.1 %collective-permute-start.10 = (bf16[16,2176]{1,0:T(8,128)(2,1)S(1)}, bf16[16,2176]{1,0:T(8,128)(2,1)S(1)}, u32[]{:S(2)}, u32[]{:S(2)}) collective-permute-start(bf16[16,2176]{1,0:T(8,128)(2,1)S(1)} %shard_map.112.refs_0_), channel_id=1, source_target_pairs={{0,8},{1,9},{2,10},{3,11},{4,12},{5,13},{6,14},{7,15},{8,0},{9,1},... | collective-permute-start | bytes 208904 | tf_op jit(solution)/shard_map/ppermute | solution.py:36
  5.4 2.6 %collective-permute-start.11 = (bf16[16,2176]{1,0:T(8,128)(2,1)S(1)}, bf16[16,2176]{1,0:T(8,128)(2,1)S(1)}, u32[]{:S(2)}, u32[]{:S(2)}) collective-permute-start(bf16[16,2176]{1,0:T(8,128)(2,1)S(1)} %shard_map.112.refs_0_), channel_id=1, source_target_pairs={{0,16},{1,17},{2,18},{3,19},{4,20},{5,21},{6,22},{7,23},{8,24},{9,... | collective-permute-start | bytes 208904 | tf_op jit(solution)/shard_map/ppermute | solution.py:36
  8.0 0.0 collective-permute-start
  8.0 0.0 collective-permute-done.10.refs_0_
  8.0 5.2 %collective-permute-done.11.refs_1_ = bf16[16,2176]{1,0:T(8,128)(2,1)S(1)} collective-permute-done((bf16[16,2176]{1,0:T(8,128)(2,1)S(1)}, bf16[16,2176]{1,0:T(8,128)(2,1)S(1)}, u32[]{:S(2)}, u32[]{:S(2)}) %collective-permute-start.11) | collective-permute-done | bytes 69664 | tf_op jit(solution)/shard_map/ppermute | solution.py:36
  13.2 1.6 %collective-permute-start.12 = (bf16[32,2176]{1,0:T(8,128)(2,1)S(1)}, bf16[32,2176]{1,0:T(8,128)(2,1)S(1)}, u32[]{:S(2)}, u32[]{:S(2)}) collective-permute-start(bf16[32,2176]{1,0:T(8,128)(2,1)S(1)} %shard_map.117.refs_0_), channel_id=1, source_target_pairs={{0,2},{1,3},{2,0},{3,1},{4,6},{5,7},{6,4},{7,5},{8,10},{9,11},{10,... | collective-permute-start | bytes 417800 | tf_op jit(solution)/shard_map/ppermute | solution.py:36
  14.7 1.5 %collective-permute-start.13 = (bf16[32,2176]{1,0:T(8,128)(2,1)S(1)}, bf16[32,2176]{1,0:T(8,128)(2,1)S(1)}, u32[]{:S(2)}, u32[]{:S(2)}) collective-permute-start(bf16[32,2176]{1,0:T(8,128)(2,1)S(1)} %shard_map.117.refs_0_), channel_id=1, source_target_pairs={{0,4},{1,5},{2,6},{3,7},{4,0},{5,1},{6,2},{7,3},{8,12},{9,13},{10,... | collective-permute-start | bytes 417800 | tf_op jit(solution)/shard_map/ppermute | solution.py:36
  16.2 0.0 collective-permute-done.refs_1_
  16.2 0.5 collective-permute-start.14
  16.7 0.0 collective-permute-done.2.refs_3_
  16.7 1.6 %collective-permute-start.1 = (bf16[32,2176]{1,0:T(8,128)(2,1)S(1)}, bf16[32,2176]{1,0:T(8,128)(2,1)S(1)}, u32[]{:S(2)}, u32[]{:S(2)}) collective-permute-start(bf16[32,2176]{1,0:T(8,128)(2,1)S(1)} %shard_map.113.refs_0_), channel_id=1, source_target_pairs={{0,2},{1,3},{2,0},{3,1},{4,6},{5,7},{6,4},{7,5},{8,10},{9,11},{10,... | collective-permute-start | bytes 417800 | tf_op jit(solution)/shard_map/ppermute | solution.py:36
  18.3 0.0 collective-permute-done.4.refs_1_
  18.3 1.5 %collective-permute-start.3 = (bf16[32,2176]{1,0:T(8,128)(2,1)S(1)}, bf16[32,2176]{1,0:T(8,128)(2,1)S(1)}, u32[]{:S(2)}, u32[]{:S(2)}) collective-permute-start(bf16[32,2176]{1,0:T(8,128)(2,1)S(1)} %shard_map.113.refs_0_), channel_id=1, source_target_pairs={{0,4},{1,5},{2,6},{3,7},{4,0},{5,1},{6,2},{7,3},{8,12},{9,13},{10,... | collective-permute-start | bytes 417800 | tf_op jit(solution)/shard_map/ppermute | solution.py:36
  19.8 0.0 collective-permute-done.12.refs_1_
  19.8 2.5 %collective-permute-start.5 = (bf16[32,2176]{1,0:T(8,128)(2,1)S(1)}, bf16[32,2176]{1,0:T(8,128)(2,1)S(1)}, u32[]{:S(2)}, u32[]{:S(2)}) collective-permute-start(bf16[32,2176]{1,0:T(8,128)(2,1)S(1)} %shard_map.113.refs_0_), channel_id=1, source_target_pairs={{0,6},{1,7},{2,4},{3,5},{4,2},{5,3},{6,0},{7,1},{8,14},{9,15},{10,... | collective-permute-start | bytes 417800 | tf_op jit(solution)/shard_map/ppermute | solution.py:36
  22.3 2.4 %shard_map.114 = (bf16[2048,768]{1,0:T(8,128)(2,1)S(1)}, bf16[2048,768]{1,0:T(8,128)(2,1)S(1)}, bf16[384,2048]{1,0:T(8,128)(2,1)S(1)}, bf16[384,2048]{1,0:T(8,128)(2,1)S(1)}) custom-call(bf16[2048,768]{1,0:T(8,128)(2,1)} %bitcast.21, bf16[2048,768]{1,0:T(8,128)(2,1)S(1)} %collective-permute-done.4.refs_1_, bf16[384,2048]{1,0:T(8,128)(2,1)} %bitcast.23, ...), custom_call_target="tpu_custom_call" | custom-call | tf_op jit(solution)/shard_map/pallas_call | solution.py:16
  24.7 0.0 collective-permute-done.13.refs_2_
  24.7 0.0 collective-permute-done.14.refs_3_
  24.8 1.7 %shard_map.118 = (bf16[32,2048]{1,0:T(8,128)(2,1)S(1)}, bf16[32,2048]{1,0:T(8,128)(2,1)S(1)}, bf16[32,2048]{1,0:T(8,128)(2,1)S(1)}, bf16[32,2048]{1,0:T(8,128)(2,1)S(1)}) custom-call(bf16[32,2176]{1,0:T(8,128)(2,1)S(1)} %shard_map.117.refs_0_, bf16[32,2176]{1,0:T(8,128)(2,1)S(1)} %collective-permute-done.12.refs_1_, ...), custom_call_target="tpu_custom_call" | custom-call | tf_op jit(solution)/shard_map/pallas_call | solution.py:16
  26.5 0.6 %collective-permute-start.15 = (bf16[32,2048]{1,0:T(8,128)(2,1)S(1)}, bf16[32,2048]{1,0:T(8,128)(2,1)S(1)}, u32[]{:S(2)}, u32[]{:S(2)}) collective-permute-start(bf16[32,2048]{1,0:T(8,128)(2,1)S(1)} %get-tuple-element.37), channel_id=1, source_target_pairs={{0,2},{1,3},{2,0},{3,1},{4,6},{5,7},{6,4},{7,5},{8,10},{9,11},{10,... | collective-permute-start | bytes 393224 | tf_op jit(solution)/shard_map/ppermute | solution.py:36
  27.1 0.5 collective-permute-start.16
  27.6 0.0 collective-permute-done.1.refs_1_
  27.6 2.5 %collective-permute-start.17 = (bf16[32,2048]{1,0:T(8,128)(2,1)S(1)}, bf16[32,2048]{1,0:T(8,128)(2,1)S(1)}, u32[]{:S(2)}, u32[]{:S(2)}) collective-permute-start(bf16[32,2048]{1,0:T(8,128)(2,1)S(1)} %get-tuple-element.39), channel_id=1, source_target_pairs={{0,6},{1,7},{2,4},{3,5},{4,2},{5,3},{6,0},{7,1},{8,14},{9,15},{10,... | collective-permute-start | bytes 393224 | tf_op jit(solution)/shard_map/ppermute | solution.py:36
  30.0 0.0 collective-permute-done.3.refs_2_
  30.0 0.0 collective-permute-done.5.refs_3_
  30.0 1.7 %shard_map.115 = (bf16[32,2048]{1,0:T(8,128)(2,1)S(1)}, bf16[32,2048]{1,0:T(8,128)(2,1)S(1)}, bf16[32,2048]{1,0:T(8,128)(2,1)S(1)}, bf16[32,2048]{1,0:T(8,128)(2,1)S(1)}) custom-call(bf16[32,2176]{1,0:T(8,128)(2,1)S(1)} %shard_map.113.refs_0_, bf16[32,2176]{1,0:T(8,128)(2,1)S(1)} %collective-permute-done.1.refs_1_, ...), custom_call_target="tpu_custom_call" | custom-call | tf_op jit(solution)/shard_map/pallas_call | solution.py:16
  31.7 0.8 %collective-permute-start.6 = (bf16[32,2048]{1,0:T(8,128)(2,1)S(1)}, bf16[32,2048]{1,0:T(8,128)(2,1)S(1)}, u32[]{:S(2)}, u32[]{:S(2)}) collective-permute-start(bf16[32,2048]{1,0:T(8,128)(2,1)S(1)} %get-tuple-element.31), channel_id=1, source_target_pairs={{0,2},{1,3},{2,0},{3,1},{4,6},{5,7},{6,4},{7,5},{8,10},{9,11},{10,... | collective-permute-start | bytes 393224 | tf_op jit(solution)/shard_map/ppermute | solution.py:36
  32.5 0.9 %collective-permute-start.7 = (bf16[32,2048]{1,0:T(8,128)(2,1)S(1)}, bf16[32,2048]{1,0:T(8,128)(2,1)S(1)}, u32[]{:S(2)}, u32[]{:S(2)}) collective-permute-start(bf16[32,2048]{1,0:T(8,128)(2,1)S(1)} %get-tuple-element.32), channel_id=1, source_target_pairs={{0,4},{1,5},{2,6},{3,7},{4,0},{5,1},{6,2},{7,3},{8,12},{9,13},{10,... | collective-permute-start | bytes 393224 | tf_op jit(solution)/shard_map/ppermute | solution.py:36
  33.5 0.0 collective-permute-done.15.refs_1_
  33.5 1.8 %collective-permute-start.8 = (bf16[32,2048]{1,0:T(8,128)(2,1)S(1)}, bf16[32,2048]{1,0:T(8,128)(2,1)S(1)}, u32[]{:S(2)}, u32[]{:S(2)}) collective-permute-start(bf16[32,2048]{1,0:T(8,128)(2,1)S(1)} %get-tuple-element.33), channel_id=1, source_target_pairs={{0,6},{1,7},{2,4},{3,5},{4,2},{5,3},{6,0},{7,1},{8,14},{9,15},{10,... | collective-permute-start | bytes 393224 | tf_op jit(solution)/shard_map/ppermute | solution.py:36
  35.3 0.0 collective-permute-done.16.refs_2_
  35.3 0.0 collective-permute-done.17.refs_3_
  35.3 0.1 shard_map.119
  35.4 2.1 %collective-permute-start.18 = (bf16[16,2048]{1,0:T(8,128)(2,1)S(1)}, bf16[16,2048]{1,0:T(8,128)(2,1)S(1)}, u32[]{:S(2)}, u32[]{:S(2)}) collective-permute-start(bf16[16,2048]{1,0:T(8,128)(2,1)S(1)} %get-tuple-element.40), channel_id=1, source_target_pairs={{0,16},{1,17},{2,18},{3,19},{4,20},{5,21},{6,22},{7,23},{8,24},{9,... | collective-permute-start | bytes 196616 | tf_op jit(solution)/shard_map/ppermute | solution.py:36
  37.5 1.1 %collective-permute-start.19 = (bf16[16,2048]{1,0:T(8,128)(2,1)S(1)}, bf16[16,2048]{1,0:T(8,128)(2,1)S(1)}, u32[]{:S(2)}, u32[]{:S(2)}) collective-permute-start(bf16[16,2048]{1,0:T(8,128)(2,1)S(1)} %get-tuple-element.41), channel_id=1, source_target_pairs={{0,8},{1,9},{2,10},{3,11},{4,12},{5,13},{6,14},{7,15},{8,0},{9,1},... | collective-permute-start | bytes 196616 | tf_op jit(solution)/shard_map/ppermute | solution.py:36
  38.6 0.0 collective-permute-done.6.refs_1_
  38.6 0.0 collective-permute-done.7.refs_2_
  38.6 0.7 %collective-permute-done.8.refs_3_ = bf16[32,2048]{1,0:T(8,128)(2,1)S(1)} collective-permute-done((bf16[32,2048]{1,0:T(8,128)(2,1)S(1)}, bf16[32,2048]{1,0:T(8,128)(2,1)S(1)}, u32[]{:S(2)}, u32[]{:S(2)}) %collective-permute-start.8) | collective-permute-done | bytes 131104 | tf_op jit(solution)/shard_map/ppermute | solution.py:36
  39.3 0.1 shard_map.116
  39.4 2.7 %collective-permute-start.9 = (bf16[16,2048]{1,0:T(8,128)(2,1)S(1)}, bf16[16,2048]{1,0:T(8,128)(2,1)S(1)}, u32[]{:S(2)}, u32[]{:S(2)}) collective-permute-start(bf16[16,2048]{1,0:T(8,128)(2,1)S(1)} %get-tuple-element.34), channel_id=1, source_target_pairs={{0,24},{1,25},{2,26},{3,27},{4,28},{5,29},{6,30},{7,31},{8,16},{9,... | collective-permute-start | bytes 196616 | tf_op jit(solution)/shard_map/ppermute | solution.py:36
  42.1 0.3 collective-permute-done.19.refs_3_
  42.3 3.2 %collective-permute-done.9.refs_0_ = bf16[16,2048]{1,0:T(8,128)(2,1)S(1)} collective-permute-done((bf16[16,2048]{1,0:T(8,128)(2,1)S(1)}, bf16[16,2048]{1,0:T(8,128)(2,1)S(1)}, u32[]{:S(2)}, u32[]{:S(2)}) %collective-permute-start.9) | collective-permute-done | bytes 65568 | tf_op jit(solution)/shard_map/ppermute | solution.py:36
  45.5 0.7 %shard_map.120 = (bf16[8,2048]{1,0:T(8,128)(2,1)}, bf16[8,2048]{1,0:T(8,128)(2,1)}, f32[32,16]{1,0:T(8,128)S(1)}) custom-call(bf16[16,2048]{1,0:T(8,128)(2,1)S(1)} %collective-permute-done.9.refs_0_, f32[16,2048]{1,0:T(8,128)S(1)} %get-tuple-element.35.refs_1_, bf16[16,2048]{1,0:T(8,128)(2,1)S(1)} %collective-permute-done.18.refs_2_, ...), custom_call_target="tpu_custom_call" | custom-call | tf_op jit(solution)/shard_map/pallas_call | solution.py:16
  46.2 11.2 %all_to_all.11 = f32[32,1,16]{2,1,0:T(1,128)S(1)} all-to-all(f32[32,1,16]{2,1,0:T(1,128)S(1)} %bitcast.19), channel_id=1, replica_groups=mesh['section'=1,'expert'=32] {'expert'}, dimensions={0} | all-to-all | bytes 4096 | tf_op jit(solution)/shard_map/all_to_all | solution.py:335
  57.4 0.5 shard_map.121
  (7 shorter events, 0.0 us)
Async XLA Ops:
  0.6 17.7 %collective-permute-start.4 = (bf16[2048,768]{1,0:T(8,128)(2,1)}, bf16[2048,768]{1,0:T(8,128)(2,1)S(1)}, u32[]{:S(2)}, u32[]{:S(2)}) collective-permute-start(bf16[2048,768]{1,0:T(8,128)(2,1)} %bitcast.20), channel_id=1, source_target_pairs={{0,1},{1,0},{2,3},{3,2},{4,5},{5,4},{6,7},{7,6},{8,9},{9,8},{10,11... | collective-permute-start | bytes 9437192 | tf_op jit(solution)/shard_map/ppermute | solution.py:36
  1.1 15.6 %collective-permute-start.2 = (bf16[384,2048]{1,0:T(8,128)(2,1)}, bf16[384,2048]{1,0:T(8,128)(2,1)S(1)}, u32[]{:S(2)}, u32[]{:S(2)}) collective-permute-start(bf16[384,2048]{1,0:T(8,128)(2,1)} %bitcast.22), channel_id=1, source_target_pairs={{0,1},{1,0},{2,3},{3,2},{4,5},{5,4},{6,7},{7,6},{8,9},{9,8},{10,11... | collective-permute-start | bytes 4718600 | tf_op jit(solution)/shard_map/ppermute | solution.py:36
  2.3 5.7 %collective-permute-start.10 = (bf16[16,2176]{1,0:T(8,128)(2,1)S(1)}, bf16[16,2176]{1,0:T(8,128)(2,1)S(1)}, u32[]{:S(2)}, u32[]{:S(2)}) collective-permute-start(bf16[16,2176]{1,0:T(8,128)(2,1)S(1)} %shard_map.112.refs_0_), channel_id=1, source_target_pairs={{0,8},{1,9},{2,10},{3,11},{4,12},{5,13},{6,14},{7,15},{8,0},{9,1},... | collective-permute-start | bytes 208904 | tf_op jit(solution)/shard_map/ppermute | solution.py:36
  5.4 7.8 %collective-permute-start.11 = (bf16[16,2176]{1,0:T(8,128)(2,1)S(1)}, bf16[16,2176]{1,0:T(8,128)(2,1)S(1)}, u32[]{:S(2)}, u32[]{:S(2)}) collective-permute-start(bf16[16,2176]{1,0:T(8,128)(2,1)S(1)} %shard_map.112.refs_0_), channel_id=1, source_target_pairs={{0,16},{1,17},{2,18},{3,19},{4,20},{5,21},{6,22},{7,23},{8,24},{9,... | collective-permute-start | bytes 208904 | tf_op jit(solution)/shard_map/ppermute | solution.py:36
  8.0 8.3 %collective-permute-start = (bf16[16,2176]{1,0:T(8,128)(2,1)S(1)}, bf16[16,2176]{1,0:T(8,128)(2,1)S(1)}, u32[]{:S(2)}, u32[]{:S(2)}) collective-permute-start(bf16[16,2176]{1,0:T(8,128)(2,1)S(1)} %shard_map.112.refs_0_), channel_id=1, source_target_pairs={{0,24},{1,25},{2,26},{3,27},{4,28},{5,29},{6,30},{7,31},{8,16},{9,... | collective-permute-start | bytes 208904 | tf_op jit(solution)/shard_map/ppermute | solution.py:36
  13.2 6.7 %collective-permute-start.12 = (bf16[32,2176]{1,0:T(8,128)(2,1)S(1)}, bf16[32,2176]{1,0:T(8,128)(2,1)S(1)}, u32[]{:S(2)}, u32[]{:S(2)}) collective-permute-start(bf16[32,2176]{1,0:T(8,128)(2,1)S(1)} %shard_map.117.refs_0_), channel_id=1, source_target_pairs={{0,2},{1,3},{2,0},{3,1},{4,6},{5,7},{6,4},{7,5},{8,10},{9,11},{10,... | collective-permute-start | bytes 417800 | tf_op jit(solution)/shard_map/ppermute | solution.py:36
  14.7 10.0 %collective-permute-start.13 = (bf16[32,2176]{1,0:T(8,128)(2,1)S(1)}, bf16[32,2176]{1,0:T(8,128)(2,1)S(1)}, u32[]{:S(2)}, u32[]{:S(2)}) collective-permute-start(bf16[32,2176]{1,0:T(8,128)(2,1)S(1)} %shard_map.117.refs_0_), channel_id=1, source_target_pairs={{0,4},{1,5},{2,6},{3,7},{4,0},{5,1},{6,2},{7,3},{8,12},{9,13},{10,... | collective-permute-start | bytes 417800 | tf_op jit(solution)/shard_map/ppermute | solution.py:36
  16.2 8.5 %collective-permute-start.14 = (bf16[32,2176]{1,0:T(8,128)(2,1)S(1)}, bf16[32,2176]{1,0:T(8,128)(2,1)S(1)}, u32[]{:S(2)}, u32[]{:S(2)}) collective-permute-start(bf16[32,2176]{1,0:T(8,128)(2,1)S(1)} %shard_map.117.refs_0_), channel_id=1, source_target_pairs={{0,6},{1,7},{2,4},{3,5},{4,2},{5,3},{6,0},{7,1},{8,14},{9,15},{10,... | collective-permute-start | bytes 417800 | tf_op jit(solution)/shard_map/ppermute | solution.py:36
  16.7 10.8 %collective-permute-start.1 = (bf16[32,2176]{1,0:T(8,128)(2,1)S(1)}, bf16[32,2176]{1,0:T(8,128)(2,1)S(1)}, u32[]{:S(2)}, u32[]{:S(2)}) collective-permute-start(bf16[32,2176]{1,0:T(8,128)(2,1)S(1)} %shard_map.113.refs_0_), channel_id=1, source_target_pairs={{0,2},{1,3},{2,0},{3,1},{4,6},{5,7},{6,4},{7,5},{8,10},{9,11},{10,... | collective-permute-start | bytes 417800 | tf_op jit(solution)/shard_map/ppermute | solution.py:36
  18.3 11.7 %collective-permute-start.3 = (bf16[32,2176]{1,0:T(8,128)(2,1)S(1)}, bf16[32,2176]{1,0:T(8,128)(2,1)S(1)}, u32[]{:S(2)}, u32[]{:S(2)}) collective-permute-start(bf16[32,2176]{1,0:T(8,128)(2,1)S(1)} %shard_map.113.refs_0_), channel_id=1, source_target_pairs={{0,4},{1,5},{2,6},{3,7},{4,0},{5,1},{6,2},{7,3},{8,12},{9,13},{10,... | collective-permute-start | bytes 417800 | tf_op jit(solution)/shard_map/ppermute | solution.py:36
  19.8 10.2 %collective-permute-start.5 = (bf16[32,2176]{1,0:T(8,128)(2,1)S(1)}, bf16[32,2176]{1,0:T(8,128)(2,1)S(1)}, u32[]{:S(2)}, u32[]{:S(2)}) collective-permute-start(bf16[32,2176]{1,0:T(8,128)(2,1)S(1)} %shard_map.113.refs_0_), channel_id=1, source_target_pairs={{0,6},{1,7},{2,4},{3,5},{4,2},{5,3},{6,0},{7,1},{8,14},{9,15},{10,... | collective-permute-start | bytes 417800 | tf_op jit(solution)/shard_map/ppermute | solution.py:36
  26.5 7.0 %collective-permute-start.15 = (bf16[32,2048]{1,0:T(8,128)(2,1)S(1)}, bf16[32,2048]{1,0:T(8,128)(2,1)S(1)}, u32[]{:S(2)}, u32[]{:S(2)}) collective-permute-start(bf16[32,2048]{1,0:T(8,128)(2,1)S(1)} %get-tuple-element.37), channel_id=1, source_target_pairs={{0,2},{1,3},{2,0},{3,1},{4,6},{5,7},{6,4},{7,5},{8,10},{9,11},{10,... | collective-permute-start | bytes 393224 | tf_op jit(solution)/shard_map/ppermute | solution.py:36
  27.1 8.2 %collective-permute-start.16 = (bf16[32,2048]{1,0:T(8,128)(2,1)S(1)}, bf16[32,2048]{1,0:T(8,128)(2,1)S(1)}, u32[]{:S(2)}, u32[]{:S(2)}) collective-permute-start(bf16[32,2048]{1,0:T(8,128)(2,1)S(1)} %get-tuple-element.38), channel_id=1, source_target_pairs={{0,4},{1,5},{2,6},{3,7},{4,0},{5,1},{6,2},{7,3},{8,12},{9,13},{10,... | collective-permute-start | bytes 393224 | tf_op jit(solution)/shard_map/ppermute | solution.py:36
  27.6 18.0 %copy-start = (s32[1,1,8,8]{3,2,1,0:T(8,128)S(1)}, s32[1,1,8,8]{3,2,1,0:T(8,128)}, u32[]{:S(2)}) copy-start(s32[1,1,8,8]{3,2,1,0:T(8,128)} %param.11) | copy-start | bytes 772
  27.6 18.0 %copy-start.1 = (f32[1,1,8,8]{3,2,1,0:T(8,128)S(1)}, f32[1,1,8,8]{3,2,1,0:T(8,128)}, u32[]{:S(2)}) copy-start(f32[1,1,8,8]{3,2,1,0:T(8,128)} %param.13) | copy-start | bytes 772
  27.6 7.7 %collective-permute-start.17 = (bf16[32,2048]{1,0:T(8,128)(2,1)S(1)}, bf16[32,2048]{1,0:T(8,128)(2,1)S(1)}, u32[]{:S(2)}, u32[]{:S(2)}) collective-permute-start(bf16[32,2048]{1,0:T(8,128)(2,1)S(1)} %get-tuple-element.39), channel_id=1, source_target_pairs={{0,6},{1,7},{2,4},{3,5},{4,2},{5,3},{6,0},{7,1},{8,14},{9,15},{10,... | collective-permute-start | bytes 393224 | tf_op jit(solution)/shard_map/ppermute | solution.py:36
  31.7 6.9 %collective-permute-start.6 = (bf16[32,2048]{1,0:T(8,128)(2,1)S(1)}, bf16[32,2048]{1,0:T(8,128)(2,1)S(1)}, u32[]{:S(2)}, u32[]{:S(2)}) collective-permute-start(bf16[32,2048]{1,0:T(8,128)(2,1)S(1)} %get-tuple-element.31), channel_id=1, source_target_pairs={{0,2},{1,3},{2,0},{3,1},{4,6},{5,7},{6,4},{7,5},{8,10},{9,11},{10,... | collective-permute-start | bytes 393224 | tf_op jit(solution)/shard_map/ppermute | solution.py:36
  32.5 6.1 %collective-permute-start.7 = (bf16[32,2048]{1,0:T(8,128)(2,1)S(1)}, bf16[32,2048]{1,0:T(8,128)(2,1)S(1)}, u32[]{:S(2)}, u32[]{:S(2)}) collective-permute-start(bf16[32,2048]{1,0:T(8,128)(2,1)S(1)} %get-tuple-element.32), channel_id=1, source_target_pairs={{0,4},{1,5},{2,6},{3,7},{4,0},{5,1},{6,2},{7,3},{8,12},{9,13},{10,... | collective-permute-start | bytes 393224 | tf_op jit(solution)/shard_map/ppermute | solution.py:36
  33.5 5.9 %collective-permute-start.8 = (bf16[32,2048]{1,0:T(8,128)(2,1)S(1)}, bf16[32,2048]{1,0:T(8,128)(2,1)S(1)}, u32[]{:S(2)}, u32[]{:S(2)}) collective-permute-start(bf16[32,2048]{1,0:T(8,128)(2,1)S(1)} %get-tuple-element.33), channel_id=1, source_target_pairs={{0,6},{1,7},{2,4},{3,5},{4,2},{5,3},{6,0},{7,1},{8,14},{9,15},{10,... | collective-permute-start | bytes 393224 | tf_op jit(solution)/shard_map/ppermute | solution.py:36
  35.4 6.7 %collective-permute-start.18 = (bf16[16,2048]{1,0:T(8,128)(2,1)S(1)}, bf16[16,2048]{1,0:T(8,128)(2,1)S(1)}, u32[]{:S(2)}, u32[]{:S(2)}) collective-permute-start(bf16[16,2048]{1,0:T(8,128)(2,1)S(1)} %get-tuple-element.40), channel_id=1, source_target_pairs={{0,16},{1,17},{2,18},{3,19},{4,20},{5,21},{6,22},{7,23},{8,24},{9,... | collective-permute-start | bytes 196616 | tf_op jit(solution)/shard_map/ppermute | solution.py:36
  37.5 4.8 %collective-permute-start.19 = (bf16[16,2048]{1,0:T(8,128)(2,1)S(1)}, bf16[16,2048]{1,0:T(8,128)(2,1)S(1)}, u32[]{:S(2)}, u32[]{:S(2)}) collective-permute-start(bf16[16,2048]{1,0:T(8,128)(2,1)S(1)} %get-tuple-element.41), channel_id=1, source_target_pairs={{0,8},{1,9},{2,10},{3,11},{4,12},{5,13},{6,14},{7,15},{8,0},{9,1},... | collective-permute-start | bytes 196616 | tf_op jit(solution)/shard_map/ppermute | solution.py:36
  39.4 6.1 %collective-permute-start.9 = (bf16[16,2048]{1,0:T(8,128)(2,1)S(1)}, bf16[16,2048]{1,0:T(8,128)(2,1)S(1)}, u32[]{:S(2)}, u32[]{:S(2)}) collective-permute-start(bf16[16,2048]{1,0:T(8,128)(2,1)S(1)} %get-tuple-element.34), channel_id=1, source_target_pairs={{0,24},{1,25},{2,26},{3,27},{4,28},{5,29},{6,30},{7,31},{8,16},{9,... | collective-permute-start | bytes 196616 | tf_op jit(solution)/shard_map/ppermute | solution.py:36

commit v6 on v5

--- a/solution.py
+++ b/solution.py
@@ -103,13 +103,12 @@
         copy.wait()
 
 
-def stage_weights(own_in, own_out, other_in, other_out):
-    weights = [in_hbm(own_in), other_in, in_hbm(own_out), other_out]
+def stage(arrays):
     return run_kernel(
-        functools.partial(stage_kernel, len(weights)),
-        [pltpu.VMEM(value.shape, value.dtype) for value in weights],
-        weights,
-        [pltpu.SemaphoreType.DMA((len(weights),))],
+        functools.partial(stage_kernel, len(arrays)),
+        [pltpu.VMEM(value.shape, value.dtype) for value in arrays],
+        arrays,
+        [pltpu.SemaphoreType.DMA((len(arrays),))],
         space=pl.ANY,
     )
 
@@ -185,13 +184,13 @@
     )
 
 
-def plane_kernel(count, *refs):
-    part_refs, out_refs = refs[:count], refs[count:]
-    rows = out_refs[0].shape[0]
-    for place, out_ref in enumerate(out_refs):
-        out_ref[...] = sum(
-            ref[place * rows : (place + 1) * rows, :].astype(jnp.float32) for ref in part_refs
-        ).astype(out_ref.dtype)
+def add_parts_kernel(kept_ref, came_ref, *out_refs):
+    filled = 0
+    for out_ref in out_refs:
+        rows = slice(filled, filled + out_ref.shape[0])
+        filled += out_ref.shape[0]
+        total = kept_ref[rows, :].astype(jnp.float32) + came_ref[rows, :].astype(jnp.float32)
+        out_ref[...] = total.astype(out_ref.dtype)
 
 
 def final_kernel(parts, factor, *refs):
@@ -237,15 +236,14 @@
     extra = -(-2 * experts // LANES) * LANES
     rows = 2 * tok_rows
     chips = devices // SPLIT
-    inner = min(4, chips)
+    inner = 4
     outer = chips // inner
-    inner_masks = [SPLIT * i for i in range(1, inner)]
+    plane_masks = [SPLIT, 2 * SPLIT]
     layer_mask = lambda j: SPLIT * inner * j
     nearer = list(range(1, outer // 2 + 1))
     streams = [[j for j in range(outer) if j not in nearer], nearer]
     own_in, own_out = w_in[0, 0], w_out[0, 0]
     other_out, other_in = exclusive(own_out, 1), exclusive(own_in, 1)
-    weights = None
 
     step_count = micro_count + section_count - 1
     carry = jnp.zeros((2, tok_rows, model_width), jnp.bfloat16)
@@ -288,29 +286,27 @@
         column = {0: packed}
         for j in streams[1][::-1] + streams[0][1:]:
             column[j] = exclusive(packed, layer_mask(j))
+        if tick == 0:
+            own = stage([in_hbm(own_in), in_hbm(own_out)])
+            other = stage([other_in, other_out])
+            weights = [own[0], other[0], own[1], other[1]]
+            column[nearer[0]] = after(column[nearer[0]], own)
         blocks = []
-        for stream, layers in enumerate(streams):
+        for layers, masks in zip(streams, (plane_masks, plane_masks[::-1])):
             joined = join_rows([column[j] for j in layers])
-            block = [joined]
-            for mask in inner_masks:
-                block.append(exclusive(joined, mask))
-                if stream == 0 and tick == 0:
-                    joined = after(joined, other_out if len(block) == 2 else other_in)
-            blocks.append(block)
-        if weights is None:
-            weights = stage_weights(own_in, own_out, other_in, other_out)
+            both = join_rows([joined, exclusive(joined, masks[0])])
+            blocks.append([both, exclusive(both, masks[1])])
         summed = []
-        for stream, layers in enumerate(streams):
-            partial = run_expert(
-                experts, blocks[stream], weights, [len(layers) * rows] * inner
+        for block, layers, masks in zip(blocks, streams, (plane_masks, plane_masks[::-1])):
+            half = block[0].shape[0] // 2
+            kept, sent = run_expert(experts, block, weights, [2 * half] * 2)
+            kept, sent = run_kernel(
+                add_parts_kernel,
+                [like(half, model_width, jnp.float32), like(half, model_width)],
+                [kept, exclusive(sent, masks[1])],
             )
-            returned = [partial[0]] + [
-                exclusive(part, mask) for part, mask in zip(partial[1:], inner_masks)
-            ]
-            outs = [like(rows, model_width)] * len(layers)
-            if stream == 0:
-                outs[0] = like(rows, model_width, jnp.float32)
-            sums = run_kernel(functools.partial(plane_kernel, inner), outs, returned)
+            outs = [like(rows, model_width, jnp.bfloat16 if j else jnp.float32) for j in layers]
+            sums = run_kernel(add_parts_kernel, outs, [kept, exclusive(sent, masks[0])])
             for j, value in list(zip(layers, sums))[::-1]:
                 summed.append(exclusive(value, layer_mask(j)) if j else value)
         round_orig, round_pruned, tick_terms, *moe = run_kernel(

time: 58.1 us -> 60 us (1.033)
  waiting for transfers between devices: 9.42 us -> 16.2 us
  starting transfers between devices: 28.3 us -> 24.3 us
  blocking collectives: 11.2 us -> 10 us
    ppermute x20 -> x16, waiting for transfers between devices: 9.42 us -> 16.2 us  [exclusive(): return lax.ppermute(value, 'expert', pairs)]
    ppermute x20 -> x16, starting transfers between devices: 28.3 us -> 24.3 us  [exclusive(): return lax.ppermute(value, 'expert', pairs)]
    all_to_all x1, blocking collectives: 11.2 us -> 10 us  [on_device(): lax.all_to_all(terms, 'expert', split_axis=0, concat_axis=0, tiled=True)]
    pallas_call x10 -> x15, Pallas kernels: 8.25 us -> 8.49 us  [run_kernel(): pl.pallas_call(body, out_shape=outs, in_specs=[pl.BlockSpec(memory_space=...]
  transfers between devices with their start and end apart: 20 -> 16, of which waited for: 4 -> 11; matrix products, arithmetic and copies ran while one was open for 0% -> 0% of each run, Pallas kernels for 12% -> 12%
where the time goes in v6:
time: 60 us; the launch traced here: 59.8 us
  starting transfers between devices  24.3 us (40%)
  waiting for transfers between devices  16.2 us (27%)
  blocking collectives  10 us (17%)
  Pallas kernels  8.49 us (14%)
  between operations  0.74 us (1%)
    ppermute x16, starting transfers between devices, exclusive(): return lax.ppermute(value, 'expert', pairs)  24.3 us
    ppermute x16, waiting for transfers between devices, exclusive(): return lax.ppermute(value, 'expert', pairs)  16.2 us
    all_to_all x1, blocking collectives, on_device(): lax.all_to_all(terms, 'expert', split_axis=0, concat_axis=0, tiled=True)  10 us
    pallas_call x15, Pallas kernels, run_kernel(): pl.pallas_call(body, out_shape=outs, in_specs=[pl.BlockSpec(memory_space=...  8.49 us
  transfers between devices with their start and end apart: 16, of which 11 were waited for; matrix products, arithmetic and copies ran while one was open for 0% of the time, Pallas kernels for 12%

profile of v6, /device:TPU:0, one launch (start us, length us, event | category | flops | bytes accessed | tf_op | source)
XLA Modules:
  0.0 59.8 jit_solution(10994351115650791646)
XLA Ops:
  0.6 0.5 collective-permute-start.3
  1.1 0.1 collective-permute-start.4
  1.2 1.1 %shard_map.112.refs_0_ = bf16[16,2176]{1,0:T(8,128)(2,1)S(1)} custom-call(bf16[8,2048]{1,0:T(8,128)(2,1)} %bitcast.24, bf16[8,2048]{1,0:T(8,128)(2,1)} %bitcast.25, s32[8,8]{1,0:T(8,128)} %bitcast.15, s32[8,8]{1,0:T(8,128)} %bitcast.26, f32[8,8]{1,0:T(8,128)} %bitcast.17, f32[8,8]{1,0:T(8,128)} %bitcast.27, s32[1,16]{1,0:T(1,128)} %refs_6_.1), custom_call_target="tpu_custom_call" | custom-call | tf_op jit(solution)/shard_map/pallas_call | solution.py:16
  2.3 5.1 %collective-permute-start = (bf16[16,2176]{1,0:T(8,128)(2,1)S(1)}, bf16[16,2176]{1,0:T(8,128)(2,1)S(1)}, u32[]{:S(2)}, u32[]{:S(2)}) collective-permute-start(bf16[16,2176]{1,0:T(8,128)(2,1)S(1)} %shard_map.112.refs_0_), channel_id=1, source_target_pairs={{0,24},{1,25},{2,26},{3,27},{4,28},{5,29},{6,30},{7,31},{8,16},{9,... | collective-permute-start | bytes 208904 | tf_op jit(solution)/shard_map/ppermute | solution.py:36
  7.4 0.0 collective-permute-start.8
  7.4 0.6 %collective-permute-start.9 = (bf16[16,2176]{1,0:T(8,128)(2,1)S(1)}, bf16[16,2176]{1,0:T(8,128)(2,1)S(1)}, u32[]{:S(2)}, u32[]{:S(2)}) collective-permute-start(bf16[16,2176]{1,0:T(8,128)(2,1)S(1)} %shard_map.112.refs_0_), channel_id=1, source_target_pairs={{0,16},{1,17},{2,18},{3,19},{4,20},{5,21},{6,22},{7,23},{8,24},{9,... | collective-permute-start | bytes 208904 | tf_op jit(solution)/shard_map/ppermute | solution.py:36
  8.1 2.4 %shard_map.115 = (bf16[2048,768]{1,0:T(8,128)(2,1)S(1)}, bf16[384,2048]{1,0:T(8,128)(2,1)S(1)}) custom-call(bf16[2048,768]{1,0:T(8,128)(2,1)} %bitcast.21, bf16[384,2048]{1,0:T(8,128)(2,1)} %bitcast.23), custom_call_target="tpu_custom_call" | custom-call | tf_op jit(solution)/shard_map/pallas_call | solution.py:16
  10.4 0.0 collective-permute-done.refs_1_
  10.5 1.8 %collective-permute-start.1 = (bf16[32,2176]{1,0:T(8,128)(2,1)S(1)}, bf16[32,2176]{1,0:T(8,128)(2,1)S(1)}, u32[]{:S(2)}, u32[]{:S(2)}) collective-permute-start(bf16[32,2176]{1,0:T(8,128)(2,1)S(1)} %shard_map.113.refs_0_), channel_id=1, source_target_pairs={{0,2},{1,3},{2,0},{3,1},{4,6},{5,7},{6,4},{7,5},{8,10},{9,11},{10,... | collective-permute-start | bytes 417800 | tf_op jit(solution)/shard_map/ppermute | solution.py:36
  12.3 0.2 collective-permute-done.8.refs_0_
  12.4 0.9 %collective-permute-done.9.refs_1_ = bf16[16,2176]{1,0:T(8,128)(2,1)S(1)} collective-permute-done((bf16[16,2176]{1,0:T(8,128)(2,1)S(1)}, bf16[16,2176]{1,0:T(8,128)(2,1)S(1)}, u32[]{:S(2)}, u32[]{:S(2)}) %collective-permute-start.9) | collective-permute-done | bytes 69664 | tf_op jit(solution)/shard_map/ppermute | solution.py:36
  13.4 1.6 %collective-permute-start.10 = (bf16[32,2176]{1,0:T(8,128)(2,1)S(1)}, bf16[32,2176]{1,0:T(8,128)(2,1)S(1)}, u32[]{:S(2)}, u32[]{:S(2)}) collective-permute-start(bf16[32,2176]{1,0:T(8,128)(2,1)S(1)} %shard_map.120.refs_0_), channel_id=1, source_target_pairs={{0,4},{1,5},{2,6},{3,7},{4,0},{5,1},{6,2},{7,3},{8,12},{9,13},{10,... | collective-permute-start | bytes 417800 | tf_op jit(solution)/shard_map/ppermute | solution.py:36
  15.0 0.6 %collective-permute-done.1.refs_1_ = bf16[32,2176]{1,0:T(8,128)(2,1)S(1)} collective-permute-done((bf16[32,2176]{1,0:T(8,128)(2,1)S(1)}, bf16[32,2176]{1,0:T(8,128)(2,1)S(1)}, u32[]{:S(2)}, u32[]{:S(2)}) %collective-permute-start.1) | collective-permute-done | bytes 139296 | tf_op jit(solution)/shard_map/ppermute | solution.py:36
  15.7 1.8 %collective-permute-start.2 = (bf16[64,2176]{1,0:T(8,128)(2,1)S(1)}, bf16[64,2176]{1,0:T(8,128)(2,1)S(1)}, u32[]{:S(2)}, u32[]{:S(2)}) collective-permute-start(bf16[64,2176]{1,0:T(8,128)(2,1)S(1)} %shard_map.114.refs_0_), channel_id=1, source_target_pairs={{0,4},{1,5},{2,6},{3,7},{4,0},{5,1},{6,2},{7,3},{8,12},{9,13},{10,... | collective-permute-start | bytes 835592 | tf_op jit(solution)/shard_map/ppermute | solution.py:36
  17.4 2.5 %collective-permute-done.10.refs_1_ = bf16[32,2176]{1,0:T(8,128)(2,1)S(1)} collective-permute-done((bf16[32,2176]{1,0:T(8,128)(2,1)S(1)}, bf16[32,2176]{1,0:T(8,128)(2,1)S(1)}, u32[]{:S(2)}, u32[]{:S(2)}) %collective-permute-start.10) | collective-permute-done | bytes 139296 | tf_op jit(solution)/shard_map/ppermute | solution.py:36
  19.9 1.6 %collective-permute-start.11 = (bf16[64,2176]{1,0:T(8,128)(2,1)S(1)}, bf16[64,2176]{1,0:T(8,128)(2,1)S(1)}, u32[]{:S(2)}, u32[]{:S(2)}) collective-permute-start(bf16[64,2176]{1,0:T(8,128)(2,1)S(1)} %shard_map.121.refs_0_), channel_id=1, source_target_pairs={{0,2},{1,3},{2,0},{3,1},{4,6},{5,7},{6,4},{7,5},{8,10},{9,11},{10,... | collective-permute-start | bytes 835592 | tf_op jit(solution)/shard_map/ppermute | solution.py:36
  21.5 0.0 collective-permute-done.4.refs_1_
  21.5 0.0 collective-permute-done.3.refs_0_
  21.5 0.3 shard_map.116
  21.9 2.2 %collective-permute-done.2.refs_1_ = bf16[64,2176]{1,0:T(8,128)(2,1)S(1)} collective-permute-done((bf16[64,2176]{1,0:T(8,128)(2,1)S(1)}, bf16[64,2176]{1,0:T(8,128)(2,1)S(1)}, u32[]{:S(2)}, u32[]{:S(2)}) %collective-permute-start.2) | collective-permute-done | bytes 278560 | tf_op jit(solution)/shard_map/ppermute | solution.py:36
  24.1 1.6 %shard_map.117 = (bf16[64,2048]{1,0:T(8,128)(2,1)S(1)}, bf16[64,2048]{1,0:T(8,128)(2,1)S(1)}) custom-call(bf16[64,2176]{1,0:T(8,128)(2,1)S(1)} %shard_map.114.refs_0_, bf16[64,2176]{1,0:T(8,128)(2,1)S(1)} %collective-permute-done.2.refs_1_, bf16[2048,768]{1,0:T(8,128)(2,1)S(1)} %get-tuple-element.23.refs_2_, ...), custom_call_target="tpu_custom_call" | custom-call | tf_op jit(solution)/shard_map/pallas_call | solution.py:16
  25.7 0.0 copy-start
  25.8 0.0 copy-start.1
  25.8 1.6 %collective-permute-start.5 = (bf16[64,2048]{1,0:T(8,128)(2,1)S(1)}, bf16[64,2048]{1,0:T(8,128)(2,1)S(1)}, u32[]{:S(2)}, u32[]{:S(2)}) collective-permute-start(bf16[64,2048]{1,0:T(8,128)(2,1)S(1)} %get-tuple-element.28), channel_id=1, source_target_pairs={{0,4},{1,5},{2,6},{3,7},{4,0},{5,1},{6,2},{7,3},{8,12},{9,13},{10,... | collective-permute-start | bytes 786440 | tf_op jit(solution)/shard_map/ppermute | solution.py:36
  27.4 0.0 collective-permute-done.11.refs_1_
  27.4 1.6 %shard_map.122 = (bf16[64,2048]{1,0:T(8,128)(2,1)S(1)}, bf16[64,2048]{1,0:T(8,128)(2,1)S(1)}) custom-call(bf16[64,2176]{1,0:T(8,128)(2,1)S(1)} %shard_map.121.refs_0_, bf16[64,2176]{1,0:T(8,128)(2,1)S(1)} %collective-permute-done.11.refs_1_, bf16[2048,768]{1,0:T(8,128)(2,1)S(1)} %get-tuple-element.23.refs_2_, ...), custom_call_target="tpu_custom_call" | custom-call | tf_op jit(solution)/shard_map/pallas_call | solution.py:16
  29.0 1.6 %collective-permute-start.12 = (bf16[64,2048]{1,0:T(8,128)(2,1)S(1)}, bf16[64,2048]{1,0:T(8,128)(2,1)S(1)}, u32[]{:S(2)}, u32[]{:S(2)}) collective-permute-start(bf16[64,2048]{1,0:T(8,128)(2,1)S(1)} %get-tuple-element.35), channel_id=1, source_target_pairs={{0,2},{1,3},{2,0},{3,1},{4,6},{5,7},{6,4},{7,5},{8,10},{9,11},{10,... | collective-permute-start | bytes 786440 | tf_op jit(solution)/shard_map/ppermute | solution.py:36
  30.6 1.8 %collective-permute-done.5.came_ref = bf16[64,2048]{1,0:T(8,128)(2,1)S(1)} collective-permute-done((bf16[64,2048]{1,0:T(8,128)(2,1)S(1)}, bf16[64,2048]{1,0:T(8,128)(2,1)S(1)}, u32[]{:S(2)}, u32[]{:S(2)}) %collective-permute-start.5) | collective-permute-done | bytes 262176 | tf_op jit(solution)/shard_map/ppermute | solution.py:36
  32.4 0.1 shard_map.118
  32.4 1.6 %collective-permute-start.6 = (bf16[32,2048]{1,0:T(8,128)(2,1)S(1)}, bf16[32,2048]{1,0:T(8,128)(2,1)S(1)}, u32[]{:S(2)}, u32[]{:S(2)}) collective-permute-start(bf16[32,2048]{1,0:T(8,128)(2,1)S(1)} %get-tuple-element.30), channel_id=1, source_target_pairs={{0,2},{1,3},{2,0},{3,1},{4,6},{5,7},{6,4},{7,5},{8,10},{9,11},{10,... | collective-permute-start | bytes 393224 | tf_op jit(solution)/shard_map/ppermute | solution.py:36
  34.0 2.7 %collective-permute-done.12.came_ref = bf16[64,2048]{1,0:T(8,128)(2,1)S(1)} collective-permute-done((bf16[64,2048]{1,0:T(8,128)(2,1)S(1)}, bf16[64,2048]{1,0:T(8,128)(2,1)S(1)}, u32[]{:S(2)}, u32[]{:S(2)}) %collective-permute-start.12) | collective-permute-done | bytes 262176 | tf_op jit(solution)/shard_map/ppermute | solution.py:36
  36.7 0.1 shard_map.123
  36.8 0.9 %collective-permute-start.13 = (bf16[32,2048]{1,0:T(8,128)(2,1)S(1)}, bf16[32,2048]{1,0:T(8,128)(2,1)S(1)}, u32[]{:S(2)}, u32[]{:S(2)}) collective-permute-start(bf16[32,2048]{1,0:T(8,128)(2,1)S(1)} %get-tuple-element.37), channel_id=1, source_target_pairs={{0,4},{1,5},{2,6},{3,7},{4,0},{5,1},{6,2},{7,3},{8,12},{9,13},{10,... | collective-permute-start | bytes 393224 | tf_op jit(solution)/shard_map/ppermute | solution.py:36
  37.7 0.4 collective-permute-done.6.came_ref
  38.2 2.6 %collective-permute-start.7 = (bf16[16,2048]{1,0:T(8,128)(2,1)S(1)}, bf16[16,2048]{1,0:T(8,128)(2,1)S(1)}, u32[]{:S(2)}, u32[]{:S(2)}) collective-permute-start(bf16[16,2048]{1,0:T(8,128)(2,1)S(1)} %get-tuple-element.31), channel_id=1, source_target_pairs={{0,24},{1,25},{2,26},{3,27},{4,28},{5,29},{6,30},{7,31},{8,16},{9,... | collective-permute-start | bytes 196616 | tf_op jit(solution)/shard_map/ppermute | solution.py:36
  40.7 1.1 %collective-permute-done.13.came_ref = bf16[32,2048]{1,0:T(8,128)(2,1)S(1)} collective-permute-done((bf16[32,2048]{1,0:T(8,128)(2,1)S(1)}, bf16[32,2048]{1,0:T(8,128)(2,1)S(1)}, u32[]{:S(2)}, u32[]{:S(2)}) %collective-permute-start.13) | collective-permute-done | bytes 131104 | tf_op jit(solution)/shard_map/ppermute | solution.py:36
  41.9 2.5 %collective-permute-start.14 = (bf16[16,2048]{1,0:T(8,128)(2,1)S(1)}, bf16[16,2048]{1,0:T(8,128)(2,1)S(1)}, u32[]{:S(2)}, u32[]{:S(2)}) collective-permute-start(bf16[16,2048]{1,0:T(8,128)(2,1)S(1)} %get-tuple-element.38), channel_id=1, source_target_pairs={{0,16},{1,17},{2,18},{3,19},{4,20},{5,21},{6,22},{7,23},{8,24},{9,... | collective-permute-start | bytes 196616 | tf_op jit(solution)/shard_map/ppermute | solution.py:36
  44.3 0.6 %collective-permute-start.15 = (bf16[16,2048]{1,0:T(8,128)(2,1)S(1)}, bf16[16,2048]{1,0:T(8,128)(2,1)S(1)}, u32[]{:S(2)}, u32[]{:S(2)}) collective-permute-start(bf16[16,2048]{1,0:T(8,128)(2,1)S(1)} %get-tuple-element.39), channel_id=1, source_target_pairs={{0,8},{1,9},{2,10},{3,11},{4,12},{5,13},{6,14},{7,15},{8,0},{9,1},... | collective-permute-start | bytes 196616 | tf_op jit(solution)/shard_map/ppermute | solution.py:36
  45.0 0.0 collective-permute-done.7.refs_0_
  45.0 2.1 %collective-permute-done.14.refs_2_ = bf16[16,2048]{1,0:T(8,128)(2,1)S(1)} collective-permute-done((bf16[16,2048]{1,0:T(8,128)(2,1)S(1)}, bf16[16,2048]{1,0:T(8,128)(2,1)S(1)}, u32[]{:S(2)}, u32[]{:S(2)}) %collective-permute-start.14) | collective-permute-done | bytes 65568 | tf_op jit(solution)/shard_map/ppermute | solution.py:36
  47.1 1.5 %collective-permute-done.15.refs_3_ = bf16[16,2048]{1,0:T(8,128)(2,1)S(1)} collective-permute-done((bf16[16,2048]{1,0:T(8,128)(2,1)S(1)}, bf16[16,2048]{1,0:T(8,128)(2,1)S(1)}, u32[]{:S(2)}, u32[]{:S(2)}) %collective-permute-start.15) | collective-permute-done | bytes 65568 | tf_op jit(solution)/shard_map/ppermute | solution.py:36
  48.6 0.0 copy-done
  48.6 0.0 copy-done.1
  48.6 0.7 %shard_map.125 = (bf16[8,2048]{1,0:T(8,128)(2,1)}, bf16[8,2048]{1,0:T(8,128)(2,1)}, f32[32,16]{1,0:T(8,128)S(1)}) custom-call(bf16[16,2048]{1,0:T(8,128)(2,1)S(1)} %collective-permute-done.7.refs_0_, f32[16,2048]{1,0:T(8,128)S(1)} %get-tuple-element.32.refs_1_, bf16[16,2048]{1,0:T(8,128)(2,1)S(1)} %collective-permute-done.14.refs_2_, ...), custom_call_target="tpu_custom_call" | custom-call | tf_op jit(solution)/shard_map/pallas_call | solution.py:16
  49.3 10.0 %all_to_all.11 = f32[32,1,16]{2,1,0:T(1,128)S(1)} all-to-all(f32[32,1,16]{2,1,0:T(1,128)S(1)} %bitcast.19), channel_id=1, replica_groups=mesh['section'=1,'expert'=32] {'expert'}, dimensions={0} | all-to-all | bytes 4096 | tf_op jit(solution)/shard_map/all_to_all | solution.py:331
  59.3 0.5 shard_map.126
  (6 shorter events, 0.1 us)
Async XLA Ops:
  0.6 20.9 %collective-permute-start.3 = (bf16[2048,768]{1,0:T(8,128)(2,1)}, bf16[2048,768]{1,0:T(8,128)(2,1)S(1)}, u32[]{:S(2)}, u32[]{:S(2)}) collective-permute-start(bf16[2048,768]{1,0:T(8,128)(2,1)} %bitcast.20), channel_id=1, source_target_pairs={{0,1},{1,0},{2,3},{3,2},{4,5},{5,4},{6,7},{7,6},{8,9},{9,8},{10,11... | collective-permute-start | bytes 9437192 | tf_op jit(solution)/shard_map/ppermute | solution.py:36
  1.1 20.4 %collective-permute-start.4 = (bf16[384,2048]{1,0:T(8,128)(2,1)}, bf16[384,2048]{1,0:T(8,128)(2,1)S(1)}, u32[]{:S(2)}, u32[]{:S(2)}) collective-permute-start(bf16[384,2048]{1,0:T(8,128)(2,1)} %bitcast.22), channel_id=1, source_target_pairs={{0,1},{1,0},{2,3},{3,2},{4,5},{5,4},{6,7},{7,6},{8,9},{9,8},{10,11... | collective-permute-start | bytes 4718600 | tf_op jit(solution)/shard_map/ppermute | solution.py:36
  2.3 8.1 %collective-permute-start = (bf16[16,2176]{1,0:T(8,128)(2,1)S(1)}, bf16[16,2176]{1,0:T(8,128)(2,1)S(1)}, u32[]{:S(2)}, u32[]{:S(2)}) collective-permute-start(bf16[16,2176]{1,0:T(8,128)(2,1)S(1)} %shard_map.112.refs_0_), channel_id=1, source_target_pairs={{0,24},{1,25},{2,26},{3,27},{4,28},{5,29},{6,30},{7,31},{8,16},{9,... | collective-permute-start | bytes 208904 | tf_op jit(solution)/shard_map/ppermute | solution.py:36
  7.4 5.0 %collective-permute-start.8 = (bf16[16,2176]{1,0:T(8,128)(2,1)S(1)}, bf16[16,2176]{1,0:T(8,128)(2,1)S(1)}, u32[]{:S(2)}, u32[]{:S(2)}) collective-permute-start(bf16[16,2176]{1,0:T(8,128)(2,1)S(1)} %shard_map.112.refs_0_), channel_id=1, source_target_pairs={{0,8},{1,9},{2,10},{3,11},{4,12},{5,13},{6,14},{7,15},{8,0},{9,1},... | collective-permute-start | bytes 208904 | tf_op jit(solution)/shard_map/ppermute | solution.py:36
  7.4 6.0 %collective-permute-start.9 = (bf16[16,2176]{1,0:T(8,128)(2,1)S(1)}, bf16[16,2176]{1,0:T(8,128)(2,1)S(1)}, u32[]{:S(2)}, u32[]{:S(2)}) collective-permute-start(bf16[16,2176]{1,0:T(8,128)(2,1)S(1)} %shard_map.112.refs_0_), channel_id=1, source_target_pairs={{0,16},{1,17},{2,18},{3,19},{4,20},{5,21},{6,22},{7,23},{8,24},{9,... | collective-permute-start | bytes 208904 | tf_op jit(solution)/shard_map/ppermute | solution.py:36
  10.5 5.2 %collective-permute-start.1 = (bf16[32,2176]{1,0:T(8,128)(2,1)S(1)}, bf16[32,2176]{1,0:T(8,128)(2,1)S(1)}, u32[]{:S(2)}, u32[]{:S(2)}) collective-permute-start(bf16[32,2176]{1,0:T(8,128)(2,1)S(1)} %shard_map.113.refs_0_), channel_id=1, source_target_pairs={{0,2},{1,3},{2,0},{3,1},{4,6},{5,7},{6,4},{7,5},{8,10},{9,11},{10,... | collective-permute-start | bytes 417800 | tf_op jit(solution)/shard_map/ppermute | solution.py:36
  13.4 6.5 %collective-permute-start.10 = (bf16[32,2176]{1,0:T(8,128)(2,1)S(1)}, bf16[32,2176]{1,0:T(8,128)(2,1)S(1)}, u32[]{:S(2)}, u32[]{:S(2)}) collective-permute-start(bf16[32,2176]{1,0:T(8,128)(2,1)S(1)} %shard_map.120.refs_0_), channel_id=1, source_target_pairs={{0,4},{1,5},{2,6},{3,7},{4,0},{5,1},{6,2},{7,3},{8,12},{9,13},{10,... | collective-permute-start | bytes 417800 | tf_op jit(solution)/shard_map/ppermute | solution.py:36
  15.7 8.4 %collective-permute-start.2 = (bf16[64,2176]{1,0:T(8,128)(2,1)S(1)}, bf16[64,2176]{1,0:T(8,128)(2,1)S(1)}, u32[]{:S(2)}, u32[]{:S(2)}) collective-permute-start(bf16[64,2176]{1,0:T(8,128)(2,1)S(1)} %shard_map.114.refs_0_), channel_id=1, source_target_pairs={{0,4},{1,5},{2,6},{3,7},{4,0},{5,1},{6,2},{7,3},{8,12},{9,13},{10,... | collective-permute-start | bytes 835592 | tf_op jit(solution)/shard_map/ppermute | solution.py:36
  19.9 7.4 %collective-permute-start.11 = (bf16[64,2176]{1,0:T(8,128)(2,1)S(1)}, bf16[64,2176]{1,0:T(8,128)(2,1)S(1)}, u32[]{:S(2)}, u32[]{:S(2)}) collective-permute-start(bf16[64,2176]{1,0:T(8,128)(2,1)S(1)} %shard_map.121.refs_0_), channel_id=1, source_target_pairs={{0,2},{1,3},{2,0},{3,1},{4,6},{5,7},{6,4},{7,5},{8,10},{9,11},{10,... | collective-permute-start | bytes 835592 | tf_op jit(solution)/shard_map/ppermute | solution.py:36
  25.7 22.9 %copy-start = (s32[1,1,8,8]{3,2,1,0:T(8,128)S(1)}, s32[1,1,8,8]{3,2,1,0:T(8,128)}, u32[]{:S(2)}) copy-start(s32[1,1,8,8]{3,2,1,0:T(8,128)} %param.11) | copy-start | bytes 772
  25.8 22.8 %copy-start.1 = (f32[1,1,8,8]{3,2,1,0:T(8,128)S(1)}, f32[1,1,8,8]{3,2,1,0:T(8,128)}, u32[]{:S(2)}) copy-start(f32[1,1,8,8]{3,2,1,0:T(8,128)} %param.13) | copy-start | bytes 772
  25.8 6.6 %collective-permute-start.5 = (bf16[64,2048]{1,0:T(8,128)(2,1)S(1)}, bf16[64,2048]{1,0:T(8,128)(2,1)S(1)}, u32[]{:S(2)}, u32[]{:S(2)}) collective-permute-start(bf16[64,2048]{1,0:T(8,128)(2,1)S(1)} %get-tuple-element.28), channel_id=1, source_target_pairs={{0,4},{1,5},{2,6},{3,7},{4,0},{5,1},{6,2},{7,3},{8,12},{9,13},{10,... | collective-permute-start | bytes 786440 | tf_op jit(solution)/shard_map/ppermute | solution.py:36
  29.0 7.7 %collective-permute-start.12 = (bf16[64,2048]{1,0:T(8,128)(2,1)S(1)}, bf16[64,2048]{1,0:T(8,128)(2,1)S(1)}, u32[]{:S(2)}, u32[]{:S(2)}) collective-permute-start(bf16[64,2048]{1,0:T(8,128)(2,1)S(1)} %get-tuple-element.35), channel_id=1, source_target_pairs={{0,2},{1,3},{2,0},{3,1},{4,6},{5,7},{6,4},{7,5},{8,10},{9,11},{10,... | collective-permute-start | bytes 786440 | tf_op jit(solution)/shard_map/ppermute | solution.py:36
  32.4 5.7 %collective-permute-start.6 = (bf16[32,2048]{1,0:T(8,128)(2,1)S(1)}, bf16[32,2048]{1,0:T(8,128)(2,1)S(1)}, u32[]{:S(2)}, u32[]{:S(2)}) collective-permute-start(bf16[32,2048]{1,0:T(8,128)(2,1)S(1)} %get-tuple-element.30), channel_id=1, source_target_pairs={{0,2},{1,3},{2,0},{3,1},{4,6},{5,7},{6,4},{7,5},{8,10},{9,11},{10,... | collective-permute-start | bytes 393224 | tf_op jit(solution)/shard_map/ppermute | solution.py:36
  36.8 5.0 %collective-permute-start.13 = (bf16[32,2048]{1,0:T(8,128)(2,1)S(1)}, bf16[32,2048]{1,0:T(8,128)(2,1)S(1)}, u32[]{:S(2)}, u32[]{:S(2)}) collective-permute-start(bf16[32,2048]{1,0:T(8,128)(2,1)S(1)} %get-tuple-element.37), channel_id=1, source_target_pairs={{0,4},{1,5},{2,6},{3,7},{4,0},{5,1},{6,2},{7,3},{8,12},{9,13},{10,... | collective-permute-start | bytes 393224 | tf_op jit(solution)/shard_map/ppermute | solution.py:36
  38.2 6.8 %collective-permute-start.7 = (bf16[16,2048]{1,0:T(8,128)(2,1)S(1)}, bf16[16,2048]{1,0:T(8,128)(2,1)S(1)}, u32[]{:S(2)}, u32[]{:S(2)}) collective-permute-start(bf16[16,2048]{1,0:T(8,128)(2,1)S(1)} %get-tuple-element.31), channel_id=1, source_target_pairs={{0,24},{1,25},{2,26},{3,27},{4,28},{5,29},{6,30},{7,31},{8,16},{9,... | collective-permute-start | bytes 196616 | tf_op jit(solution)/shard_map/ppermute | solution.py:36
  41.9 5.2 %collective-permute-start.14 = (bf16[16,2048]{1,0:T(8,128)(2,1)S(1)}, bf16[16,2048]{1,0:T(8,128)(2,1)S(1)}, u32[]{:S(2)}, u32[]{:S(2)}) collective-permute-start(bf16[16,2048]{1,0:T(8,128)(2,1)S(1)} %get-tuple-element.38), channel_id=1, source_target_pairs={{0,16},{1,17},{2,18},{3,19},{4,20},{5,21},{6,22},{7,23},{8,24},{9,... | collective-permute-start | bytes 196616 | tf_op jit(solution)/shard_map/ppermute | solution.py:36
  44.3 4.3 %collective-permute-start.15 = (bf16[16,2048]{1,0:T(8,128)(2,1)S(1)}, bf16[16,2048]{1,0:T(8,128)(2,1)S(1)}, u32[]{:S(2)}, u32[]{:S(2)}) collective-permute-start(bf16[16,2048]{1,0:T(8,128)(2,1)S(1)} %get-tuple-element.39), channel_id=1, source_target_pairs={{0,8},{1,9},{2,10},{3,11},{4,12},{5,13},{6,14},{7,15},{8,0},{9,1},... | collective-permute-start | bytes 196616 | tf_op jit(solution)/shard_map/ppermute | solution.py:36

commit v7 on v5

--- a/solution.py
+++ b/solution.py
@@ -241,8 +241,7 @@
     outer = chips // inner
     inner_masks = [SPLIT * i for i in range(1, inner)]
     layer_mask = lambda j: SPLIT * inner * j
-    nearer = list(range(1, outer // 2 + 1))
-    streams = [[j for j in range(outer) if j not in nearer], nearer]
+    streams = [list(range(outer // 2)), list(range(outer // 2, outer))]
     own_in, own_out = w_in[0, 0], w_out[0, 0]
     other_out, other_in = exclusive(own_out, 1), exclusive(own_in, 1)
     weights = None
@@ -286,16 +285,16 @@
             space=pl.ANY,
         )
         column = {0: packed}
-        for j in streams[1][::-1] + streams[0][1:]:
+        for j in streams[0][1:] + streams[1][::-1]:
             column[j] = exclusive(packed, layer_mask(j))
         blocks = []
         for stream, layers in enumerate(streams):
             joined = join_rows([column[j] for j in layers])
+            if stream == 1:
+                joined = after(joined, blocks[0][1])
             block = [joined]
             for mask in inner_masks:
                 block.append(exclusive(joined, mask))
-                if stream == 0 and tick == 0:
-                    joined = after(joined, other_out if len(block) == 2 else other_in)
             blocks.append(block)
         if weights is None:
             weights = stage_weights(own_in, own_out, other_in, other_out)

time: 58.1 us -> 58 us (level)
  waiting for transfers between devices: 9.42 us -> 13.4 us
  starting transfers between devices: 28.3 us -> 26.2 us
  blocking collectives: 11.2 us -> 9.24 us
    ppermute x20, waiting for transfers between devices: 9.42 us -> 13.4 us  [exclusive(): return lax.ppermute(value, 'expert', pairs)]
    ppermute x20, starting transfers between devices: 28.3 us -> 26.2 us  [exclusive(): return lax.ppermute(value, 'expert', pairs)]
    all_to_all x1, blocking collectives: 11.2 us -> 9.24 us  [on_device(): lax.all_to_all(terms, 'expert', split_axis=0, concat_axis=0, tiled=True)]
  transfers between devices with their start and end apart: 20 -> 20, of which waited for: 4 -> 8; matrix products, arithmetic and copies ran while one was open for 0% -> 0% of each run, Pallas kernels for 12% -> 12%
where the time goes in v7:
time: 58 us; the launch traced here: 57.8 us
  starting transfers between devices  26.2 us (45%)
  waiting for transfers between devices  13.4 us (23%)
  blocking collectives  9.24 us (16%)
  Pallas kernels  8.25 us (14%)
  between operations  0.71 us (1%)
    ppermute x20, starting transfers between devices, exclusive(): return lax.ppermute(value, 'expert', pairs)  26.2 us
    ppermute x20, waiting for transfers between devices, exclusive(): return lax.ppermute(value, 'expert', pairs)  13.4 us
    all_to_all x1, blocking collectives, on_device(): lax.all_to_all(terms, 'expert', split_axis=0, concat_axis=0, tiled=True)  9.24 us
    pallas_call x10, Pallas kernels, run_kernel(): pl.pallas_call(body, out_shape=outs, in_specs=[pl.BlockSpec(memory_space=...  8.25 us
  transfers between devices with their start and end apart: 20, of which 8 were waited for; matrix products, arithmetic and copies ran while one was open for 0% of the time, Pallas kernels for 12%

profile of v7, /device:TPU:0, one launch (start us, length us, event | category | flops | bytes accessed | tf_op | source)
XLA Modules:
  0.0 57.8 jit_solution(15563521264382657970)
XLA Ops:
  0.6 0.5 collective-permute-start.4
  1.1 0.1 collective-permute-start.5
  1.2 1.1 %shard_map.112.refs_0_ = bf16[16,2176]{1,0:T(8,128)(2,1)S(1)} custom-call(bf16[8,2048]{1,0:T(8,128)(2,1)} %bitcast.24, bf16[8,2048]{1,0:T(8,128)(2,1)} %bitcast.25, s32[8,8]{1,0:T(8,128)} %bitcast.15, s32[8,8]{1,0:T(8,128)} %bitcast.26, f32[8,8]{1,0:T(8,128)} %bitcast.17, f32[8,8]{1,0:T(8,128)} %bitcast.27, s32[1,16]{1,0:T(1,128)} %refs_6_.1), custom_call_target="tpu_custom_call" | custom-call | tf_op jit(solution)/shard_map/pallas_call | solution.py:16
  2.3 3.1 %collective-permute-start = (bf16[16,2176]{1,0:T(8,128)(2,1)S(1)}, bf16[16,2176]{1,0:T(8,128)(2,1)S(1)}, u32[]{:S(2)}, u32[]{:S(2)}) collective-permute-start(bf16[16,2176]{1,0:T(8,128)(2,1)S(1)} %shard_map.112.refs_0_), channel_id=1, source_target_pairs={{0,8},{1,9},{2,10},{3,11},{4,12},{5,13},{6,14},{7,15},{8,0},{9,1},... | collective-permute-start | bytes 208904 | tf_op jit(solution)/shard_map/ppermute | solution.py:36
  5.4 2.6 %collective-permute-start.10 = (bf16[16,2176]{1,0:T(8,128)(2,1)S(1)}, bf16[16,2176]{1,0:T(8,128)(2,1)S(1)}, u32[]{:S(2)}, u32[]{:S(2)}) collective-permute-start(bf16[16,2176]{1,0:T(8,128)(2,1)S(1)} %shard_map.112.refs_0_), channel_id=1, source_target_pairs={{0,16},{1,17},{2,18},{3,19},{4,20},{5,21},{6,22},{7,23},{8,24},{9,... | collective-permute-start | bytes 208904 | tf_op jit(solution)/shard_map/ppermute | solution.py:36
  8.0 0.0 collective-permute-start.11
  8.0 0.0 collective-permute-done.refs_1_
  8.0 1.8 %collective-permute-start.1 = (bf16[32,2176]{1,0:T(8,128)(2,1)S(1)}, bf16[32,2176]{1,0:T(8,128)(2,1)S(1)}, u32[]{:S(2)}, u32[]{:S(2)}) collective-permute-start(bf16[32,2176]{1,0:T(8,128)(2,1)S(1)} %shard_map.113.refs_0_), channel_id=1, source_target_pairs={{0,2},{1,3},{2,0},{3,1},{4,6},{5,7},{6,4},{7,5},{8,10},{9,11},{10,... | collective-permute-start | bytes 417800 | tf_op jit(solution)/shard_map/ppermute | solution.py:36
  9.8 3.4 %collective-permute-done.10.refs_0_ = bf16[16,2176]{1,0:T(8,128)(2,1)S(1)} collective-permute-done((bf16[16,2176]{1,0:T(8,128)(2,1)S(1)}, bf16[16,2176]{1,0:T(8,128)(2,1)S(1)}, u32[]{:S(2)}, u32[]{:S(2)}) %collective-permute-start.10) | collective-permute-done | bytes 69664 | tf_op jit(solution)/shard_map/ppermute | solution.py:36
  13.2 1.5 %collective-permute-start.2 = (bf16[32,2176]{1,0:T(8,128)(2,1)S(1)}, bf16[32,2176]{1,0:T(8,128)(2,1)S(1)}, u32[]{:S(2)}, u32[]{:S(2)}) collective-permute-start(bf16[32,2176]{1,0:T(8,128)(2,1)S(1)} %shard_map.113.refs_0_), channel_id=1, source_target_pairs={{0,4},{1,5},{2,6},{3,7},{4,0},{5,1},{6,2},{7,3},{8,12},{9,13},{10,... | collective-permute-start | bytes 417800 | tf_op jit(solution)/shard_map/ppermute | solution.py:36
  14.7 0.0 collective-permute-done.11.refs_1_
  14.7 2.0 %collective-permute-start.3 = (bf16[32,2176]{1,0:T(8,128)(2,1)S(1)}, bf16[32,2176]{1,0:T(8,128)(2,1)S(1)}, u32[]{:S(2)}, u32[]{:S(2)}) collective-permute-start(bf16[32,2176]{1,0:T(8,128)(2,1)S(1)} %shard_map.113.refs_0_), channel_id=1, source_target_pairs={{0,6},{1,7},{2,4},{3,5},{4,2},{5,3},{6,0},{7,1},{8,14},{9,15},{10,... | collective-permute-start | bytes 417800 | tf_op jit(solution)/shard_map/ppermute | solution.py:36
  16.6 0.0 collective-permute-done.1.refs_1_
  16.7 0.6 %collective-permute-start.12 = (bf16[32,2176]{1,0:T(8,128)(2,1)S(1)}, bf16[32,2176]{1,0:T(8,128)(2,1)S(1)}, u32[]{:S(2)}, u32[]{:S(2)}) collective-permute-start(bf16[32,2176]{1,0:T(8,128)(2,1)S(1)} %shard_map.117.refs_0_), channel_id=1, source_target_pairs={{0,2},{1,3},{2,0},{3,1},{4,6},{5,7},{6,4},{7,5},{8,10},{9,11},{10,... | collective-permute-start | bytes 417800 | tf_op jit(solution)/shard_map/ppermute | solution.py:36
  17.3 0.0 collective-permute-done.5.refs_3_
  17.3 1.0 %collective-permute-start.13 = (bf16[32,2176]{1,0:T(8,128)(2,1)S(1)}, bf16[32,2176]{1,0:T(8,128)(2,1)S(1)}, u32[]{:S(2)}, u32[]{:S(2)}) collective-permute-start(bf16[32,2176]{1,0:T(8,128)(2,1)S(1)} %shard_map.117.refs_0_), channel_id=1, source_target_pairs={{0,4},{1,5},{2,6},{3,7},{4,0},{5,1},{6,2},{7,3},{8,12},{9,13},{10,... | collective-permute-start | bytes 417800 | tf_op jit(solution)/shard_map/ppermute | solution.py:36
  18.3 0.0 collective-permute-done.4.refs_1_
  18.3 2.0 %collective-permute-start.14 = (bf16[32,2176]{1,0:T(8,128)(2,1)S(1)}, bf16[32,2176]{1,0:T(8,128)(2,1)S(1)}, u32[]{:S(2)}, u32[]{:S(2)}) collective-permute-start(bf16[32,2176]{1,0:T(8,128)(2,1)S(1)} %shard_map.117.refs_0_), channel_id=1, source_target_pairs={{0,6},{1,7},{2,4},{3,5},{4,2},{5,3},{6,0},{7,1},{8,14},{9,15},{10,... | collective-permute-start | bytes 417800 | tf_op jit(solution)/shard_map/ppermute | solution.py:36
  20.2 2.4 %shard_map.114 = (bf16[2048,768]{1,0:T(8,128)(2,1)S(1)}, bf16[2048,768]{1,0:T(8,128)(2,1)S(1)}, bf16[384,2048]{1,0:T(8,128)(2,1)S(1)}, bf16[384,2048]{1,0:T(8,128)(2,1)S(1)}) custom-call(bf16[2048,768]{1,0:T(8,128)(2,1)} %bitcast.21, bf16[2048,768]{1,0:T(8,128)(2,1)S(1)} %collective-permute-done.4.refs_1_, bf16[384,2048]{1,0:T(8,128)(2,1)} %bitcast.23, ...), custom_call_target="tpu_custom_call" | custom-call | tf_op jit(solution)/shard_map/pallas_call | solution.py:16
  22.7 0.6 %collective-permute-done.2.refs_2_ = bf16[32,2176]{1,0:T(8,128)(2,1)S(1)} collective-permute-done((bf16[32,2176]{1,0:T(8,128)(2,1)S(1)}, bf16[32,2176]{1,0:T(8,128)(2,1)S(1)}, u32[]{:S(2)}, u32[]{:S(2)}) %collective-permute-start.2) | collective-permute-done | bytes 139296 | tf_op jit(solution)/shard_map/ppermute | solution.py:36
  23.3 0.0 collective-permute-done.3.refs_3_
  23.3 1.7 %shard_map.115 = (bf16[32,2048]{1,0:T(8,128)(2,1)S(1)}, bf16[32,2048]{1,0:T(8,128)(2,1)S(1)}, bf16[32,2048]{1,0:T(8,128)(2,1)S(1)}, bf16[32,2048]{1,0:T(8,128)(2,1)S(1)}) custom-call(bf16[32,2176]{1,0:T(8,128)(2,1)S(1)} %shard_map.113.refs_0_, bf16[32,2176]{1,0:T(8,128)(2,1)S(1)} %collective-permute-done.1.refs_1_, ...), custom_call_target="tpu_custom_call" | custom-call | tf_op jit(solution)/shard_map/pallas_call | solution.py:16
  25.0 1.6 %collective-permute-start.6 = (bf16[32,2048]{1,0:T(8,128)(2,1)S(1)}, bf16[32,2048]{1,0:T(8,128)(2,1)S(1)}, u32[]{:S(2)}, u32[]{:S(2)}) collective-permute-start(bf16[32,2048]{1,0:T(8,128)(2,1)S(1)} %get-tuple-element.28), channel_id=1, source_target_pairs={{0,2},{1,3},{2,0},{3,1},{4,6},{5,7},{6,4},{7,5},{8,10},{9,11},{10,... | collective-permute-start | bytes 393224 | tf_op jit(solution)/shard_map/ppermute | solution.py:36
  26.6 1.6 %collective-permute-start.7 = (bf16[32,2048]{1,0:T(8,128)(2,1)S(1)}, bf16[32,2048]{1,0:T(8,128)(2,1)S(1)}, u32[]{:S(2)}, u32[]{:S(2)}) collective-permute-start(bf16[32,2048]{1,0:T(8,128)(2,1)S(1)} %get-tuple-element.29), channel_id=1, source_target_pairs={{0,4},{1,5},{2,6},{3,7},{4,0},{5,1},{6,2},{7,3},{8,12},{9,13},{10,... | collective-permute-start | bytes 393224 | tf_op jit(solution)/shard_map/ppermute | solution.py:36
  28.2 0.0 collective-permute-done.12.refs_1_
  28.2 0.4 collective-permute-start.8
  28.6 0.5 collective-permute-done.13.refs_2_
  29.1 1.7 %shard_map.118 = (bf16[32,2048]{1,0:T(8,128)(2,1)S(1)}, bf16[32,2048]{1,0:T(8,128)(2,1)S(1)}, bf16[32,2048]{1,0:T(8,128)(2,1)S(1)}, bf16[32,2048]{1,0:T(8,128)(2,1)S(1)}) custom-call(bf16[32,2176]{1,0:T(8,128)(2,1)S(1)} %shard_map.117.refs_0_, bf16[32,2176]{1,0:T(8,128)(2,1)S(1)} %collective-permute-done.12.refs_1_, ...), custom_call_target="tpu_custom_call" | custom-call | tf_op jit(solution)/shard_map/pallas_call | solution.py:16
  30.7 1.1 %collective-permute-start.15 = (bf16[32,2048]{1,0:T(8,128)(2,1)S(1)}, bf16[32,2048]{1,0:T(8,128)(2,1)S(1)}, u32[]{:S(2)}, u32[]{:S(2)}) collective-permute-start(bf16[32,2048]{1,0:T(8,128)(2,1)S(1)} %get-tuple-element.35), channel_id=1, source_target_pairs={{0,2},{1,3},{2,0},{3,1},{4,6},{5,7},{6,4},{7,5},{8,10},{9,11},{10,... | collective-permute-start | bytes 393224 | tf_op jit(solution)/shard_map/ppermute | solution.py:36
  31.8 2.1 %collective-permute-start.16 = (bf16[32,2048]{1,0:T(8,128)(2,1)S(1)}, bf16[32,2048]{1,0:T(8,128)(2,1)S(1)}, u32[]{:S(2)}, u32[]{:S(2)}) collective-permute-start(bf16[32,2048]{1,0:T(8,128)(2,1)S(1)} %get-tuple-element.36), channel_id=1, source_target_pairs={{0,4},{1,5},{2,6},{3,7},{4,0},{5,1},{6,2},{7,3},{8,12},{9,13},{10,... | collective-permute-start | bytes 393224 | tf_op jit(solution)/shard_map/ppermute | solution.py:36
  33.9 0.0 collective-permute-done.6.refs_1_
  33.9 0.4 collective-permute-start.17
  34.3 0.5 collective-permute-done.7.refs_2_
  34.8 0.0 collective-permute-done.8.refs_3_
  34.8 0.1 shard_map.116
  34.9 1.6 %collective-permute-start.9 = (bf16[16,2048]{1,0:T(8,128)(2,1)S(1)}, bf16[16,2048]{1,0:T(8,128)(2,1)S(1)}, u32[]{:S(2)}, u32[]{:S(2)}) collective-permute-start(bf16[16,2048]{1,0:T(8,128)(2,1)S(1)} %get-tuple-element.31), channel_id=1, source_target_pairs={{0,8},{1,9},{2,10},{3,11},{4,12},{5,13},{6,14},{7,15},{8,0},{9,1},... | collective-permute-start | bytes 196616 | tf_op jit(solution)/shard_map/ppermute | solution.py:36
  36.5 0.0 collective-permute-done.15.refs_1_
  36.5 1.3 %collective-permute-done.16.refs_2_ = bf16[32,2048]{1,0:T(8,128)(2,1)S(1)} collective-permute-done((bf16[32,2048]{1,0:T(8,128)(2,1)S(1)}, bf16[32,2048]{1,0:T(8,128)(2,1)S(1)}, u32[]{:S(2)}, u32[]{:S(2)}) %collective-permute-start.16) | collective-permute-done | bytes 131104 | tf_op jit(solution)/shard_map/ppermute | solution.py:36
  37.8 1.9 %collective-permute-done.17.refs_3_ = bf16[32,2048]{1,0:T(8,128)(2,1)S(1)} collective-permute-done((bf16[32,2048]{1,0:T(8,128)(2,1)S(1)}, bf16[32,2048]{1,0:T(8,128)(2,1)S(1)}, u32[]{:S(2)}, u32[]{:S(2)}) %collective-permute-start.17) | collective-permute-done | bytes 131104 | tf_op jit(solution)/shard_map/ppermute | solution.py:36
  39.8 0.1 shard_map.119
  39.9 1.6 %collective-permute-start.18 = (bf16[16,2048]{1,0:T(8,128)(2,1)S(1)}, bf16[16,2048]{1,0:T(8,128)(2,1)S(1)}, u32[]{:S(2)}, u32[]{:S(2)}) collective-permute-start(bf16[16,2048]{1,0:T(8,128)(2,1)S(1)} %get-tuple-element.38), channel_id=1, source_target_pairs={{0,24},{1,25},{2,26},{3,27},{4,28},{5,29},{6,30},{7,31},{8,16},{9,... | collective-permute-start | bytes 196616 | tf_op jit(solution)/shard_map/ppermute | solution.py:36
  41.5 0.8 %collective-permute-start.19 = (bf16[16,2048]{1,0:T(8,128)(2,1)S(1)}, bf16[16,2048]{1,0:T(8,128)(2,1)S(1)}, u32[]{:S(2)}, u32[]{:S(2)}) collective-permute-start(bf16[16,2048]{1,0:T(8,128)(2,1)S(1)} %get-tuple-element.39), channel_id=1, source_target_pairs={{0,16},{1,17},{2,18},{3,19},{4,20},{5,21},{6,22},{7,23},{8,24},{9,... | collective-permute-start | bytes 196616 | tf_op jit(solution)/shard_map/ppermute | solution.py:36
  42.3 0.0 collective-permute-done.9.refs_0_
  42.3 3.7 %collective-permute-done.18.refs_2_ = bf16[16,2048]{1,0:T(8,128)(2,1)S(1)} collective-permute-done((bf16[16,2048]{1,0:T(8,128)(2,1)S(1)}, bf16[16,2048]{1,0:T(8,128)(2,1)S(1)}, u32[]{:S(2)}, u32[]{:S(2)}) %collective-permute-start.18) | collective-permute-done | bytes 65568 | tf_op jit(solution)/shard_map/ppermute | solution.py:36
  46.0 1.4 %collective-permute-done.19.refs_3_ = bf16[16,2048]{1,0:T(8,128)(2,1)S(1)} collective-permute-done((bf16[16,2048]{1,0:T(8,128)(2,1)S(1)}, bf16[16,2048]{1,0:T(8,128)(2,1)S(1)}, u32[]{:S(2)}, u32[]{:S(2)}) %collective-permute-start.19) | collective-permute-done | bytes 65568 | tf_op jit(solution)/shard_map/ppermute | solution.py:36
  47.4 0.7 %shard_map.120 = (bf16[8,2048]{1,0:T(8,128)(2,1)}, bf16[8,2048]{1,0:T(8,128)(2,1)}, f32[32,16]{1,0:T(8,128)S(1)}) custom-call(bf16[16,2048]{1,0:T(8,128)(2,1)S(1)} %collective-permute-done.9.refs_0_, f32[16,2048]{1,0:T(8,128)S(1)} %get-tuple-element.32.refs_1_, bf16[16,2048]{1,0:T(8,128)(2,1)S(1)} %collective-permute-done.18.refs_2_, ...), custom_call_target="tpu_custom_call" | custom-call | tf_op jit(solution)/shard_map/pallas_call | solution.py:16
  48.1 9.2 %all_to_all.11 = f32[32,1,16]{2,1,0:T(1,128)S(1)} all-to-all(f32[32,1,16]{2,1,0:T(1,128)S(1)} %bitcast.19), channel_id=1, replica_groups=mesh['section'=1,'expert'=32] {'expert'}, dimensions={0} | all-to-all | bytes 4096 | tf_op jit(solution)/shard_map/all_to_all | solution.py:334
  57.3 0.5 shard_map.121
  (7 shorter events, 0.0 us)
Async XLA Ops:
  0.6 17.6 %collective-permute-start.4 = (bf16[2048,768]{1,0:T(8,128)(2,1)}, bf16[2048,768]{1,0:T(8,128)(2,1)S(1)}, u32[]{:S(2)}, u32[]{:S(2)}) collective-permute-start(bf16[2048,768]{1,0:T(8,128)(2,1)} %bitcast.20), channel_id=1, source_target_pairs={{0,1},{1,0},{2,3},{3,2},{4,5},{5,4},{6,7},{7,6},{8,9},{9,8},{10,11... | collective-permute-start | bytes 9437192 | tf_op jit(solution)/shard_map/ppermute | solution.py:36
  1.1 16.1 %collective-permute-start.5 = (bf16[384,2048]{1,0:T(8,128)(2,1)}, bf16[384,2048]{1,0:T(8,128)(2,1)S(1)}, u32[]{:S(2)}, u32[]{:S(2)}) collective-permute-start(bf16[384,2048]{1,0:T(8,128)(2,1)} %bitcast.22), channel_id=1, source_target_pairs={{0,1},{1,0},{2,3},{3,2},{4,5},{5,4},{6,7},{7,6},{8,9},{9,8},{10,11... | collective-permute-start | bytes 4718600 | tf_op jit(solution)/shard_map/ppermute | solution.py:36
  2.3 5.7 %collective-permute-start = (bf16[16,2176]{1,0:T(8,128)(2,1)S(1)}, bf16[16,2176]{1,0:T(8,128)(2,1)S(1)}, u32[]{:S(2)}, u32[]{:S(2)}) collective-permute-start(bf16[16,2176]{1,0:T(8,128)(2,1)S(1)} %shard_map.112.refs_0_), channel_id=1, source_target_pairs={{0,8},{1,9},{2,10},{3,11},{4,12},{5,13},{6,14},{7,15},{8,0},{9,1},... | collective-permute-start | bytes 208904 | tf_op jit(solution)/shard_map/ppermute | solution.py:36
  5.4 7.8 %collective-permute-start.10 = (bf16[16,2176]{1,0:T(8,128)(2,1)S(1)}, bf16[16,2176]{1,0:T(8,128)(2,1)S(1)}, u32[]{:S(2)}, u32[]{:S(2)}) collective-permute-start(bf16[16,2176]{1,0:T(8,128)(2,1)S(1)} %shard_map.112.refs_0_), channel_id=1, source_target_pairs={{0,16},{1,17},{2,18},{3,19},{4,20},{5,21},{6,22},{7,23},{8,24},{9,... | collective-permute-start | bytes 208904 | tf_op jit(solution)/shard_map/ppermute | solution.py:36
  8.0 6.7 %collective-permute-start.11 = (bf16[16,2176]{1,0:T(8,128)(2,1)S(1)}, bf16[16,2176]{1,0:T(8,128)(2,1)S(1)}, u32[]{:S(2)}, u32[]{:S(2)}) collective-permute-start(bf16[16,2176]{1,0:T(8,128)(2,1)S(1)} %shard_map.112.refs_0_), channel_id=1, source_target_pairs={{0,24},{1,25},{2,26},{3,27},{4,28},{5,29},{6,30},{7,31},{8,16},{9,... | collective-permute-start | bytes 208904 | tf_op jit(solution)/shard_map/ppermute | solution.py:36
  8.0 8.7 %collective-permute-start.1 = (bf16[32,2176]{1,0:T(8,128)(2,1)S(1)}, bf16[32,2176]{1,0:T(8,128)(2,1)S(1)}, u32[]{:S(2)}, u32[]{:S(2)}) collective-permute-start(bf16[32,2176]{1,0:T(8,128)(2,1)S(1)} %shard_map.113.refs_0_), channel_id=1, source_target_pairs={{0,2},{1,3},{2,0},{3,1},{4,6},{5,7},{6,4},{7,5},{8,10},{9,11},{10,... | collective-permute-start | bytes 417800 | tf_op jit(solution)/shard_map/ppermute | solution.py:36
  13.2 10.1 %collective-permute-start.2 = (bf16[32,2176]{1,0:T(8,128)(2,1)S(1)}, bf16[32,2176]{1,0:T(8,128)(2,1)S(1)}, u32[]{:S(2)}, u32[]{:S(2)}) collective-permute-start(bf16[32,2176]{1,0:T(8,128)(2,1)S(1)} %shard_map.113.refs_0_), channel_id=1, source_target_pairs={{0,4},{1,5},{2,6},{3,7},{4,0},{5,1},{6,2},{7,3},{8,12},{9,13},{10,... | collective-permute-start | bytes 417800 | tf_op jit(solution)/shard_map/ppermute | solution.py:36
  14.7 8.6 %collective-permute-start.3 = (bf16[32,2176]{1,0:T(8,128)(2,1)S(1)}, bf16[32,2176]{1,0:T(8,128)(2,1)S(1)}, u32[]{:S(2)}, u32[]{:S(2)}) collective-permute-start(bf16[32,2176]{1,0:T(8,128)(2,1)S(1)} %shard_map.113.refs_0_), channel_id=1, source_target_pairs={{0,6},{1,7},{2,4},{3,5},{4,2},{5,3},{6,0},{7,1},{8,14},{9,15},{10,... | collective-permute-start | bytes 417800 | tf_op jit(solution)/shard_map/ppermute | solution.py:36
  16.7 11.6 %collective-permute-start.12 = (bf16[32,2176]{1,0:T(8,128)(2,1)S(1)}, bf16[32,2176]{1,0:T(8,128)(2,1)S(1)}, u32[]{:S(2)}, u32[]{:S(2)}) collective-permute-start(bf16[32,2176]{1,0:T(8,128)(2,1)S(1)} %shard_map.117.refs_0_), channel_id=1, source_target_pairs={{0,2},{1,3},{2,0},{3,1},{4,6},{5,7},{6,4},{7,5},{8,10},{9,11},{10,... | collective-permute-start | bytes 417800 | tf_op jit(solution)/shard_map/ppermute | solution.py:36
  17.3 11.8 %collective-permute-start.13 = (bf16[32,2176]{1,0:T(8,128)(2,1)S(1)}, bf16[32,2176]{1,0:T(8,128)(2,1)S(1)}, u32[]{:S(2)}, u32[]{:S(2)}) collective-permute-start(bf16[32,2176]{1,0:T(8,128)(2,1)S(1)} %shard_map.117.refs_0_), channel_id=1, source_target_pairs={{0,4},{1,5},{2,6},{3,7},{4,0},{5,1},{6,2},{7,3},{8,12},{9,13},{10,... | collective-permute-start | bytes 417800 | tf_op jit(solution)/shard_map/ppermute | solution.py:36
  18.3 10.8 %collective-permute-start.14 = (bf16[32,2176]{1,0:T(8,128)(2,1)S(1)}, bf16[32,2176]{1,0:T(8,128)(2,1)S(1)}, u32[]{:S(2)}, u32[]{:S(2)}) collective-permute-start(bf16[32,2176]{1,0:T(8,128)(2,1)S(1)} %shard_map.117.refs_0_), channel_id=1, source_target_pairs={{0,6},{1,7},{2,4},{3,5},{4,2},{5,3},{6,0},{7,1},{8,14},{9,15},{10,... | collective-permute-start | bytes 417800 | tf_op jit(solution)/shard_map/ppermute | solution.py:36
  25.0 8.9 %collective-permute-start.6 = (bf16[32,2048]{1,0:T(8,128)(2,1)S(1)}, bf16[32,2048]{1,0:T(8,128)(2,1)S(1)}, u32[]{:S(2)}, u32[]{:S(2)}) collective-permute-start(bf16[32,2048]{1,0:T(8,128)(2,1)S(1)} %get-tuple-element.28), channel_id=1, source_target_pairs={{0,2},{1,3},{2,0},{3,1},{4,6},{5,7},{6,4},{7,5},{8,10},{9,11},{10,... | collective-permute-start | bytes 393224 | tf_op jit(solution)/shard_map/ppermute | solution.py:36
  26.6 8.3 %collective-permute-start.7 = (bf16[32,2048]{1,0:T(8,128)(2,1)S(1)}, bf16[32,2048]{1,0:T(8,128)(2,1)S(1)}, u32[]{:S(2)}, u32[]{:S(2)}) collective-permute-start(bf16[32,2048]{1,0:T(8,128)(2,1)S(1)} %get-tuple-element.29), channel_id=1, source_target_pairs={{0,4},{1,5},{2,6},{3,7},{4,0},{5,1},{6,2},{7,3},{8,12},{9,13},{10,... | collective-permute-start | bytes 393224 | tf_op jit(solution)/shard_map/ppermute | solution.py:36
  28.2 19.2 %copy-start = (s32[1,1,8,8]{3,2,1,0:T(8,128)S(1)}, s32[1,1,8,8]{3,2,1,0:T(8,128)}, u32[]{:S(2)}) copy-start(s32[1,1,8,8]{3,2,1,0:T(8,128)} %param.11) | copy-start | bytes 772
  28.2 19.2 %copy-start.1 = (f32[1,1,8,8]{3,2,1,0:T(8,128)S(1)}, f32[1,1,8,8]{3,2,1,0:T(8,128)}, u32[]{:S(2)}) copy-start(f32[1,1,8,8]{3,2,1,0:T(8,128)} %param.13) | copy-start | bytes 772
  28.2 6.6 %collective-permute-start.8 = (bf16[32,2048]{1,0:T(8,128)(2,1)S(1)}, bf16[32,2048]{1,0:T(8,128)(2,1)S(1)}, u32[]{:S(2)}, u32[]{:S(2)}) collective-permute-start(bf16[32,2048]{1,0:T(8,128)(2,1)S(1)} %get-tuple-element.30), channel_id=1, source_target_pairs={{0,6},{1,7},{2,4},{3,5},{4,2},{5,3},{6,0},{7,1},{8,14},{9,15},{10,... | collective-permute-start | bytes 393224 | tf_op jit(solution)/shard_map/ppermute | solution.py:36
  30.7 5.8 %collective-permute-start.15 = (bf16[32,2048]{1,0:T(8,128)(2,1)S(1)}, bf16[32,2048]{1,0:T(8,128)(2,1)S(1)}, u32[]{:S(2)}, u32[]{:S(2)}) collective-permute-start(bf16[32,2048]{1,0:T(8,128)(2,1)S(1)} %get-tuple-element.35), channel_id=1, source_target_pairs={{0,2},{1,3},{2,0},{3,1},{4,6},{5,7},{6,4},{7,5},{8,10},{9,11},{10,... | collective-permute-start | bytes 393224 | tf_op jit(solution)/shard_map/ppermute | solution.py:36
  31.8 6.0 %collective-permute-start.16 = (bf16[32,2048]{1,0:T(8,128)(2,1)S(1)}, bf16[32,2048]{1,0:T(8,128)(2,1)S(1)}, u32[]{:S(2)}, u32[]{:S(2)}) collective-permute-start(bf16[32,2048]{1,0:T(8,128)(2,1)S(1)} %get-tuple-element.36), channel_id=1, source_target_pairs={{0,4},{1,5},{2,6},{3,7},{4,0},{5,1},{6,2},{7,3},{8,12},{9,13},{10,... | collective-permute-start | bytes 393224 | tf_op jit(solution)/shard_map/ppermute | solution.py:36
  33.9 5.9 %collective-permute-start.17 = (bf16[32,2048]{1,0:T(8,128)(2,1)S(1)}, bf16[32,2048]{1,0:T(8,128)(2,1)S(1)}, u32[]{:S(2)}, u32[]{:S(2)}) collective-permute-start(bf16[32,2048]{1,0:T(8,128)(2,1)S(1)} %get-tuple-element.37), channel_id=1, source_target_pairs={{0,6},{1,7},{2,4},{3,5},{4,2},{5,3},{6,0},{7,1},{8,14},{9,15},{10,... | collective-permute-start | bytes 393224 | tf_op jit(solution)/shard_map/ppermute | solution.py:36
  34.9 7.4 %collective-permute-start.9 = (bf16[16,2048]{1,0:T(8,128)(2,1)S(1)}, bf16[16,2048]{1,0:T(8,128)(2,1)S(1)}, u32[]{:S(2)}, u32[]{:S(2)}) collective-permute-start(bf16[16,2048]{1,0:T(8,128)(2,1)S(1)} %get-tuple-element.31), channel_id=1, source_target_pairs={{0,8},{1,9},{2,10},{3,11},{4,12},{5,13},{6,14},{7,15},{8,0},{9,1},... | collective-permute-start | bytes 196616 | tf_op jit(solution)/shard_map/ppermute | solution.py:36
  39.9 6.1 %collective-permute-start.18 = (bf16[16,2048]{1,0:T(8,128)(2,1)S(1)}, bf16[16,2048]{1,0:T(8,128)(2,1)S(1)}, u32[]{:S(2)}, u32[]{:S(2)}) collective-permute-start(bf16[16,2048]{1,0:T(8,128)(2,1)S(1)} %get-tuple-element.38), channel_id=1, source_target_pairs={{0,24},{1,25},{2,26},{3,27},{4,28},{5,29},{6,30},{7,31},{8,16},{9,... | collective-permute-start | bytes 196616 | tf_op jit(solution)/shard_map/ppermute | solution.py:36
  41.5 5.9 %collective-permute-start.19 = (bf16[16,2048]{1,0:T(8,128)(2,1)S(1)}, bf16[16,2048]{1,0:T(8,128)(2,1)S(1)}, u32[]{:S(2)}, u32[]{:S(2)}) collective-permute-start(bf16[16,2048]{1,0:T(8,128)(2,1)S(1)} %get-tuple-element.39), channel_id=1, source_target_pairs={{0,16},{1,17},{2,18},{3,19},{4,20},{5,21},{6,22},{7,23},{8,24},{9,... | collective-permute-start | bytes 196616 | tf_op jit(solution)/shard_map/ppermute | solution.py:36

commit v8 on v7

--- a/solution.py
+++ b/solution.py
@@ -103,13 +103,12 @@
         copy.wait()
 
 
-def stage_weights(own_in, own_out, other_in, other_out):
-    weights = [in_hbm(own_in), other_in, in_hbm(own_out), other_out]
+def stage(arrays):
     return run_kernel(
-        functools.partial(stage_kernel, len(weights)),
-        [pltpu.VMEM(value.shape, value.dtype) for value in weights],
-        weights,
-        [pltpu.SemaphoreType.DMA((len(weights),))],
+        functools.partial(stage_kernel, len(arrays)),
+        [pltpu.VMEM(value.shape, value.dtype) for value in arrays],
+        arrays,
+        [pltpu.SemaphoreType.DMA((len(arrays),))],
         space=pl.ANY,
     )
 
@@ -241,10 +240,9 @@
     outer = chips // inner
     inner_masks = [SPLIT * i for i in range(1, inner)]
     layer_mask = lambda j: SPLIT * inner * j
-    streams = [list(range(outer // 2)), list(range(outer // 2, outer))]
+    streams = [list(range(0, outer, 2)), list(range(1, outer, 2))]
     own_in, own_out = w_in[0, 0], w_out[0, 0]
     other_out, other_in = exclusive(own_out, 1), exclusive(own_in, 1)
-    weights = None
 
     step_count = micro_count + section_count - 1
     carry = jnp.zeros((2, tok_rows, model_width), jnp.bfloat16)
@@ -287,17 +285,22 @@
         column = {0: packed}
         for j in streams[0][1:] + streams[1][::-1]:
             column[j] = exclusive(packed, layer_mask(j))
+        if tick == 0:
+            own = stage([in_hbm(own_in), in_hbm(own_out)])
         blocks = []
         for stream, layers in enumerate(streams):
             joined = join_rows([column[j] for j in layers])
-            if stream == 1:
+            if stream == 0:
+                joined = after(joined, own)
+            else:
                 joined = after(joined, blocks[0][1])
             block = [joined]
             for mask in inner_masks:
                 block.append(exclusive(joined, mask))
             blocks.append(block)
-        if weights is None:
-            weights = stage_weights(own_in, own_out, other_in, other_out)
+        if tick == 0:
+            other = stage([other_in, other_out])
+            weights = [own[0], other[0], own[1], other[1]]
         summed = []
         for stream, layers in enumerate(streams):
             partial = run_expert(

time: 58 us -> 61.3 us (1.057)
  starting transfers between devices: 26.2 us -> 31 us
  waiting for transfers between devices: 13.4 us -> 10.9 us
  blocking collectives: 9.24 us -> 10 us
    ppermute x20, starting transfers between devices: 26.2 us -> 31 us  [exclusive(): return lax.ppermute(value, 'expert', pairs)]
    ppermute x20, waiting for transfers between devices: 13.4 us -> 10.9 us  [exclusive(): return lax.ppermute(value, 'expert', pairs)]
    all_to_all x1, blocking collectives: 9.24 us -> 10 us  [on_device(): lax.all_to_all(terms, 'expert', split_axis=0, concat_axis=0, tiled=True)]
    pallas_call x10 -> x11, Pallas kernels: 8.25 us -> 8.5 us  [run_kernel(): pl.pallas_call(body, out_shape=outs, in_specs=[pl.BlockSpec(memory_space=...]
  transfers between devices with their start and end apart: 20 -> 20, of which waited for: 8 -> 7; matrix products, arithmetic and copies ran while one was open for 0% -> 0% of each run, Pallas kernels for 12% -> 12%
where the time goes in v8:
time: 61.3 us; the launch traced here: 61.1 us
  starting transfers between devices  31 us (51%)
  waiting for transfers between devices  10.9 us (18%)
  blocking collectives  10 us (16%)
  Pallas kernels  8.5 us (14%)
  between operations  0.72 us (1%)
    ppermute x20, starting transfers between devices, exclusive(): return lax.ppermute(value, 'expert', pairs)  31 us
    ppermute x20, waiting for transfers between devices, exclusive(): return lax.ppermute(value, 'expert', pairs)  10.9 us
    all_to_all x1, blocking collectives, on_device(): lax.all_to_all(terms, 'expert', split_axis=0, concat_axis=0, tiled=True)  10 us
    pallas_call x11, Pallas kernels, run_kernel(): pl.pallas_call(body, out_shape=outs, in_specs=[pl.BlockSpec(memory_space=...  8.5 us
  transfers between devices with their start and end apart: 20, of which 7 were waited for; matrix products, arithmetic and copies ran while one was open for 0% of the time, Pallas kernels for 12%

profile of v8, /device:TPU:0, one launch (start us, length us, event | category | flops | bytes accessed | tf_op | source)
XLA Modules:
  0.0 61.1 jit_solution(10496896624787167068)
XLA Ops:
  0.6 0.5 collective-permute-start.4
  1.1 0.1 collective-permute-start.5
  1.2 1.1 %shard_map.112.refs_0_ = bf16[16,2176]{1,0:T(8,128)(2,1)S(1)} custom-call(bf16[8,2048]{1,0:T(8,128)(2,1)} %bitcast.24, bf16[8,2048]{1,0:T(8,128)(2,1)} %bitcast.25, s32[8,8]{1,0:T(8,128)} %bitcast.15, s32[8,8]{1,0:T(8,128)} %bitcast.26, f32[8,8]{1,0:T(8,128)} %bitcast.17, f32[8,8]{1,0:T(8,128)} %bitcast.27, s32[1,16]{1,0:T(1,128)} %refs_6_.1), custom_call_target="tpu_custom_call" | custom-call | tf_op jit(solution)/shard_map/pallas_call | solution.py:16
  2.3 4.1 %collective-permute-start = (bf16[16,2176]{1,0:T(8,128)(2,1)S(1)}, bf16[16,2176]{1,0:T(8,128)(2,1)S(1)}, u32[]{:S(2)}, u32[]{:S(2)}) collective-permute-start(bf16[16,2176]{1,0:T(8,128)(2,1)S(1)} %shard_map.112.refs_0_), channel_id=1, source_target_pairs={{0,16},{1,17},{2,18},{3,19},{4,20},{5,21},{6,22},{7,23},{8,24},{9,... | collective-permute-start | bytes 208904 | tf_op jit(solution)/shard_map/ppermute | solution.py:36
  6.4 1.3 %collective-permute-start.11 = (bf16[16,2176]{1,0:T(8,128)(2,1)S(1)}, bf16[16,2176]{1,0:T(8,128)(2,1)S(1)}, u32[]{:S(2)}, u32[]{:S(2)}) collective-permute-start(bf16[16,2176]{1,0:T(8,128)(2,1)S(1)} %shard_map.112.refs_0_), channel_id=1, source_target_pairs={{0,24},{1,25},{2,26},{3,27},{4,28},{5,29},{6,30},{7,31},{8,16},{9,... | collective-permute-start | bytes 208904 | tf_op jit(solution)/shard_map/ppermute | solution.py:36
  7.7 0.2 collective-permute-start.10
  8.0 2.4 %shard_map.114 = (bf16[2048,768]{1,0:T(8,128)(2,1)S(1)}, bf16[384,2048]{1,0:T(8,128)(2,1)S(1)}) custom-call(bf16[2048,768]{1,0:T(8,128)(2,1)} %bitcast.21, bf16[384,2048]{1,0:T(8,128)(2,1)} %bitcast.23), custom_call_target="tpu_custom_call" | custom-call | tf_op jit(solution)/shard_map/pallas_call | solution.py:16
  10.4 0.2 collective-permute-done.refs_1_
  10.6 2.8 %collective-permute-start.1 = (bf16[32,2176]{1,0:T(8,128)(2,1)S(1)}, bf16[32,2176]{1,0:T(8,128)(2,1)S(1)}, u32[]{:S(2)}, u32[]{:S(2)}) collective-permute-start(bf16[32,2176]{1,0:T(8,128)(2,1)S(1)} %shard_map.113.refs_0_), channel_id=1, source_target_pairs={{0,2},{1,3},{2,0},{3,1},{4,6},{5,7},{6,4},{7,5},{8,10},{9,11},{10,... | collective-permute-start | bytes 417800 | tf_op jit(solution)/shard_map/ppermute | solution.py:36
  13.3 0.0 collective-permute-done.11.refs_1_
  13.3 2.0 %collective-permute-start.3 = (bf16[32,2176]{1,0:T(8,128)(2,1)S(1)}, bf16[32,2176]{1,0:T(8,128)(2,1)S(1)}, u32[]{:S(2)}, u32[]{:S(2)}) collective-permute-start(bf16[32,2176]{1,0:T(8,128)(2,1)S(1)} %shard_map.113.refs_0_), channel_id=1, source_target_pairs={{0,6},{1,7},{2,4},{3,5},{4,2},{5,3},{6,0},{7,1},{8,14},{9,15},{10,... | collective-permute-start | bytes 417800 | tf_op jit(solution)/shard_map/ppermute | solution.py:36
  15.3 0.0 collective-permute-done.10.refs_0_
  15.3 0.5 collective-permute-start.2
  15.9 2.0 %collective-permute-done.1.refs_1_ = bf16[32,2176]{1,0:T(8,128)(2,1)S(1)} collective-permute-done((bf16[32,2176]{1,0:T(8,128)(2,1)S(1)}, bf16[32,2176]{1,0:T(8,128)(2,1)S(1)}, u32[]{:S(2)}, u32[]{:S(2)}) %collective-permute-start.1) | collective-permute-done | bytes 139296 | tf_op jit(solution)/shard_map/ppermute | solution.py:36
  17.8 2.3 %collective-permute-start.14 = (bf16[32,2176]{1,0:T(8,128)(2,1)S(1)}, bf16[32,2176]{1,0:T(8,128)(2,1)S(1)}, u32[]{:S(2)}, u32[]{:S(2)}) collective-permute-start(bf16[32,2176]{1,0:T(8,128)(2,1)S(1)} %shard_map.118.refs_0_), channel_id=1, source_target_pairs={{0,6},{1,7},{2,4},{3,5},{4,2},{5,3},{6,0},{7,1},{8,14},{9,15},{10,... | collective-permute-start | bytes 417800 | tf_op jit(solution)/shard_map/ppermute | solution.py:36
  20.1 0.0 collective-permute-done.5.refs_1_
  20.1 1.0 %collective-permute-start.13 = (bf16[32,2176]{1,0:T(8,128)(2,1)S(1)}, bf16[32,2176]{1,0:T(8,128)(2,1)S(1)}, u32[]{:S(2)}, u32[]{:S(2)}) collective-permute-start(bf16[32,2176]{1,0:T(8,128)(2,1)S(1)} %shard_map.118.refs_0_), channel_id=1, source_target_pairs={{0,4},{1,5},{2,6},{3,7},{4,0},{5,1},{6,2},{7,3},{8,12},{9,13},{10,... | collective-permute-start | bytes 417800 | tf_op jit(solution)/shard_map/ppermute | solution.py:36
  21.2 0.0 collective-permute-done.4.refs_0_
  21.2 0.1 collective-permute-start.12
  21.3 0.3 shard_map.115
  21.7 0.0 collective-permute-done.3.refs_3_
  21.7 3.8 %collective-permute-done.2.refs_2_ = bf16[32,2176]{1,0:T(8,128)(2,1)S(1)} collective-permute-done((bf16[32,2176]{1,0:T(8,128)(2,1)S(1)}, bf16[32,2176]{1,0:T(8,128)(2,1)S(1)}, u32[]{:S(2)}, u32[]{:S(2)}) %collective-permute-start.2) | collective-permute-done | bytes 139296 | tf_op jit(solution)/shard_map/ppermute | solution.py:36
  25.5 1.7 %shard_map.116 = (bf16[32,2048]{1,0:T(8,128)(2,1)S(1)}, bf16[32,2048]{1,0:T(8,128)(2,1)S(1)}, bf16[32,2048]{1,0:T(8,128)(2,1)S(1)}, bf16[32,2048]{1,0:T(8,128)(2,1)S(1)}) custom-call(bf16[32,2176]{1,0:T(8,128)(2,1)S(1)} %shard_map.113.refs_0_, bf16[32,2176]{1,0:T(8,128)(2,1)S(1)} %collective-permute-done.1.refs_1_, ...), custom_call_target="tpu_custom_call" | custom-call | tf_op jit(solution)/shard_map/pallas_call | solution.py:16
  27.1 1.5 %collective-permute-start.6 = (bf16[32,2048]{1,0:T(8,128)(2,1)S(1)}, bf16[32,2048]{1,0:T(8,128)(2,1)S(1)}, u32[]{:S(2)}, u32[]{:S(2)}) collective-permute-start(bf16[32,2048]{1,0:T(8,128)(2,1)S(1)} %get-tuple-element.30), channel_id=1, source_target_pairs={{0,2},{1,3},{2,0},{3,1},{4,6},{5,7},{6,4},{7,5},{8,10},{9,11},{10,... | collective-permute-start | bytes 393224 | tf_op jit(solution)/shard_map/ppermute | solution.py:36
  28.6 1.0 %collective-permute-start.7 = (bf16[32,2048]{1,0:T(8,128)(2,1)S(1)}, bf16[32,2048]{1,0:T(8,128)(2,1)S(1)}, u32[]{:S(2)}, u32[]{:S(2)}) collective-permute-start(bf16[32,2048]{1,0:T(8,128)(2,1)S(1)} %get-tuple-element.31), channel_id=1, source_target_pairs={{0,4},{1,5},{2,6},{3,7},{4,0},{5,1},{6,2},{7,3},{8,12},{9,13},{10,... | collective-permute-start | bytes 393224 | tf_op jit(solution)/shard_map/ppermute | solution.py:36
  29.7 0.0 collective-permute-done.14.refs_3_
  29.7 1.1 %collective-permute-start.8 = (bf16[32,2048]{1,0:T(8,128)(2,1)S(1)}, bf16[32,2048]{1,0:T(8,128)(2,1)S(1)}, u32[]{:S(2)}, u32[]{:S(2)}) collective-permute-start(bf16[32,2048]{1,0:T(8,128)(2,1)S(1)} %get-tuple-element.32), channel_id=1, source_target_pairs={{0,6},{1,7},{2,4},{3,5},{4,2},{5,3},{6,0},{7,1},{8,14},{9,15},{10,... | collective-permute-start | bytes 393224 | tf_op jit(solution)/shard_map/ppermute | solution.py:36
  30.7 0.0 collective-permute-done.13.refs_2_
  30.7 1.7 %shard_map.119 = (bf16[32,2048]{1,0:T(8,128)(2,1)S(1)}, bf16[32,2048]{1,0:T(8,128)(2,1)S(1)}, bf16[32,2048]{1,0:T(8,128)(2,1)S(1)}, bf16[32,2048]{1,0:T(8,128)(2,1)S(1)}) custom-call(bf16[32,2176]{1,0:T(8,128)(2,1)S(1)} %shard_map.118.refs_0_, bf16[32,2176]{1,0:T(8,128)(2,1)S(1)} %collective-permute-done.12.refs_1_, ...), custom_call_target="tpu_custom_call" | custom-call | tf_op jit(solution)/shard_map/pallas_call | solution.py:16
  32.4 1.5 %collective-permute-start.15 = (bf16[32,2048]{1,0:T(8,128)(2,1)S(1)}, bf16[32,2048]{1,0:T(8,128)(2,1)S(1)}, u32[]{:S(2)}, u32[]{:S(2)}) collective-permute-start(bf16[32,2048]{1,0:T(8,128)(2,1)S(1)} %get-tuple-element.37), channel_id=1, source_target_pairs={{0,2},{1,3},{2,0},{3,1},{4,6},{5,7},{6,4},{7,5},{8,10},{9,11},{10,... | collective-permute-start | bytes 393224 | tf_op jit(solution)/shard_map/ppermute | solution.py:36
  33.9 1.0 %collective-permute-start.16 = (bf16[32,2048]{1,0:T(8,128)(2,1)S(1)}, bf16[32,2048]{1,0:T(8,128)(2,1)S(1)}, u32[]{:S(2)}, u32[]{:S(2)}) collective-permute-start(bf16[32,2048]{1,0:T(8,128)(2,1)S(1)} %get-tuple-element.38), channel_id=1, source_target_pairs={{0,4},{1,5},{2,6},{3,7},{4,0},{5,1},{6,2},{7,3},{8,12},{9,13},{10,... | collective-permute-start | bytes 393224 | tf_op jit(solution)/shard_map/ppermute | solution.py:36
  34.9 1.1 %collective-permute-start.17 = (bf16[32,2048]{1,0:T(8,128)(2,1)S(1)}, bf16[32,2048]{1,0:T(8,128)(2,1)S(1)}, u32[]{:S(2)}, u32[]{:S(2)}) collective-permute-start(bf16[32,2048]{1,0:T(8,128)(2,1)S(1)} %get-tuple-element.39), channel_id=1, source_target_pairs={{0,6},{1,7},{2,4},{3,5},{4,2},{5,3},{6,0},{7,1},{8,14},{9,15},{10,... | collective-permute-start | bytes 393224 | tf_op jit(solution)/shard_map/ppermute | solution.py:36
  36.0 0.8 %collective-permute-done.7.refs_2_ = bf16[32,2048]{1,0:T(8,128)(2,1)S(1)} collective-permute-done((bf16[32,2048]{1,0:T(8,128)(2,1)S(1)}, bf16[32,2048]{1,0:T(8,128)(2,1)S(1)}, u32[]{:S(2)}, u32[]{:S(2)}) %collective-permute-start.7) | collective-permute-done | bytes 131104 | tf_op jit(solution)/shard_map/ppermute | solution.py:36
  36.8 0.0 collective-permute-done.8.refs_3_
  36.8 0.1 shard_map.117
  36.9 3.8 %collective-permute-start.9 = (bf16[16,2048]{1,0:T(8,128)(2,1)S(1)}, bf16[16,2048]{1,0:T(8,128)(2,1)S(1)}, u32[]{:S(2)}, u32[]{:S(2)}) collective-permute-start(bf16[16,2048]{1,0:T(8,128)(2,1)S(1)} %get-tuple-element.33), channel_id=1, source_target_pairs={{0,16},{1,17},{2,18},{3,19},{4,20},{5,21},{6,22},{7,23},{8,24},{9,... | collective-permute-start | bytes 196616 | tf_op jit(solution)/shard_map/ppermute | solution.py:36
  40.7 0.0 collective-permute-done.15.refs_1_
  40.7 0.0 collective-permute-done.16.refs_2_
  40.7 0.1 collective-permute-done.17.refs_3_
  40.8 0.1 shard_map.120
  40.8 4.8 %collective-permute-start.18 = (bf16[16,2048]{1,0:T(8,128)(2,1)S(1)}, bf16[16,2048]{1,0:T(8,128)(2,1)S(1)}, u32[]{:S(2)}, u32[]{:S(2)}) collective-permute-start(bf16[16,2048]{1,0:T(8,128)(2,1)S(1)} %get-tuple-element.40), channel_id=1, source_target_pairs={{0,24},{1,25},{2,26},{3,27},{4,28},{5,29},{6,30},{7,31},{8,16},{9,... | collective-permute-start | bytes 196616 | tf_op jit(solution)/shard_map/ppermute | solution.py:36
  45.6 0.3 collective-permute-start.19
  45.9 0.0 collective-permute-done.9.refs_0_
  45.9 2.0 %collective-permute-done.18.refs_2_ = bf16[16,2048]{1,0:T(8,128)(2,1)S(1)} collective-permute-done((bf16[16,2048]{1,0:T(8,128)(2,1)S(1)}, bf16[16,2048]{1,0:T(8,128)(2,1)S(1)}, u32[]{:S(2)}, u32[]{:S(2)}) %collective-permute-start.18) | collective-permute-done | bytes 65568 | tf_op jit(solution)/shard_map/ppermute | solution.py:36
  48.0 1.9 %collective-permute-done.19.refs_3_ = bf16[16,2048]{1,0:T(8,128)(2,1)S(1)} collective-permute-done((bf16[16,2048]{1,0:T(8,128)(2,1)S(1)}, bf16[16,2048]{1,0:T(8,128)(2,1)S(1)}, u32[]{:S(2)}, u32[]{:S(2)}) %collective-permute-start.19) | collective-permute-done | bytes 65568 | tf_op jit(solution)/shard_map/ppermute | solution.py:36
  49.9 0.7 %shard_map.121 = (bf16[8,2048]{1,0:T(8,128)(2,1)}, bf16[8,2048]{1,0:T(8,128)(2,1)}, f32[32,16]{1,0:T(8,128)S(1)}) custom-call(bf16[16,2048]{1,0:T(8,128)(2,1)S(1)} %collective-permute-done.9.refs_0_, f32[16,2048]{1,0:T(8,128)S(1)} %get-tuple-element.34.refs_1_, bf16[16,2048]{1,0:T(8,128)(2,1)S(1)} %collective-permute-done.18.refs_2_, ...), custom_call_target="tpu_custom_call" | custom-call | tf_op jit(solution)/shard_map/pallas_call | solution.py:16
  50.5 10.0 %all_to_all.11 = f32[32,1,16]{2,1,0:T(1,128)S(1)} all-to-all(f32[32,1,16]{2,1,0:T(1,128)S(1)} %bitcast.19), channel_id=1, replica_groups=mesh['section'=1,'expert'=32] {'expert'}, dimensions={0} | all-to-all | bytes 4096 | tf_op jit(solution)/shard_map/all_to_all | solution.py:337
  60.5 0.5 shard_map.122
  (8 shorter events, 0.0 us)
Async XLA Ops:
  0.6 20.5 %collective-permute-start.4 = (bf16[2048,768]{1,0:T(8,128)(2,1)}, bf16[2048,768]{1,0:T(8,128)(2,1)S(1)}, u32[]{:S(2)}, u32[]{:S(2)}) collective-permute-start(bf16[2048,768]{1,0:T(8,128)(2,1)} %bitcast.20), channel_id=1, source_target_pairs={{0,1},{1,0},{2,3},{3,2},{4,5},{5,4},{6,7},{7,6},{8,9},{9,8},{10,11... | collective-permute-start | bytes 9437192 | tf_op jit(solution)/shard_map/ppermute | solution.py:36
  1.1 19.0 %collective-permute-start.5 = (bf16[384,2048]{1,0:T(8,128)(2,1)}, bf16[384,2048]{1,0:T(8,128)(2,1)S(1)}, u32[]{:S(2)}, u32[]{:S(2)}) collective-permute-start(bf16[384,2048]{1,0:T(8,128)(2,1)} %bitcast.22), channel_id=1, source_target_pairs={{0,1},{1,0},{2,3},{3,2},{4,5},{5,4},{6,7},{7,6},{8,9},{9,8},{10,11... | collective-permute-start | bytes 4718600 | tf_op jit(solution)/shard_map/ppermute | solution.py:36
  2.3 8.2 %collective-permute-start = (bf16[16,2176]{1,0:T(8,128)(2,1)S(1)}, bf16[16,2176]{1,0:T(8,128)(2,1)S(1)}, u32[]{:S(2)}, u32[]{:S(2)}) collective-permute-start(bf16[16,2176]{1,0:T(8,128)(2,1)S(1)} %shard_map.112.refs_0_), channel_id=1, source_target_pairs={{0,16},{1,17},{2,18},{3,19},{4,20},{5,21},{6,22},{7,23},{8,24},{9,... | collective-permute-start | bytes 208904 | tf_op jit(solution)/shard_map/ppermute | solution.py:36
  6.4 6.9 %collective-permute-start.11 = (bf16[16,2176]{1,0:T(8,128)(2,1)S(1)}, bf16[16,2176]{1,0:T(8,128)(2,1)S(1)}, u32[]{:S(2)}, u32[]{:S(2)}) collective-permute-start(bf16[16,2176]{1,0:T(8,128)(2,1)S(1)} %shard_map.112.refs_0_), channel_id=1, source_target_pairs={{0,24},{1,25},{2,26},{3,27},{4,28},{5,29},{6,30},{7,31},{8,16},{9,... | collective-permute-start | bytes 208904 | tf_op jit(solution)/shard_map/ppermute | solution.py:36
  7.7 7.6 %collective-permute-start.10 = (bf16[16,2176]{1,0:T(8,128)(2,1)S(1)}, bf16[16,2176]{1,0:T(8,128)(2,1)S(1)}, u32[]{:S(2)}, u32[]{:S(2)}) collective-permute-start(bf16[16,2176]{1,0:T(8,128)(2,1)S(1)} %shard_map.112.refs_0_), channel_id=1, source_target_pairs={{0,8},{1,9},{2,10},{3,11},{4,12},{5,13},{6,14},{7,15},{8,0},{9,1},... | collective-permute-start | bytes 208904 | tf_op jit(solution)/shard_map/ppermute | solution.py:36
  10.6 7.3 %collective-permute-start.1 = (bf16[32,2176]{1,0:T(8,128)(2,1)S(1)}, bf16[32,2176]{1,0:T(8,128)(2,1)S(1)}, u32[]{:S(2)}, u32[]{:S(2)}) collective-permute-start(bf16[32,2176]{1,0:T(8,128)(2,1)S(1)} %shard_map.113.refs_0_), channel_id=1, source_target_pairs={{0,2},{1,3},{2,0},{3,1},{4,6},{5,7},{6,4},{7,5},{8,10},{9,11},{10,... | collective-permute-start | bytes 417800 | tf_op jit(solution)/shard_map/ppermute | solution.py:36
  13.3 8.4 %collective-permute-start.3 = (bf16[32,2176]{1,0:T(8,128)(2,1)S(1)}, bf16[32,2176]{1,0:T(8,128)(2,1)S(1)}, u32[]{:S(2)}, u32[]{:S(2)}) collective-permute-start(bf16[32,2176]{1,0:T(8,128)(2,1)S(1)} %shard_map.113.refs_0_), channel_id=1, source_target_pairs={{0,6},{1,7},{2,4},{3,5},{4,2},{5,3},{6,0},{7,1},{8,14},{9,15},{10,... | collective-permute-start | bytes 417800 | tf_op jit(solution)/shard_map/ppermute | solution.py:36
  15.3 10.1 %collective-permute-start.2 = (bf16[32,2176]{1,0:T(8,128)(2,1)S(1)}, bf16[32,2176]{1,0:T(8,128)(2,1)S(1)}, u32[]{:S(2)}, u32[]{:S(2)}) collective-permute-start(bf16[32,2176]{1,0:T(8,128)(2,1)S(1)} %shard_map.113.refs_0_), channel_id=1, source_target_pairs={{0,4},{1,5},{2,6},{3,7},{4,0},{5,1},{6,2},{7,3},{8,12},{9,13},{10,... | collective-permute-start | bytes 417800 | tf_op jit(solution)/shard_map/ppermute | solution.py:36
  17.8 11.8 %collective-permute-start.14 = (bf16[32,2176]{1,0:T(8,128)(2,1)S(1)}, bf16[32,2176]{1,0:T(8,128)(2,1)S(1)}, u32[]{:S(2)}, u32[]{:S(2)}) collective-permute-start(bf16[32,2176]{1,0:T(8,128)(2,1)S(1)} %shard_map.118.refs_0_), channel_id=1, source_target_pairs={{0,6},{1,7},{2,4},{3,5},{4,2},{5,3},{6,0},{7,1},{8,14},{9,15},{10,... | collective-permute-start | bytes 417800 | tf_op jit(solution)/shard_map/ppermute | solution.py:36
  20.1 10.6 %collective-permute-start.13 = (bf16[32,2176]{1,0:T(8,128)(2,1)S(1)}, bf16[32,2176]{1,0:T(8,128)(2,1)S(1)}, u32[]{:S(2)}, u32[]{:S(2)}) collective-permute-start(bf16[32,2176]{1,0:T(8,128)(2,1)S(1)} %shard_map.118.refs_0_), channel_id=1, source_target_pairs={{0,4},{1,5},{2,6},{3,7},{4,0},{5,1},{6,2},{7,3},{8,12},{9,13},{10,... | collective-permute-start | bytes 417800 | tf_op jit(solution)/shard_map/ppermute | solution.py:36
  21.2 9.5 %collective-permute-start.12 = (bf16[32,2176]{1,0:T(8,128)(2,1)S(1)}, bf16[32,2176]{1,0:T(8,128)(2,1)S(1)}, u32[]{:S(2)}, u32[]{:S(2)}) collective-permute-start(bf16[32,2176]{1,0:T(8,128)(2,1)S(1)} %shard_map.118.refs_0_), channel_id=1, source_target_pairs={{0,2},{1,3},{2,0},{3,1},{4,6},{5,7},{6,4},{7,5},{8,10},{9,11},{10,... | collective-permute-start | bytes 417800 | tf_op jit(solution)/shard_map/ppermute | solution.py:36
  27.1 7.8 %collective-permute-start.6 = (bf16[32,2048]{1,0:T(8,128)(2,1)S(1)}, bf16[32,2048]{1,0:T(8,128)(2,1)S(1)}, u32[]{:S(2)}, u32[]{:S(2)}) collective-permute-start(bf16[32,2048]{1,0:T(8,128)(2,1)S(1)} %get-tuple-element.30), channel_id=1, source_target_pairs={{0,2},{1,3},{2,0},{3,1},{4,6},{5,7},{6,4},{7,5},{8,10},{9,11},{10,... | collective-permute-start | bytes 393224 | tf_op jit(solution)/shard_map/ppermute | solution.py:36
  28.6 8.2 %collective-permute-start.7 = (bf16[32,2048]{1,0:T(8,128)(2,1)S(1)}, bf16[32,2048]{1,0:T(8,128)(2,1)S(1)}, u32[]{:S(2)}, u32[]{:S(2)}) collective-permute-start(bf16[32,2048]{1,0:T(8,128)(2,1)S(1)} %get-tuple-element.31), channel_id=1, source_target_pairs={{0,4},{1,5},{2,6},{3,7},{4,0},{5,1},{6,2},{7,3},{8,12},{9,13},{10,... | collective-permute-start | bytes 393224 | tf_op jit(solution)/shard_map/ppermute | solution.py:36
  29.7 20.2 %copy-start = (s32[1,1,8,8]{3,2,1,0:T(8,128)S(1)}, s32[1,1,8,8]{3,2,1,0:T(8,128)}, u32[]{:S(2)}) copy-start(s32[1,1,8,8]{3,2,1,0:T(8,128)} %param.11) | copy-start | bytes 772
  29.7 20.2 %copy-start.1 = (f32[1,1,8,8]{3,2,1,0:T(8,128)S(1)}, f32[1,1,8,8]{3,2,1,0:T(8,128)}, u32[]{:S(2)}) copy-start(f32[1,1,8,8]{3,2,1,0:T(8,128)} %param.13) | copy-start | bytes 772
  29.7 7.2 %collective-permute-start.8 = (bf16[32,2048]{1,0:T(8,128)(2,1)S(1)}, bf16[32,2048]{1,0:T(8,128)(2,1)S(1)}, u32[]{:S(2)}, u32[]{:S(2)}) collective-permute-start(bf16[32,2048]{1,0:T(8,128)(2,1)S(1)} %get-tuple-element.32), channel_id=1, source_target_pairs={{0,6},{1,7},{2,4},{3,5},{4,2},{5,3},{6,0},{7,1},{8,14},{9,15},{10,... | collective-permute-start | bytes 393224 | tf_op jit(solution)/shard_map/ppermute | solution.py:36
  32.4 8.3 %collective-permute-start.15 = (bf16[32,2048]{1,0:T(8,128)(2,1)S(1)}, bf16[32,2048]{1,0:T(8,128)(2,1)S(1)}, u32[]{:S(2)}, u32[]{:S(2)}) collective-permute-start(bf16[32,2048]{1,0:T(8,128)(2,1)S(1)} %get-tuple-element.37), channel_id=1, source_target_pairs={{0,2},{1,3},{2,0},{3,1},{4,6},{5,7},{6,4},{7,5},{8,10},{9,11},{10,... | collective-permute-start | bytes 393224 | tf_op jit(solution)/shard_map/ppermute | solution.py:36
  33.9 6.8 %collective-permute-start.16 = (bf16[32,2048]{1,0:T(8,128)(2,1)S(1)}, bf16[32,2048]{1,0:T(8,128)(2,1)S(1)}, u32[]{:S(2)}, u32[]{:S(2)}) collective-permute-start(bf16[32,2048]{1,0:T(8,128)(2,1)S(1)} %get-tuple-element.38), channel_id=1, source_target_pairs={{0,4},{1,5},{2,6},{3,7},{4,0},{5,1},{6,2},{7,3},{8,12},{9,13},{10,... | collective-permute-start | bytes 393224 | tf_op jit(solution)/shard_map/ppermute | solution.py:36
  34.9 5.9 %collective-permute-start.17 = (bf16[32,2048]{1,0:T(8,128)(2,1)S(1)}, bf16[32,2048]{1,0:T(8,128)(2,1)S(1)}, u32[]{:S(2)}, u32[]{:S(2)}) collective-permute-start(bf16[32,2048]{1,0:T(8,128)(2,1)S(1)} %get-tuple-element.39), channel_id=1, source_target_pairs={{0,6},{1,7},{2,4},{3,5},{4,2},{5,3},{6,0},{7,1},{8,14},{9,15},{10,... | collective-permute-start | bytes 393224 | tf_op jit(solution)/shard_map/ppermute | solution.py:36
  36.9 9.0 %collective-permute-start.9 = (bf16[16,2048]{1,0:T(8,128)(2,1)S(1)}, bf16[16,2048]{1,0:T(8,128)(2,1)S(1)}, u32[]{:S(2)}, u32[]{:S(2)}) collective-permute-start(bf16[16,2048]{1,0:T(8,128)(2,1)S(1)} %get-tuple-element.33), channel_id=1, source_target_pairs={{0,16},{1,17},{2,18},{3,19},{4,20},{5,21},{6,22},{7,23},{8,24},{9,... | collective-permute-start | bytes 196616 | tf_op jit(solution)/shard_map/ppermute | solution.py:36
  40.8 7.1 %collective-permute-start.18 = (bf16[16,2048]{1,0:T(8,128)(2,1)S(1)}, bf16[16,2048]{1,0:T(8,128)(2,1)S(1)}, u32[]{:S(2)}, u32[]{:S(2)}) collective-permute-start(bf16[16,2048]{1,0:T(8,128)(2,1)S(1)} %get-tuple-element.40), channel_id=1, source_target_pairs={{0,24},{1,25},{2,26},{3,27},{4,28},{5,29},{6,30},{7,31},{8,16},{9,... | collective-permute-start | bytes 196616 | tf_op jit(solution)/shard_map/ppermute | solution.py:36
  45.6 4.3 %collective-permute-start.19 = (bf16[16,2048]{1,0:T(8,128)(2,1)S(1)}, bf16[16,2048]{1,0:T(8,128)(2,1)S(1)}, u32[]{:S(2)}, u32[]{:S(2)}) collective-permute-start(bf16[16,2048]{1,0:T(8,128)(2,1)S(1)} %get-tuple-element.41), channel_id=1, source_target_pairs={{0,8},{1,9},{2,10},{3,11},{4,12},{5,13},{6,14},{7,15},{8,0},{9,1},... | collective-permute-start | bytes 196616 | tf_op jit(solution)/shard_map/ppermute | solution.py:36

commit v9 on v7

--- a/solution.py
+++ b/solution.py
@@ -12,11 +12,12 @@
 MIB = 2**20
 
 
-def run_kernel(body, outs, operands, scratch=(), limit=16, space=pltpu.VMEM):
+def run_kernel(body, outs, operands, scratch=(), limit=16, space=pltpu.VMEM, tail=0):
+    spaces = [space] * (len(operands) - tail) + [pl.ANY] * tail
     return pl.pallas_call(
         body,
         out_shape=outs,
-        in_specs=[pl.BlockSpec(memory_space=space)] * len(operands),
+        in_specs=[pl.BlockSpec(memory_space=place) for place in spaces],
         out_specs=jax.tree.map(lambda _: pl.BlockSpec(memory_space=pltpu.VMEM), outs),
         scratch_shapes=list(scratch),
         compiler_params=pltpu.CompilerParams(vmem_limit_bytes=limit * MIB),
@@ -32,7 +33,10 @@
 
 
 def exclusive(value, mask):
-    pairs = [(source, source ^ mask) for source in range(lax.axis_size("expert"))]
+    masks = mask if isinstance(mask, tuple) else (mask,) * SPLIT
+    pairs = [
+        (source, source ^ masks[source % SPLIT]) for source in range(lax.axis_size("expert"))
+    ]
     return lax.ppermute(value, "expert", pairs)
 
 
@@ -91,29 +95,6 @@
     ).astype(jnp.bfloat16)
 
 
-def stage_kernel(count, *refs):
-    sources, targets, sems = refs[:count], refs[count : 2 * count], refs[2 * count]
-    copies = [
-        pltpu.make_async_copy(source, target, sems.at[place])
-        for place, (source, target) in enumerate(zip(sources, targets))
-    ]
-    for copy in copies:
-        copy.start()
-    for copy in copies:
-        copy.wait()
-
-
-def stage_weights(own_in, own_out, other_in, other_out):
-    weights = [in_hbm(own_in), other_in, in_hbm(own_out), other_out]
-    return run_kernel(
-        functools.partial(stage_kernel, len(weights)),
-        [pltpu.VMEM(value.shape, value.dtype) for value in weights],
-        weights,
-        [pltpu.SemaphoreType.DMA((len(weights),))],
-        space=pl.ANY,
-    )
-
-
 def after(value, *awaited):
     return lax.optimization_barrier((value, awaited))[0]
 
@@ -130,9 +111,20 @@
     return run_kernel(join_kernel, like(len(parts) * rows, columns), parts)
 
 
-def expert_kernel(experts, row_count, sizes, *refs):
+def expert_kernel(experts, row_count, sizes, loads, *refs):
     row_refs, refs = refs[:row_count], refs[row_count:]
     in_refs, out_refs, refs = refs[:SPLIT], refs[SPLIT : 2 * SPLIT], refs[2 * SPLIT :]
+    copies = [None] * 2
+    if loads:
+        own_refs, refs = refs[:2], refs[2:]
+        held_refs = refs[len(sizes) : len(sizes) + 2]
+        refs, sems = refs[: len(sizes)] + refs[len(sizes) + 2 : -1], refs[-1]
+        copies = [
+            pltpu.make_async_copy(own_ref, held_ref, sems.at[place])
+            for place, (own_ref, held_ref) in enumerate(zip(own_refs, held_refs))
+        ]
+        for copy in copies:
+            copy.start()
     result_refs, (rows, hidden) = refs[: len(sizes)], refs[len(sizes) :]
     half, model_width = out_refs[0].shape
     expert = lax.axis_index("expert") // SPLIT
@@ -148,11 +140,15 @@
         weights.append(jnp.sum(jnp.where(mine, extra, 0.0), axis=1, keepdims=True))
     weight = jnp.concatenate(weights, axis=0)
     for place, in_ref in enumerate(in_refs):
+        if loads and place == SPLIT - 1:
+            copies[0].wait()
         both = jnp.dot(rows[...], in_ref[...], preferred_element_type=jnp.float32)
         gate, up = both[:, :half], both[:, half:]
         hidden[:, place * half : (place + 1) * half] = (
             gate / (1.0 + jnp.exp(-gate)) * up
         ).astype(jnp.bfloat16)
+    if loads:
+        copies[1].wait()
     step = min(512, model_width)
     for start in range(0, model_width, step):
         value = sum(
@@ -170,19 +166,50 @@
             filled += size
 
 
-def run_expert(experts, row_arrays, weights, sizes):
+def loading_kernel(experts, row_count, sizes, *refs):
+    inputs, (other_in, other_out, own_in, own_out) = refs[:row_count], refs[row_count : row_count + 4]
+    refs = refs[row_count + 4 :]
+    held_in, held_out = refs[len(sizes) : len(sizes) + 2]
+    expert_kernel(
+        experts,
+        row_count,
+        sizes,
+        True,
+        *inputs,
+        other_in,
+        held_in,
+        other_out,
+        held_out,
+        own_in,
+        own_out,
+        *refs,
+    )
+
+
+def run_expert(experts, row_arrays, weights, sizes, loads):
     total = sum(array.shape[0] for array in row_arrays)
-    half, model_width = weights[-1].shape
+    other_out = weights[1] if loads else weights[2]
+    half, model_width = other_out.shape
+    outs = [like(size, model_width) for size in sizes]
+    scratch = [
+        pltpu.VMEM((total, model_width), jnp.bfloat16),
+        pltpu.VMEM((total, SPLIT * half), jnp.bfloat16),
+    ]
+    if loads:
+        body = functools.partial(loading_kernel, experts, len(row_arrays), sizes)
+        outs += [pltpu.VMEM(value.shape, value.dtype) for value in weights[2:]]
+        scratch.append(pltpu.SemaphoreType.DMA((2,)))
+    else:
+        body = functools.partial(expert_kernel, experts, len(row_arrays), sizes, False)
     return run_kernel(
-        functools.partial(expert_kernel, experts, len(row_arrays), sizes),
-        [like(size, model_width) for size in sizes],
-        list(row_arrays) + list(weights),
-        [
-            pltpu.VMEM((total, model_width), jnp.bfloat16),
-            pltpu.VMEM((total, SPLIT * half), jnp.bfloat16),
-        ],
-        limit=24,
+        body, outs, list(row_arrays) + list(weights), scratch, limit=24, tail=2 if loads else 0
     )
+
+
+def relay_kernel(mine_ref, came_ref, out_ref):
+    out_ref[...] = (
+        mine_ref[...].astype(jnp.float32) + came_ref[...].astype(jnp.float32)
+    ).astype(out_ref.dtype)
 
 
 def plane_kernel(count, *refs):
@@ -237,14 +264,13 @@
     extra = -(-2 * experts // LANES) * LANES
     rows = 2 * tok_rows
     chips = devices // SPLIT
-    inner = min(4, chips)
+    inner = 4
     outer = chips // inner
-    inner_masks = [SPLIT * i for i in range(1, inner)]
+    first_axis, second_axis = (SPLIT, 2 * SPLIT), (2 * SPLIT, SPLIT)
     layer_mask = lambda j: SPLIT * inner * j
     streams = [list(range(outer // 2)), list(range(outer // 2, outer))]
     own_in, own_out = w_in[0, 0], w_out[0, 0]
     other_out, other_in = exclusive(own_out, 1), exclusive(own_in, 1)
-    weights = None
 
     step_count = micro_count + section_count - 1
     carry = jnp.zeros((2, tok_rows, model_width), jnp.bfloat16)
@@ -290,26 +316,29 @@
         blocks = []
         for stream, layers in enumerate(streams):
             joined = join_rows([column[j] for j in layers])
-            if stream == 1:
-                joined = after(joined, blocks[0][1])
-            block = [joined]
-            for mask in inner_masks:
-                block.append(exclusive(joined, mask))
-            blocks.append(block)
-        if weights is None:
-            weights = stage_weights(own_in, own_out, other_in, other_out)
+            first = exclusive(joined, first_axis)
+            second = exclusive(joined, second_axis)
+            blocks.append([joined, first, second, exclusive(first, second_axis)])
         summed = []
         for stream, layers in enumerate(streams):
-            partial = run_expert(
-                experts, blocks[stream], weights, [len(layers) * rows] * inner
-            )
-            returned = [partial[0]] + [
-                exclusive(part, mask) for part, mask in zip(partial[1:], inner_masks)
-            ]
+            sizes = [len(layers) * rows] * inner
+            if tick == 0 and stream == 0:
+                weights = [other_in, other_out, in_hbm(own_in), in_hbm(own_out)]
+                *partial, held_in, held_out = run_expert(
+                    experts, blocks[stream], weights, sizes, True
+                )
+                weights = [other_in, held_in, other_out, held_out]
+            else:
+                partial = run_expert(experts, blocks[stream], weights, sizes, False)
+            mine, first, second, across = partial
+            across = exclusive(across, first_axis)
+            first = exclusive(first, first_axis)
+            second = run_kernel(relay_kernel, like(*second.shape), [second, across])
+            returned = [mine, first, exclusive(second, second_axis)]
             outs = [like(rows, model_width)] * len(layers)
             if stream == 0:
                 outs[0] = like(rows, model_width, jnp.float32)
-            sums = run_kernel(functools.partial(plane_kernel, inner), outs, returned)
+            sums = run_kernel(functools.partial(plane_kernel, len(returned)), outs, returned)
             for j, value in list(zip(layers, sums))[::-1]:
                 summed.append(exclusive(value, layer_mask(j)) if j else value)
         round_orig, round_pruned, tick_terms, *moe = run_kernel(

time: 58 us -> 59.6 us (1.028)
  waiting for transfers between devices: 13.4 us -> 15.6 us
  Pallas kernels: 8.25 us -> 7.49 us
  blocking collectives: 9.24 us -> 9.84 us
    ppermute x20, waiting for transfers between devices: 13.4 us -> 15.6 us  [exclusive(): return lax.ppermute(value, 'expert', pairs)]
    pallas_call x10 -> x11, Pallas kernels: 8.25 us -> 7.49 us  [run_kernel(): pl.pallas_call(body, out_shape=outs, in_specs=[pl.BlockSpec(memory_space=...]
  transfers between devices with their start and end apart: 20 -> 20, of which waited for: 8 -> 10; matrix products, arithmetic and copies ran while one was open for 0% -> 0% of each run, Pallas kernels for 12% -> 11%
where the time goes in v9:
time: 59.6 us; the launch traced here: 59.4 us
  starting transfers between devices  25.8 us (43%)
  waiting for transfers between devices  15.6 us (26%)
  blocking collectives  9.84 us (17%)
  Pallas kernels  7.49 us (13%)
  between operations  0.71 us (1%)
    ppermute x20, starting transfers between devices, exclusive(): return lax.ppermute(value, 'expert', pairs)  25.8 us
    ppermute x20, waiting for transfers between devices, exclusive(): return lax.ppermute(value, 'expert', pairs)  15.6 us
    all_to_all x1, blocking collectives, on_device(): lax.all_to_all(terms, 'expert', split_axis=0, concat_axis=0, tiled=True)  9.84 us
    pallas_call x11, Pallas kernels, run_kernel(): pl.pallas_call(body, out_shape=outs, in_specs=[pl.BlockSpec(memory_space=...  7.49 us
  transfers between devices with their start and end apart: 20, of which 10 were waited for; matrix products, arithmetic and copies ran while one was open for 0% of the time, Pallas kernels for 11%

profile of v9, /device:TPU:0, one launch (start us, length us, event | category | flops | bytes accessed | tf_op | source)
XLA Modules:
  0.0 59.4 jit_solution(5751435058940437205)
XLA Ops:
  0.6 0.5 collective-permute-start.4
  1.1 0.1 collective-permute-start.5
  1.2 1.1 %shard_map.112.refs_0_ = bf16[16,2176]{1,0:T(8,128)(2,1)S(1)} custom-call(bf16[8,2048]{1,0:T(8,128)(2,1)} %bitcast.24, bf16[8,2048]{1,0:T(8,128)(2,1)} %bitcast.25, s32[8,8]{1,0:T(8,128)} %bitcast.15, s32[8,8]{1,0:T(8,128)} %bitcast.26, f32[8,8]{1,0:T(8,128)} %bitcast.17, f32[8,8]{1,0:T(8,128)} %bitcast.27, s32[1,16]{1,0:T(1,128)} %refs_6_.1), custom_call_target="tpu_custom_call" | custom-call | tf_op jit(solution)/shard_map/pallas_call | solution.py:17
  2.3 3.1 %collective-permute-start = (bf16[16,2176]{1,0:T(8,128)(2,1)S(1)}, bf16[16,2176]{1,0:T(8,128)(2,1)S(1)}, u32[]{:S(2)}, u32[]{:S(2)}) collective-permute-start(bf16[16,2176]{1,0:T(8,128)(2,1)S(1)} %shard_map.112.refs_0_), channel_id=1, source_target_pairs={{0,8},{1,9},{2,10},{3,11},{4,12},{5,13},{6,14},{7,15},{8,0},{9,1},... | collective-permute-start | bytes 208904 | tf_op jit(solution)/shard_map/ppermute | solution.py:40
  5.4 2.6 %collective-permute-start.10 = (bf16[16,2176]{1,0:T(8,128)(2,1)S(1)}, bf16[16,2176]{1,0:T(8,128)(2,1)S(1)}, u32[]{:S(2)}, u32[]{:S(2)}) collective-permute-start(bf16[16,2176]{1,0:T(8,128)(2,1)S(1)} %shard_map.112.refs_0_), channel_id=1, source_target_pairs={{0,16},{1,17},{2,18},{3,19},{4,20},{5,21},{6,22},{7,23},{8,24},{9,... | collective-permute-start | bytes 208904 | tf_op jit(solution)/shard_map/ppermute | solution.py:40
  8.0 0.0 collective-permute-start.11
  8.0 0.0 collective-permute-done.refs_1_
  8.0 1.8 %collective-permute-start.1 = (bf16[32,2176]{1,0:T(8,128)(2,1)S(1)}, bf16[32,2176]{1,0:T(8,128)(2,1)S(1)}, u32[]{:S(2)}, u32[]{:S(2)}) collective-permute-start(bf16[32,2176]{1,0:T(8,128)(2,1)S(1)} %shard_map.113.refs_0_), channel_id=1, source_target_pairs={{0,2},{1,5},{2,0},{3,7},{4,6},{5,1},{6,4},{7,3},{8,10},{9,13},{10,... | collective-permute-start | bytes 417800 | tf_op jit(solution)/shard_map/ppermute | solution.py:40
  9.8 3.4 %collective-permute-done.10.refs_0_ = bf16[16,2176]{1,0:T(8,128)(2,1)S(1)} collective-permute-done((bf16[16,2176]{1,0:T(8,128)(2,1)S(1)}, bf16[16,2176]{1,0:T(8,128)(2,1)S(1)}, u32[]{:S(2)}, u32[]{:S(2)}) %collective-permute-start.10) | collective-permute-done | bytes 69664 | tf_op jit(solution)/shard_map/ppermute | solution.py:40
  13.2 1.5 %collective-permute-start.2 = (bf16[32,2176]{1,0:T(8,128)(2,1)S(1)}, bf16[32,2176]{1,0:T(8,128)(2,1)S(1)}, u32[]{:S(2)}, u32[]{:S(2)}) collective-permute-start(bf16[32,2176]{1,0:T(8,128)(2,1)S(1)} %shard_map.113.refs_0_), channel_id=1, source_target_pairs={{0,4},{1,3},{2,6},{3,1},{4,0},{5,7},{6,2},{7,5},{8,12},{9,11},{10,... | collective-permute-start | bytes 417800 | tf_op jit(solution)/shard_map/ppermute | solution.py:40
  14.7 0.0 collective-permute-done.11.refs_1_
  14.7 1.6 %collective-permute-start.12 = (bf16[32,2176]{1,0:T(8,128)(2,1)S(1)}, bf16[32,2176]{1,0:T(8,128)(2,1)S(1)}, u32[]{:S(2)}, u32[]{:S(2)}) collective-permute-start(bf16[32,2176]{1,0:T(8,128)(2,1)S(1)} %shard_map.117.refs_0_), channel_id=1, source_target_pairs={{0,2},{1,5},{2,0},{3,7},{4,6},{5,1},{6,4},{7,3},{8,10},{9,13},{10,... | collective-permute-start | bytes 417800 | tf_op jit(solution)/shard_map/ppermute | solution.py:40
  16.2 0.0 collective-permute-done.1.refs_1_
  16.2 1.1 %collective-permute-start.3 = (bf16[32,2176]{1,0:T(8,128)(2,1)S(1)}, bf16[32,2176]{1,0:T(8,128)(2,1)S(1)}, u32[]{:S(2)}, u32[]{:S(2)}) collective-permute-start(bf16[32,2176]{1,0:T(8,128)(2,1)S(1)} %collective-permute-done.1.refs_1_), channel_id=1, source_target_pairs={{0,4},{1,3},{2,6},{3,1},{4,0},{5,7},{6,2},{7,5},{8,12},{9,11},{10,... | collective-permute-start | bytes 417800 | tf_op jit(solution)/shard_map/ppermute | solution.py:40
  17.3 0.9 %collective-permute-done.2.refs_2_ = bf16[32,2176]{1,0:T(8,128)(2,1)S(1)} collective-permute-done((bf16[32,2176]{1,0:T(8,128)(2,1)S(1)}, bf16[32,2176]{1,0:T(8,128)(2,1)S(1)}, u32[]{:S(2)}, u32[]{:S(2)}) %collective-permute-start.2) | collective-permute-done | bytes 139296 | tf_op jit(solution)/shard_map/ppermute | solution.py:40
  18.2 1.5 %collective-permute-start.13 = (bf16[32,2176]{1,0:T(8,128)(2,1)S(1)}, bf16[32,2176]{1,0:T(8,128)(2,1)S(1)}, u32[]{:S(2)}, u32[]{:S(2)}) collective-permute-start(bf16[32,2176]{1,0:T(8,128)(2,1)S(1)} %shard_map.117.refs_0_), channel_id=1, source_target_pairs={{0,4},{1,3},{2,6},{3,1},{4,0},{5,7},{6,2},{7,5},{8,12},{9,11},{10,... | collective-permute-start | bytes 417800 | tf_op jit(solution)/shard_map/ppermute | solution.py:40
  19.7 1.6 %collective-permute-done.12.refs_1_ = bf16[32,2176]{1,0:T(8,128)(2,1)S(1)} collective-permute-done((bf16[32,2176]{1,0:T(8,128)(2,1)S(1)}, bf16[32,2176]{1,0:T(8,128)(2,1)S(1)}, u32[]{:S(2)}, u32[]{:S(2)}) %collective-permute-start.12) | collective-permute-done | bytes 139296 | tf_op jit(solution)/shard_map/ppermute | solution.py:40
  21.4 0.9 %collective-permute-start.14 = (bf16[32,2176]{1,0:T(8,128)(2,1)S(1)}, bf16[32,2176]{1,0:T(8,128)(2,1)S(1)}, u32[]{:S(2)}, u32[]{:S(2)}) collective-permute-start(bf16[32,2176]{1,0:T(8,128)(2,1)S(1)} %collective-permute-done.12.refs_1_), channel_id=1, source_target_pairs={{0,4},{1,3},{2,6},{3,1},{4,0},{5,7},{6,2},{7,5},{8,12},{9,11},{10,... | collective-permute-start | bytes 417800 | tf_op jit(solution)/shard_map/ppermute | solution.py:40
  22.3 0.0 collective-permute-done.3.refs_3_
  22.3 0.0 collective-permute-done.5.refs_5_.refs_6_
  22.3 0.0 collective-permute-done.4.refs_4_
  22.3 3.4 %shard_map.114 = (bf16[32,2048]{1,0:T(8,128)(2,1)S(1)}, bf16[32,2048]{1,0:T(8,128)(2,1)S(1)}, bf16[32,2048]{1,0:T(8,128)(2,1)S(1)}, bf16[32,2048]{1,0:T(8,128)(2...) custom-call(bf16[32,2176]{1,0:T(8,128)(2,1)S(1)} %shard_map.113.refs_0_, ...), custom_call_target="tpu_custom_call" | custom-call | tf_op jit(solution)/shard_map/pallas_call | solution.py:17
  25.7 1.5 %collective-permute-start.7 = (bf16[32,2048]{1,0:T(8,128)(2,1)S(1)}, bf16[32,2048]{1,0:T(8,128)(2,1)S(1)}, u32[]{:S(2)}, u32[]{:S(2)}) collective-permute-start(bf16[32,2048]{1,0:T(8,128)(2,1)S(1)} %get-tuple-element.23), channel_id=1, source_target_pairs={{0,2},{1,5},{2,0},{3,7},{4,6},{5,1},{6,4},{7,3},{8,10},{9,13},{10,... | collective-permute-start | bytes 393224 | tf_op jit(solution)/shard_map/ppermute | solution.py:40
  27.2 0.0 collective-permute-done.13.refs_2_
  27.2 0.0 collective-permute-done.14.refs_3_
  27.3 0.0 copy-start.1
  27.3 1.7 %shard_map.118 = (bf16[32,2048]{1,0:T(8,128)(2,1)S(1)}, bf16[32,2048]{1,0:T(8,128)(2,1)S(1)}, bf16[32,2048]{1,0:T(8,128)(2,1)S(1)}, bf16[32,2048]{1,0:T(8,128)(2,1)S(1)}) custom-call(bf16[32,2176]{1,0:T(8,128)(2,1)S(1)} %shard_map.117.refs_0_, bf16[32,2176]{1,0:T(8,128)(2,1)S(1)} %collective-permute-done.12.refs_1_, ...), custom_call_target="tpu_custom_call" | custom-call | tf_op jit(solution)/shard_map/pallas_call | solution.py:17
  28.9 1.3 %collective-permute-start.16 = (bf16[32,2048]{1,0:T(8,128)(2,1)S(1)}, bf16[32,2048]{1,0:T(8,128)(2,1)S(1)}, u32[]{:S(2)}, u32[]{:S(2)}) collective-permute-start(bf16[32,2048]{1,0:T(8,128)(2,1)S(1)} %get-tuple-element.31), channel_id=1, source_target_pairs={{0,2},{1,5},{2,0},{3,7},{4,6},{5,1},{6,4},{7,3},{8,10},{9,13},{10,... | collective-permute-start | bytes 393224 | tf_op jit(solution)/shard_map/ppermute | solution.py:40
  30.2 0.8 %collective-permute-start.6 = (bf16[32,2048]{1,0:T(8,128)(2,1)S(1)}, bf16[32,2048]{1,0:T(8,128)(2,1)S(1)}, u32[]{:S(2)}, u32[]{:S(2)}) collective-permute-start(bf16[32,2048]{1,0:T(8,128)(2,1)S(1)} %get-tuple-element.21), channel_id=1, source_target_pairs={{0,2},{1,5},{2,0},{3,7},{4,6},{5,1},{6,4},{7,3},{8,10},{9,13},{10,... | collective-permute-start | bytes 393224 | tf_op jit(solution)/shard_map/ppermute | solution.py:40
  31.0 1.0 %collective-permute-done.7.came_ref = bf16[32,2048]{1,0:T(8,128)(2,1)S(1)} collective-permute-done((bf16[32,2048]{1,0:T(8,128)(2,1)S(1)}, bf16[32,2048]{1,0:T(8,128)(2,1)S(1)}, u32[]{:S(2)}, u32[]{:S(2)}) %collective-permute-start.7) | collective-permute-done | bytes 131104 | tf_op jit(solution)/shard_map/ppermute | solution.py:40
  32.1 1.2 %collective-permute-start.8 = (bf16[32,2048]{1,0:T(8,128)(2,1)S(1)}, bf16[32,2048]{1,0:T(8,128)(2,1)S(1)}, u32[]{:S(2)}, u32[]{:S(2)}) collective-permute-start(bf16[32,2048]{1,0:T(8,128)(2,1)S(1)} %shard_map.115), channel_id=1, source_target_pairs={{0,4},{1,3},{2,6},{3,1},{4,0},{5,7},{6,2},{7,5},{8,12},{9,11},{10,... | collective-permute-start | bytes 393224 | tf_op jit(solution)/shard_map/ppermute | solution.py:40
  33.3 0.8 %collective-permute-start.15 = (bf16[32,2048]{1,0:T(8,128)(2,1)S(1)}, bf16[32,2048]{1,0:T(8,128)(2,1)S(1)}, u32[]{:S(2)}, u32[]{:S(2)}) collective-permute-start(bf16[32,2048]{1,0:T(8,128)(2,1)S(1)} %get-tuple-element.29), channel_id=1, source_target_pairs={{0,2},{1,5},{2,0},{3,7},{4,6},{5,1},{6,4},{7,3},{8,10},{9,13},{10,... | collective-permute-start | bytes 393224 | tf_op jit(solution)/shard_map/ppermute | solution.py:40
  34.1 0.3 collective-permute-done.16.came_ref
  34.4 1.5 %collective-permute-start.17 = (bf16[32,2048]{1,0:T(8,128)(2,1)S(1)}, bf16[32,2048]{1,0:T(8,128)(2,1)S(1)}, u32[]{:S(2)}, u32[]{:S(2)}) collective-permute-start(bf16[32,2048]{1,0:T(8,128)(2,1)S(1)} %shard_map.119), channel_id=1, source_target_pairs={{0,4},{1,3},{2,6},{3,1},{4,0},{5,7},{6,2},{7,5},{8,12},{9,11},{10,... | collective-permute-start | bytes 393224 | tf_op jit(solution)/shard_map/ppermute | solution.py:40
  36.0 0.0 collective-permute-done.6.refs_1_
  36.0 1.2 %collective-permute-done.8.refs_2_ = bf16[32,2048]{1,0:T(8,128)(2,1)S(1)} collective-permute-done((bf16[32,2048]{1,0:T(8,128)(2,1)S(1)}, bf16[32,2048]{1,0:T(8,128)(2,1)S(1)}, u32[]{:S(2)}, u32[]{:S(2)}) %collective-permute-start.8) | collective-permute-done | bytes 131104 | tf_op jit(solution)/shard_map/ppermute | solution.py:40
  37.2 0.7 %collective-permute-start.9 = (bf16[16,2048]{1,0:T(8,128)(2,1)S(1)}, bf16[16,2048]{1,0:T(8,128)(2,1)S(1)}, u32[]{:S(2)}, u32[]{:S(2)}) collective-permute-start(bf16[16,2048]{1,0:T(8,128)(2,1)S(1)} %get-tuple-element.24), channel_id=1, source_target_pairs={{0,8},{1,9},{2,10},{3,11},{4,12},{5,13},{6,14},{7,15},{8,0},{9,1},... | collective-permute-start | bytes 196616 | tf_op jit(solution)/shard_map/ppermute | solution.py:40
  37.9 0.4 collective-permute-done.15.refs_1_
  38.3 1.2 %collective-permute-done.17.refs_2_ = bf16[32,2048]{1,0:T(8,128)(2,1)S(1)} collective-permute-done((bf16[32,2048]{1,0:T(8,128)(2,1)S(1)}, bf16[32,2048]{1,0:T(8,128)(2,1)S(1)}, u32[]{:S(2)}, u32[]{:S(2)}) %collective-permute-start.17) | collective-permute-done | bytes 131104 | tf_op jit(solution)/shard_map/ppermute | solution.py:40
  39.5 0.1 shard_map.120
  39.5 3.2 %collective-permute-start.18 = (bf16[16,2048]{1,0:T(8,128)(2,1)S(1)}, bf16[16,2048]{1,0:T(8,128)(2,1)S(1)}, u32[]{:S(2)}, u32[]{:S(2)}) collective-permute-start(bf16[16,2048]{1,0:T(8,128)(2,1)S(1)} %get-tuple-element.32), channel_id=1, source_target_pairs={{0,24},{1,25},{2,26},{3,27},{4,28},{5,29},{6,30},{7,31},{8,16},{9,... | collective-permute-start | bytes 196616 | tf_op jit(solution)/shard_map/ppermute | solution.py:40
  42.8 0.0 collective-permute-start.19
  42.8 0.0 collective-permute-done.9.refs_0_
  42.8 2.9 %collective-permute-done.18.refs_2_ = bf16[16,2048]{1,0:T(8,128)(2,1)S(1)} collective-permute-done((bf16[16,2048]{1,0:T(8,128)(2,1)S(1)}, bf16[16,2048]{1,0:T(8,128)(2,1)S(1)}, u32[]{:S(2)}, u32[]{:S(2)}) %collective-permute-start.18) | collective-permute-done | bytes 65568 | tf_op jit(solution)/shard_map/ppermute | solution.py:40
  45.7 2.6 %collective-permute-done.19.refs_3_ = bf16[16,2048]{1,0:T(8,128)(2,1)S(1)} collective-permute-done((bf16[16,2048]{1,0:T(8,128)(2,1)S(1)}, bf16[16,2048]{1,0:T(8,128)(2,1)S(1)}, u32[]{:S(2)}, u32[]{:S(2)}) %collective-permute-start.19) | collective-permute-done | bytes 65568 | tf_op jit(solution)/shard_map/ppermute | solution.py:40
  48.4 0.7 %shard_map.121 = (bf16[8,2048]{1,0:T(8,128)(2,1)}, bf16[8,2048]{1,0:T(8,128)(2,1)}, f32[32,16]{1,0:T(8,128)S(1)}) custom-call(bf16[16,2048]{1,0:T(8,128)(2,1)S(1)} %collective-permute-done.9.refs_0_, f32[16,2048]{1,0:T(8,128)S(1)} %get-tuple-element.25.refs_1_, bf16[16,2048]{1,0:T(8,128)(2,1)S(1)} %collective-permute-done.18.refs_2_, ...), custom_call_target="tpu_custom_call" | custom-call | tf_op jit(solution)/shard_map/pallas_call | solution.py:17
  49.0 9.8 %all_to_all.11 = f32[32,1,16]{2,1,0:T(1,128)S(1)} all-to-all(f32[32,1,16]{2,1,0:T(1,128)S(1)} %bitcast.19), channel_id=1, replica_groups=mesh['section'=1,'expert'=32] {'expert'}, dimensions={0} | all-to-all | bytes 4096 | tf_op jit(solution)/shard_map/all_to_all | solution.py:363
  58.9 0.5 shard_map.122
  (8 shorter events, 0.1 us)
Async XLA Ops:
  0.6 21.7 %collective-permute-start.4 = (bf16[2048,768]{1,0:T(8,128)(2,1)}, bf16[2048,768]{1,0:T(8,128)(2,1)S(1)}, u32[]{:S(2)}, u32[]{:S(2)}) collective-permute-start(bf16[2048,768]{1,0:T(8,128)(2,1)} %bitcast.20), channel_id=1, source_target_pairs={{0,1},{1,0},{2,3},{3,2},{4,5},{5,4},{6,7},{7,6},{8,9},{9,8},{10,11... | collective-permute-start | bytes 9437192 | tf_op jit(solution)/shard_map/ppermute | solution.py:40
  1.1 21.2 %collective-permute-start.5 = (bf16[384,2048]{1,0:T(8,128)(2,1)}, bf16[384,2048]{1,0:T(8,128)(2,1)S(1)}, u32[]{:S(2)}, u32[]{:S(2)}) collective-permute-start(bf16[384,2048]{1,0:T(8,128)(2,1)} %bitcast.22), channel_id=1, source_target_pairs={{0,1},{1,0},{2,3},{3,2},{4,5},{5,4},{6,7},{7,6},{8,9},{9,8},{10,11... | collective-permute-start | bytes 4718600 | tf_op jit(solution)/shard_map/ppermute | solution.py:40
  2.3 5.7 %collective-permute-start = (bf16[16,2176]{1,0:T(8,128)(2,1)S(1)}, bf16[16,2176]{1,0:T(8,128)(2,1)S(1)}, u32[]{:S(2)}, u32[]{:S(2)}) collective-permute-start(bf16[16,2176]{1,0:T(8,128)(2,1)S(1)} %shard_map.112.refs_0_), channel_id=1, source_target_pairs={{0,8},{1,9},{2,10},{3,11},{4,12},{5,13},{6,14},{7,15},{8,0},{9,1},... | collective-permute-start | bytes 208904 | tf_op jit(solution)/shard_map/ppermute | solution.py:40
  5.4 7.8 %collective-permute-start.10 = (bf16[16,2176]{1,0:T(8,128)(2,1)S(1)}, bf16[16,2176]{1,0:T(8,128)(2,1)S(1)}, u32[]{:S(2)}, u32[]{:S(2)}) collective-permute-start(bf16[16,2176]{1,0:T(8,128)(2,1)S(1)} %shard_map.112.refs_0_), channel_id=1, source_target_pairs={{0,16},{1,17},{2,18},{3,19},{4,20},{5,21},{6,22},{7,23},{8,24},{9,... | collective-permute-start | bytes 208904 | tf_op jit(solution)/shard_map/ppermute | solution.py:40
  8.0 6.7 %collective-permute-start.11 = (bf16[16,2176]{1,0:T(8,128)(2,1)S(1)}, bf16[16,2176]{1,0:T(8,128)(2,1)S(1)}, u32[]{:S(2)}, u32[]{:S(2)}) collective-permute-start(bf16[16,2176]{1,0:T(8,128)(2,1)S(1)} %shard_map.112.refs_0_), channel_id=1, source_target_pairs={{0,24},{1,25},{2,26},{3,27},{4,28},{5,29},{6,30},{7,31},{8,16},{9,... | collective-permute-start | bytes 208904 | tf_op jit(solution)/shard_map/ppermute | solution.py:40
  8.0 8.3 %collective-permute-start.1 = (bf16[32,2176]{1,0:T(8,128)(2,1)S(1)}, bf16[32,2176]{1,0:T(8,128)(2,1)S(1)}, u32[]{:S(2)}, u32[]{:S(2)}) collective-permute-start(bf16[32,2176]{1,0:T(8,128)(2,1)S(1)} %shard_map.113.refs_0_), channel_id=1, source_target_pairs={{0,2},{1,5},{2,0},{3,7},{4,6},{5,1},{6,4},{7,3},{8,10},{9,13},{10,... | collective-permute-start | bytes 417800 | tf_op jit(solution)/shard_map/ppermute | solution.py:40
  13.2 5.1 %collective-permute-start.2 = (bf16[32,2176]{1,0:T(8,128)(2,1)S(1)}, bf16[32,2176]{1,0:T(8,128)(2,1)S(1)}, u32[]{:S(2)}, u32[]{:S(2)}) collective-permute-start(bf16[32,2176]{1,0:T(8,128)(2,1)S(1)} %shard_map.113.refs_0_), channel_id=1, source_target_pairs={{0,4},{1,3},{2,6},{3,1},{4,0},{5,7},{6,2},{7,5},{8,12},{9,11},{10,... | collective-permute-start | bytes 417800 | tf_op jit(solution)/shard_map/ppermute | solution.py:40
  14.7 6.7 %collective-permute-start.12 = (bf16[32,2176]{1,0:T(8,128)(2,1)S(1)}, bf16[32,2176]{1,0:T(8,128)(2,1)S(1)}, u32[]{:S(2)}, u32[]{:S(2)}) collective-permute-start(bf16[32,2176]{1,0:T(8,128)(2,1)S(1)} %shard_map.117.refs_0_), channel_id=1, source_target_pairs={{0,2},{1,5},{2,0},{3,7},{4,6},{5,1},{6,4},{7,3},{8,10},{9,13},{10,... | collective-permute-start | bytes 417800 | tf_op jit(solution)/shard_map/ppermute | solution.py:40
  16.2 6.0 %collective-permute-start.3 = (bf16[32,2176]{1,0:T(8,128)(2,1)S(1)}, bf16[32,2176]{1,0:T(8,128)(2,1)S(1)}, u32[]{:S(2)}, u32[]{:S(2)}) collective-permute-start(bf16[32,2176]{1,0:T(8,128)(2,1)S(1)} %collective-permute-done.1.refs_1_), channel_id=1, source_target_pairs={{0,4},{1,3},{2,6},{3,1},{4,0},{5,7},{6,2},{7,5},{8,12},{9,11},{10,... | collective-permute-start | bytes 417800 | tf_op jit(solution)/shard_map/ppermute | solution.py:40
  18.2 9.0 %collective-permute-start.13 = (bf16[32,2176]{1,0:T(8,128)(2,1)S(1)}, bf16[32,2176]{1,0:T(8,128)(2,1)S(1)}, u32[]{:S(2)}, u32[]{:S(2)}) collective-permute-start(bf16[32,2176]{1,0:T(8,128)(2,1)S(1)} %shard_map.117.refs_0_), channel_id=1, source_target_pairs={{0,4},{1,3},{2,6},{3,1},{4,0},{5,7},{6,2},{7,5},{8,12},{9,11},{10,... | collective-permute-start | bytes 417800 | tf_op jit(solution)/shard_map/ppermute | solution.py:40
  21.4 5.9 %collective-permute-start.14 = (bf16[32,2176]{1,0:T(8,128)(2,1)S(1)}, bf16[32,2176]{1,0:T(8,128)(2,1)S(1)}, u32[]{:S(2)}, u32[]{:S(2)}) collective-permute-start(bf16[32,2176]{1,0:T(8,128)(2,1)S(1)} %collective-permute-done.12.refs_1_), channel_id=1, source_target_pairs={{0,4},{1,3},{2,6},{3,1},{4,0},{5,7},{6,2},{7,5},{8,12},{9,11},{10,... | collective-permute-start | bytes 417800 | tf_op jit(solution)/shard_map/ppermute | solution.py:40
  25.7 6.4 %collective-permute-start.7 = (bf16[32,2048]{1,0:T(8,128)(2,1)S(1)}, bf16[32,2048]{1,0:T(8,128)(2,1)S(1)}, u32[]{:S(2)}, u32[]{:S(2)}) collective-permute-start(bf16[32,2048]{1,0:T(8,128)(2,1)S(1)} %get-tuple-element.23), channel_id=1, source_target_pairs={{0,2},{1,5},{2,0},{3,7},{4,6},{5,1},{6,4},{7,3},{8,10},{9,13},{10,... | collective-permute-start | bytes 393224 | tf_op jit(solution)/shard_map/ppermute | solution.py:40
  27.2 21.1 %copy-start = (s32[1,1,8,8]{3,2,1,0:T(8,128)S(1)}, s32[1,1,8,8]{3,2,1,0:T(8,128)}, u32[]{:S(2)}) copy-start(s32[1,1,8,8]{3,2,1,0:T(8,128)} %param.11) | copy-start | bytes 772
  27.3 21.1 %copy-start.1 = (f32[1,1,8,8]{3,2,1,0:T(8,128)S(1)}, f32[1,1,8,8]{3,2,1,0:T(8,128)}, u32[]{:S(2)}) copy-start(f32[1,1,8,8]{3,2,1,0:T(8,128)} %param.13) | copy-start | bytes 772
  28.9 5.5 %collective-permute-start.16 = (bf16[32,2048]{1,0:T(8,128)(2,1)S(1)}, bf16[32,2048]{1,0:T(8,128)(2,1)S(1)}, u32[]{:S(2)}, u32[]{:S(2)}) collective-permute-start(bf16[32,2048]{1,0:T(8,128)(2,1)S(1)} %get-tuple-element.31), channel_id=1, source_target_pairs={{0,2},{1,5},{2,0},{3,7},{4,6},{5,1},{6,4},{7,3},{8,10},{9,13},{10,... | collective-permute-start | bytes 393224 | tf_op jit(solution)/shard_map/ppermute | solution.py:40
  30.2 5.8 %collective-permute-start.6 = (bf16[32,2048]{1,0:T(8,128)(2,1)S(1)}, bf16[32,2048]{1,0:T(8,128)(2,1)S(1)}, u32[]{:S(2)}, u32[]{:S(2)}) collective-permute-start(bf16[32,2048]{1,0:T(8,128)(2,1)S(1)} %get-tuple-element.21), channel_id=1, source_target_pairs={{0,2},{1,5},{2,0},{3,7},{4,6},{5,1},{6,4},{7,3},{8,10},{9,13},{10,... | collective-permute-start | bytes 393224 | tf_op jit(solution)/shard_map/ppermute | solution.py:40
  32.1 5.0 %collective-permute-start.8 = (bf16[32,2048]{1,0:T(8,128)(2,1)S(1)}, bf16[32,2048]{1,0:T(8,128)(2,1)S(1)}, u32[]{:S(2)}, u32[]{:S(2)}) collective-permute-start(bf16[32,2048]{1,0:T(8,128)(2,1)S(1)} %shard_map.115), channel_id=1, source_target_pairs={{0,4},{1,3},{2,6},{3,1},{4,0},{5,7},{6,2},{7,5},{8,12},{9,11},{10,... | collective-permute-start | bytes 393224 | tf_op jit(solution)/shard_map/ppermute | solution.py:40
  33.3 5.0 %collective-permute-start.15 = (bf16[32,2048]{1,0:T(8,128)(2,1)S(1)}, bf16[32,2048]{1,0:T(8,128)(2,1)S(1)}, u32[]{:S(2)}, u32[]{:S(2)}) collective-permute-start(bf16[32,2048]{1,0:T(8,128)(2,1)S(1)} %get-tuple-element.29), channel_id=1, source_target_pairs={{0,2},{1,5},{2,0},{3,7},{4,6},{5,1},{6,4},{7,3},{8,10},{9,13},{10,... | collective-permute-start | bytes 393224 | tf_op jit(solution)/shard_map/ppermute | solution.py:40
  34.4 5.0 %collective-permute-start.17 = (bf16[32,2048]{1,0:T(8,128)(2,1)S(1)}, bf16[32,2048]{1,0:T(8,128)(2,1)S(1)}, u32[]{:S(2)}, u32[]{:S(2)}) collective-permute-start(bf16[32,2048]{1,0:T(8,128)(2,1)S(1)} %shard_map.119), channel_id=1, source_target_pairs={{0,4},{1,3},{2,6},{3,1},{4,0},{5,7},{6,2},{7,5},{8,12},{9,11},{10,... | collective-permute-start | bytes 393224 | tf_op jit(solution)/shard_map/ppermute | solution.py:40
  37.2 5.6 %collective-permute-start.9 = (bf16[16,2048]{1,0:T(8,128)(2,1)S(1)}, bf16[16,2048]{1,0:T(8,128)(2,1)S(1)}, u32[]{:S(2)}, u32[]{:S(2)}) collective-permute-start(bf16[16,2048]{1,0:T(8,128)(2,1)S(1)} %get-tuple-element.24), channel_id=1, source_target_pairs={{0,8},{1,9},{2,10},{3,11},{4,12},{5,13},{6,14},{7,15},{8,0},{9,1},... | collective-permute-start | bytes 196616 | tf_op jit(solution)/shard_map/ppermute | solution.py:40
  39.5 6.2 %collective-permute-start.18 = (bf16[16,2048]{1,0:T(8,128)(2,1)S(1)}, bf16[16,2048]{1,0:T(8,128)(2,1)S(1)}, u32[]{:S(2)}, u32[]{:S(2)}) collective-permute-start(bf16[16,2048]{1,0:T(8,128)(2,1)S(1)} %get-tuple-element.32), channel_id=1, source_target_pairs={{0,24},{1,25},{2,26},{3,27},{4,28},{5,29},{6,30},{7,31},{8,16},{9,... | collective-permute-start | bytes 196616 | tf_op jit(solution)/shard_map/ppermute | solution.py:40
  42.8 5.6 %collective-permute-start.19 = (bf16[16,2048]{1,0:T(8,128)(2,1)S(1)}, bf16[16,2048]{1,0:T(8,128)(2,1)S(1)}, u32[]{:S(2)}, u32[]{:S(2)}) collective-permute-start(bf16[16,2048]{1,0:T(8,128)(2,1)S(1)} %get-tuple-element.33), channel_id=1, source_target_pairs={{0,16},{1,17},{2,18},{3,19},{4,20},{5,21},{6,22},{7,23},{8,24},{9,... | collective-permute-start | bytes 196616 | tf_op jit(solution)/shard_map/ppermute | solution.py:40

commit v10 on v8

--- a/solution.py
+++ b/solution.py
@@ -12,11 +12,12 @@
 MIB = 2**20
 
 
-def run_kernel(body, outs, operands, scratch=(), limit=16, space=pltpu.VMEM):
+def run_kernel(body, outs, operands, scratch=(), limit=16, space=pltpu.VMEM, tail=0):
+    spaces = [space] * (len(operands) - tail) + [pl.ANY] * tail
     return pl.pallas_call(
         body,
         out_shape=outs,
-        in_specs=[pl.BlockSpec(memory_space=space)] * len(operands),
+        in_specs=[pl.BlockSpec(memory_space=place) for place in spaces],
         out_specs=jax.tree.map(lambda _: pl.BlockSpec(memory_space=pltpu.VMEM), outs),
         scratch_shapes=list(scratch),
         compiler_params=pltpu.CompilerParams(vmem_limit_bytes=limit * MIB),
@@ -32,7 +33,10 @@
 
 
 def exclusive(value, mask):
-    pairs = [(source, source ^ mask) for source in range(lax.axis_size("expert"))]
+    masks = mask if isinstance(mask, tuple) else (mask,) * SPLIT
+    pairs = [
+        (source, source ^ masks[source % SPLIT]) for source in range(lax.axis_size("expert"))
+    ]
     return lax.ppermute(value, "expert", pairs)
 
 
@@ -91,6 +95,10 @@
     ).astype(jnp.bfloat16)
 
 
+def after(value, *awaited):
+    return lax.optimization_barrier((value, awaited))[0]
+
+
 def stage_kernel(count, *refs):
     sources, targets, sems = refs[:count], refs[count : 2 * count], refs[2 * count]
     copies = [
@@ -111,10 +119,6 @@
         [pltpu.SemaphoreType.DMA((len(arrays),))],
         space=pl.ANY,
     )
-
-
-def after(value, *awaited):
-    return lax.optimization_barrier((value, awaited))[0]
 
 
 def join_kernel(*refs):
@@ -236,11 +240,12 @@
     extra = -(-2 * experts // LANES) * LANES
     rows = 2 * tok_rows
     chips = devices // SPLIT
-    inner = min(4, chips)
+    inner = 4
     outer = chips // inner
-    inner_masks = [SPLIT * i for i in range(1, inner)]
+    first_axis, second_axis, both_axes = (SPLIT, 2 * SPLIT), (2 * SPLIT, SPLIT), 3 * SPLIT
     layer_mask = lambda j: SPLIT * inner * j
-    streams = [list(range(0, outer, 2)), list(range(1, outer, 2))]
+    nearer = list(range(1, outer // 2 + 1))
+    streams = [[j for j in range(outer) if j not in nearer], nearer]
     own_in, own_out = w_in[0, 0], w_out[0, 0]
     other_out, other_in = exclusive(own_out, 1), exclusive(own_in, 1)
 
@@ -287,32 +292,26 @@
             column[j] = exclusive(packed, layer_mask(j))
         if tick == 0:
             own = stage([in_hbm(own_in), in_hbm(own_out)])
+            weights = [own[0], other_in, own[1], other_out]
         blocks = []
         for stream, layers in enumerate(streams):
             joined = join_rows([column[j] for j in layers])
-            if stream == 0:
-                joined = after(joined, own)
-            else:
-                joined = after(joined, blocks[0][1])
-            block = [joined]
-            for mask in inner_masks:
-                block.append(exclusive(joined, mask))
-            blocks.append(block)
-        if tick == 0:
-            other = stage([other_in, other_out])
-            weights = [own[0], other[0], own[1], other[1]]
+            first = exclusive(joined, first_axis)
+            second = exclusive(joined, second_axis)
+            blocks.append([joined, first, second, exclusive(first, second_axis)])
         summed = []
         for stream, layers in enumerate(streams):
             partial = run_expert(
                 experts, blocks[stream], weights, [len(layers) * rows] * inner
             )
             returned = [partial[0]] + [
-                exclusive(part, mask) for part, mask in zip(partial[1:], inner_masks)
+                exclusive(part, axes)
+                for part, axes in zip(partial[1:], (first_axis, second_axis, both_axes))
             ]
             outs = [like(rows, model_width)] * len(layers)
             if stream == 0:
                 outs[0] = like(rows, model_width, jnp.float32)
-            sums = run_kernel(functools.partial(plane_kernel, inner), outs, returned)
+            sums = run_kernel(functools.partial(plane_kernel, len(returned)), outs, returned)
             for j, value in list(zip(layers, sums))[::-1]:
                 summed.append(exclusive(value, layer_mask(j)) if j else value)
         round_orig, round_pruned, tick_terms, *moe = run_kernel(

time: 61.3 us -> 62.8 us (1.024)
  waiting for transfers between devices: 10.9 us -> 12.6 us
  blocking collectives: 10 us -> 11.4 us
  starting transfers between devices: 31 us -> 29.7 us
    ppermute x20, waiting for transfers between devices: 10.9 us -> 12.6 us  [exclusive(): return lax.ppermute(value, 'expert', pairs)]
    all_to_all x1, blocking collectives: 10 us -> 11.4 us  [on_device(): lax.all_to_all(terms, 'expert', split_axis=0, concat_axis=0, tiled=True)]
    ppermute x20, starting transfers between devices: 31 us -> 29.7 us  [exclusive(): return lax.ppermute(value, 'expert', pairs)]
    pallas_call x11 -> x10, Pallas kernels: 8.5 us -> 8.17 us  [run_kernel(): pl.pallas_call(body, out_shape=outs, in_specs=[pl.BlockSpec(memory_space=...]
  transfers between devices with their start and end apart: 20 -> 20, of which waited for: 7 -> 7; matrix products, arithmetic and copies ran while one was open for 0% -> 0% of each run, Pallas kernels for 12% -> 11%
where the time goes in v10:
time: 62.8 us; the launch traced here: 62.6 us
  starting transfers between devices  29.7 us (47%)
  waiting for transfers between devices  12.6 us (20%)
  blocking collectives  11.4 us (18%)
  Pallas kernels  8.17 us (13%)
  between operations  0.72 us (1%)
    ppermute x20, starting transfers between devices, exclusive(): return lax.ppermute(value, 'expert', pairs)  29.7 us
    ppermute x20, waiting for transfers between devices, exclusive(): return lax.ppermute(value, 'expert', pairs)  12.6 us
    all_to_all x1, blocking collectives, on_device(): lax.all_to_all(terms, 'expert', split_axis=0, concat_axis=0, tiled=True)  11.4 us
    pallas_call x10, Pallas kernels, run_kernel(): pl.pallas_call(body, out_shape=outs, in_specs=[pl.BlockSpec(memory_space=...  8.17 us
  transfers between devices with their start and end apart: 20, of which 7 were waited for; matrix products, arithmetic and copies ran while one was open for 0% of the time, Pallas kernels for 11%

profile of v10, /device:TPU:0, one launch (start us, length us, event | category | flops | bytes accessed | tf_op | source)
XLA Modules:
  0.0 62.6 jit_solution(14567709545225134881)
XLA Ops:
  0.6 0.5 collective-permute-start.4
  1.1 0.1 collective-permute-start.5
  1.2 1.1 %shard_map.112.refs_0_ = bf16[16,2176]{1,0:T(8,128)(2,1)S(1)} custom-call(bf16[8,2048]{1,0:T(8,128)(2,1)} %bitcast.24, bf16[8,2048]{1,0:T(8,128)(2,1)} %bitcast.25, s32[8,8]{1,0:T(8,128)} %bitcast.15, s32[8,8]{1,0:T(8,128)} %bitcast.26, f32[8,8]{1,0:T(8,128)} %bitcast.17, f32[8,8]{1,0:T(8,128)} %bitcast.27, s32[1,16]{1,0:T(1,128)} %refs_6_.1), custom_call_target="tpu_custom_call" | custom-call | tf_op jit(solution)/shard_map/pallas_call | solution.py:17
  2.3 3.1 %collective-permute-start.10 = (bf16[16,2176]{1,0:T(8,128)(2,1)S(1)}, bf16[16,2176]{1,0:T(8,128)(2,1)S(1)}, u32[]{:S(2)}, u32[]{:S(2)}) collective-permute-start(bf16[16,2176]{1,0:T(8,128)(2,1)S(1)} %shard_map.112.refs_0_), channel_id=1, source_target_pairs={{0,8},{1,9},{2,10},{3,11},{4,12},{5,13},{6,14},{7,15},{8,0},{9,1},... | collective-permute-start | bytes 208904 | tf_op jit(solution)/shard_map/ppermute | solution.py:40
  5.4 2.6 %collective-permute-start.11 = (bf16[16,2176]{1,0:T(8,128)(2,1)S(1)}, bf16[16,2176]{1,0:T(8,128)(2,1)S(1)}, u32[]{:S(2)}, u32[]{:S(2)}) collective-permute-start(bf16[16,2176]{1,0:T(8,128)(2,1)S(1)} %shard_map.112.refs_0_), channel_id=1, source_target_pairs={{0,16},{1,17},{2,18},{3,19},{4,20},{5,21},{6,22},{7,23},{8,24},{9,... | collective-permute-start | bytes 208904 | tf_op jit(solution)/shard_map/ppermute | solution.py:40
  8.0 0.0 collective-permute-done.10.refs_0_
  8.0 3.7 %collective-permute-done.11.refs_1_ = bf16[16,2176]{1,0:T(8,128)(2,1)S(1)} collective-permute-done((bf16[16,2176]{1,0:T(8,128)(2,1)S(1)}, bf16[16,2176]{1,0:T(8,128)(2,1)S(1)}, u32[]{:S(2)}, u32[]{:S(2)}) %collective-permute-start.11) | collective-permute-done | bytes 69664 | tf_op jit(solution)/shard_map/ppermute | solution.py:40
  11.7 1.6 %collective-permute-start.12 = (bf16[32,2176]{1,0:T(8,128)(2,1)S(1)}, bf16[32,2176]{1,0:T(8,128)(2,1)S(1)}, u32[]{:S(2)}, u32[]{:S(2)}) collective-permute-start(bf16[32,2176]{1,0:T(8,128)(2,1)S(1)} %shard_map.117.refs_0_), channel_id=1, source_target_pairs={{0,2},{1,5},{2,0},{3,7},{4,6},{5,1},{6,4},{7,3},{8,10},{9,13},{10,... | collective-permute-start | bytes 417800 | tf_op jit(solution)/shard_map/ppermute | solution.py:40
  13.3 2.7 %collective-permute-start = (bf16[16,2176]{1,0:T(8,128)(2,1)S(1)}, bf16[16,2176]{1,0:T(8,128)(2,1)S(1)}, u32[]{:S(2)}, u32[]{:S(2)}) collective-permute-start(bf16[16,2176]{1,0:T(8,128)(2,1)S(1)} %shard_map.112.refs_0_), channel_id=1, source_target_pairs={{0,24},{1,25},{2,26},{3,27},{4,28},{5,29},{6,30},{7,31},{8,16},{9,... | collective-permute-start | bytes 208904 | tf_op jit(solution)/shard_map/ppermute | solution.py:40
  16.0 1.5 %collective-permute-start.13 = (bf16[32,2176]{1,0:T(8,128)(2,1)S(1)}, bf16[32,2176]{1,0:T(8,128)(2,1)S(1)}, u32[]{:S(2)}, u32[]{:S(2)}) collective-permute-start(bf16[32,2176]{1,0:T(8,128)(2,1)S(1)} %shard_map.117.refs_0_), channel_id=1, source_target_pairs={{0,4},{1,3},{2,6},{3,1},{4,0},{5,7},{6,2},{7,5},{8,12},{9,11},{10,... | collective-permute-start | bytes 417800 | tf_op jit(solution)/shard_map/ppermute | solution.py:40
  17.5 1.9 %collective-permute-done.refs_1_ = bf16[16,2176]{1,0:T(8,128)(2,1)S(1)} collective-permute-done((bf16[16,2176]{1,0:T(8,128)(2,1)S(1)}, bf16[16,2176]{1,0:T(8,128)(2,1)S(1)}, u32[]{:S(2)}, u32[]{:S(2)}) %collective-permute-start) | collective-permute-done | bytes 69664 | tf_op jit(solution)/shard_map/ppermute | solution.py:40
  19.4 0.6 collective-permute-start.1
  20.0 0.0 collective-permute-done.12.refs_1_
  20.0 1.5 %collective-permute-start.14 = (bf16[32,2176]{1,0:T(8,128)(2,1)S(1)}, bf16[32,2176]{1,0:T(8,128)(2,1)S(1)}, u32[]{:S(2)}, u32[]{:S(2)}) collective-permute-start(bf16[32,2176]{1,0:T(8,128)(2,1)S(1)} %collective-permute-done.12.refs_1_), channel_id=1, source_target_pairs={{0,4},{1,3},{2,6},{3,1},{4,0},{5,7},{6,2},{7,5},{8,12},{9,11},{10,... | collective-permute-start | bytes 417800 | tf_op jit(solution)/shard_map/ppermute | solution.py:40
  21.5 0.0 collective-permute-done.13.refs_2_
  21.5 1.0 %collective-permute-start.2 = (bf16[32,2176]{1,0:T(8,128)(2,1)S(1)}, bf16[32,2176]{1,0:T(8,128)(2,1)S(1)}, u32[]{:S(2)}, u32[]{:S(2)}) collective-permute-start(bf16[32,2176]{1,0:T(8,128)(2,1)S(1)} %shard_map.113.refs_0_), channel_id=1, source_target_pairs={{0,4},{1,3},{2,6},{3,1},{4,0},{5,7},{6,2},{7,5},{8,12},{9,11},{10,... | collective-permute-start | bytes 417800 | tf_op jit(solution)/shard_map/ppermute | solution.py:40
  22.6 2.6 %collective-permute-done.1.refs_1_ = bf16[32,2176]{1,0:T(8,128)(2,1)S(1)} collective-permute-done((bf16[32,2176]{1,0:T(8,128)(2,1)S(1)}, bf16[32,2176]{1,0:T(8,128)(2,1)S(1)}, u32[]{:S(2)}, u32[]{:S(2)}) %collective-permute-start.1) | collective-permute-done | bytes 139296 | tf_op jit(solution)/shard_map/ppermute | solution.py:40
  25.2 1.2 %collective-permute-start.3 = (bf16[32,2176]{1,0:T(8,128)(2,1)S(1)}, bf16[32,2176]{1,0:T(8,128)(2,1)S(1)}, u32[]{:S(2)}, u32[]{:S(2)}) collective-permute-start(bf16[32,2176]{1,0:T(8,128)(2,1)S(1)} %collective-permute-done.1.refs_1_), channel_id=1, source_target_pairs={{0,4},{1,3},{2,6},{3,1},{4,0},{5,7},{6,2},{7,5},{8,12},{9,11},{10,... | collective-permute-start | bytes 417800 | tf_op jit(solution)/shard_map/ppermute | solution.py:40
  26.4 2.4 %shard_map.114 = (bf16[2048,768]{1,0:T(8,128)(2,1)S(1)}, bf16[384,2048]{1,0:T(8,128)(2,1)S(1)}) custom-call(bf16[2048,768]{1,0:T(8,128)(2,1)} %bitcast.21, bf16[384,2048]{1,0:T(8,128)(2,1)} %bitcast.23), custom_call_target="tpu_custom_call" | custom-call | tf_op jit(solution)/shard_map/pallas_call | solution.py:17
  28.8 0.0 collective-permute-done.14.refs_3_
  28.8 0.0 collective-permute-done.5.refs_7_
  28.8 0.0 collective-permute-done.4.refs_5_
  28.8 1.7 %shard_map.118 = (bf16[32,2048]{1,0:T(8,128)(2,1)S(1)}, bf16[32,2048]{1,0:T(8,128)(2,1)S(1)}, bf16[32,2048]{1,0:T(8,128)(2,1)S(1)}, bf16[32,2048]{1,0:T(8,128)(2,1)S(1)}) custom-call(bf16[32,2176]{1,0:T(8,128)(2,1)S(1)} %shard_map.117.refs_0_, bf16[32,2176]{1,0:T(8,128)(2,1)S(1)} %collective-permute-done.12.refs_1_, ...), custom_call_target="tpu_custom_call" | custom-call | tf_op jit(solution)/shard_map/pallas_call | solution.py:17
  30.6 1.6 %collective-permute-start.15 = (bf16[32,2048]{1,0:T(8,128)(2,1)S(1)}, bf16[32,2048]{1,0:T(8,128)(2,1)S(1)}, u32[]{:S(2)}, u32[]{:S(2)}) collective-permute-start(bf16[32,2048]{1,0:T(8,128)(2,1)S(1)} %get-tuple-element.29), channel_id=1, source_target_pairs={{0,2},{1,5},{2,0},{3,7},{4,6},{5,1},{6,4},{7,3},{8,10},{9,13},{10,... | collective-permute-start | bytes 393224 | tf_op jit(solution)/shard_map/ppermute | solution.py:40
  32.2 0.0 collective-permute-start.16
  32.2 1.9 %collective-permute-start.17 = (bf16[32,2048]{1,0:T(8,128)(2,1)S(1)}, bf16[32,2048]{1,0:T(8,128)(2,1)S(1)}, u32[]{:S(2)}, u32[]{:S(2)}) collective-permute-start(bf16[32,2048]{1,0:T(8,128)(2,1)S(1)} %get-tuple-element.31), channel_id=1, source_target_pairs={{0,6},{1,7},{2,4},{3,5},{4,2},{5,3},{6,0},{7,1},{8,14},{9,15},{10,... | collective-permute-start | bytes 393224 | tf_op jit(solution)/shard_map/ppermute | solution.py:40
  34.1 0.0 collective-permute-done.2.refs_2_
  34.1 0.0 collective-permute-done.3.refs_3_
  34.2 1.6 %shard_map.115 = (bf16[32,2048]{1,0:T(8,128)(2,1)S(1)}, bf16[32,2048]{1,0:T(8,128)(2,1)S(1)}, bf16[32,2048]{1,0:T(8,128)(2,1)S(1)}, bf16[32,2048]{1,0:T(8,128)(2,1)S(1)}) custom-call(bf16[32,2176]{1,0:T(8,128)(2,1)S(1)} %shard_map.113.refs_0_, bf16[32,2176]{1,0:T(8,128)(2,1)S(1)} %collective-permute-done.1.refs_1_, ...), custom_call_target="tpu_custom_call" | custom-call | tf_op jit(solution)/shard_map/pallas_call | solution.py:17
  35.8 1.6 %collective-permute-start.6 = (bf16[32,2048]{1,0:T(8,128)(2,1)S(1)}, bf16[32,2048]{1,0:T(8,128)(2,1)S(1)}, u32[]{:S(2)}, u32[]{:S(2)}) collective-permute-start(bf16[32,2048]{1,0:T(8,128)(2,1)S(1)} %get-tuple-element.23), channel_id=1, source_target_pairs={{0,2},{1,5},{2,0},{3,7},{4,6},{5,1},{6,4},{7,3},{8,10},{9,13},{10,... | collective-permute-start | bytes 393224 | tf_op jit(solution)/shard_map/ppermute | solution.py:40
  37.4 0.0 collective-permute-start.7
  37.4 0.0 collective-permute-done.15.refs_1_
  37.4 1.9 %collective-permute-start.8 = (bf16[32,2048]{1,0:T(8,128)(2,1)S(1)}, bf16[32,2048]{1,0:T(8,128)(2,1)S(1)}, u32[]{:S(2)}, u32[]{:S(2)}) collective-permute-start(bf16[32,2048]{1,0:T(8,128)(2,1)S(1)} %get-tuple-element.25), channel_id=1, source_target_pairs={{0,6},{1,7},{2,4},{3,5},{4,2},{5,3},{6,0},{7,1},{8,14},{9,15},{10,... | collective-permute-start | bytes 393224 | tf_op jit(solution)/shard_map/ppermute | solution.py:40
  39.4 0.0 collective-permute-done.16.refs_2_
  39.4 0.2 collective-permute-done.17.refs_3_
  39.5 0.1 shard_map.119
  39.6 0.3 collective-permute-start.18
  39.9 3.3 %collective-permute-start.19 = (bf16[16,2048]{1,0:T(8,128)(2,1)S(1)}, bf16[16,2048]{1,0:T(8,128)(2,1)S(1)}, u32[]{:S(2)}, u32[]{:S(2)}) collective-permute-start(bf16[16,2048]{1,0:T(8,128)(2,1)S(1)} %get-tuple-element.33), channel_id=1, source_target_pairs={{0,8},{1,9},{2,10},{3,11},{4,12},{5,13},{6,14},{7,15},{8,0},{9,1},... | collective-permute-start | bytes 196616 | tf_op jit(solution)/shard_map/ppermute | solution.py:40
  43.3 0.0 collective-permute-done.6.refs_1_
  43.3 0.5 collective-permute-done.7.refs_2_
  43.8 0.1 shard_map.116
  43.9 2.6 %collective-permute-start.9 = (bf16[16,2048]{1,0:T(8,128)(2,1)S(1)}, bf16[16,2048]{1,0:T(8,128)(2,1)S(1)}, u32[]{:S(2)}, u32[]{:S(2)}) collective-permute-start(bf16[16,2048]{1,0:T(8,128)(2,1)S(1)} %get-tuple-element.26), channel_id=1, source_target_pairs={{0,24},{1,25},{2,26},{3,27},{4,28},{5,29},{6,30},{7,31},{8,16},{9,... | collective-permute-start | bytes 196616 | tf_op jit(solution)/shard_map/ppermute | solution.py:40
  46.4 0.0 collective-permute-done.18.refs_2_
  46.4 0.3 collective-permute-done.19.refs_3_
  46.7 3.3 %collective-permute-done.9.refs_0_ = bf16[16,2048]{1,0:T(8,128)(2,1)S(1)} collective-permute-done((bf16[16,2048]{1,0:T(8,128)(2,1)S(1)}, bf16[16,2048]{1,0:T(8,128)(2,1)S(1)}, u32[]{:S(2)}, u32[]{:S(2)}) %collective-permute-start.9) | collective-permute-done | bytes 65568 | tf_op jit(solution)/shard_map/ppermute | solution.py:40
  50.0 0.7 %shard_map.120 = (bf16[8,2048]{1,0:T(8,128)(2,1)}, bf16[8,2048]{1,0:T(8,128)(2,1)}, f32[32,16]{1,0:T(8,128)S(1)}) custom-call(bf16[16,2048]{1,0:T(8,128)(2,1)S(1)} %collective-permute-done.9.refs_0_, f32[16,2048]{1,0:T(8,128)S(1)} %get-tuple-element.27.refs_1_, bf16[16,2048]{1,0:T(8,128)(2,1)S(1)} %collective-permute-done.18.refs_2_, ...), custom_call_target="tpu_custom_call" | custom-call | tf_op jit(solution)/shard_map/pallas_call | solution.py:17
  50.7 11.4 %all_to_all.11 = f32[32,1,16]{2,1,0:T(1,128)S(1)} all-to-all(f32[32,1,16]{2,1,0:T(1,128)S(1)} %bitcast.19), channel_id=1, replica_groups=mesh['section'=1,'expert'=32] {'expert'}, dimensions={0} | all-to-all | bytes 4096 | tf_op jit(solution)/shard_map/all_to_all | solution.py:336
  62.0 0.5 shard_map.121
  (7 shorter events, 0.0 us)
Async XLA Ops:
  0.6 28.2 %collective-permute-start.4 = (bf16[2048,768]{1,0:T(8,128)(2,1)}, bf16[2048,768]{1,0:T(8,128)(2,1)S(1)}, u32[]{:S(2)}, u32[]{:S(2)}) collective-permute-start(bf16[2048,768]{1,0:T(8,128)(2,1)} %bitcast.20), channel_id=1, source_target_pairs={{0,1},{1,0},{2,3},{3,2},{4,5},{5,4},{6,7},{7,6},{8,9},{9,8},{10,11... | collective-permute-start | bytes 9437192 | tf_op jit(solution)/shard_map/ppermute | solution.py:40
  1.1 27.7 %collective-permute-start.5 = (bf16[384,2048]{1,0:T(8,128)(2,1)}, bf16[384,2048]{1,0:T(8,128)(2,1)S(1)}, u32[]{:S(2)}, u32[]{:S(2)}) collective-permute-start(bf16[384,2048]{1,0:T(8,128)(2,1)} %bitcast.22), channel_id=1, source_target_pairs={{0,1},{1,0},{2,3},{3,2},{4,5},{5,4},{6,7},{7,6},{8,9},{9,8},{10,11... | collective-permute-start | bytes 4718600 | tf_op jit(solution)/shard_map/ppermute | solution.py:40
  2.3 5.7 %collective-permute-start.10 = (bf16[16,2176]{1,0:T(8,128)(2,1)S(1)}, bf16[16,2176]{1,0:T(8,128)(2,1)S(1)}, u32[]{:S(2)}, u32[]{:S(2)}) collective-permute-start(bf16[16,2176]{1,0:T(8,128)(2,1)S(1)} %shard_map.112.refs_0_), channel_id=1, source_target_pairs={{0,8},{1,9},{2,10},{3,11},{4,12},{5,13},{6,14},{7,15},{8,0},{9,1},... | collective-permute-start | bytes 208904 | tf_op jit(solution)/shard_map/ppermute | solution.py:40
  5.4 6.3 %collective-permute-start.11 = (bf16[16,2176]{1,0:T(8,128)(2,1)S(1)}, bf16[16,2176]{1,0:T(8,128)(2,1)S(1)}, u32[]{:S(2)}, u32[]{:S(2)}) collective-permute-start(bf16[16,2176]{1,0:T(8,128)(2,1)S(1)} %shard_map.112.refs_0_), channel_id=1, source_target_pairs={{0,16},{1,17},{2,18},{3,19},{4,20},{5,21},{6,22},{7,23},{8,24},{9,... | collective-permute-start | bytes 208904 | tf_op jit(solution)/shard_map/ppermute | solution.py:40
  11.7 8.3 %collective-permute-start.12 = (bf16[32,2176]{1,0:T(8,128)(2,1)S(1)}, bf16[32,2176]{1,0:T(8,128)(2,1)S(1)}, u32[]{:S(2)}, u32[]{:S(2)}) collective-permute-start(bf16[32,2176]{1,0:T(8,128)(2,1)S(1)} %shard_map.117.refs_0_), channel_id=1, source_target_pairs={{0,2},{1,5},{2,0},{3,7},{4,6},{5,1},{6,4},{7,3},{8,10},{9,13},{10,... | collective-permute-start | bytes 417800 | tf_op jit(solution)/shard_map/ppermute | solution.py:40
  13.3 6.1 %collective-permute-start = (bf16[16,2176]{1,0:T(8,128)(2,1)S(1)}, bf16[16,2176]{1,0:T(8,128)(2,1)S(1)}, u32[]{:S(2)}, u32[]{:S(2)}) collective-permute-start(bf16[16,2176]{1,0:T(8,128)(2,1)S(1)} %shard_map.112.refs_0_), channel_id=1, source_target_pairs={{0,24},{1,25},{2,26},{3,27},{4,28},{5,29},{6,30},{7,31},{8,16},{9,... | collective-permute-start | bytes 208904 | tf_op jit(solution)/shard_map/ppermute | solution.py:40
  16.0 5.6 %collective-permute-start.13 = (bf16[32,2176]{1,0:T(8,128)(2,1)S(1)}, bf16[32,2176]{1,0:T(8,128)(2,1)S(1)}, u32[]{:S(2)}, u32[]{:S(2)}) collective-permute-start(bf16[32,2176]{1,0:T(8,128)(2,1)S(1)} %shard_map.117.refs_0_), channel_id=1, source_target_pairs={{0,4},{1,3},{2,6},{3,1},{4,0},{5,7},{6,2},{7,5},{8,12},{9,11},{10,... | collective-permute-start | bytes 417800 | tf_op jit(solution)/shard_map/ppermute | solution.py:40
  19.4 5.8 %collective-permute-start.1 = (bf16[32,2176]{1,0:T(8,128)(2,1)S(1)}, bf16[32,2176]{1,0:T(8,128)(2,1)S(1)}, u32[]{:S(2)}, u32[]{:S(2)}) collective-permute-start(bf16[32,2176]{1,0:T(8,128)(2,1)S(1)} %shard_map.113.refs_0_), channel_id=1, source_target_pairs={{0,2},{1,5},{2,0},{3,7},{4,6},{5,1},{6,4},{7,3},{8,10},{9,13},{10,... | collective-permute-start | bytes 417800 | tf_op jit(solution)/shard_map/ppermute | solution.py:40
  20.0 8.8 %collective-permute-start.14 = (bf16[32,2176]{1,0:T(8,128)(2,1)S(1)}, bf16[32,2176]{1,0:T(8,128)(2,1)S(1)}, u32[]{:S(2)}, u32[]{:S(2)}) collective-permute-start(bf16[32,2176]{1,0:T(8,128)(2,1)S(1)} %collective-permute-done.12.refs_1_), channel_id=1, source_target_pairs={{0,4},{1,3},{2,6},{3,1},{4,0},{5,7},{6,2},{7,5},{8,12},{9,11},{10,... | collective-permute-start | bytes 417800 | tf_op jit(solution)/shard_map/ppermute | solution.py:40
  21.5 12.6 %collective-permute-start.2 = (bf16[32,2176]{1,0:T(8,128)(2,1)S(1)}, bf16[32,2176]{1,0:T(8,128)(2,1)S(1)}, u32[]{:S(2)}, u32[]{:S(2)}) collective-permute-start(bf16[32,2176]{1,0:T(8,128)(2,1)S(1)} %shard_map.113.refs_0_), channel_id=1, source_target_pairs={{0,4},{1,3},{2,6},{3,1},{4,0},{5,7},{6,2},{7,5},{8,12},{9,11},{10,... | collective-permute-start | bytes 417800 | tf_op jit(solution)/shard_map/ppermute | solution.py:40
  25.2 9.0 %collective-permute-start.3 = (bf16[32,2176]{1,0:T(8,128)(2,1)S(1)}, bf16[32,2176]{1,0:T(8,128)(2,1)S(1)}, u32[]{:S(2)}, u32[]{:S(2)}) collective-permute-start(bf16[32,2176]{1,0:T(8,128)(2,1)S(1)} %collective-permute-done.1.refs_1_), channel_id=1, source_target_pairs={{0,4},{1,3},{2,6},{3,1},{4,0},{5,7},{6,2},{7,5},{8,12},{9,11},{10,... | collective-permute-start | bytes 417800 | tf_op jit(solution)/shard_map/ppermute | solution.py:40
  30.6 6.8 %collective-permute-start.15 = (bf16[32,2048]{1,0:T(8,128)(2,1)S(1)}, bf16[32,2048]{1,0:T(8,128)(2,1)S(1)}, u32[]{:S(2)}, u32[]{:S(2)}) collective-permute-start(bf16[32,2048]{1,0:T(8,128)(2,1)S(1)} %get-tuple-element.29), channel_id=1, source_target_pairs={{0,2},{1,5},{2,0},{3,7},{4,6},{5,1},{6,4},{7,3},{8,10},{9,13},{10,... | collective-permute-start | bytes 393224 | tf_op jit(solution)/shard_map/ppermute | solution.py:40
  32.2 7.2 %collective-permute-start.16 = (bf16[32,2048]{1,0:T(8,128)(2,1)S(1)}, bf16[32,2048]{1,0:T(8,128)(2,1)S(1)}, u32[]{:S(2)}, u32[]{:S(2)}) collective-permute-start(bf16[32,2048]{1,0:T(8,128)(2,1)S(1)} %get-tuple-element.30), channel_id=1, source_target_pairs={{0,4},{1,3},{2,6},{3,1},{4,0},{5,7},{6,2},{7,5},{8,12},{9,11},{10,... | collective-permute-start | bytes 393224 | tf_op jit(solution)/shard_map/ppermute | solution.py:40
  32.2 17.8 %copy-start = (s32[1,1,8,8]{3,2,1,0:T(8,128)S(1)}, s32[1,1,8,8]{3,2,1,0:T(8,128)}, u32[]{:S(2)}) copy-start(s32[1,1,8,8]{3,2,1,0:T(8,128)} %param.11) | copy-start | bytes 772
  32.2 17.8 %copy-start.1 = (f32[1,1,8,8]{3,2,1,0:T(8,128)S(1)}, f32[1,1,8,8]{3,2,1,0:T(8,128)}, u32[]{:S(2)}) copy-start(f32[1,1,8,8]{3,2,1,0:T(8,128)} %param.13) | copy-start | bytes 772
  32.2 7.3 %collective-permute-start.17 = (bf16[32,2048]{1,0:T(8,128)(2,1)S(1)}, bf16[32,2048]{1,0:T(8,128)(2,1)S(1)}, u32[]{:S(2)}, u32[]{:S(2)}) collective-permute-start(bf16[32,2048]{1,0:T(8,128)(2,1)S(1)} %get-tuple-element.31), channel_id=1, source_target_pairs={{0,6},{1,7},{2,4},{3,5},{4,2},{5,3},{6,0},{7,1},{8,14},{9,15},{10,... | collective-permute-start | bytes 393224 | tf_op jit(solution)/shard_map/ppermute | solution.py:40
  35.8 7.5 %collective-permute-start.6 = (bf16[32,2048]{1,0:T(8,128)(2,1)S(1)}, bf16[32,2048]{1,0:T(8,128)(2,1)S(1)}, u32[]{:S(2)}, u32[]{:S(2)}) collective-permute-start(bf16[32,2048]{1,0:T(8,128)(2,1)S(1)} %get-tuple-element.23), channel_id=1, source_target_pairs={{0,2},{1,5},{2,0},{3,7},{4,6},{5,1},{6,4},{7,3},{8,10},{9,13},{10,... | collective-permute-start | bytes 393224 | tf_op jit(solution)/shard_map/ppermute | solution.py:40
  37.4 6.4 %collective-permute-start.7 = (bf16[32,2048]{1,0:T(8,128)(2,1)S(1)}, bf16[32,2048]{1,0:T(8,128)(2,1)S(1)}, u32[]{:S(2)}, u32[]{:S(2)}) collective-permute-start(bf16[32,2048]{1,0:T(8,128)(2,1)S(1)} %get-tuple-element.24), channel_id=1, source_target_pairs={{0,4},{1,3},{2,6},{3,1},{4,0},{5,7},{6,2},{7,5},{8,12},{9,11},{10,... | collective-permute-start | bytes 393224 | tf_op jit(solution)/shard_map/ppermute | solution.py:40
  37.4 6.4 %collective-permute-start.8 = (bf16[32,2048]{1,0:T(8,128)(2,1)S(1)}, bf16[32,2048]{1,0:T(8,128)(2,1)S(1)}, u32[]{:S(2)}, u32[]{:S(2)}) collective-permute-start(bf16[32,2048]{1,0:T(8,128)(2,1)S(1)} %get-tuple-element.25), channel_id=1, source_target_pairs={{0,6},{1,7},{2,4},{3,5},{4,2},{5,3},{6,0},{7,1},{8,14},{9,15},{10,... | collective-permute-start | bytes 393224 | tf_op jit(solution)/shard_map/ppermute | solution.py:40
  39.6 6.8 %collective-permute-start.18 = (bf16[16,2048]{1,0:T(8,128)(2,1)S(1)}, bf16[16,2048]{1,0:T(8,128)(2,1)S(1)}, u32[]{:S(2)}, u32[]{:S(2)}) collective-permute-start(bf16[16,2048]{1,0:T(8,128)(2,1)S(1)} %get-tuple-element.32), channel_id=1, source_target_pairs={{0,16},{1,17},{2,18},{3,19},{4,20},{5,21},{6,22},{7,23},{8,24},{9,... | collective-permute-start | bytes 196616 | tf_op jit(solution)/shard_map/ppermute | solution.py:40
  39.9 6.8 %collective-permute-start.19 = (bf16[16,2048]{1,0:T(8,128)(2,1)S(1)}, bf16[16,2048]{1,0:T(8,128)(2,1)S(1)}, u32[]{:S(2)}, u32[]{:S(2)}) collective-permute-start(bf16[16,2048]{1,0:T(8,128)(2,1)S(1)} %get-tuple-element.33), channel_id=1, source_target_pairs={{0,8},{1,9},{2,10},{3,11},{4,12},{5,13},{6,14},{7,15},{8,0},{9,1},... | collective-permute-start | bytes 196616 | tf_op jit(solution)/shard_map/ppermute | solution.py:40
  43.9 6.1 %collective-permute-start.9 = (bf16[16,2048]{1,0:T(8,128)(2,1)S(1)}, bf16[16,2048]{1,0:T(8,128)(2,1)S(1)}, u32[]{:S(2)}, u32[]{:S(2)}) collective-permute-start(bf16[16,2048]{1,0:T(8,128)(2,1)S(1)} %get-tuple-element.26), channel_id=1, source_target_pairs={{0,24},{1,25},{2,26},{3,27},{4,28},{5,29},{6,30},{7,31},{8,16},{9,... | collective-permute-start | bytes 196616 | tf_op jit(solution)/shard_map/ppermute | solution.py:40
